TPU v7x, 32 devices: a whole 2x2x4 slice. The times are simulated.
32 devices in a mesh: panel: 2 (over y), row: 4 (over z), layer: 4 (over x, core).
Axes of the slice: x: 2, y: 2, z: 4, core: 2. Of those that a mesh axis runs over, the one named last changes fastest.
Arguments:
- layers: bfloat16 [4, 8192, 512], P('layer', 'row', 'panel'), parts along dimension 2, may hold values from -6 to 6
- table: bfloat16 [16, 128, 64], replicated, may hold values from -0.375 to 0.375
- fitting: bfloat16 [8192, 6600], P('row', 'layer'), may hold values from -0.09375 to 0.09375
- owner: int32 [4, 128, 1], P('layer', 'row'), may hold values from 0 to 3; in each aligned block of 32 rows (0 to 31, 32 to 63, ..., all dimensions but the last counted through in order) at most 16 rows name the same one
- local_slice: int32 [4, 128], P('layer', 'row'), may hold values from 0 to 15
- block_index: int32 [4, 128], P('layer', 'row'), may hold values from 0 to 31
- weight_index: int32 [4, 128], P('layer', 'row'), may hold values from 0 to 15
Outputs:
- actuators: bfloat16 [512, 6600], P(('panel', 'row'), 'layer'), parts along dimension 0
There are 2 independent parts, one for each index of `panel`. A program takes and returns all parts, laid end to end along the dimension named above; an argument that names none is the same for every part. Nothing has to cross between parts.
Inputs may be any that keep to these rules, and one draw needn't show every extreme that they name: `owner`: within the 32 entries of one layer on one row device (aligned blocks of 32 entries), no value is named more than 16 times, and in every draw some block names one value exactly 16 times.
All inputs are finite; a program needn't handle non-finite values.
Results may differ from a plain program's by a relative error of at most 0.0058.
Values may be sent and summed in bfloat16 or wider, within the bound.
No kernel may reach another device: no remote copies, remote signals or barrier semaphores. Data moves between devices by JAX's collectives and lax.ppermute only.
A program may use at most 64 MiB of HBM per device.

v0:
```python
import functools

import jax
import jax.numpy as jnp
from jax import lax
from jax.experimental import pallas as pl
from jax.experimental.pallas import tpu as pltpu
from jax.sharding import PartitionSpec as P

LANES = 128
CODE_ROWS = 16
F32, BF16 = jnp.float32, jnp.bfloat16
VMEM = pl.BlockSpec(memory_space=pltpu.VMEM)
ANY = pl.BlockSpec(memory_space=pl.ANY)
PARAMS = dict(vmem_limit_bytes=16 * 1024 * 1024)


def turn_kernel(n_layer, n_row, halves, half, layers_ref, extra_ref, *refs):
    outs, codes = refs[:n_layer], refs[-1]
    rows_dev, columns = layers_ref.shape
    per_half = columns // halves
    each = per_half // n_layer
    chunk, part = columns // n_row, columns // n_row // halves
    first = lax.axis_index("layer") * each
    row = lax.broadcasted_iota(jnp.int32, (per_half, columns), 0)
    col = lax.broadcasted_iota(jnp.int32, (per_half, columns), 1)
    place = lax.rem(row + first, per_half)
    wanted = (place // part) * chunk + lax.rem(place, part) + half * part
    pick = (col == wanted).astype(BF16)
    turned = lax.dot_general(
        pick, layers_ref[...], (((1,), (1,)), ((), ())), preferred_element_type=F32
    ).astype(BF16)
    for k, out in enumerate(outs):
        out[:, :rows_dev] = turned[k * each : (k + 1) * each]
    if half == 0:
        codes[...] = jnp.zeros_like(codes)
        codes[: extra_ref.shape[0], : extra_ref.shape[1]] = extra_ref[...]
        tail = codes[...].astype(F32).astype(BF16)
        for out in outs:
            out[:, rows_dev:] = jnp.zeros((each, LANES), BF16)
            out[:CODE_ROWS, rows_dev:] = tail


def pad_kernel(table_ref, padded):
    weights, block_rows = table_ref.shape[:2]
    padded[...] = jnp.zeros_like(padded)
    for half in range(LANES // block_rows):
        start = half * block_rows
        padded[half * weights : (half + 1) * weights, start : start + block_rows] = table_ref[...]


def pupil_kernel(n_layer, n_row, entries, unroll, padded, *refs):
    coded, parts = refs[:n_layer], refs[n_layer : 2 * n_layer]
    outs = refs[2 * n_layer : 2 * n_layer + n_row]
    total, codes, code, sem = refs[-4:]
    weights = padded.shape[0] // 2
    owned = outs[0].shape[1] // LANES
    for j, ref in enumerate(coded):
        tail = ref[:CODE_ROWS, ref.shape[1] - LANES :]
        codes[j * CODE_ROWS : (j + 1) * CODE_ROWS] = tail.astype(F32).astype(jnp.int32)
    copy = pltpu.make_async_copy(codes, code, sem)
    copy.start()
    total[...] = jnp.zeros_like(total)
    copy.wait()
    for j, part in enumerate(parts):
        base = j * CODE_ROWS

        def step(group, carry):
            terms = []
            for u in range(unroll):
                e = group * unroll + u
                block = code[base + 2, e]
                source = part[:, pl.ds(pl.multiple_of((block // 2) * LANES, LANES), LANES)]
                weight = padded[lax.rem(block, 2) * weights + code[base + 3, e]]
                dest = code[base, e] * owned + code[base + 1, e]
                terms.append((dest, jnp.dot(source, weight, preferred_element_type=F32)))
            for dest, term in terms:
                total[dest] += term
            return carry

        lax.fori_loop(0, entries // unroll, step, 0)
    me = lax.axis_index("row")
    for k, out in enumerate(outs):
        base = lax.rem(me + k, n_row) * owned
        for s in range(owned):
            out[:, s * LANES : (s + 1) * LANES] = total[base + s].astype(BF16)


def sum_kernel(*refs):
    refs[-1][...] = sum(ref[...].astype(F32) for ref in refs[:-1]).astype(BF16)


def fit_kernel(n_layer, n_row, fitting_ref, *refs):
    pieces, outs = refs[:n_layer], refs[n_layer : n_layer + n_row]
    left, product = refs[-2], refs[-1]
    aligned = n_layer == n_row
    me, row = lax.axis_index("layer"), lax.axis_index("row")
    for j, piece in enumerate(pieces):
        place = me + n_layer - j
        left[lax.rem(place + n_row - row if aligned else place, n_layer)] = piece[...]
    columns = left.shape[0] * left.shape[1]
    found = lax.dot_general(
        left[...].reshape(columns, left.shape[2]),
        fitting_ref[...],
        (((1,), (1,)), ((), ())),
        preferred_element_type=F32,
    )
    each = columns // n_row
    if aligned:
        for k, out in enumerate(outs):
            out[...] = found[k * each : (k + 1) * each].astype(BF16)
    else:
        product[...] = found
        for k, out in enumerate(outs):
            start = pl.multiple_of(lax.rem(row + k, n_row) * each, each)
            out[...] = product[pl.ds(start, each), :].astype(BF16)


def exchange(chunks, axis):
    n = len(chunks)
    return [
        chunk if k == 0 else lax.ppermute(chunk, axis, [(i, (i + k) % n) for i in range(n)])
        for k, chunk in enumerate(chunks)
    ]


def total_of(parts):
    return sum(part.astype(F32) for part in parts).astype(BF16)


def call(kernel, shapes, scratch, *args, after=()):
    given = len(args)

    def body(*refs):
        kernel(*refs[:given], *refs[given + len(after) :])

    return pl.pallas_call(
        body,
        out_shape=[jax.ShapeDtypeStruct(shape, BF16) for shape in shapes],
        in_specs=[VMEM] * len(args) + [ANY] * len(after),
        out_specs=[VMEM] * len(shapes),
        scratch_shapes=scratch,
        compiler_params=pltpu.CompilerParams(**PARAMS),
    )(*args, *after)


def local(layers, table, fitting, owner, local_slice, block_index, weight_index):
    n_layer, n_row = lax.axis_size("layer"), lax.axis_size("row")
    rows_dev, columns = layers.shape[1:]
    entries = owner.shape[1]
    weights, slice_rows, block_rows = table.shape
    points, actuators = fitting.shape
    owned = points // slice_rows
    chunk = columns // n_row
    halves = 2 if chunk % 32 == 0 else 1
    per_half = columns // halves
    each = per_half // n_layer

    indices = jnp.concatenate([owner[:, :, 0], local_slice, block_index, weight_index], 0)
    parts, before = [], ()
    for h in range(halves):
        turned = call(
            functools.partial(turn_kernel, n_layer, n_row, halves, h),
            [(each, rows_dev + (LANES if h == 0 else 0))] * n_layer,
            [pltpu.VMEM((CODE_ROWS, LANES), jnp.int32)],
            layers[0],
            indices,
            after=before,
        )
        before = (turned[0],)
        parts.append(exchange(turned, "layer"))
    (padded,) = call(
        pad_kernel,
        [(LANES // block_rows * weights, LANES, slice_rows)],
        [],
        jnp.swapaxes(table, 1, 2),
        after=before,
    )

    received, before = [], ()
    for h in range(halves):
        shares = call(
            functools.partial(pupil_kernel, n_layer, n_row, entries, entries),
            [(each, points)] * n_row,
            [
                pltpu.VMEM((n_row * owned, each, slice_rows), F32),
                pltpu.VMEM((n_layer * CODE_ROWS, LANES), jnp.int32),
                pltpu.SMEM((n_layer * CODE_ROWS, LANES), jnp.int32),
                pltpu.SemaphoreType.DMA,
            ],
            padded,
            *parts[0],
            *parts[h],
            after=before,
        )
        before = (shares[0],)
        received.append(exchange(shares, "row"))
    results = []
    for h in range(halves):
        (pupil,) = call(sum_kernel, [(each, points)], [], *received[h], after=before)
        pieces = exchange([pupil] * n_layer, "layer")
        partial = call(
            functools.partial(fit_kernel, n_layer, n_row),
            [(chunk // halves, actuators)] * n_row,
            [pltpu.VMEM((n_layer, each, points), BF16), pltpu.VMEM((per_half, actuators), F32)],
            fitting.T,
            *pieces,
        )
        before = (partial[0],)
        results.append(exchange(partial, "row"))
    return jnp.concatenate([total_of(result) for result in results], 0)


def solution(mesh):
    return jax.shard_map(
        local,
        mesh=mesh,
        in_specs=(
            P("layer", "row", "panel"),
            P(),
            P("row", "layer"),
            P("layer", "row", None),
            P("layer", "row"),
            P("layer", "row"),
            P("layer", "row"),
        ),
        out_specs=P(("panel", "row"), "layer"),
        check_vma=False,
    )
```

profile of v0, /device:TPU:0, one launch (start us, length us, event | category | flops | bytes accessed | tf_op | source)
XLA Modules:
  0.0 69.7 jit_solution(5069151101546736915)
XLA Ops:
  0.9 1.3 %copy-done.1 = bf16[1,2048,256]{2,1,0:T(8,128)(2,1)S(1)} copy-done((bf16[1,2048,256]{2,1,0:T(8,128)(2,1)S(1)}, bf16[1,2048,256]{2,1,0:T(8,128)(2,1)}, u32[]{:S(2)}) %copy-start.1) | copy-done | bytes 1048600
  3.2 2.6 %collective-permute-start.1 = (bf16[32,2176]{1,0:T(8,128)(2,1)S(1)}, bf16[32,2176]{1,0:T(8,128)(2,1)S(1)}, u32[]{:S(2)}, u32[]{:S(2)}) collective-permute-start(bf16[32,2176]{1,0:T(8,128)(2,1)S(1)} %get-tuple-element.32), channel_id=1, source_target_pairs={{0,2},{1,3},{2,0},{3,1},{4,6},{5,7},{6,4},{7,5},{8,10},{9,11},{10,... | collective-permute-start | bytes 417800 | tf_op jit(solution)/shard_map/ppermute | solution.py:122
  5.8 1.4 %collective-permute-start.2 = (bf16[32,2176]{1,0:T(8,128)(2,1)S(1)}, bf16[32,2176]{1,0:T(8,128)(2,1)S(1)}, u32[]{:S(2)}, u32[]{:S(2)}) collective-permute-start(bf16[32,2176]{1,0:T(8,128)(2,1)S(1)} %get-tuple-element.33), channel_id=1, source_target_pairs={{0,3},{1,0},{2,1},{3,2},{4,7},{5,4},{6,5},{7,6},{8,11},{9,8},{10,9... | collective-permute-start | bytes 417800 | tf_op jit(solution)/shard_map/ppermute | solution.py:122
  9.3 1.5 %collective-permute-start.8 = (bf16[32,2048]{1,0:T(8,128)(2,1)S(1)}, bf16[32,2048]{1,0:T(8,128)(2,1)S(1)}, u32[]{:S(2)}, u32[]{:S(2)}) collective-permute-start(bf16[32,2048]{1,0:T(8,128)(2,1)S(1)} %get-tuple-element.40), channel_id=1, source_target_pairs={{0,3},{1,0},{2,1},{3,2},{4,7},{5,4},{6,5},{7,6},{8,11},{9,8},{10,9... | collective-permute-start | bytes 393224 | tf_op jit(solution)/shard_map/ppermute | solution.py:122
  10.7 2.1 %collective-permute-done.2.refs_4_.refs_8_ = bf16[32,2176]{1,0:T(8,128)(2,1)S(1)} collective-permute-done((bf16[32,2176]{1,0:T(8,128)(2,1)S(1)}, bf16[32,2176]{1,0:T(8,128)(2,1)S(1)}, u32[]{:S(2)}, u32[]{:S(2)}) %collective-permute-start.2) | collective-permute-done | bytes 139296 | tf_op jit(solution)/shard_map/ppermute | solution.py:122
  12.8 2.6 %shard_map.76 = (bf16[32,2048]{1,0:T(8,128)(2,1)S(1)}, bf16[32,2048]{1,0:T(8,128)(2,1)S(1)}, bf16[32,2048]{1,0:T(8,128)(2,1)S(1)}, bf16[32,2048]{1,0:T(8,128)(2,1)S(1)}) custom-call(bf16[32,128,128]{2,1,0:T(8,128)(2,1)S(1)} %shard_map.75.refs_0_, bf16[32,2176]{1,0:T(8,128)(2,1)S(1)} %get-tuple-element.29.refs_2_.refs_1_.refs_5_, ...), custom_call_target="tpu_custom_call" | custom-call | tf_op jit(solution)/shard_map/pallas_call | solution.py:137
  15.3 1.6 %collective-permute-start.3 = (bf16[32,2048]{1,0:T(8,128)(2,1)S(1)}, bf16[32,2048]{1,0:T(8,128)(2,1)S(1)}, u32[]{:S(2)}, u32[]{:S(2)}) collective-permute-start(bf16[32,2048]{1,0:T(8,128)(2,1)S(1)} %get-tuple-element.35), channel_id=1, source_target_pairs={{0,4},{4,8},{8,12},{12,0},{1,5},{5,9},{9,13},{13,1},{2,6},{6,10},{... | collective-permute-start | bytes 393224 | tf_op jit(solution)/shard_map/ppermute | solution.py:122
  17.0 2.6 %collective-permute-start.4 = (bf16[32,2048]{1,0:T(8,128)(2,1)S(1)}, bf16[32,2048]{1,0:T(8,128)(2,1)S(1)}, u32[]{:S(2)}, u32[]{:S(2)}) collective-permute-start(bf16[32,2048]{1,0:T(8,128)(2,1)S(1)} %get-tuple-element.36), channel_id=1, source_target_pairs={{0,8},{4,12},{8,0},{12,4},{1,9},{5,13},{9,1},{13,5},{2,10},{6,14},... | collective-permute-start | bytes 393224 | tf_op jit(solution)/shard_map/ppermute | solution.py:122
  19.6 1.3 %collective-permute-start.5 = (bf16[32,2048]{1,0:T(8,128)(2,1)S(1)}, bf16[32,2048]{1,0:T(8,128)(2,1)S(1)}, u32[]{:S(2)}, u32[]{:S(2)}) collective-permute-start(bf16[32,2048]{1,0:T(8,128)(2,1)S(1)} %get-tuple-element.37), channel_id=1, source_target_pairs={{0,12},{4,0},{8,4},{12,8},{1,13},{5,1},{9,5},{13,9},{2,14},{6,2},{... | collective-permute-start | bytes 393224 | tf_op jit(solution)/shard_map/ppermute | solution.py:122
  20.9 2.5 %shard_map.77 = (bf16[32,2048]{1,0:T(8,128)(2,1)S(1)}, bf16[32,2048]{1,0:T(8,128)(2,1)S(1)}, bf16[32,2048]{1,0:T(8,128)(2,1)S(1)}, bf16[32,2048]{1,0:T(8,128)(2,1)S(1)}) custom-call(bf16[32,128,128]{2,1,0:T(8,128)(2,1)S(1)} %shard_map.75.refs_0_, bf16[32,2176]{1,0:T(8,128)(2,1)S(1)} %get-tuple-element.29.refs_2_.refs_1_.refs_5_, ...), custom_call_target="tpu_custom_call" | custom-call | tf_op jit(solution)/shard_map/pallas_call | solution.py:137
  23.5 5.6 %collective-permute-done.4.refs_2_ = bf16[32,2048]{1,0:T(8,128)(2,1)S(1)} collective-permute-done((bf16[32,2048]{1,0:T(8,128)(2,1)S(1)}, bf16[32,2048]{1,0:T(8,128)(2,1)S(1)}, u32[]{:S(2)}, u32[]{:S(2)}) %collective-permute-start.4) | collective-permute-done | bytes 131104 | tf_op jit(solution)/shard_map/ppermute | solution.py:122
  29.4 1.7 %collective-permute-start.10 = (bf16[32,2048]{1,0:T(8,128)(2,1)S(1)}, bf16[32,2048]{1,0:T(8,128)(2,1)S(1)}, u32[]{:S(2)}, u32[]{:S(2)}) collective-permute-start(bf16[32,2048]{1,0:T(8,128)(2,1)S(1)} %shard_map.78.refs_1_), channel_id=1, source_target_pairs={{0,2},{1,3},{2,0},{3,1},{4,6},{5,7},{6,4},{7,5},{8,10},{9,11},{10,... | collective-permute-start | bytes 393224 | tf_op jit(solution)/shard_map/ppermute | solution.py:122
  31.0 3.4 %collective-permute-start.15 = (bf16[32,2048]{1,0:T(8,128)(2,1)S(1)}, bf16[32,2048]{1,0:T(8,128)(2,1)S(1)}, u32[]{:S(2)}, u32[]{:S(2)}) collective-permute-start(bf16[32,2048]{1,0:T(8,128)(2,1)S(1)} %get-tuple-element.46), channel_id=1, source_target_pairs={{0,4},{4,8},{8,12},{12,0},{1,5},{5,9},{9,13},{13,1},{2,6},{6,10},{... | collective-permute-start | bytes 393224 | tf_op jit(solution)/shard_map/ppermute | solution.py:122
  34.4 1.6 %collective-permute-start.16 = (bf16[32,2048]{1,0:T(8,128)(2,1)S(1)}, bf16[32,2048]{1,0:T(8,128)(2,1)S(1)}, u32[]{:S(2)}, u32[]{:S(2)}) collective-permute-start(bf16[32,2048]{1,0:T(8,128)(2,1)S(1)} %get-tuple-element.47), channel_id=1, source_target_pairs={{0,8},{4,12},{8,0},{12,4},{1,9},{5,13},{9,1},{13,5},{2,10},{6,14},... | collective-permute-start | bytes 393224 | tf_op jit(solution)/shard_map/ppermute | solution.py:122
  36.0 1.7 %collective-permute-start.17 = (bf16[32,2048]{1,0:T(8,128)(2,1)S(1)}, bf16[32,2048]{1,0:T(8,128)(2,1)S(1)}, u32[]{:S(2)}, u32[]{:S(2)}) collective-permute-start(bf16[32,2048]{1,0:T(8,128)(2,1)S(1)} %get-tuple-element.48), channel_id=1, source_target_pairs={{0,12},{4,0},{8,4},{12,8},{1,13},{5,1},{9,5},{13,9},{2,14},{6,2},{... | collective-permute-start | bytes 393224 | tf_op jit(solution)/shard_map/ppermute | solution.py:122
  38.0 2.3 %shard_map.79 = (bf16[32,1650]{1,0:T(8,128)(2,1)S(1)}, bf16[32,1650]{1,0:T(8,128)(2,1)S(1)}, bf16[32,1650]{1,0:T(8,128)(2,1)S(1)}, bf16[32,1650]{1,0:T(8,128)(2,1)S(1)}) custom-call(bf16[1650,2048]{1,0:T(8,128)(2,1)S(1)} %bitcast.4, bf16[32,2048]{1,0:T(8,128)(2,1)S(1)} %shard_map.78.refs_1_, bf16[32,2048]{1,0:T(8,128)(2,1)S(1)} %collective-permute-done.9.refs_2_, ...), custom_call_target="tpu_custom_call" | custom-call | tf_op jit(solution)/shard_map/pallas_call | solution.py:137
  40.4 4.9 %collective-permute-done.16.refs_2_ = bf16[32,2048]{1,0:T(8,128)(2,1)S(1)} collective-permute-done((bf16[32,2048]{1,0:T(8,128)(2,1)S(1)}, bf16[32,2048]{1,0:T(8,128)(2,1)S(1)}, u32[]{:S(2)}, u32[]{:S(2)}) %collective-permute-start.16) | collective-permute-done | bytes 131104 | tf_op jit(solution)/shard_map/ppermute | solution.py:122
  47.0 3.4 %collective-permute-start.12 = (bf16[32,1650]{1,0:T(8,128)(2,1)S(1)}, bf16[32,1650]{1,0:T(8,128)(2,1)S(1)}, u32[]{:S(2)}, u32[]{:S(2)}) collective-permute-start(bf16[32,1650]{1,0:T(8,128)(2,1)S(1)} %get-tuple-element.43), channel_id=1, source_target_pairs={{0,4},{4,8},{8,12},{12,0},{1,5},{5,9},{9,13},{13,1},{2,6},{6,10},{... | collective-permute-start | bytes 316808 | tf_op jit(solution)/shard_map/ppermute | solution.py:122
  51.6 1.9 %collective-permute-start.14 = (bf16[32,1650]{1,0:T(8,128)(2,1)S(1)}, bf16[32,1650]{1,0:T(8,128)(2,1)S(1)}, u32[]{:S(2)}, u32[]{:S(2)}) collective-permute-start(bf16[32,1650]{1,0:T(8,128)(2,1)S(1)} %get-tuple-element.45), channel_id=1, source_target_pairs={{0,12},{4,0},{8,4},{12,8},{1,13},{5,1},{9,5},{13,9},{2,14},{6,2},{... | collective-permute-start | bytes 316808 | tf_op jit(solution)/shard_map/ppermute | solution.py:122
  54.1 2.3 %shard_map.81 = (bf16[32,1650]{1,0:T(8,128)(2,1)S(1)}, bf16[32,1650]{1,0:T(8,128)(2,1)S(1)}, bf16[32,1650]{1,0:T(8,128)(2,1)S(1)}, bf16[32,1650]{1,0:T(8,128)(2,1)S(1)}) custom-call(bf16[1650,2048]{1,0:T(8,128)(2,1)S(1)} %bitcast.5, bf16[32,2048]{1,0:T(8,128)(2,1)S(1)} %shard_map.80.refs_1_, bf16[32,2048]{1,0:T(8,128)(2,1)S(1)} %collective-permute-done.18.refs_2_, ...), custom_call_target="tpu_custom_call" | custom-call | tf_op jit(solution)/shard_map/pallas_call | solution.py:137
  56.4 3.4 %collective-permute-start.21 = (bf16[32,1650]{1,0:T(8,128)(2,1)S(1)}, bf16[32,1650]{1,0:T(8,128)(2,1)S(1)}, u32[]{:S(2)}, u32[]{:S(2)}) collective-permute-start(bf16[32,1650]{1,0:T(8,128)(2,1)S(1)} %get-tuple-element.50), channel_id=1, source_target_pairs={{0,4},{4,8},{8,12},{12,0},{1,5},{5,9},{9,13},{13,1},{2,6},{6,10},{... | collective-permute-start | bytes 316808 | tf_op jit(solution)/shard_map/ppermute | solution.py:122
  59.8 1.3 %collective-permute-start.22 = (bf16[32,1650]{1,0:T(8,128)(2,1)S(1)}, bf16[32,1650]{1,0:T(8,128)(2,1)S(1)}, u32[]{:S(2)}, u32[]{:S(2)}) collective-permute-start(bf16[32,1650]{1,0:T(8,128)(2,1)S(1)} %get-tuple-element.51), channel_id=1, source_target_pairs={{0,8},{4,12},{8,0},{12,4},{1,9},{5,13},{9,1},{13,5},{2,10},{6,14},... | collective-permute-start | bytes 316808 | tf_op jit(solution)/shard_map/ppermute | solution.py:122
  62.3 2.2 %collective-permute-done.21 = bf16[32,1650]{1,0:T(8,128)(2,1)S(1)} collective-permute-done((bf16[32,1650]{1,0:T(8,128)(2,1)S(1)}, bf16[32,1650]{1,0:T(8,128)(2,1)S(1)}, u32[]{:S(2)}, u32[]{:S(2)}) %collective-permute-start.21) | collective-permute-done | bytes 105632 | tf_op jit(solution)/shard_map/ppermute | solution.py:122
  64.5 4.5 %collective-permute-done.22 = bf16[32,1650]{1,0:T(8,128)(2,1)S(1)} collective-permute-done((bf16[32,1650]{1,0:T(8,128)(2,1)S(1)}, bf16[32,1650]{1,0:T(8,128)(2,1)S(1)}, u32[]{:S(2)}, u32[]{:S(2)}) %collective-permute-start.22) | collective-permute-done | bytes 105632 | tf_op jit(solution)/shard_map/ppermute | solution.py:122
  (43 shorter events, 10.1 us)
Async XLA Ops:
  2.7 6.5 %collective-permute-start = (bf16[32,2176]{1,0:T(8,128)(2,1)S(1)}, bf16[32,2176]{1,0:T(8,128)(2,1)S(1)}, u32[]{:S(2)}, u32[]{:S(2)}) collective-permute-start(bf16[32,2176]{1,0:T(8,128)(2,1)S(1)} %get-tuple-element.31), channel_id=1, source_target_pairs={{0,1},{1,2},{2,3},{3,0},{4,5},{5,6},{6,7},{7,4},{8,9},{9,10},{10,1... | collective-permute-start | bytes 417800 | tf_op jit(solution)/shard_map/ppermute | solution.py:122
  3.2 7.5 %collective-permute-start.1 = (bf16[32,2176]{1,0:T(8,128)(2,1)S(1)}, bf16[32,2176]{1,0:T(8,128)(2,1)S(1)}, u32[]{:S(2)}, u32[]{:S(2)}) collective-permute-start(bf16[32,2176]{1,0:T(8,128)(2,1)S(1)} %get-tuple-element.32), channel_id=1, source_target_pairs={{0,2},{1,3},{2,0},{3,1},{4,6},{5,7},{6,4},{7,5},{8,10},{9,11},{10,... | collective-permute-start | bytes 417800 | tf_op jit(solution)/shard_map/ppermute | solution.py:122
  5.8 7.0 %collective-permute-start.2 = (bf16[32,2176]{1,0:T(8,128)(2,1)S(1)}, bf16[32,2176]{1,0:T(8,128)(2,1)S(1)}, u32[]{:S(2)}, u32[]{:S(2)}) collective-permute-start(bf16[32,2176]{1,0:T(8,128)(2,1)S(1)} %get-tuple-element.33), channel_id=1, source_target_pairs={{0,3},{1,0},{2,1},{3,2},{4,7},{5,4},{6,5},{7,6},{8,11},{9,8},{10,9... | collective-permute-start | bytes 417800 | tf_op jit(solution)/shard_map/ppermute | solution.py:122
  7.6 11.9 %collective-permute-start.6 = (bf16[32,2048]{1,0:T(8,128)(2,1)S(1)}, bf16[32,2048]{1,0:T(8,128)(2,1)S(1)}, u32[]{:S(2)}, u32[]{:S(2)}) collective-permute-start(bf16[32,2048]{1,0:T(8,128)(2,1)S(1)} %get-tuple-element.38), channel_id=1, source_target_pairs={{0,1},{1,2},{2,3},{3,0},{4,5},{5,6},{6,7},{7,4},{8,9},{9,10},{10,1... | collective-permute-start | bytes 393224 | tf_op jit(solution)/shard_map/ppermute | solution.py:122
  7.7 13.2 %collective-permute-start.7 = (bf16[32,2048]{1,0:T(8,128)(2,1)S(1)}, bf16[32,2048]{1,0:T(8,128)(2,1)S(1)}, u32[]{:S(2)}, u32[]{:S(2)}) collective-permute-start(bf16[32,2048]{1,0:T(8,128)(2,1)S(1)} %get-tuple-element.39), channel_id=1, source_target_pairs={{0,2},{1,3},{2,0},{3,1},{4,6},{5,7},{6,4},{7,5},{8,10},{9,11},{10,... | collective-permute-start | bytes 393224 | tf_op jit(solution)/shard_map/ppermute | solution.py:122
  9.3 11.7 %collective-permute-start.8 = (bf16[32,2048]{1,0:T(8,128)(2,1)S(1)}, bf16[32,2048]{1,0:T(8,128)(2,1)S(1)}, u32[]{:S(2)}, u32[]{:S(2)}) collective-permute-start(bf16[32,2048]{1,0:T(8,128)(2,1)S(1)} %get-tuple-element.40), channel_id=1, source_target_pairs={{0,3},{1,0},{2,1},{3,2},{4,7},{5,4},{6,5},{7,6},{8,11},{9,8},{10,9... | collective-permute-start | bytes 393224 | tf_op jit(solution)/shard_map/ppermute | solution.py:122
  15.3 8.2 %collective-permute-start.3 = (bf16[32,2048]{1,0:T(8,128)(2,1)S(1)}, bf16[32,2048]{1,0:T(8,128)(2,1)S(1)}, u32[]{:S(2)}, u32[]{:S(2)}) collective-permute-start(bf16[32,2048]{1,0:T(8,128)(2,1)S(1)} %get-tuple-element.35), channel_id=1, source_target_pairs={{0,4},{4,8},{8,12},{12,0},{1,5},{5,9},{9,13},{13,1},{2,6},{6,10},{... | collective-permute-start | bytes 393224 | tf_op jit(solution)/shard_map/ppermute | solution.py:122
  17.0 12.2 %collective-permute-start.4 = (bf16[32,2048]{1,0:T(8,128)(2,1)S(1)}, bf16[32,2048]{1,0:T(8,128)(2,1)S(1)}, u32[]{:S(2)}, u32[]{:S(2)}) collective-permute-start(bf16[32,2048]{1,0:T(8,128)(2,1)S(1)} %get-tuple-element.36), channel_id=1, source_target_pairs={{0,8},{4,12},{8,0},{12,4},{1,9},{5,13},{9,1},{13,5},{2,10},{6,14},... | collective-permute-start | bytes 393224 | tf_op jit(solution)/shard_map/ppermute | solution.py:122
  19.6 9.6 %collective-permute-start.5 = (bf16[32,2048]{1,0:T(8,128)(2,1)S(1)}, bf16[32,2048]{1,0:T(8,128)(2,1)S(1)}, u32[]{:S(2)}, u32[]{:S(2)}) collective-permute-start(bf16[32,2048]{1,0:T(8,128)(2,1)S(1)} %get-tuple-element.37), channel_id=1, source_target_pairs={{0,12},{4,0},{8,4},{12,8},{1,13},{5,1},{9,5},{13,9},{2,14},{6,2},{... | collective-permute-start | bytes 393224 | tf_op jit(solution)/shard_map/ppermute | solution.py:122
  29.3 6.7 %collective-permute-start.11 = (bf16[32,2048]{1,0:T(8,128)(2,1)S(1)}, bf16[32,2048]{1,0:T(8,128)(2,1)S(1)}, u32[]{:S(2)}, u32[]{:S(2)}) collective-permute-start(bf16[32,2048]{1,0:T(8,128)(2,1)S(1)} %shard_map.78.refs_1_), channel_id=1, source_target_pairs={{0,3},{1,0},{2,1},{3,2},{4,7},{5,4},{6,5},{7,6},{8,11},{9,8},{10,9... | collective-permute-start | bytes 393224 | tf_op jit(solution)/shard_map/ppermute | solution.py:122
  29.4 8.7 %collective-permute-start.10 = (bf16[32,2048]{1,0:T(8,128)(2,1)S(1)}, bf16[32,2048]{1,0:T(8,128)(2,1)S(1)}, u32[]{:S(2)}, u32[]{:S(2)}) collective-permute-start(bf16[32,2048]{1,0:T(8,128)(2,1)S(1)} %shard_map.78.refs_1_), channel_id=1, source_target_pairs={{0,2},{1,3},{2,0},{3,1},{4,6},{5,7},{6,4},{7,5},{8,10},{9,11},{10,... | collective-permute-start | bytes 393224 | tf_op jit(solution)/shard_map/ppermute | solution.py:122
  31.0 7.0 %collective-permute-start.9 = (bf16[32,2048]{1,0:T(8,128)(2,1)S(1)}, bf16[32,2048]{1,0:T(8,128)(2,1)S(1)}, u32[]{:S(2)}, u32[]{:S(2)}) collective-permute-start(bf16[32,2048]{1,0:T(8,128)(2,1)S(1)} %shard_map.78.refs_1_), channel_id=1, source_target_pairs={{0,1},{1,2},{2,3},{3,0},{4,5},{5,6},{6,7},{7,4},{8,9},{9,10},{10,1... | collective-permute-start | bytes 393224 | tf_op jit(solution)/shard_map/ppermute | solution.py:122
  31.0 9.3 %collective-permute-start.15 = (bf16[32,2048]{1,0:T(8,128)(2,1)S(1)}, bf16[32,2048]{1,0:T(8,128)(2,1)S(1)}, u32[]{:S(2)}, u32[]{:S(2)}) collective-permute-start(bf16[32,2048]{1,0:T(8,128)(2,1)S(1)} %get-tuple-element.46), channel_id=1, source_target_pairs={{0,4},{4,8},{8,12},{12,0},{1,5},{5,9},{9,13},{13,1},{2,6},{6,10},{... | collective-permute-start | bytes 393224 | tf_op jit(solution)/shard_map/ppermute | solution.py:122
  34.4 10.8 %collective-permute-start.16 = (bf16[32,2048]{1,0:T(8,128)(2,1)S(1)}, bf16[32,2048]{1,0:T(8,128)(2,1)S(1)}, u32[]{:S(2)}, u32[]{:S(2)}) collective-permute-start(bf16[32,2048]{1,0:T(8,128)(2,1)S(1)} %get-tuple-element.47), channel_id=1, source_target_pairs={{0,8},{4,12},{8,0},{12,4},{1,9},{5,13},{9,1},{13,5},{2,10},{6,14},... | collective-permute-start | bytes 393224 | tf_op jit(solution)/shard_map/ppermute | solution.py:122
  36.0 9.3 %collective-permute-start.17 = (bf16[32,2048]{1,0:T(8,128)(2,1)S(1)}, bf16[32,2048]{1,0:T(8,128)(2,1)S(1)}, u32[]{:S(2)}, u32[]{:S(2)}) collective-permute-start(bf16[32,2048]{1,0:T(8,128)(2,1)S(1)} %get-tuple-element.48), channel_id=1, source_target_pairs={{0,12},{4,0},{8,4},{12,8},{1,13},{5,1},{9,5},{13,9},{2,14},{6,2},{... | collective-permute-start | bytes 393224 | tf_op jit(solution)/shard_map/ppermute | solution.py:122
  45.3 6.3 %collective-permute-start.20 = (bf16[32,2048]{1,0:T(8,128)(2,1)S(1)}, bf16[32,2048]{1,0:T(8,128)(2,1)S(1)}, u32[]{:S(2)}, u32[]{:S(2)}) collective-permute-start(bf16[32,2048]{1,0:T(8,128)(2,1)S(1)} %shard_map.80.refs_1_), channel_id=1, source_target_pairs={{0,3},{1,0},{2,1},{3,2},{4,7},{5,4},{6,5},{7,6},{8,11},{9,8},{10,9... | collective-permute-start | bytes 393224 | tf_op jit(solution)/shard_map/ppermute | solution.py:122
  46.0 8.1 %collective-permute-start.19 = (bf16[32,2048]{1,0:T(8,128)(2,1)S(1)}, bf16[32,2048]{1,0:T(8,128)(2,1)S(1)}, u32[]{:S(2)}, u32[]{:S(2)}) collective-permute-start(bf16[32,2048]{1,0:T(8,128)(2,1)S(1)} %shard_map.80.refs_1_), channel_id=1, source_target_pairs={{0,2},{1,3},{2,0},{3,1},{4,6},{5,7},{6,4},{7,5},{8,10},{9,11},{10,... | collective-permute-start | bytes 393224 | tf_op jit(solution)/shard_map/ppermute | solution.py:122
  47.0 7.1 %collective-permute-start.18 = (bf16[32,2048]{1,0:T(8,128)(2,1)S(1)}, bf16[32,2048]{1,0:T(8,128)(2,1)S(1)}, u32[]{:S(2)}, u32[]{:S(2)}) collective-permute-start(bf16[32,2048]{1,0:T(8,128)(2,1)S(1)} %shard_map.80.refs_1_), channel_id=1, source_target_pairs={{0,1},{1,2},{2,3},{3,0},{4,5},{5,6},{6,7},{7,4},{8,9},{9,10},{10,1... | collective-permute-start | bytes 393224 | tf_op jit(solution)/shard_map/ppermute | solution.py:122
  47.0 14.1 %collective-permute-start.12 = (bf16[32,1650]{1,0:T(8,128)(2,1)S(1)}, bf16[32,1650]{1,0:T(8,128)(2,1)S(1)}, u32[]{:S(2)}, u32[]{:S(2)}) collective-permute-start(bf16[32,1650]{1,0:T(8,128)(2,1)S(1)} %get-tuple-element.43), channel_id=1, source_target_pairs={{0,4},{4,8},{8,12},{12,0},{1,5},{5,9},{9,13},{13,1},{2,6},{6,10},{... | collective-permute-start | bytes 316808 | tf_op jit(solution)/shard_map/ppermute | solution.py:122
  50.4 11.9 %collective-permute-start.13 = (bf16[32,1650]{1,0:T(8,128)(2,1)S(1)}, bf16[32,1650]{1,0:T(8,128)(2,1)S(1)}, u32[]{:S(2)}, u32[]{:S(2)}) collective-permute-start(bf16[32,1650]{1,0:T(8,128)(2,1)S(1)} %get-tuple-element.44), channel_id=1, source_target_pairs={{0,8},{4,12},{8,0},{12,4},{1,9},{5,13},{9,1},{13,5},{2,10},{6,14},... | collective-permute-start | bytes 316808 | tf_op jit(solution)/shard_map/ppermute | solution.py:122
  51.6 10.6 %collective-permute-start.14 = (bf16[32,1650]{1,0:T(8,128)(2,1)S(1)}, bf16[32,1650]{1,0:T(8,128)(2,1)S(1)}, u32[]{:S(2)}, u32[]{:S(2)}) collective-permute-start(bf16[32,1650]{1,0:T(8,128)(2,1)S(1)} %get-tuple-element.45), channel_id=1, source_target_pairs={{0,12},{4,0},{8,4},{12,8},{1,13},{5,1},{9,5},{13,9},{2,14},{6,2},{... | collective-permute-start | bytes 316808 | tf_op jit(solution)/shard_map/ppermute | solution.py:122
  56.4 8.1 %collective-permute-start.21 = (bf16[32,1650]{1,0:T(8,128)(2,1)S(1)}, bf16[32,1650]{1,0:T(8,128)(2,1)S(1)}, u32[]{:S(2)}, u32[]{:S(2)}) collective-permute-start(bf16[32,1650]{1,0:T(8,128)(2,1)S(1)} %get-tuple-element.50), channel_id=1, source_target_pairs={{0,4},{4,8},{8,12},{12,0},{1,5},{5,9},{9,13},{13,1},{2,6},{6,10},{... | collective-permute-start | bytes 316808 | tf_op jit(solution)/shard_map/ppermute | solution.py:122
  59.8 9.2 %collective-permute-start.22 = (bf16[32,1650]{1,0:T(8,128)(2,1)S(1)}, bf16[32,1650]{1,0:T(8,128)(2,1)S(1)}, u32[]{:S(2)}, u32[]{:S(2)}) collective-permute-start(bf16[32,1650]{1,0:T(8,128)(2,1)S(1)} %get-tuple-element.51), channel_id=1, source_target_pairs={{0,8},{4,12},{8,0},{12,4},{1,9},{5,13},{9,1},{13,5},{2,10},{6,14},... | collective-permute-start | bytes 316808 | tf_op jit(solution)/shard_map/ppermute | solution.py:122
  61.1 7.9 %collective-permute-start.23 = (bf16[32,1650]{1,0:T(8,128)(2,1)S(1)}, bf16[32,1650]{1,0:T(8,128)(2,1)S(1)}, u32[]{:S(2)}, u32[]{:S(2)}) collective-permute-start(bf16[32,1650]{1,0:T(8,128)(2,1)S(1)} %get-tuple-element.52), channel_id=1, source_target_pairs={{0,12},{4,0},{8,4},{12,8},{1,13},{5,1},{9,5},{13,9},{2,14},{6,2},{... | collective-permute-start | bytes 316808 | tf_op jit(solution)/shard_map/ppermute | solution.py:122
  (3 other events, 40.3 us)
where the time goes:
time: 69.9 us; the launch traced here: 69.7 us
  starting transfers between devices  34.3 us (49%)
  waiting for transfers between devices  20.3 us (29%)
  Pallas kernels  11 us (16%)
  local copies, waits for them, and re-layouts  2.29 us (3%)
  other arithmetic  1.7 us (2%)
    ppermute x24, starting transfers between devices, exchange(): lax.ppermute(chunk, axis, [(i, (i + k) % n) for i in range(n)])  34.3 us
    ppermute x24, waiting for transfers between devices, exchange(): lax.ppermute(chunk, axis, [(i, (i + k) % n) for i in range(n)])  20.3 us
    pallas_call x9, Pallas kernels, call(): pl.pallas_call(body, out_shape=[jax.ShapeDtypeStruct(shape, BF16) for sha...  11 us
    unnamed x6, local copies, waits for them, and re-layouts  2.29 us
  transfers between devices with their start and end apart: 24, of which 8 were waited for; matrix products, arithmetic and copies ran while one was open for 0% of the time, Pallas kernels for 15%

commit v1 on v0

--- a/solution.py
+++ b/solution.py
@@ -51,10 +51,9 @@
 
 def pupil_kernel(n_layer, n_row, entries, unroll, padded, *refs):
     coded, parts = refs[:n_layer], refs[n_layer : 2 * n_layer]
-    outs = refs[2 * n_layer : 2 * n_layer + n_row]
-    total, codes, code, sem = refs[-4:]
+    out, total, codes, code, sem = refs[-5:]
     weights = padded.shape[0] // 2
-    owned = outs[0].shape[1] // LANES
+    owned = out.shape[2] // LANES
     for j, ref in enumerate(coded):
         tail = ref[:CODE_ROWS, ref.shape[1] - LANES :]
         codes[j * CODE_ROWS : (j + 1) * CODE_ROWS] = tail.astype(F32).astype(jnp.int32)
@@ -79,41 +78,30 @@
             return carry
 
         lax.fori_loop(0, entries // unroll, step, 0)
-    me = lax.axis_index("row")
-    for k, out in enumerate(outs):
-        base = lax.rem(me + k, n_row) * owned
+    for r in range(n_row):
         for s in range(owned):
-            out[:, s * LANES : (s + 1) * LANES] = total[base + s].astype(BF16)
-
-
-def sum_kernel(*refs):
-    refs[-1][...] = sum(ref[...].astype(F32) for ref in refs[:-1]).astype(BF16)
-
-
-def fit_kernel(n_layer, n_row, fitting_ref, *refs):
-    pieces, outs = refs[:n_layer], refs[n_layer : n_layer + n_row]
-    left, product = refs[-2], refs[-1]
-    aligned = n_layer == n_row
-    me, row = lax.axis_index("layer"), lax.axis_index("row")
+            out[r, :, s * LANES : (s + 1) * LANES] = total[r * owned + s].astype(BF16)
+
+
+def sum_kernel(parts_ref, out_ref):
+    parts = [parts_ref[r].astype(F32) for r in range(parts_ref.shape[0])]
+    out_ref[...] = sum(parts).astype(BF16)
+
+
+def fit_kernel(n_layer, fitting_ref, *refs):
+    pieces, (out, left) = refs[:n_layer], refs[n_layer:]
+    me = lax.axis_index("layer")
     for j, piece in enumerate(pieces):
-        place = me + n_layer - j
-        left[lax.rem(place + n_row - row if aligned else place, n_layer)] = piece[...]
-    columns = left.shape[0] * left.shape[1]
+        left[lax.rem(me + n_layer - j, n_layer)] = piece[...]
+    n_row, each, _ = out.shape
     found = lax.dot_general(
-        left[...].reshape(columns, left.shape[2]),
+        left[...].reshape(n_row * each, left.shape[2]),
         fitting_ref[...],
         (((1,), (1,)), ((), ())),
         preferred_element_type=F32,
     )
-    each = columns // n_row
-    if aligned:
-        for k, out in enumerate(outs):
-            out[...] = found[k * each : (k + 1) * each].astype(BF16)
-    else:
-        product[...] = found
-        for k, out in enumerate(outs):
-            start = pl.multiple_of(lax.rem(row + k, n_row) * each, each)
-            out[...] = product[pl.ds(start, each), :].astype(BF16)
+    for r in range(n_row):
+        out[r] = found[r * each : (r + 1) * each].astype(BF16)
 
 
 def exchange(chunks, axis):
@@ -124,8 +112,8 @@
     ]
 
 
-def total_of(parts):
-    return sum(part.astype(F32) for part in parts).astype(BF16)
+def swap(chunks, axis):
+    return lax.all_to_all(chunks, axis, split_axis=0, concat_axis=0, tiled=True)
 
 
 def call(kernel, shapes, scratch, *args, after=()):
@@ -181,7 +169,7 @@
     for h in range(halves):
         shares = call(
             functools.partial(pupil_kernel, n_layer, n_row, entries, entries),
-            [(each, points)] * n_row,
+            [(n_row, each, points)],
             [
                 pltpu.VMEM((n_row * owned, each, slice_rows), F32),
                 pltpu.VMEM((n_layer * CODE_ROWS, LANES), jnp.int32),
@@ -194,21 +182,22 @@
             after=before,
         )
         before = (shares[0],)
-        received.append(exchange(shares, "row"))
+        received.append(swap(shares[0], "row"))
     results = []
     for h in range(halves):
-        (pupil,) = call(sum_kernel, [(each, points)], [], *received[h], after=before)
+        (pupil,) = call(sum_kernel, [(each, points)], [], received[h], after=before)
         pieces = exchange([pupil] * n_layer, "layer")
         partial = call(
-            functools.partial(fit_kernel, n_layer, n_row),
-            [(chunk // halves, actuators)] * n_row,
-            [pltpu.VMEM((n_layer, each, points), BF16), pltpu.VMEM((per_half, actuators), F32)],
+            functools.partial(fit_kernel, n_layer),
+            [(n_row, chunk // halves, actuators)],
+            [pltpu.VMEM((n_layer, each, points), BF16)],
             fitting.T,
             *pieces,
         )
         before = (partial[0],)
-        results.append(exchange(partial, "row"))
-    return jnp.concatenate([total_of(result) for result in results], 0)
+        results.append(swap(partial[0], "row"))
+    sums = [result.astype(F32).sum(0).astype(BF16) for result in results]
+    return jnp.concatenate(sums, 0)
 
 
 def solution(mesh):

time: 69.9 us -> 90.2 us (1.29)
  waiting for transfers between devices: 20.3 us -> 38.8 us
  starting transfers between devices: 34.3 us -> 27.4 us
  local copies, waits for them, and re-layouts: 2.29 us -> 8.02 us
  Pallas kernels: 11 us -> 13.8 us
    ppermute x24 -> x12, starting transfers between devices: 34.3 us -> 9.22 us  [exchange(): lax.ppermute(chunk, axis, [(i, (i + k) % n) for i in range(n)])]
    all_to_all x0 -> x4, starting transfers between devices: none -> 18.2 us  [swap(): return lax.all_to_all(chunks, axis, split_axis=0, concat_axis=0, tiled=True)]
    all_to_all x0 -> x4, waiting for transfers between devices: none -> 16.5 us  [swap(): return lax.all_to_all(chunks, axis, split_axis=0, concat_axis=0, tiled=True)]
    unnamed x6 -> x8, local copies, waits for them, and re-layouts: 2.29 us -> 8.02 us
    pallas_call x9, Pallas kernels: 11 us -> 13.8 us  [call(): pl.pallas_call(body, out_shape=[jax.ShapeDtypeStruct(shape, BF16) for sha...]
    ppermute x24 -> x12, waiting for transfers between devices: 20.3 us -> 22.3 us  [exchange(): lax.ppermute(chunk, axis, [(i, (i + k) % n) for i in range(n)])]
  transfers between devices with their start and end apart: 24 -> 16, of which waited for: 8 -> 12; matrix products, arithmetic and copies ran while one was open for 0% -> 0% of each run, Pallas kernels for 15% -> 11%
where the time goes in v1:
time: 90.2 us; the launch traced here: 89.7 us
  waiting for transfers between devices  38.8 us (43%)
  starting transfers between devices  27.4 us (30%)
  Pallas kernels  13.8 us (15%)
  local copies, waits for them, and re-layouts  8.02 us (9%)
  other arithmetic  1.55 us (2%)
    ppermute x12, waiting for transfers between devices, exchange(): lax.ppermute(chunk, axis, [(i, (i + k) % n) for i in range(n)])  22.3 us
    all_to_all x4, starting transfers between devices, swap(): return lax.all_to_all(chunks, axis, split_axis=0, concat_axis=0, tiled=True)  18.2 us
    all_to_all x4, waiting for transfers between devices, swap(): return lax.all_to_all(chunks, axis, split_axis=0, concat_axis=0, tiled=True)  16.5 us
    pallas_call x9, Pallas kernels, call(): pl.pallas_call(body, out_shape=[jax.ShapeDtypeStruct(shape, BF16) for sha...  13.8 us
    ppermute x12, starting transfers between devices, exchange(): lax.ppermute(chunk, axis, [(i, (i + k) % n) for i in range(n)])  9.22 us
    unnamed x8, local copies, waits for them, and re-layouts  8.02 us
  transfers between devices with their start and end apart: 16, of which 12 were waited for; matrix products, arithmetic and copies ran while one was open for 0% of the time, Pallas kernels for 11%

profile of v1, /device:TPU:0, one launch (start us, length us, event | category | flops | bytes accessed | tf_op | source)
XLA Modules:
  0.0 89.7 jit_solution(2489750215894920930)
XLA Ops:
  0.7 1.2 %copy-done.2 = bf16[1,2048,256]{2,1,0:T(8,128)(2,1)S(1)} copy-done((bf16[1,2048,256]{2,1,0:T(8,128)(2,1)S(1)}, bf16[1,2048,256]{2,1,0:T(8,128)(2,1)}, u32[]{:S(2)}) %copy-start.2) | copy-done | bytes 1048600
  2.9 2.6 %collective-permute-start.1 = (bf16[32,2176]{1,0:T(8,128)(2,1)S(1)}, bf16[32,2176]{1,0:T(8,128)(2,1)S(1)}, u32[]{:S(2)}, u32[]{:S(2)}) collective-permute-start(bf16[32,2176]{1,0:T(8,128)(2,1)S(1)} %get-tuple-element.16), channel_id=1, source_target_pairs={{0,2},{1,3},{2,0},{3,1},{4,6},{5,7},{6,4},{7,5},{8,10},{9,11},{10,... | collective-permute-start | bytes 417800 | tf_op jit(solution)/shard_map/ppermute | solution.py:110
  5.5 1.4 %collective-permute-start.2 = (bf16[32,2176]{1,0:T(8,128)(2,1)S(1)}, bf16[32,2176]{1,0:T(8,128)(2,1)S(1)}, u32[]{:S(2)}, u32[]{:S(2)}) collective-permute-start(bf16[32,2176]{1,0:T(8,128)(2,1)S(1)} %get-tuple-element.17), channel_id=1, source_target_pairs={{0,3},{1,0},{2,1},{3,2},{4,7},{5,4},{6,5},{7,6},{8,11},{9,8},{10,9... | collective-permute-start | bytes 417800 | tf_op jit(solution)/shard_map/ppermute | solution.py:110
  8.5 1.5 %collective-permute-done.1.refs_3_.refs_7_ = bf16[32,2176]{1,0:T(8,128)(2,1)S(1)} collective-permute-done((bf16[32,2176]{1,0:T(8,128)(2,1)S(1)}, bf16[32,2176]{1,0:T(8,128)(2,1)S(1)}, u32[]{:S(2)}, u32[]{:S(2)}) %collective-permute-start.1) | collective-permute-done | bytes 139296 | tf_op jit(solution)/shard_map/ppermute | solution.py:110
  10.0 1.9 %collective-permute-done.2.refs_4_.refs_8_ = bf16[32,2176]{1,0:T(8,128)(2,1)S(1)} collective-permute-done((bf16[32,2176]{1,0:T(8,128)(2,1)S(1)}, bf16[32,2176]{1,0:T(8,128)(2,1)S(1)}, u32[]{:S(2)}, u32[]{:S(2)}) %collective-permute-start.2) | collective-permute-done | bytes 139296 | tf_op jit(solution)/shard_map/ppermute | solution.py:110
  11.9 3.2 %shard_map.76.refs_9_ = bf16[4,32,2048]{2,1,0:T(8,128)(2,1)} custom-call(bf16[32,128,128]{2,1,0:T(8,128)(2,1)S(1)} %shard_map.75.refs_0_, bf16[32,2176]{1,0:T(8,128)(2,1)S(1)} %get-tuple-element.13.refs_2_.refs_1_.refs_5_, bf16[32,2176]{1,0:T(8,128)(2,1)S(1)} %collective-permute-done.refs_2_.refs_6_, ...), custom_call_target="tpu_custom_call" | custom-call | tf_op jit(solution)/shard_map/pallas_call | solution.py:125
  15.1 4.9 %all-to-all-start = ((bf16[4,32,2048]{2,1,0:T(8,128)(2,1)}), bf16[4,32,2048]{2,1,0:T(8,128)(2,1)S(1)}, u32[]{:S(2)}, u32[]{:S(2)}) async-start(bf16[4,32,2048]{2,1,0:T(8,128)(2,1)} %shard_map.76.refs_9_), calls=%async_computation | async-start | bytes 1048576 | tf_op jit(solution)/shard_map/all_to_all | solution.py:116
  20.5 1.5 %collective-permute-start.4 = (bf16[32,2048]{1,0:T(8,128)(2,1)S(1)}, bf16[32,2048]{1,0:T(8,128)(2,1)S(1)}, u32[]{:S(2)}, u32[]{:S(2)}) collective-permute-start(bf16[32,2048]{1,0:T(8,128)(2,1)S(1)} %get-tuple-element.19), channel_id=1, source_target_pairs={{0,2},{1,3},{2,0},{3,1},{4,6},{5,7},{6,4},{7,5},{8,10},{9,11},{10,... | collective-permute-start | bytes 393224 | tf_op jit(solution)/shard_map/ppermute | solution.py:110
  22.0 2.6 %collective-permute-done.3.refs_6_ = bf16[32,2048]{1,0:T(8,128)(2,1)S(1)} collective-permute-done((bf16[32,2048]{1,0:T(8,128)(2,1)S(1)}, bf16[32,2048]{1,0:T(8,128)(2,1)S(1)}, u32[]{:S(2)}, u32[]{:S(2)}) %collective-permute-start.3) | collective-permute-done | bytes 131104 | tf_op jit(solution)/shard_map/ppermute | solution.py:110
  24.6 2.2 %collective-permute-done.4.refs_7_ = bf16[32,2048]{1,0:T(8,128)(2,1)S(1)} collective-permute-done((bf16[32,2048]{1,0:T(8,128)(2,1)S(1)}, bf16[32,2048]{1,0:T(8,128)(2,1)S(1)}, u32[]{:S(2)}, u32[]{:S(2)}) %collective-permute-start.4) | collective-permute-done | bytes 131104 | tf_op jit(solution)/shard_map/ppermute | solution.py:110
  26.9 3.2 %shard_map.77.refs_1_ = bf16[4,32,2048]{2,1,0:T(8,128)(2,1)} custom-call(bf16[32,128,128]{2,1,0:T(8,128)(2,1)S(1)} %shard_map.75.refs_0_, bf16[32,2176]{1,0:T(8,128)(2,1)S(1)} %get-tuple-element.13.refs_2_.refs_1_.refs_5_, bf16[32,2176]{1,0:T(8,128)(2,1)S(1)} %collective-permute-done.refs_2_.refs_6_, ...), custom_call_target="tpu_custom_call" | custom-call | tf_op jit(solution)/shard_map/pallas_call | solution.py:125
  30.1 5.3 %all-to-all-done.refs_0_ = bf16[4,32,2048]{2,1,0:T(8,128)(2,1)S(1)} async-done(((bf16[4,32,2048]{2,1,0:T(8,128)(2,1)}), bf16[4,32,2048]{2,1,0:T(8,128)(2,1)S(1)}, u32[]{:S(2)}, u32[]{:S(2)}) %all-to-all-start) | async-done | bytes 524320 | tf_op jit(solution)/shard_map/all_to_all | solution.py:116
  35.4 3.5 %all-to-all-start.2 = ((bf16[4,32,2048]{2,1,0:T(8,128)(2,1)}), bf16[4,32,2048]{2,1,0:T(8,128)(2,1)S(1)}, u32[]{:S(2)}, u32[]{:S(2)}) async-start(bf16[4,32,2048]{2,1,0:T(8,128)(2,1)} %shard_map.77.refs_1_), calls=%async_computation.2 | async-start | bytes 1048576 | tf_op jit(solution)/shard_map/all_to_all | solution.py:116
  40.4 2.9 %collective-permute-done.8.refs_4_ = bf16[32,2048]{1,0:T(8,128)(2,1)S(1)} collective-permute-done((bf16[32,2048]{1,0:T(8,128)(2,1)S(1)}, bf16[32,2048]{1,0:T(8,128)(2,1)S(1)}, u32[]{:S(2)}, u32[]{:S(2)}) %collective-permute-start.8) | collective-permute-done | bytes 131104 | tf_op jit(solution)/shard_map/ppermute | solution.py:110
  43.3 4.1 %collective-permute-done.7.refs_3_ = bf16[32,2048]{1,0:T(8,128)(2,1)S(1)} collective-permute-done((bf16[32,2048]{1,0:T(8,128)(2,1)S(1)}, bf16[32,2048]{1,0:T(8,128)(2,1)S(1)}, u32[]{:S(2)}, u32[]{:S(2)}) %collective-permute-start.7) | collective-permute-done | bytes 131104 | tf_op jit(solution)/shard_map/ppermute | solution.py:110
  47.6 2.9 %copy-done = bf16[2048,1650]{0,1:T(8,128)(2,1)S(1)} copy-done((bf16[2048,1650]{0,1:T(8,128)(2,1)S(1)}, bf16[2048,1650]{0,1:T(8,128)(2,1)}, u32[]{:S(2)}) %copy-start) | copy-done | bytes 6758424
  50.5 3.1 %shard_map.79.refs_1_ = bf16[4,32,1650]{2,1,0:T(8,128)(2,1)} custom-call(bf16[1650,2048]{1,0:T(8,128)(2,1)S(1)} %bitcast.4, bf16[32,2048]{1,0:T(8,128)(2,1)S(1)} %shard_map.78.refs_1_, bf16[32,2048]{1,0:T(8,128)(2,1)S(1)} %collective-permute-done.6.refs_2_, bf16[32,2048]{1,0:T(8,128)(2,1)S(1)} %collective-permute-done.7.refs_3_, ...), custom_call_target="tpu_custom_call" | custom-call | tf_op jit(solution)/shard_map/pallas_call | solution.py:125
  53.6 4.8 %all-to-all-start.1 = ((bf16[4,32,1650]{2,1,0:T(8,128)(2,1)}), bf16[4,32,1650]{2,1,0:T(8,128)(2,1)S(1)}, u32[]{:S(2)}, u32[]{:S(2)}) async-start(bf16[4,32,1650]{2,1,0:T(8,128)(2,1)} %shard_map.79.refs_1_), calls=%async_computation.1 | async-start | bytes 851968 | tf_op jit(solution)/shard_map/all_to_all | solution.py:116
  59.7 2.2 %collective-permute-done.11.refs_4_ = bf16[32,2048]{1,0:T(8,128)(2,1)S(1)} collective-permute-done((bf16[32,2048]{1,0:T(8,128)(2,1)S(1)}, bf16[32,2048]{1,0:T(8,128)(2,1)S(1)}, u32[]{:S(2)}, u32[]{:S(2)}) %collective-permute-start.11) | collective-permute-done | bytes 131104 | tf_op jit(solution)/shard_map/ppermute | solution.py:110
  61.9 4.2 %collective-permute-done.10.refs_3_ = bf16[32,2048]{1,0:T(8,128)(2,1)S(1)} collective-permute-done((bf16[32,2048]{1,0:T(8,128)(2,1)S(1)}, bf16[32,2048]{1,0:T(8,128)(2,1)S(1)}, u32[]{:S(2)}, u32[]{:S(2)}) %collective-permute-start.10) | collective-permute-done | bytes 131104 | tf_op jit(solution)/shard_map/ppermute | solution.py:110
  66.6 2.9 %copy-done.1 = bf16[2048,1650]{0,1:T(8,128)(2,1)S(1)} copy-done((bf16[2048,1650]{0,1:T(8,128)(2,1)S(1)}, bf16[2048,1650]{0,1:T(8,128)(2,1)}, u32[]{:S(2)}) %copy-start.1) | copy-done | bytes 6758424
  69.5 3.0 %shard_map.81 = bf16[4,32,1650]{2,1,0:T(8,128)(2,1)} custom-call(bf16[1650,2048]{1,0:T(8,128)(2,1)S(1)} %bitcast.5, bf16[32,2048]{1,0:T(8,128)(2,1)S(1)} %shard_map.80.refs_1_, bf16[32,2048]{1,0:T(8,128)(2,1)S(1)} %collective-permute-done.9.refs_2_, bf16[32,2048]{1,0:T(8,128)(2,1)S(1)} %collective-permute-done.10.refs_3_, ...), custom_call_target="tpu_custom_call" | custom-call | tf_op jit(solution)/shard_map/pallas_call | solution.py:125
  72.6 5.1 %all-to-all-start.3 = ((bf16[4,32,1650]{2,1,0:T(8,128)(2,1)}), bf16[4,32,1650]{2,1,0:T(8,128)(2,1)S(1)}, u32[]{:S(2)}, u32[]{:S(2)}) async-start(bf16[4,32,1650]{2,1,0:T(8,128)(2,1)} %shard_map.81), calls=%async_computation.3 | async-start | bytes 851968 | tf_op jit(solution)/shard_map/all_to_all | solution.py:116
  77.8 11.2 %all-to-all-done.3 = bf16[4,32,1650]{2,1,0:T(8,128)(2,1)S(1)} async-done(((bf16[4,32,1650]{2,1,0:T(8,128)(2,1)}), bf16[4,32,1650]{2,1,0:T(8,128)(2,1)S(1)}, u32[]{:S(2)}, u32[]{:S(2)}) %all-to-all-start.3) | async-done | bytes 422432 | tf_op jit(solution)/shard_map/all_to_all | solution.py:116
  (29 shorter events, 8.3 us)
Async XLA Ops:
  0.7 1.2 %copy-start.2 = (bf16[1,2048,256]{2,1,0:T(8,128)(2,1)S(1)}, bf16[1,2048,256]{2,1,0:T(8,128)(2,1)}, u32[]{:S(2)}) copy-start(bf16[1,2048,256]{2,1,0:T(8,128)(2,1)} %param.7) | copy-start | bytes 3145732
  2.4 6.1 %collective-permute-start = (bf16[32,2176]{1,0:T(8,128)(2,1)S(1)}, bf16[32,2176]{1,0:T(8,128)(2,1)S(1)}, u32[]{:S(2)}, u32[]{:S(2)}) collective-permute-start(bf16[32,2176]{1,0:T(8,128)(2,1)S(1)} %get-tuple-element.15), channel_id=1, source_target_pairs={{0,1},{1,2},{2,3},{3,0},{4,5},{5,6},{6,7},{7,4},{8,9},{9,10},{10,1... | collective-permute-start | bytes 417800 | tf_op jit(solution)/shard_map/ppermute | solution.py:110
  2.9 7.1 %collective-permute-start.1 = (bf16[32,2176]{1,0:T(8,128)(2,1)S(1)}, bf16[32,2176]{1,0:T(8,128)(2,1)S(1)}, u32[]{:S(2)}, u32[]{:S(2)}) collective-permute-start(bf16[32,2176]{1,0:T(8,128)(2,1)S(1)} %get-tuple-element.16), channel_id=1, source_target_pairs={{0,2},{1,3},{2,0},{3,1},{4,6},{5,7},{6,4},{7,5},{8,10},{9,11},{10,... | collective-permute-start | bytes 417800 | tf_op jit(solution)/shard_map/ppermute | solution.py:110
  5.5 6.4 %collective-permute-start.2 = (bf16[32,2176]{1,0:T(8,128)(2,1)S(1)}, bf16[32,2176]{1,0:T(8,128)(2,1)S(1)}, u32[]{:S(2)}, u32[]{:S(2)}) collective-permute-start(bf16[32,2176]{1,0:T(8,128)(2,1)S(1)} %get-tuple-element.17), channel_id=1, source_target_pairs={{0,3},{1,0},{2,1},{3,2},{4,7},{5,4},{6,5},{7,6},{8,11},{9,8},{10,9... | collective-permute-start | bytes 417800 | tf_op jit(solution)/shard_map/ppermute | solution.py:110
  7.4 1.0 %copy-start.3 = (bf16[16,128,64]{1,2,0:T(8,128)(2,1)S(1)}, bf16[16,128,64]{1,2,0:T(8,128)(2,1)}, u32[]{:S(2)}) copy-start(bf16[16,128,64]{1,2,0:T(8,128)(2,1)} %param.8) | copy-start | bytes 786436
  15.1 20.4 %all-to-all-start = ((bf16[4,32,2048]{2,1,0:T(8,128)(2,1)}), bf16[4,32,2048]{2,1,0:T(8,128)(2,1)S(1)}, u32[]{:S(2)}, u32[]{:S(2)}) async-start(bf16[4,32,2048]{2,1,0:T(8,128)(2,1)} %shard_map.76.refs_9_), calls=%async_computation | async-start | bytes 1048576 | tf_op jit(solution)/shard_map/all_to_all | solution.py:116
  20.0 4.7 %collective-permute-start.3 = (bf16[32,2048]{1,0:T(8,128)(2,1)S(1)}, bf16[32,2048]{1,0:T(8,128)(2,1)S(1)}, u32[]{:S(2)}, u32[]{:S(2)}) collective-permute-start(bf16[32,2048]{1,0:T(8,128)(2,1)S(1)} %get-tuple-element.18), channel_id=1, source_target_pairs={{0,1},{1,2},{2,3},{3,0},{4,5},{5,6},{6,7},{7,4},{8,9},{9,10},{10,1... | collective-permute-start | bytes 393224 | tf_op jit(solution)/shard_map/ppermute | solution.py:110
  20.5 6.4 %collective-permute-start.4 = (bf16[32,2048]{1,0:T(8,128)(2,1)S(1)}, bf16[32,2048]{1,0:T(8,128)(2,1)S(1)}, u32[]{:S(2)}, u32[]{:S(2)}) collective-permute-start(bf16[32,2048]{1,0:T(8,128)(2,1)S(1)} %get-tuple-element.19), channel_id=1, source_target_pairs={{0,2},{1,3},{2,0},{3,1},{4,6},{5,7},{6,4},{7,5},{8,10},{9,11},{10,... | collective-permute-start | bytes 393224 | tf_op jit(solution)/shard_map/ppermute | solution.py:110
  22.0 4.9 %collective-permute-start.5 = (bf16[32,2048]{1,0:T(8,128)(2,1)S(1)}, bf16[32,2048]{1,0:T(8,128)(2,1)S(1)}, u32[]{:S(2)}, u32[]{:S(2)}) collective-permute-start(bf16[32,2048]{1,0:T(8,128)(2,1)S(1)} %get-tuple-element.20), channel_id=1, source_target_pairs={{0,3},{1,0},{2,1},{3,2},{4,7},{5,4},{6,5},{7,6},{8,11},{9,8},{10,9... | collective-permute-start | bytes 393224 | tf_op jit(solution)/shard_map/ppermute | solution.py:110
  35.4 18.1 %all-to-all-start.2 = ((bf16[4,32,2048]{2,1,0:T(8,128)(2,1)}), bf16[4,32,2048]{2,1,0:T(8,128)(2,1)S(1)}, u32[]{:S(2)}, u32[]{:S(2)}) async-start(bf16[4,32,2048]{2,1,0:T(8,128)(2,1)} %shard_map.77.refs_1_), calls=%async_computation.2 | async-start | bytes 1048576 | tf_op jit(solution)/shard_map/all_to_all | solution.py:116
  39.0 4.3 %collective-permute-start.8 = (bf16[32,2048]{1,0:T(8,128)(2,1)S(1)}, bf16[32,2048]{1,0:T(8,128)(2,1)S(1)}, u32[]{:S(2)}, u32[]{:S(2)}) collective-permute-start(bf16[32,2048]{1,0:T(8,128)(2,1)S(1)} %shard_map.78.refs_1_), channel_id=1, source_target_pairs={{0,3},{1,0},{2,1},{3,2},{4,7},{5,4},{6,5},{7,6},{8,11},{9,8},{10,9... | collective-permute-start | bytes 393224 | tf_op jit(solution)/shard_map/ppermute | solution.py:110
  39.4 8.0 %collective-permute-start.7 = (bf16[32,2048]{1,0:T(8,128)(2,1)S(1)}, bf16[32,2048]{1,0:T(8,128)(2,1)S(1)}, u32[]{:S(2)}, u32[]{:S(2)}) collective-permute-start(bf16[32,2048]{1,0:T(8,128)(2,1)S(1)} %shard_map.78.refs_1_), channel_id=1, source_target_pairs={{0,2},{1,3},{2,0},{3,1},{4,6},{5,7},{6,4},{7,5},{8,10},{9,11},{10,... | collective-permute-start | bytes 393224 | tf_op jit(solution)/shard_map/ppermute | solution.py:110
  40.4 7.2 %collective-permute-start.6 = (bf16[32,2048]{1,0:T(8,128)(2,1)S(1)}, bf16[32,2048]{1,0:T(8,128)(2,1)S(1)}, u32[]{:S(2)}, u32[]{:S(2)}) collective-permute-start(bf16[32,2048]{1,0:T(8,128)(2,1)S(1)} %shard_map.78.refs_1_), channel_id=1, source_target_pairs={{0,1},{1,2},{2,3},{3,0},{4,5},{5,6},{6,7},{7,4},{8,9},{9,10},{10,1... | collective-permute-start | bytes 393224 | tf_op jit(solution)/shard_map/ppermute | solution.py:110
  47.6 2.9 %copy-start = (bf16[2048,1650]{0,1:T(8,128)(2,1)S(1)}, bf16[2048,1650]{0,1:T(8,128)(2,1)}, u32[]{:S(2)}) copy-start(bf16[2048,1650]{0,1:T(8,128)(2,1)} %param.9) | copy-start | bytes 20275204
  53.6 19.0 %all-to-all-start.1 = ((bf16[4,32,1650]{2,1,0:T(8,128)(2,1)}), bf16[4,32,1650]{2,1,0:T(8,128)(2,1)S(1)}, u32[]{:S(2)}, u32[]{:S(2)}) async-start(bf16[4,32,1650]{2,1,0:T(8,128)(2,1)} %shard_map.79.refs_1_), calls=%async_computation.1 | async-start | bytes 851968 | tf_op jit(solution)/shard_map/all_to_all | solution.py:116
  58.4 3.5 %collective-permute-start.11 = (bf16[32,2048]{1,0:T(8,128)(2,1)S(1)}, bf16[32,2048]{1,0:T(8,128)(2,1)S(1)}, u32[]{:S(2)}, u32[]{:S(2)}) collective-permute-start(bf16[32,2048]{1,0:T(8,128)(2,1)S(1)} %shard_map.80.refs_1_), channel_id=1, source_target_pairs={{0,3},{1,0},{2,1},{3,2},{4,7},{5,4},{6,5},{7,6},{8,11},{9,8},{10,9... | collective-permute-start | bytes 393224 | tf_op jit(solution)/shard_map/ppermute | solution.py:110
  58.5 7.6 %collective-permute-start.10 = (bf16[32,2048]{1,0:T(8,128)(2,1)S(1)}, bf16[32,2048]{1,0:T(8,128)(2,1)S(1)}, u32[]{:S(2)}, u32[]{:S(2)}) collective-permute-start(bf16[32,2048]{1,0:T(8,128)(2,1)S(1)} %shard_map.80.refs_1_), channel_id=1, source_target_pairs={{0,2},{1,3},{2,0},{3,1},{4,6},{5,7},{6,4},{7,5},{8,10},{9,11},{10,... | collective-permute-start | bytes 393224 | tf_op jit(solution)/shard_map/ppermute | solution.py:110
  59.5 7.1 %collective-permute-start.9 = (bf16[32,2048]{1,0:T(8,128)(2,1)S(1)}, bf16[32,2048]{1,0:T(8,128)(2,1)S(1)}, u32[]{:S(2)}, u32[]{:S(2)}) collective-permute-start(bf16[32,2048]{1,0:T(8,128)(2,1)S(1)} %shard_map.80.refs_1_), channel_id=1, source_target_pairs={{0,1},{1,2},{2,3},{3,0},{4,5},{5,6},{6,7},{7,4},{8,9},{9,10},{10,1... | collective-permute-start | bytes 393224 | tf_op jit(solution)/shard_map/ppermute | solution.py:110
  66.6 2.9 %copy-start.1 = (bf16[2048,1650]{0,1:T(8,128)(2,1)S(1)}, bf16[2048,1650]{0,1:T(8,128)(2,1)}, u32[]{:S(2)}) copy-start(bf16[2048,1650]{0,1:T(8,128)(2,1)} %param.9) | copy-start | bytes 20275204
  72.6 16.3 %all-to-all-start.3 = ((bf16[4,32,1650]{2,1,0:T(8,128)(2,1)}), bf16[4,32,1650]{2,1,0:T(8,128)(2,1)S(1)}, u32[]{:S(2)}, u32[]{:S(2)}) async-start(bf16[4,32,1650]{2,1,0:T(8,128)(2,1)} %shard_map.81), calls=%async_computation.3 | async-start | bytes 851968 | tf_op jit(solution)/shard_map/all_to_all | solution.py:116

commit v2 on v0

--- a/solution.py
+++ b/solution.py
@@ -21,10 +21,10 @@
     per_half = columns // halves
     each = per_half // n_layer
     chunk, part = columns // n_row, columns // n_row // halves
-    first = lax.axis_index("layer") * each
+    me = lax.axis_index("layer")
     row = lax.broadcasted_iota(jnp.int32, (per_half, columns), 0)
     col = lax.broadcasted_iota(jnp.int32, (per_half, columns), 1)
-    place = lax.rem(row + first, per_half)
+    place = lax.bitwise_xor(row // each, me) * each + lax.rem(row, each)
     wanted = (place // part) * chunk + lax.rem(place, part) + half * part
     pick = (col == wanted).astype(BF16)
     turned = lax.dot_general(
@@ -51,10 +51,9 @@
 
 def pupil_kernel(n_layer, n_row, entries, unroll, padded, *refs):
     coded, parts = refs[:n_layer], refs[n_layer : 2 * n_layer]
-    outs = refs[2 * n_layer : 2 * n_layer + n_row]
-    total, codes, code, sem = refs[-4:]
+    keep, send, total, codes, code, sem = refs[-6:]
     weights = padded.shape[0] // 2
-    owned = outs[0].shape[1] // LANES
+    owned = keep.shape[2] // LANES
     for j, ref in enumerate(coded):
         tail = ref[:CODE_ROWS, ref.shape[1] - LANES :]
         codes[j * CODE_ROWS : (j + 1) * CODE_ROWS] = tail.astype(F32).astype(jnp.int32)
@@ -80,24 +79,24 @@
 
         lax.fori_loop(0, entries // unroll, step, 0)
     me = lax.axis_index("row")
-    for k, out in enumerate(outs):
-        base = lax.rem(me + k, n_row) * owned
+    for k in range(n_row):
+        base = lax.bitwise_xor(me, k) * owned
+        out = send if k % 2 else keep
         for s in range(owned):
-            out[:, s * LANES : (s + 1) * LANES] = total[base + s].astype(BF16)
-
-
-def sum_kernel(*refs):
-    refs[-1][...] = sum(ref[...].astype(F32) for ref in refs[:-1]).astype(BF16)
+            out[k // 2, :, s * LANES : (s + 1) * LANES] = total[base + s].astype(out.dtype)
+
+
+def sum_kernel(kept_ref, got_ref, out_ref):
+    out_ref[...] = (kept_ref[0] + got_ref[0].astype(F32)).astype(BF16)
 
 
 def fit_kernel(n_layer, n_row, fitting_ref, *refs):
-    pieces, outs = refs[:n_layer], refs[n_layer : n_layer + n_row]
-    left, product = refs[-2], refs[-1]
+    pieces, (keep, send, left, product) = refs[:n_layer], refs[n_layer:]
+    me, row = lax.axis_index("layer"), lax.axis_index("row")
     aligned = n_layer == n_row
-    me, row = lax.axis_index("layer"), lax.axis_index("row")
     for j, piece in enumerate(pieces):
-        place = me + n_layer - j
-        left[lax.rem(place + n_row - row if aligned else place, n_layer)] = piece[...]
+        place = lax.bitwise_xor(me, j)
+        left[lax.bitwise_xor(place, row) if aligned else place] = piece[...]
     columns = left.shape[0] * left.shape[1]
     found = lax.dot_general(
         left[...].reshape(columns, left.shape[2]),
@@ -106,29 +105,46 @@
         preferred_element_type=F32,
     )
     each = columns // n_row
-    if aligned:
-        for k, out in enumerate(outs):
-            out[...] = found[k * each : (k + 1) * each].astype(BF16)
-    else:
+    if not aligned:
         product[...] = found
-        for k, out in enumerate(outs):
-            start = pl.multiple_of(lax.rem(row + k, n_row) * each, each)
-            out[...] = product[pl.ds(start, each), :].astype(BF16)
+    for k in range(n_row):
+        out = send if k % 2 else keep
+        if aligned:
+            part = found[k * each : (k + 1) * each]
+        else:
+            start = pl.multiple_of(lax.bitwise_xor(row, k) * each, each)
+            part = product[pl.ds(start, each), :]
+        out[k // 2] = part.astype(out.dtype)
+
+
+def trade(chunk, axis, k):
+    return lax.ppermute(chunk, axis, [(i, i ^ k) for i in range(lax.axis_size(axis))])
 
 
 def exchange(chunks, axis):
-    n = len(chunks)
-    return [
-        chunk if k == 0 else lax.ppermute(chunk, axis, [(i, (i + k) % n) for i in range(n)])
-        for k, chunk in enumerate(chunks)
-    ]
-
-
-def total_of(parts):
-    return sum(part.astype(F32) for part in parts).astype(BF16)
-
-
-def call(kernel, shapes, scratch, *args, after=()):
+    return [chunk if k == 0 else trade(chunk, axis, k) for k, chunk in enumerate(chunks)]
+
+
+def gather(piece, axis):
+    got = []
+    for k in range(0, lax.axis_size(axis), 2):
+        got.append(trade(piece, axis, k) if k else piece)
+        got.append(trade(got[-1], axis, 1))
+    return got
+
+
+def reduce(keep, send, axis):
+    step = 1
+    while True:
+        got = trade(send, axis, step)
+        if keep.shape[0] == 1:
+            return keep, got
+        added = keep + got.astype(F32)
+        keep, send = added[::2], added[1::2].astype(BF16)
+        step *= 2
+
+
+def call(kernel, shapes, scratch, *args, types=None, after=()):
     given = len(args)
 
     def body(*refs):
@@ -136,7 +152,10 @@
 
     return pl.pallas_call(
         body,
-        out_shape=[jax.ShapeDtypeStruct(shape, BF16) for shape in shapes],
+        out_shape=[
+            jax.ShapeDtypeStruct(shape, kind)
+            for shape, kind in zip(shapes, types or [BF16] * len(shapes))
+        ],
         in_specs=[VMEM] * len(args) + [ANY] * len(after),
         out_specs=[VMEM] * len(shapes),
         scratch_shapes=scratch,
@@ -177,11 +196,11 @@
         after=before,
     )
 
-    received, before = [], ()
+    received, before = [], tuple(parts[-1][1:2])
     for h in range(halves):
         shares = call(
             functools.partial(pupil_kernel, n_layer, n_row, entries, entries),
-            [(each, points)] * n_row,
+            [(n_row // 2, each, points)] * 2,
             [
                 pltpu.VMEM((n_row * owned, each, slice_rows), F32),
                 pltpu.VMEM((n_layer * CODE_ROWS, LANES), jnp.int32),
@@ -191,24 +210,28 @@
             padded,
             *parts[0],
             *parts[h],
+            types=(F32, BF16),
             after=before,
         )
         before = (shares[0],)
-        received.append(exchange(shares, "row"))
+        received.append(shares)
     results = []
     for h in range(halves):
-        (pupil,) = call(sum_kernel, [(each, points)], [], *received[h], after=before)
-        pieces = exchange([pupil] * n_layer, "layer")
+        kept, got = reduce(*received[h], "row")
+        (pupil,) = call(sum_kernel, [(each, points)], [], kept, got, after=before)
+        pieces = gather(pupil, "layer")
         partial = call(
             functools.partial(fit_kernel, n_layer, n_row),
-            [(chunk // halves, actuators)] * n_row,
+            [(n_row // 2, chunk // halves, actuators)] * 2,
             [pltpu.VMEM((n_layer, each, points), BF16), pltpu.VMEM((per_half, actuators), F32)],
             fitting.T,
             *pieces,
+            types=(F32, BF16),
         )
         before = (partial[0],)
-        results.append(exchange(partial, "row"))
-    return jnp.concatenate([total_of(result) for result in results], 0)
+        kept, got = reduce(*partial, "row")
+        results.append((kept[0] + got[0].astype(F32)).astype(BF16))
+    return jnp.concatenate(results, 0)
 
 
 def solution(mesh):

time: 69.9 us -> 73.3 us (1.049)
  waiting for transfers between devices: 20.3 us -> 40.1 us
  starting transfers between devices: 34.3 us -> 17.9 us
    ppermute x24 -> x20, waiting for transfers between devices: 20.3 us -> 40.1 us  [trade(): lax.ppermute(chunk, axis, [(i, i ^ k) for i in range(lax.axis_size(axis))])]
    ppermute x24 -> x20, starting transfers between devices: 34.3 us -> 17.9 us  [trade(): lax.ppermute(chunk, axis, [(i, i ^ k) for i in range(lax.axis_size(axis))])]
    unnamed x6 -> x8, local copies, waits for them, and re-layouts: 2.29 us -> 2.18 us
  transfers between devices with their start and end apart: 24 -> 20, of which waited for: 8 -> 12; matrix products, arithmetic and copies ran while one was open for 0% -> 0% of each run, Pallas kernels for 15% -> 11%
where the time goes in v2:
time: 73.3 us; the launch traced here: 73.1 us
  waiting for transfers between devices  40.1 us (55%)
  starting transfers between devices  17.9 us (24%)
  Pallas kernels  10.9 us (15%)
  local copies, waits for them, and re-layouts  2.28 us (3%)
  other arithmetic  1.66 us (2%)
    ppermute x20, waiting for transfers between devices, trade(): lax.ppermute(chunk, axis, [(i, i ^ k) for i in range(lax.axis_size(axis))])  40.1 us
    ppermute x20, starting transfers between devices, trade(): lax.ppermute(chunk, axis, [(i, i ^ k) for i in range(lax.axis_size(axis))])  17.9 us
    pallas_call x9, Pallas kernels, call(): pl.pallas_call(body, out_shape=[jax.ShapeDtypeStruct(shape, kind) for sha...  10.9 us
    unnamed x8, local copies, waits for them, and re-layouts  2.18 us
  transfers between devices with their start and end apart: 20, of which 12 were waited for; matrix products, arithmetic and copies ran while one was open for 0% of the time, Pallas kernels for 11%

profile of v2, /device:TPU:0, one launch (start us, length us, event | category | flops | bytes accessed | tf_op | source)
XLA Modules:
  0.0 73.1 jit_solution(7762070279432035141)
XLA Ops:
  0.7 1.2 %copy-done = bf16[1,2048,256]{2,1,0:T(8,128)(2,1)S(1)} copy-done((bf16[1,2048,256]{2,1,0:T(8,128)(2,1)S(1)}, bf16[1,2048,256]{2,1,0:T(8,128)(2,1)}, u32[]{:S(2)}) %copy-start) | copy-done | bytes 1048600
  2.9 2.6 %collective-permute-start.1 = (bf16[32,2176]{1,0:T(8,128)(2,1)S(1)}, bf16[32,2176]{1,0:T(8,128)(2,1)S(1)}, u32[]{:S(2)}, u32[]{:S(2)}) collective-permute-start(bf16[32,2176]{1,0:T(8,128)(2,1)S(1)} %get-tuple-element.24), channel_id=1, source_target_pairs={{0,2},{1,3},{2,0},{3,1},{4,6},{5,7},{6,4},{7,5},{8,10},{9,11},{10,... | collective-permute-start | bytes 417800 | tf_op jit(solution)/shard_map/ppermute | solution.py:121
  7.5 2.6 %collective-permute-done.1.refs_3_.refs_7_ = bf16[32,2176]{1,0:T(8,128)(2,1)S(1)} collective-permute-done((bf16[32,2176]{1,0:T(8,128)(2,1)S(1)}, bf16[32,2176]{1,0:T(8,128)(2,1)S(1)}, u32[]{:S(2)}, u32[]{:S(2)}) %collective-permute-start.1) | collective-permute-done | bytes 139296 | tf_op jit(solution)/shard_map/ppermute | solution.py:121
  10.0 2.5 %collective-permute-done.2.refs_4_.refs_8_ = bf16[32,2176]{1,0:T(8,128)(2,1)S(1)} collective-permute-done((bf16[32,2176]{1,0:T(8,128)(2,1)S(1)}, bf16[32,2176]{1,0:T(8,128)(2,1)S(1)}, u32[]{:S(2)}, u32[]{:S(2)}) %collective-permute-start.2) | collective-permute-done | bytes 139296 | tf_op jit(solution)/shard_map/ppermute | solution.py:121
  12.5 2.6 %shard_map.76 = (f32[2,32,2048]{2,1,0:T(8,128)S(1)}, bf16[2,32,2048]{2,1,0:T(8,128)(2,1)S(1)}) custom-call(bf16[32,128,128]{2,1,0:T(8,128)(2,1)S(1)} %shard_map.75.refs_0_, bf16[32,2176]{1,0:T(8,128)(2,1)S(1)} %get-tuple-element.21.refs_2_.refs_1_.refs_5_, bf16[32,2176]{1,0:T(8,128)(2,1)S(1)} %collective-permute-done.refs_2_.refs_6_, ...), custom_call_target="tpu_custom_call" | custom-call | tf_op jit(solution)/shard_map/pallas_call | solution.py:153
  15.1 1.7 %collective-permute-start.4 = (bf16[2,32,2048]{2,1,0:T(8,128)(2,1)S(1)}, bf16[2,32,2048]{2,1,0:T(8,128)(2,1)S(1)}, u32[]{:S(2)}, u32[]{:S(2)}) collective-permute-start(bf16[2,32,2048]{2,1,0:T(8,128)(2,1)S(1)} %get-tuple-element.28), channel_id=1, source_target_pairs={{0,4},{4,0},{8,12},{12,8},{1,5},{5,1},{9,13},{13,9},{2,6},{6,2},{1... | collective-permute-start | bytes 786440 | tf_op jit(solution)/shard_map/ppermute | solution.py:121
  16.8 1.5 %collective-permute-start.6 = (bf16[32,2048]{1,0:T(8,128)(2,1)S(1)}, bf16[32,2048]{1,0:T(8,128)(2,1)S(1)}, u32[]{:S(2)}, u32[]{:S(2)}) collective-permute-start(bf16[32,2048]{1,0:T(8,128)(2,1)S(1)} %get-tuple-element.29), channel_id=1, source_target_pairs={{0,2},{1,3},{2,0},{3,1},{4,6},{5,7},{6,4},{7,5},{8,10},{9,11},{10,... | collective-permute-start | bytes 393224 | tf_op jit(solution)/shard_map/ppermute | solution.py:121
  18.3 5.2 %collective-permute-done.4 = bf16[2,32,2048]{2,1,0:T(8,128)(2,1)S(1)} collective-permute-done((bf16[2,32,2048]{2,1,0:T(8,128)(2,1)S(1)}, bf16[2,32,2048]{2,1,0:T(8,128)(2,1)S(1)}, u32[]{:S(2)}, u32[]{:S(2)}) %collective-permute-start.4) | collective-permute-done | bytes 262176 | tf_op jit(solution)/shard_map/ppermute | solution.py:121
  23.6 2.8 %collective-permute-start.5 = (bf16[1,32,2048]{2,1,0:T(8,128)(2,1)S(1)}, bf16[1,32,2048]{2,1,0:T(8,128)(2,1)S(1)}, u32[]{:S(2)}, u32[]{:S(2)}) collective-permute-start(bf16[1,32,2048]{2,1,0:T(8,128)(2,1)S(1)} %slice.67), channel_id=1, source_target_pairs={{0,8},{4,12},{8,0},{12,4},{1,9},{5,13},{9,1},{13,5},{2,10},{6,14},... | collective-permute-start | bytes 393224 | tf_op jit(solution)/shard_map/ppermute | solution.py:121
  26.4 2.6 %shard_map.77 = (f32[2,32,2048]{2,1,0:T(8,128)S(1)}, bf16[2,32,2048]{2,1,0:T(8,128)(2,1)S(1)}) custom-call(bf16[32,128,128]{2,1,0:T(8,128)(2,1)S(1)} %shard_map.75.refs_0_, bf16[32,2176]{1,0:T(8,128)(2,1)S(1)} %get-tuple-element.21.refs_2_.refs_1_.refs_5_, bf16[32,2176]{1,0:T(8,128)(2,1)S(1)} %collective-permute-done.refs_2_.refs_6_, ...), custom_call_target="tpu_custom_call" | custom-call | tf_op jit(solution)/shard_map/pallas_call | solution.py:153
  29.0 1.6 %collective-permute-start.13 = (bf16[2,32,2048]{2,1,0:T(8,128)(2,1)S(1)}, bf16[2,32,2048]{2,1,0:T(8,128)(2,1)S(1)}, u32[]{:S(2)}, u32[]{:S(2)}) collective-permute-start(bf16[2,32,2048]{2,1,0:T(8,128)(2,1)S(1)} %get-tuple-element.34), channel_id=1, source_target_pairs={{0,4},{4,0},{8,12},{12,8},{1,5},{5,1},{9,13},{13,9},{2,6},{6,2},{1... | collective-permute-start | bytes 786440 | tf_op jit(solution)/shard_map/ppermute | solution.py:121
  30.7 1.8 %collective-permute-done.5.refs_1_ = bf16[1,32,2048]{2,1,0:T(8,128)(2,1)S(1)} collective-permute-done((bf16[1,32,2048]{2,1,0:T(8,128)(2,1)S(1)}, bf16[1,32,2048]{2,1,0:T(8,128)(2,1)S(1)}, u32[]{:S(2)}, u32[]{:S(2)}) %collective-permute-start.5) | collective-permute-done | bytes 131104 | tf_op jit(solution)/shard_map/ppermute | solution.py:121
  32.5 1.6 %collective-permute-start.9 = (bf16[32,2048]{1,0:T(8,128)(2,1)S(1)}, bf16[32,2048]{1,0:T(8,128)(2,1)S(1)}, u32[]{:S(2)}, u32[]{:S(2)}) collective-permute-start(bf16[32,2048]{1,0:T(8,128)(2,1)S(1)} %shard_map.78.refs_1_), channel_id=1, source_target_pairs={{0,2},{1,3},{2,0},{3,1},{4,6},{5,7},{6,4},{7,5},{8,10},{9,11},{10,... | collective-permute-start | bytes 393224 | tf_op jit(solution)/shard_map/ppermute | solution.py:121
  34.1 3.4 %collective-permute-done.9.refs_3_ = bf16[32,2048]{1,0:T(8,128)(2,1)S(1)} collective-permute-done((bf16[32,2048]{1,0:T(8,128)(2,1)S(1)}, bf16[32,2048]{1,0:T(8,128)(2,1)S(1)}, u32[]{:S(2)}, u32[]{:S(2)}) %collective-permute-start.9) | collective-permute-done | bytes 131104 | tf_op jit(solution)/shard_map/ppermute | solution.py:121
  38.1 1.1 %collective-permute-start.14 = (bf16[1,32,2048]{2,1,0:T(8,128)(2,1)S(1)}, bf16[1,32,2048]{2,1,0:T(8,128)(2,1)S(1)}, u32[]{:S(2)}, u32[]{:S(2)}) collective-permute-start(bf16[1,32,2048]{2,1,0:T(8,128)(2,1)S(1)} %slice.66), channel_id=1, source_target_pairs={{0,8},{4,12},{8,0},{12,4},{1,9},{5,13},{9,1},{13,5},{2,10},{6,14},... | collective-permute-start | bytes 393224 | tf_op jit(solution)/shard_map/ppermute | solution.py:121
  39.2 2.3 %shard_map.79 = (f32[2,32,1650]{2,1,0:T(8,128)S(1)}, bf16[2,32,1650]{2,1,0:T(8,128)(2,1)S(1)}) custom-call(bf16[1650,2048]{1,0:T(8,128)(2,1)S(1)} %bitcast.10, bf16[32,2048]{1,0:T(8,128)(2,1)S(1)} %shard_map.78.refs_1_, bf16[32,2048]{1,0:T(8,128)(2,1)S(1)} %collective-permute-done.8.refs_2_, bf16[32,2048]{1,0:T(8,128)(2,1)S(1)} %collective-permute-done.9.refs_3_, ...), custom_call_target="tpu_custom_call" | custom-call | tf_op jit(solution)/shard_map/pallas_call | solution.py:153
  41.5 5.8 %collective-permute-done.14.refs_1_ = bf16[1,32,2048]{2,1,0:T(8,128)(2,1)S(1)} collective-permute-done((bf16[1,32,2048]{2,1,0:T(8,128)(2,1)S(1)}, bf16[1,32,2048]{2,1,0:T(8,128)(2,1)S(1)}, u32[]{:S(2)}, u32[]{:S(2)}) %collective-permute-start.14) | collective-permute-done | bytes 131104 | tf_op jit(solution)/shard_map/ppermute | solution.py:121
  47.3 1.6 %collective-permute-start.16 = (bf16[32,2048]{1,0:T(8,128)(2,1)S(1)}, bf16[32,2048]{1,0:T(8,128)(2,1)S(1)}, u32[]{:S(2)}, u32[]{:S(2)}) collective-permute-start(bf16[32,2048]{1,0:T(8,128)(2,1)S(1)} %shard_map.80.refs_1_), channel_id=1, source_target_pairs={{0,2},{1,3},{2,0},{3,1},{4,6},{5,7},{6,4},{7,5},{8,10},{9,11},{10,... | collective-permute-start | bytes 393224 | tf_op jit(solution)/shard_map/ppermute | solution.py:121
  48.9 3.4 %collective-permute-done.16.refs_3_ = bf16[32,2048]{1,0:T(8,128)(2,1)S(1)} collective-permute-done((bf16[32,2048]{1,0:T(8,128)(2,1)S(1)}, bf16[32,2048]{1,0:T(8,128)(2,1)S(1)}, u32[]{:S(2)}, u32[]{:S(2)}) %collective-permute-start.16) | collective-permute-done | bytes 131104 | tf_op jit(solution)/shard_map/ppermute | solution.py:121
  52.4 1.3 %collective-permute-done.17.refs_4_ = bf16[32,2048]{1,0:T(8,128)(2,1)S(1)} collective-permute-done((bf16[32,2048]{1,0:T(8,128)(2,1)S(1)}, bf16[32,2048]{1,0:T(8,128)(2,1)S(1)}, u32[]{:S(2)}, u32[]{:S(2)}) %collective-permute-start.17) | collective-permute-done | bytes 131104 | tf_op jit(solution)/shard_map/ppermute | solution.py:121
  53.7 2.3 %shard_map.81 = (f32[2,32,1650]{2,1,0:T(8,128)S(1)}, bf16[2,32,1650]{2,1,0:T(8,128)(2,1)S(1)}) custom-call(bf16[1650,2048]{1,0:T(8,128)(2,1)S(1)} %bitcast.11, bf16[32,2048]{1,0:T(8,128)(2,1)S(1)} %shard_map.80.refs_1_, bf16[32,2048]{1,0:T(8,128)(2,1)S(1)} %collective-permute-done.15.refs_2_, bf16[32,2048]{1,0:T(8,128)(2,1)S(1)} %collective-permute-done.16.refs_3_, ...), custom_call_target="tpu_custom_call" | custom-call | tf_op jit(solution)/shard_map/pallas_call | solution.py:153
  56.1 2.4 %collective-permute-start.12 = (bf16[1,32,1650]{2,1,0:T(8,128)(2,1)S(1)}, bf16[1,32,1650]{2,1,0:T(8,128)(2,1)S(1)}, u32[]{:S(2)}, u32[]{:S(2)}) collective-permute-start(bf16[1,32,1650]{2,1,0:T(8,128)(2,1)S(1)} %slice.69), channel_id=1, source_target_pairs={{0,8},{4,12},{8,0},{12,4},{1,9},{5,13},{9,1},{13,5},{2,10},{6,14},... | collective-permute-start | bytes 316808 | tf_op jit(solution)/shard_map/ppermute | solution.py:121
  58.6 7.0 %collective-permute-done.18 = bf16[2,32,1650]{2,1,0:T(8,128)(2,1)S(1)} collective-permute-done((bf16[2,32,1650]{2,1,0:T(8,128)(2,1)S(1)}, bf16[2,32,1650]{2,1,0:T(8,128)(2,1)S(1)}, u32[]{:S(2)}, u32[]{:S(2)}) %collective-permute-start.18) | collective-permute-done | bytes 211232 | tf_op jit(solution)/shard_map/ppermute | solution.py:121
  65.8 6.5 %collective-permute-done.19 = bf16[1,32,1650]{2,1,0:T(8,128)(2,1)S(1)} collective-permute-done((bf16[1,32,1650]{2,1,0:T(8,128)(2,1)S(1)}, bf16[1,32,1650]{2,1,0:T(8,128)(2,1)S(1)}, u32[]{:S(2)}, u32[]{:S(2)}) %collective-permute-start.19) | collective-permute-done | bytes 105632 | tf_op jit(solution)/shard_map/ppermute | solution.py:121
  (48 shorter events, 5.4 us)
Async XLA Ops:
  0.7 1.2 %copy-start = (bf16[1,2048,256]{2,1,0:T(8,128)(2,1)S(1)}, bf16[1,2048,256]{2,1,0:T(8,128)(2,1)}, u32[]{:S(2)}) copy-start(bf16[1,2048,256]{2,1,0:T(8,128)(2,1)} %param.7) | copy-start | bytes 3145732
  1.9 37.3 %slice-start = ((s8[6782976]{0:T(1024)(128)(4,1)}), s8[4194304]{0:T(1024)(128)(4,1)S(1)}, s32[]{:S(2)}) async-start(s8[6782976]{0:T(1024)(128)(4,1)} %bitcast.8), calls=%async_computation | async-start | bytes 8388608
  2.4 5.1 %collective-permute-start = (bf16[32,2176]{1,0:T(8,128)(2,1)S(1)}, bf16[32,2176]{1,0:T(8,128)(2,1)S(1)}, u32[]{:S(2)}, u32[]{:S(2)}) collective-permute-start(bf16[32,2176]{1,0:T(8,128)(2,1)S(1)} %get-tuple-element.23), channel_id=1, source_target_pairs={{0,1},{1,0},{2,3},{3,2},{4,5},{5,4},{6,7},{7,6},{8,9},{9,8},{10,11... | collective-permute-start | bytes 417800 | tf_op jit(solution)/shard_map/ppermute | solution.py:121
  2.9 7.1 %collective-permute-start.1 = (bf16[32,2176]{1,0:T(8,128)(2,1)S(1)}, bf16[32,2176]{1,0:T(8,128)(2,1)S(1)}, u32[]{:S(2)}, u32[]{:S(2)}) collective-permute-start(bf16[32,2176]{1,0:T(8,128)(2,1)S(1)} %get-tuple-element.24), channel_id=1, source_target_pairs={{0,2},{1,3},{2,0},{3,1},{4,6},{5,7},{6,4},{7,5},{8,10},{9,11},{10,... | collective-permute-start | bytes 417800 | tf_op jit(solution)/shard_map/ppermute | solution.py:121
  5.5 7.0 %collective-permute-start.2 = (bf16[32,2176]{1,0:T(8,128)(2,1)S(1)}, bf16[32,2176]{1,0:T(8,128)(2,1)S(1)}, u32[]{:S(2)}, u32[]{:S(2)}) collective-permute-start(bf16[32,2176]{1,0:T(8,128)(2,1)S(1)} %get-tuple-element.25), channel_id=1, source_target_pairs={{0,3},{1,2},{2,1},{3,0},{4,7},{5,6},{6,5},{7,4},{8,11},{9,10},{10,... | collective-permute-start | bytes 417800 | tf_op jit(solution)/shard_map/ppermute | solution.py:121
  6.1 1.4 %collective-permute-start.3 = (bf16[32,2048]{1,0:T(8,128)(2,1)S(1)}, bf16[32,2048]{1,0:T(8,128)(2,1)S(1)}, u32[]{:S(2)}, u32[]{:S(2)}) collective-permute-start(bf16[32,2048]{1,0:T(8,128)(2,1)S(1)} %get-tuple-element.26), channel_id=1, source_target_pairs={{0,1},{1,0},{2,3},{3,2},{4,5},{5,4},{6,7},{7,6},{8,9},{9,8},{10,11... | collective-permute-start | bytes 393224 | tf_op jit(solution)/shard_map/ppermute | solution.py:121
  6.3 0.9 %copy-start.1 = (bf16[16,128,64]{1,2,0:T(8,128)(2,1)S(1)}, bf16[16,128,64]{1,2,0:T(8,128)(2,1)}, u32[]{:S(2)}) copy-start(bf16[16,128,64]{1,2,0:T(8,128)(2,1)} %param.8) | copy-start | bytes 786436
  15.1 8.5 %collective-permute-start.4 = (bf16[2,32,2048]{2,1,0:T(8,128)(2,1)S(1)}, bf16[2,32,2048]{2,1,0:T(8,128)(2,1)S(1)}, u32[]{:S(2)}, u32[]{:S(2)}) collective-permute-start(bf16[2,32,2048]{2,1,0:T(8,128)(2,1)S(1)} %get-tuple-element.28), channel_id=1, source_target_pairs={{0,4},{4,0},{8,12},{12,8},{1,5},{5,1},{9,13},{13,9},{2,6},{6,2},{1... | collective-permute-start | bytes 786440 | tf_op jit(solution)/shard_map/ppermute | solution.py:121
  16.8 9.7 %collective-permute-start.6 = (bf16[32,2048]{1,0:T(8,128)(2,1)S(1)}, bf16[32,2048]{1,0:T(8,128)(2,1)S(1)}, u32[]{:S(2)}, u32[]{:S(2)}) collective-permute-start(bf16[32,2048]{1,0:T(8,128)(2,1)S(1)} %get-tuple-element.29), channel_id=1, source_target_pairs={{0,2},{1,3},{2,0},{3,1},{4,6},{5,7},{6,4},{7,5},{8,10},{9,11},{10,... | collective-permute-start | bytes 393224 | tf_op jit(solution)/shard_map/ppermute | solution.py:121
  18.3 8.2 %collective-permute-start.7 = (bf16[32,2048]{1,0:T(8,128)(2,1)S(1)}, bf16[32,2048]{1,0:T(8,128)(2,1)S(1)}, u32[]{:S(2)}, u32[]{:S(2)}) collective-permute-start(bf16[32,2048]{1,0:T(8,128)(2,1)S(1)} %get-tuple-element.30), channel_id=1, source_target_pairs={{0,3},{1,2},{2,1},{3,0},{4,7},{5,6},{6,5},{7,4},{8,11},{9,10},{10,... | collective-permute-start | bytes 393224 | tf_op jit(solution)/shard_map/ppermute | solution.py:121
  23.5 15.7 %slice-start.1 = ((s8[6782976]{0:T(1024)(128)(4,1)}), s8[2588672]{0:T(1024)(128)(4,1)S(1)}, s32[]{:S(2)}) async-start(s8[6782976]{0:T(1024)(128)(4,1)} %bitcast.8), calls=%async_computation.1 | async-start | bytes 5177344
  23.6 8.9 %collective-permute-start.5 = (bf16[1,32,2048]{2,1,0:T(8,128)(2,1)S(1)}, bf16[1,32,2048]{2,1,0:T(8,128)(2,1)S(1)}, u32[]{:S(2)}, u32[]{:S(2)}) collective-permute-start(bf16[1,32,2048]{2,1,0:T(8,128)(2,1)S(1)} %slice.67), channel_id=1, source_target_pairs={{0,8},{4,12},{8,0},{12,4},{1,9},{5,13},{9,1},{13,5},{2,10},{6,14},... | collective-permute-start | bytes 393224 | tf_op jit(solution)/shard_map/ppermute | solution.py:121
  29.0 9.0 %collective-permute-start.13 = (bf16[2,32,2048]{2,1,0:T(8,128)(2,1)S(1)}, bf16[2,32,2048]{2,1,0:T(8,128)(2,1)S(1)}, u32[]{:S(2)}, u32[]{:S(2)}) collective-permute-start(bf16[2,32,2048]{2,1,0:T(8,128)(2,1)S(1)} %get-tuple-element.34), channel_id=1, source_target_pairs={{0,4},{4,0},{8,12},{12,8},{1,5},{5,1},{9,13},{13,9},{2,6},{6,2},{1... | collective-permute-start | bytes 786440 | tf_op jit(solution)/shard_map/ppermute | solution.py:121
  32.5 5.0 %collective-permute-start.9 = (bf16[32,2048]{1,0:T(8,128)(2,1)S(1)}, bf16[32,2048]{1,0:T(8,128)(2,1)S(1)}, u32[]{:S(2)}, u32[]{:S(2)}) collective-permute-start(bf16[32,2048]{1,0:T(8,128)(2,1)S(1)} %shard_map.78.refs_1_), channel_id=1, source_target_pairs={{0,2},{1,3},{2,0},{3,1},{4,6},{5,7},{6,4},{7,5},{8,10},{9,11},{10,... | collective-permute-start | bytes 393224 | tf_op jit(solution)/shard_map/ppermute | solution.py:121
  34.1 5.1 %collective-permute-start.8 = (bf16[32,2048]{1,0:T(8,128)(2,1)S(1)}, bf16[32,2048]{1,0:T(8,128)(2,1)S(1)}, u32[]{:S(2)}, u32[]{:S(2)}) collective-permute-start(bf16[32,2048]{1,0:T(8,128)(2,1)S(1)} %shard_map.78.refs_1_), channel_id=1, source_target_pairs={{0,1},{1,0},{2,3},{3,2},{4,5},{5,4},{6,7},{7,6},{8,9},{9,8},{10,11... | collective-permute-start | bytes 393224 | tf_op jit(solution)/shard_map/ppermute | solution.py:121
  37.5 1.7 %collective-permute-start.10 = (bf16[32,2048]{1,0:T(8,128)(2,1)S(1)}, bf16[32,2048]{1,0:T(8,128)(2,1)S(1)}, u32[]{:S(2)}, u32[]{:S(2)}) collective-permute-start(bf16[32,2048]{1,0:T(8,128)(2,1)S(1)} %collective-permute-done.9.refs_3_), channel_id=1, source_target_pairs={{0,1},{1,0},{2,3},{3,2},{4,5},{5,4},{6,7},{7,6},{8,9},{9,8},{10,11... | collective-permute-start | bytes 393224 | tf_op jit(solution)/shard_map/ppermute | solution.py:121
  38.1 9.2 %collective-permute-start.14 = (bf16[1,32,2048]{2,1,0:T(8,128)(2,1)S(1)}, bf16[1,32,2048]{2,1,0:T(8,128)(2,1)S(1)}, u32[]{:S(2)}, u32[]{:S(2)}) collective-permute-start(bf16[1,32,2048]{2,1,0:T(8,128)(2,1)S(1)} %slice.66), channel_id=1, source_target_pairs={{0,8},{4,12},{8,0},{12,4},{1,9},{5,13},{9,1},{13,5},{2,10},{6,14},... | collective-permute-start | bytes 393224 | tf_op jit(solution)/shard_map/ppermute | solution.py:121
  47.3 5.0 %collective-permute-start.16 = (bf16[32,2048]{1,0:T(8,128)(2,1)S(1)}, bf16[32,2048]{1,0:T(8,128)(2,1)S(1)}, u32[]{:S(2)}, u32[]{:S(2)}) collective-permute-start(bf16[32,2048]{1,0:T(8,128)(2,1)S(1)} %shard_map.80.refs_1_), channel_id=1, source_target_pairs={{0,2},{1,3},{2,0},{3,1},{4,6},{5,7},{6,4},{7,5},{8,10},{9,11},{10,... | collective-permute-start | bytes 393224 | tf_op jit(solution)/shard_map/ppermute | solution.py:121
  48.9 7.1 %collective-permute-start.11 = (bf16[2,32,1650]{2,1,0:T(8,128)(2,1)S(1)}, bf16[2,32,1650]{2,1,0:T(8,128)(2,1)S(1)}, u32[]{:S(2)}, u32[]{:S(2)}) collective-permute-start(bf16[2,32,1650]{2,1,0:T(8,128)(2,1)S(1)} %get-tuple-element.33), channel_id=1, source_target_pairs={{0,4},{4,0},{8,12},{12,8},{1,5},{5,1},{9,13},{13,9},{2,6},{6,2},{1... | collective-permute-start | bytes 633608 | tf_op jit(solution)/shard_map/ppermute | solution.py:121
  48.9 3.4 %collective-permute-start.15 = (bf16[32,2048]{1,0:T(8,128)(2,1)S(1)}, bf16[32,2048]{1,0:T(8,128)(2,1)S(1)}, u32[]{:S(2)}, u32[]{:S(2)}) collective-permute-start(bf16[32,2048]{1,0:T(8,128)(2,1)S(1)} %shard_map.80.refs_1_), channel_id=1, source_target_pairs={{0,1},{1,0},{2,3},{3,2},{4,5},{5,4},{6,7},{7,6},{8,9},{9,8},{10,11... | collective-permute-start | bytes 393224 | tf_op jit(solution)/shard_map/ppermute | solution.py:121
  52.4 1.3 %collective-permute-start.17 = (bf16[32,2048]{1,0:T(8,128)(2,1)S(1)}, bf16[32,2048]{1,0:T(8,128)(2,1)S(1)}, u32[]{:S(2)}, u32[]{:S(2)}) collective-permute-start(bf16[32,2048]{1,0:T(8,128)(2,1)S(1)} %collective-permute-done.16.refs_3_), channel_id=1, source_target_pairs={{0,1},{1,0},{2,3},{3,2},{4,5},{5,4},{6,7},{7,6},{8,9},{9,8},{10,11... | collective-permute-start | bytes 393224 | tf_op jit(solution)/shard_map/ppermute | solution.py:121
  56.0 9.7 %collective-permute-start.18 = (bf16[2,32,1650]{2,1,0:T(8,128)(2,1)S(1)}, bf16[2,32,1650]{2,1,0:T(8,128)(2,1)S(1)}, u32[]{:S(2)}, u32[]{:S(2)}) collective-permute-start(bf16[2,32,1650]{2,1,0:T(8,128)(2,1)S(1)} %get-tuple-element.36), channel_id=1, source_target_pairs={{0,4},{4,0},{8,12},{12,8},{1,5},{5,1},{9,13},{13,9},{2,6},{6,2},{1... | collective-permute-start | bytes 633608 | tf_op jit(solution)/shard_map/ppermute | solution.py:121
  56.1 9.6 %collective-permute-start.12 = (bf16[1,32,1650]{2,1,0:T(8,128)(2,1)S(1)}, bf16[1,32,1650]{2,1,0:T(8,128)(2,1)S(1)}, u32[]{:S(2)}, u32[]{:S(2)}) collective-permute-start(bf16[1,32,1650]{2,1,0:T(8,128)(2,1)S(1)} %slice.69), channel_id=1, source_target_pairs={{0,8},{4,12},{8,0},{12,4},{1,9},{5,13},{9,1},{13,5},{2,10},{6,14},... | collective-permute-start | bytes 316808 | tf_op jit(solution)/shard_map/ppermute | solution.py:121
  65.7 6.6 %collective-permute-start.19 = (bf16[1,32,1650]{2,1,0:T(8,128)(2,1)S(1)}, bf16[1,32,1650]{2,1,0:T(8,128)(2,1)S(1)}, u32[]{:S(2)}, u32[]{:S(2)}) collective-permute-start(bf16[1,32,1650]{2,1,0:T(8,128)(2,1)S(1)} %slice.68), channel_id=1, source_target_pairs={{0,8},{4,12},{8,0},{12,4},{1,9},{5,13},{9,1},{13,5},{2,10},{6,14},... | collective-permute-start | bytes 316808 | tf_op jit(solution)/shard_map/ppermute | solution.py:121

commit v3 on v0

--- a/solution.py
+++ b/solution.py
@@ -21,10 +21,10 @@
     per_half = columns // halves
     each = per_half // n_layer
     chunk, part = columns // n_row, columns // n_row // halves
-    first = lax.axis_index("layer") * each
+    me = lax.axis_index("layer")
     row = lax.broadcasted_iota(jnp.int32, (per_half, columns), 0)
     col = lax.broadcasted_iota(jnp.int32, (per_half, columns), 1)
-    place = lax.rem(row + first, per_half)
+    place = lax.bitwise_xor(row // each, me) * each + lax.rem(row, each)
     wanted = (place // part) * chunk + lax.rem(place, part) + half * part
     pick = (col == wanted).astype(BF16)
     turned = lax.dot_general(
@@ -81,7 +81,7 @@
         lax.fori_loop(0, entries // unroll, step, 0)
     me = lax.axis_index("row")
     for k, out in enumerate(outs):
-        base = lax.rem(me + k, n_row) * owned
+        base = lax.bitwise_xor(me, k) * owned
         for s in range(owned):
             out[:, s * LANES : (s + 1) * LANES] = total[base + s].astype(BF16)
 
@@ -96,8 +96,8 @@
     aligned = n_layer == n_row
     me, row = lax.axis_index("layer"), lax.axis_index("row")
     for j, piece in enumerate(pieces):
-        place = me + n_layer - j
-        left[lax.rem(place + n_row - row if aligned else place, n_layer)] = piece[...]
+        place = lax.bitwise_xor(me, j)
+        left[lax.bitwise_xor(place, row) if aligned else place] = piece[...]
     columns = left.shape[0] * left.shape[1]
     found = lax.dot_general(
         left[...].reshape(columns, left.shape[2]),
@@ -112,14 +112,14 @@
     else:
         product[...] = found
         for k, out in enumerate(outs):
-            start = pl.multiple_of(lax.rem(row + k, n_row) * each, each)
+            start = pl.multiple_of(lax.bitwise_xor(row, k) * each, each)
             out[...] = product[pl.ds(start, each), :].astype(BF16)
 
 
 def exchange(chunks, axis):
     n = len(chunks)
     return [
-        chunk if k == 0 else lax.ppermute(chunk, axis, [(i, (i + k) % n) for i in range(n)])
+        chunk if k == 0 else lax.ppermute(chunk, axis, [(i, i ^ k) for i in range(n)])
         for k, chunk in enumerate(chunks)
     ]
 
@@ -195,18 +195,20 @@
         )
         before = (shares[0],)
         received.append(exchange(shares, "row"))
+    pupils = []
+    for h in range(halves):
+        pupils += call(sum_kernel, [(each, points)], [], *received[h], after=before)
     results = []
     for h in range(halves):
-        (pupil,) = call(sum_kernel, [(each, points)], [], *received[h], after=before)
-        pieces = exchange([pupil] * n_layer, "layer")
+        pieces = exchange([pupils[h]] * n_layer, "layer")
         partial = call(
             functools.partial(fit_kernel, n_layer, n_row),
             [(chunk // halves, actuators)] * n_row,
             [pltpu.VMEM((n_layer, each, points), BF16), pltpu.VMEM((per_half, actuators), F32)],
             fitting.T,
             *pieces,
+            after=pupils[h + 1 :],
         )
-        before = (partial[0],)
         results.append(exchange(partial, "row"))
     return jnp.concatenate([total_of(result) for result in results], 0)
 

time: 69.9 us -> 71.4 us (1.021)
  waiting for transfers between devices: 20.3 us -> 26.6 us
  starting transfers between devices: 34.3 us -> 29.6 us
    ppermute x24, waiting for transfers between devices: 20.3 us -> 26.6 us  [exchange(): lax.ppermute(chunk, axis, [(i, i ^ k) for i in range(n)])]
    ppermute x24, starting transfers between devices: 34.3 us -> 29.6 us  [exchange(): lax.ppermute(chunk, axis, [(i, i ^ k) for i in range(n)])]
  transfers between devices with their start and end apart: 24 -> 24, of which waited for: 8 -> 7; matrix products, arithmetic and copies ran while one was open for 0% -> 0% of each run, Pallas kernels for 15% -> 15%
where the time goes in v3:
time: 71.4 us; the launch traced here: 71.2 us
  starting transfers between devices  29.6 us (41%)
  waiting for transfers between devices  26.6 us (37%)
  Pallas kernels  10.9 us (15%)
  local copies, waits for them, and re-layouts  2.29 us (3%)
  other arithmetic  1.7 us (2%)
    ppermute x24, starting transfers between devices, exchange(): lax.ppermute(chunk, axis, [(i, i ^ k) for i in range(n)])  29.6 us
    ppermute x24, waiting for transfers between devices, exchange(): lax.ppermute(chunk, axis, [(i, i ^ k) for i in range(n)])  26.6 us
    pallas_call x9, Pallas kernels, call(): pl.pallas_call(body, out_shape=[jax.ShapeDtypeStruct(shape, BF16) for sha...  10.9 us
    unnamed x6, local copies, waits for them, and re-layouts  2.29 us
  transfers between devices with their start and end apart: 24, of which 7 were waited for; matrix products, arithmetic and copies ran while one was open for 0% of the time, Pallas kernels for 15%

profile of v3, /device:TPU:0, one launch (start us, length us, event | category | flops | bytes accessed | tf_op | source)
XLA Modules:
  0.0 71.2 jit_solution(10042789083199703432)
XLA Ops:
  0.9 1.3 %copy-done.1 = bf16[1,2048,256]{2,1,0:T(8,128)(2,1)S(1)} copy-done((bf16[1,2048,256]{2,1,0:T(8,128)(2,1)S(1)}, bf16[1,2048,256]{2,1,0:T(8,128)(2,1)}, u32[]{:S(2)}) %copy-start.1) | copy-done | bytes 1048600
  3.2 2.6 %collective-permute-start.1 = (bf16[32,2176]{1,0:T(8,128)(2,1)S(1)}, bf16[32,2176]{1,0:T(8,128)(2,1)S(1)}, u32[]{:S(2)}, u32[]{:S(2)}) collective-permute-start(bf16[32,2176]{1,0:T(8,128)(2,1)S(1)} %get-tuple-element.32), channel_id=1, source_target_pairs={{0,2},{1,3},{2,0},{3,1},{4,6},{5,7},{6,4},{7,5},{8,10},{9,11},{10,... | collective-permute-start | bytes 417800 | tf_op jit(solution)/shard_map/ppermute | solution.py:122
  6.5 1.9 %collective-permute-start.7 = (bf16[32,2048]{1,0:T(8,128)(2,1)S(1)}, bf16[32,2048]{1,0:T(8,128)(2,1)S(1)}, u32[]{:S(2)}, u32[]{:S(2)}) collective-permute-start(bf16[32,2048]{1,0:T(8,128)(2,1)S(1)} %get-tuple-element.39), channel_id=1, source_target_pairs={{0,2},{1,3},{2,0},{3,1},{4,6},{5,7},{6,4},{7,5},{8,10},{9,11},{10,... | collective-permute-start | bytes 393224 | tf_op jit(solution)/shard_map/ppermute | solution.py:122
  8.5 0.9 %copy-done.2 = bf16[16,128,64]{1,2,0:T(8,128)(2,1)S(1)} copy-done((bf16[16,128,64]{1,2,0:T(8,128)(2,1)S(1)}, bf16[16,128,64]{1,2,0:T(8,128)(2,1)}, u32[]{:S(2)}) %copy-start.2) | copy-done | bytes 262168
  10.3 2.5 %collective-permute-done.2.refs_4_.refs_8_ = bf16[32,2176]{1,0:T(8,128)(2,1)S(1)} collective-permute-done((bf16[32,2176]{1,0:T(8,128)(2,1)S(1)}, bf16[32,2176]{1,0:T(8,128)(2,1)S(1)}, u32[]{:S(2)}, u32[]{:S(2)}) %collective-permute-start.2) | collective-permute-done | bytes 139296 | tf_op jit(solution)/shard_map/ppermute | solution.py:122
  12.8 2.6 %shard_map.76 = (bf16[32,2048]{1,0:T(8,128)(2,1)S(1)}, bf16[32,2048]{1,0:T(8,128)(2,1)S(1)}, bf16[32,2048]{1,0:T(8,128)(2,1)S(1)}, bf16[32,2048]{1,0:T(8,128)(2,1)S(1)}) custom-call(bf16[32,128,128]{2,1,0:T(8,128)(2,1)S(1)} %shard_map.75.refs_0_, bf16[32,2176]{1,0:T(8,128)(2,1)S(1)} %get-tuple-element.29.refs_2_.refs_1_.refs_5_, ...), custom_call_target="tpu_custom_call" | custom-call | tf_op jit(solution)/shard_map/pallas_call | solution.py:137
  15.3 1.7 %collective-permute-start.3 = (bf16[32,2048]{1,0:T(8,128)(2,1)S(1)}, bf16[32,2048]{1,0:T(8,128)(2,1)S(1)}, u32[]{:S(2)}, u32[]{:S(2)}) collective-permute-start(bf16[32,2048]{1,0:T(8,128)(2,1)S(1)} %get-tuple-element.35), channel_id=1, source_target_pairs={{0,4},{4,0},{8,12},{12,8},{1,5},{5,1},{9,13},{13,9},{2,6},{6,2},{1... | collective-permute-start | bytes 393224 | tf_op jit(solution)/shard_map/ppermute | solution.py:122
  17.0 2.6 %collective-permute-start.4 = (bf16[32,2048]{1,0:T(8,128)(2,1)S(1)}, bf16[32,2048]{1,0:T(8,128)(2,1)S(1)}, u32[]{:S(2)}, u32[]{:S(2)}) collective-permute-start(bf16[32,2048]{1,0:T(8,128)(2,1)S(1)} %get-tuple-element.36), channel_id=1, source_target_pairs={{0,8},{4,12},{8,0},{12,4},{1,9},{5,13},{9,1},{13,5},{2,10},{6,14},... | collective-permute-start | bytes 393224 | tf_op jit(solution)/shard_map/ppermute | solution.py:122
  19.8 2.5 %shard_map.77 = (bf16[32,2048]{1,0:T(8,128)(2,1)S(1)}, bf16[32,2048]{1,0:T(8,128)(2,1)S(1)}, bf16[32,2048]{1,0:T(8,128)(2,1)S(1)}, bf16[32,2048]{1,0:T(8,128)(2,1)S(1)}) custom-call(bf16[32,128,128]{2,1,0:T(8,128)(2,1)S(1)} %shard_map.75.refs_0_, bf16[32,2176]{1,0:T(8,128)(2,1)S(1)} %get-tuple-element.29.refs_2_.refs_1_.refs_5_, ...), custom_call_target="tpu_custom_call" | custom-call | tf_op jit(solution)/shard_map/pallas_call | solution.py:137
  23.2 3.5 %collective-permute-start.13 = (bf16[32,2048]{1,0:T(8,128)(2,1)S(1)}, bf16[32,2048]{1,0:T(8,128)(2,1)S(1)}, u32[]{:S(2)}, u32[]{:S(2)}) collective-permute-start(bf16[32,2048]{1,0:T(8,128)(2,1)S(1)} %get-tuple-element.43), channel_id=1, source_target_pairs={{0,8},{4,12},{8,0},{12,4},{1,9},{5,13},{9,1},{13,5},{2,10},{6,14},... | collective-permute-start | bytes 393224 | tf_op jit(solution)/shard_map/ppermute | solution.py:122
  26.8 3.1 %collective-permute-done.4.refs_2_ = bf16[32,2048]{1,0:T(8,128)(2,1)S(1)} collective-permute-done((bf16[32,2048]{1,0:T(8,128)(2,1)S(1)}, bf16[32,2048]{1,0:T(8,128)(2,1)S(1)}, u32[]{:S(2)}, u32[]{:S(2)}) %collective-permute-start.4) | collective-permute-done | bytes 131104 | tf_op jit(solution)/shard_map/ppermute | solution.py:122
  30.4 1.2 %collective-permute-start.10 = (bf16[32,2048]{1,0:T(8,128)(2,1)S(1)}, bf16[32,2048]{1,0:T(8,128)(2,1)S(1)}, u32[]{:S(2)}, u32[]{:S(2)}) collective-permute-start(bf16[32,2048]{1,0:T(8,128)(2,1)S(1)} %shard_map.78.refs_1_), channel_id=1, source_target_pairs={{0,2},{1,3},{2,0},{3,1},{4,6},{5,7},{6,4},{7,5},{8,10},{9,11},{10,... | collective-permute-start | bytes 393224 | tf_op jit(solution)/shard_map/ppermute | solution.py:122
  32.0 9.2 %collective-permute-done.13.refs_2_ = bf16[32,2048]{1,0:T(8,128)(2,1)S(1)} collective-permute-done((bf16[32,2048]{1,0:T(8,128)(2,1)S(1)}, bf16[32,2048]{1,0:T(8,128)(2,1)S(1)}, u32[]{:S(2)}, u32[]{:S(2)}) %collective-permute-start.13) | collective-permute-done | bytes 131104 | tf_op jit(solution)/shard_map/ppermute | solution.py:122
  41.6 1.3 %collective-permute-start.19 = (bf16[32,2048]{1,0:T(8,128)(2,1)S(1)}, bf16[32,2048]{1,0:T(8,128)(2,1)S(1)}, u32[]{:S(2)}, u32[]{:S(2)}) collective-permute-start(bf16[32,2048]{1,0:T(8,128)(2,1)S(1)} %shard_map.79.refs_5_.refs_1_), channel_id=1, source_target_pairs={{0,2},{1,3},{2,0},{3,1},{4,6},{5,7},{6,4},{7,5},{8,10},{9,11},{10,... | collective-permute-start | bytes 393224 | tf_op jit(solution)/shard_map/ppermute | solution.py:122
  43.2 2.3 %shard_map.80 = (bf16[32,1650]{1,0:T(8,128)(2,1)S(1)}, bf16[32,1650]{1,0:T(8,128)(2,1)S(1)}, bf16[32,1650]{1,0:T(8,128)(2,1)S(1)}, bf16[32,1650]{1,0:T(8,128)(2,1)S(1)}) custom-call(bf16[1650,2048]{1,0:T(8,128)(2,1)S(1)} %bitcast.4, bf16[32,2048]{1,0:T(8,128)(2,1)S(1)} %shard_map.78.refs_1_, bf16[32,2048]{1,0:T(8,128)(2,1)S(1)} %collective-permute-done.9.refs_2_, ...), custom_call_target="tpu_custom_call" | custom-call | tf_op jit(solution)/shard_map/pallas_call | solution.py:137
  45.5 4.6 %collective-permute-start.15 = (bf16[32,1650]{1,0:T(8,128)(2,1)S(1)}, bf16[32,1650]{1,0:T(8,128)(2,1)S(1)}, u32[]{:S(2)}, u32[]{:S(2)}) collective-permute-start(bf16[32,1650]{1,0:T(8,128)(2,1)S(1)} %get-tuple-element.46), channel_id=1, source_target_pairs={{0,4},{4,0},{8,12},{12,8},{1,5},{5,1},{9,13},{13,9},{2,6},{6,2},{1... | collective-permute-start | bytes 316808 | tf_op jit(solution)/shard_map/ppermute | solution.py:122
  50.1 1.1 %collective-permute-start.16 = (bf16[32,1650]{1,0:T(8,128)(2,1)S(1)}, bf16[32,1650]{1,0:T(8,128)(2,1)S(1)}, u32[]{:S(2)}, u32[]{:S(2)}) collective-permute-start(bf16[32,1650]{1,0:T(8,128)(2,1)S(1)} %get-tuple-element.47), channel_id=1, source_target_pairs={{0,8},{4,12},{8,0},{12,4},{1,9},{5,13},{9,1},{13,5},{2,10},{6,14},... | collective-permute-start | bytes 316808 | tf_op jit(solution)/shard_map/ppermute | solution.py:122
  51.2 1.4 %collective-permute-start.17 = (bf16[32,1650]{1,0:T(8,128)(2,1)S(1)}, bf16[32,1650]{1,0:T(8,128)(2,1)S(1)}, u32[]{:S(2)}, u32[]{:S(2)}) collective-permute-start(bf16[32,1650]{1,0:T(8,128)(2,1)S(1)} %get-tuple-element.48), channel_id=1, source_target_pairs={{0,12},{4,8},{8,4},{12,0},{1,13},{5,9},{9,5},{13,1},{2,14},{6,10},... | collective-permute-start | bytes 316808 | tf_op jit(solution)/shard_map/ppermute | solution.py:122
  52.6 2.3 %shard_map.81 = (bf16[32,1650]{1,0:T(8,128)(2,1)S(1)}, bf16[32,1650]{1,0:T(8,128)(2,1)S(1)}, bf16[32,1650]{1,0:T(8,128)(2,1)S(1)}, bf16[32,1650]{1,0:T(8,128)(2,1)S(1)}) custom-call(bf16[1650,2048]{1,0:T(8,128)(2,1)S(1)} %bitcast.5, bf16[32,2048]{1,0:T(8,128)(2,1)S(1)} %shard_map.79.refs_5_.refs_1_, bf16[32,2048]{1,0:T(8,128)(2,1)S(1)} %collective-permute-done.18.refs_2_, ...), custom_call_target="tpu_custom_call" | custom-call | tf_op jit(solution)/shard_map/pallas_call | solution.py:137
  54.9 1.1 %collective-permute-start.21 = (bf16[32,1650]{1,0:T(8,128)(2,1)S(1)}, bf16[32,1650]{1,0:T(8,128)(2,1)S(1)}, u32[]{:S(2)}, u32[]{:S(2)}) collective-permute-start(bf16[32,1650]{1,0:T(8,128)(2,1)S(1)} %get-tuple-element.50), channel_id=1, source_target_pairs={{0,4},{4,0},{8,12},{12,8},{1,5},{5,1},{9,13},{13,9},{2,6},{6,2},{1... | collective-permute-start | bytes 316808 | tf_op jit(solution)/shard_map/ppermute | solution.py:122
  55.9 2.0 %collective-permute-start.22 = (bf16[32,1650]{1,0:T(8,128)(2,1)S(1)}, bf16[32,1650]{1,0:T(8,128)(2,1)S(1)}, u32[]{:S(2)}, u32[]{:S(2)}) collective-permute-start(bf16[32,1650]{1,0:T(8,128)(2,1)S(1)} %get-tuple-element.51), channel_id=1, source_target_pairs={{0,8},{4,12},{8,0},{12,4},{1,9},{5,13},{9,1},{13,5},{2,10},{6,14},... | collective-permute-start | bytes 316808 | tf_op jit(solution)/shard_map/ppermute | solution.py:122
  57.9 1.4 %collective-permute-start.23 = (bf16[32,1650]{1,0:T(8,128)(2,1)S(1)}, bf16[32,1650]{1,0:T(8,128)(2,1)S(1)}, u32[]{:S(2)}, u32[]{:S(2)}) collective-permute-start(bf16[32,1650]{1,0:T(8,128)(2,1)S(1)} %get-tuple-element.52), channel_id=1, source_target_pairs={{0,12},{4,8},{8,4},{12,0},{1,13},{5,9},{9,5},{13,1},{2,14},{6,10},... | collective-permute-start | bytes 316808 | tf_op jit(solution)/shard_map/ppermute | solution.py:122
  59.3 2.0 %collective-permute-done.16 = bf16[32,1650]{1,0:T(8,128)(2,1)S(1)} collective-permute-done((bf16[32,1650]{1,0:T(8,128)(2,1)S(1)}, bf16[32,1650]{1,0:T(8,128)(2,1)S(1)}, u32[]{:S(2)}, u32[]{:S(2)}) %collective-permute-start.16) | collective-permute-done | bytes 105632 | tf_op jit(solution)/shard_map/ppermute | solution.py:122
  62.3 8.1 %collective-permute-done.22 = bf16[32,1650]{1,0:T(8,128)(2,1)S(1)} collective-permute-done((bf16[32,1650]{1,0:T(8,128)(2,1)S(1)}, bf16[32,1650]{1,0:T(8,128)(2,1)S(1)}, u32[]{:S(2)}, u32[]{:S(2)}) %collective-permute-start.22) | collective-permute-done | bytes 105632 | tf_op jit(solution)/shard_map/ppermute | solution.py:122
  (43 shorter events, 7.9 us)
Async XLA Ops:
  2.7 5.8 %collective-permute-start = (bf16[32,2176]{1,0:T(8,128)(2,1)S(1)}, bf16[32,2176]{1,0:T(8,128)(2,1)S(1)}, u32[]{:S(2)}, u32[]{:S(2)}) collective-permute-start(bf16[32,2176]{1,0:T(8,128)(2,1)S(1)} %get-tuple-element.31), channel_id=1, source_target_pairs={{0,1},{1,0},{2,3},{3,2},{4,5},{5,4},{6,7},{7,6},{8,9},{9,8},{10,11... | collective-permute-start | bytes 417800 | tf_op jit(solution)/shard_map/ppermute | solution.py:122
  3.2 7.1 %collective-permute-start.1 = (bf16[32,2176]{1,0:T(8,128)(2,1)S(1)}, bf16[32,2176]{1,0:T(8,128)(2,1)S(1)}, u32[]{:S(2)}, u32[]{:S(2)}) collective-permute-start(bf16[32,2176]{1,0:T(8,128)(2,1)S(1)} %get-tuple-element.32), channel_id=1, source_target_pairs={{0,2},{1,3},{2,0},{3,1},{4,6},{5,7},{6,4},{7,5},{8,10},{9,11},{10,... | collective-permute-start | bytes 417800 | tf_op jit(solution)/shard_map/ppermute | solution.py:122
  5.8 7.0 %collective-permute-start.2 = (bf16[32,2176]{1,0:T(8,128)(2,1)S(1)}, bf16[32,2176]{1,0:T(8,128)(2,1)S(1)}, u32[]{:S(2)}, u32[]{:S(2)}) collective-permute-start(bf16[32,2176]{1,0:T(8,128)(2,1)S(1)} %get-tuple-element.33), channel_id=1, source_target_pairs={{0,3},{1,2},{2,1},{3,0},{4,7},{5,6},{6,5},{7,4},{8,11},{9,10},{10,... | collective-permute-start | bytes 417800 | tf_op jit(solution)/shard_map/ppermute | solution.py:122
  6.3 13.3 %collective-permute-start.6 = (bf16[32,2048]{1,0:T(8,128)(2,1)S(1)}, bf16[32,2048]{1,0:T(8,128)(2,1)S(1)}, u32[]{:S(2)}, u32[]{:S(2)}) collective-permute-start(bf16[32,2048]{1,0:T(8,128)(2,1)S(1)} %get-tuple-element.38), channel_id=1, source_target_pairs={{0,1},{1,0},{2,3},{3,2},{4,5},{5,4},{6,7},{7,6},{8,9},{9,8},{10,11... | collective-permute-start | bytes 393224 | tf_op jit(solution)/shard_map/ppermute | solution.py:122
  6.5 13.3 %collective-permute-start.7 = (bf16[32,2048]{1,0:T(8,128)(2,1)S(1)}, bf16[32,2048]{1,0:T(8,128)(2,1)S(1)}, u32[]{:S(2)}, u32[]{:S(2)}) collective-permute-start(bf16[32,2048]{1,0:T(8,128)(2,1)S(1)} %get-tuple-element.39), channel_id=1, source_target_pairs={{0,2},{1,3},{2,0},{3,1},{4,6},{5,7},{6,4},{7,5},{8,10},{9,11},{10,... | collective-permute-start | bytes 393224 | tf_op jit(solution)/shard_map/ppermute | solution.py:122
  8.5 11.3 %collective-permute-start.8 = (bf16[32,2048]{1,0:T(8,128)(2,1)S(1)}, bf16[32,2048]{1,0:T(8,128)(2,1)S(1)}, u32[]{:S(2)}, u32[]{:S(2)}) collective-permute-start(bf16[32,2048]{1,0:T(8,128)(2,1)S(1)} %get-tuple-element.40), channel_id=1, source_target_pairs={{0,3},{1,2},{2,1},{3,0},{4,7},{5,6},{6,5},{7,4},{8,11},{9,10},{10,... | collective-permute-start | bytes 393224 | tf_op jit(solution)/shard_map/ppermute | solution.py:122
  15.3 11.3 %collective-permute-start.3 = (bf16[32,2048]{1,0:T(8,128)(2,1)S(1)}, bf16[32,2048]{1,0:T(8,128)(2,1)S(1)}, u32[]{:S(2)}, u32[]{:S(2)}) collective-permute-start(bf16[32,2048]{1,0:T(8,128)(2,1)S(1)} %get-tuple-element.35), channel_id=1, source_target_pairs={{0,4},{4,0},{8,12},{12,8},{1,5},{5,1},{9,13},{13,9},{2,6},{6,2},{1... | collective-permute-start | bytes 393224 | tf_op jit(solution)/shard_map/ppermute | solution.py:122
  17.0 12.9 %collective-permute-start.4 = (bf16[32,2048]{1,0:T(8,128)(2,1)S(1)}, bf16[32,2048]{1,0:T(8,128)(2,1)S(1)}, u32[]{:S(2)}, u32[]{:S(2)}) collective-permute-start(bf16[32,2048]{1,0:T(8,128)(2,1)S(1)} %get-tuple-element.36), channel_id=1, source_target_pairs={{0,8},{4,12},{8,0},{12,4},{1,9},{5,13},{9,1},{13,5},{2,10},{6,14},... | collective-permute-start | bytes 393224 | tf_op jit(solution)/shard_map/ppermute | solution.py:122
  19.6 10.3 %collective-permute-start.5 = (bf16[32,2048]{1,0:T(8,128)(2,1)S(1)}, bf16[32,2048]{1,0:T(8,128)(2,1)S(1)}, u32[]{:S(2)}, u32[]{:S(2)}) collective-permute-start(bf16[32,2048]{1,0:T(8,128)(2,1)S(1)} %get-tuple-element.37), channel_id=1, source_target_pairs={{0,12},{4,8},{8,4},{12,0},{1,13},{5,9},{9,5},{13,1},{2,14},{6,10},... | collective-permute-start | bytes 393224 | tf_op jit(solution)/shard_map/ppermute | solution.py:122
  22.4 9.3 %collective-permute-start.12 = (bf16[32,2048]{1,0:T(8,128)(2,1)S(1)}, bf16[32,2048]{1,0:T(8,128)(2,1)S(1)}, u32[]{:S(2)}, u32[]{:S(2)}) collective-permute-start(bf16[32,2048]{1,0:T(8,128)(2,1)S(1)} %get-tuple-element.42), channel_id=1, source_target_pairs={{0,4},{4,0},{8,12},{12,8},{1,5},{5,1},{9,13},{13,9},{2,6},{6,2},{1... | collective-permute-start | bytes 393224 | tf_op jit(solution)/shard_map/ppermute | solution.py:122
  23.2 18.0 %collective-permute-start.13 = (bf16[32,2048]{1,0:T(8,128)(2,1)S(1)}, bf16[32,2048]{1,0:T(8,128)(2,1)S(1)}, u32[]{:S(2)}, u32[]{:S(2)}) collective-permute-start(bf16[32,2048]{1,0:T(8,128)(2,1)S(1)} %get-tuple-element.43), channel_id=1, source_target_pairs={{0,8},{4,12},{8,0},{12,4},{1,9},{5,13},{9,1},{13,5},{2,10},{6,14},... | collective-permute-start | bytes 393224 | tf_op jit(solution)/shard_map/ppermute | solution.py:122
  26.7 14.5 %collective-permute-start.14 = (bf16[32,2048]{1,0:T(8,128)(2,1)S(1)}, bf16[32,2048]{1,0:T(8,128)(2,1)S(1)}, u32[]{:S(2)}, u32[]{:S(2)}) collective-permute-start(bf16[32,2048]{1,0:T(8,128)(2,1)S(1)} %get-tuple-element.44), channel_id=1, source_target_pairs={{0,12},{4,8},{8,4},{12,0},{1,13},{5,9},{9,5},{13,1},{2,14},{6,10},... | collective-permute-start | bytes 393224 | tf_op jit(solution)/shard_map/ppermute | solution.py:122
  30.0 12.9 %collective-permute-start.11 = (bf16[32,2048]{1,0:T(8,128)(2,1)S(1)}, bf16[32,2048]{1,0:T(8,128)(2,1)S(1)}, u32[]{:S(2)}, u32[]{:S(2)}) collective-permute-start(bf16[32,2048]{1,0:T(8,128)(2,1)S(1)} %shard_map.78.refs_1_), channel_id=1, source_target_pairs={{0,3},{1,2},{2,1},{3,0},{4,7},{5,6},{6,5},{7,4},{8,11},{9,10},{10,... | collective-permute-start | bytes 393224 | tf_op jit(solution)/shard_map/ppermute | solution.py:122
  30.4 12.8 %collective-permute-start.10 = (bf16[32,2048]{1,0:T(8,128)(2,1)S(1)}, bf16[32,2048]{1,0:T(8,128)(2,1)S(1)}, u32[]{:S(2)}, u32[]{:S(2)}) collective-permute-start(bf16[32,2048]{1,0:T(8,128)(2,1)S(1)} %shard_map.78.refs_1_), channel_id=1, source_target_pairs={{0,2},{1,3},{2,0},{3,1},{4,6},{5,7},{6,4},{7,5},{8,10},{9,11},{10,... | collective-permute-start | bytes 393224 | tf_op jit(solution)/shard_map/ppermute | solution.py:122
  31.7 11.5 %collective-permute-start.9 = (bf16[32,2048]{1,0:T(8,128)(2,1)S(1)}, bf16[32,2048]{1,0:T(8,128)(2,1)S(1)}, u32[]{:S(2)}, u32[]{:S(2)}) collective-permute-start(bf16[32,2048]{1,0:T(8,128)(2,1)S(1)} %shard_map.78.refs_1_), channel_id=1, source_target_pairs={{0,1},{1,0},{2,3},{3,2},{4,5},{5,4},{6,7},{7,6},{8,9},{9,8},{10,11... | collective-permute-start | bytes 393224 | tf_op jit(solution)/shard_map/ppermute | solution.py:122
  41.3 9.9 %collective-permute-start.20 = (bf16[32,2048]{1,0:T(8,128)(2,1)S(1)}, bf16[32,2048]{1,0:T(8,128)(2,1)S(1)}, u32[]{:S(2)}, u32[]{:S(2)}) collective-permute-start(bf16[32,2048]{1,0:T(8,128)(2,1)S(1)} %shard_map.79.refs_5_.refs_1_), channel_id=1, source_target_pairs={{0,3},{1,2},{2,1},{3,0},{4,7},{5,6},{6,5},{7,4},{8,11},{9,10},{10,... | collective-permute-start | bytes 393224 | tf_op jit(solution)/shard_map/ppermute | solution.py:122
  41.6 10.9 %collective-permute-start.19 = (bf16[32,2048]{1,0:T(8,128)(2,1)S(1)}, bf16[32,2048]{1,0:T(8,128)(2,1)S(1)}, u32[]{:S(2)}, u32[]{:S(2)}) collective-permute-start(bf16[32,2048]{1,0:T(8,128)(2,1)S(1)} %shard_map.79.refs_5_.refs_1_), channel_id=1, source_target_pairs={{0,2},{1,3},{2,0},{3,1},{4,6},{5,7},{6,4},{7,5},{8,10},{9,11},{10,... | collective-permute-start | bytes 393224 | tf_op jit(solution)/shard_map/ppermute | solution.py:122
  42.9 9.7 %collective-permute-start.18 = (bf16[32,2048]{1,0:T(8,128)(2,1)S(1)}, bf16[32,2048]{1,0:T(8,128)(2,1)S(1)}, u32[]{:S(2)}, u32[]{:S(2)}) collective-permute-start(bf16[32,2048]{1,0:T(8,128)(2,1)S(1)} %shard_map.79.refs_5_.refs_1_), channel_id=1, source_target_pairs={{0,1},{1,0},{2,3},{3,2},{4,5},{5,4},{6,7},{7,6},{8,9},{9,8},{10,11... | collective-permute-start | bytes 393224 | tf_op jit(solution)/shard_map/ppermute | solution.py:122
  45.5 12.4 %collective-permute-start.15 = (bf16[32,1650]{1,0:T(8,128)(2,1)S(1)}, bf16[32,1650]{1,0:T(8,128)(2,1)S(1)}, u32[]{:S(2)}, u32[]{:S(2)}) collective-permute-start(bf16[32,1650]{1,0:T(8,128)(2,1)S(1)} %get-tuple-element.46), channel_id=1, source_target_pairs={{0,4},{4,0},{8,12},{12,8},{1,5},{5,1},{9,13},{13,9},{2,6},{6,2},{1... | collective-permute-start | bytes 316808 | tf_op jit(solution)/shard_map/ppermute | solution.py:122
  50.1 11.2 %collective-permute-start.16 = (bf16[32,1650]{1,0:T(8,128)(2,1)S(1)}, bf16[32,1650]{1,0:T(8,128)(2,1)S(1)}, u32[]{:S(2)}, u32[]{:S(2)}) collective-permute-start(bf16[32,1650]{1,0:T(8,128)(2,1)S(1)} %get-tuple-element.47), channel_id=1, source_target_pairs={{0,8},{4,12},{8,0},{12,4},{1,9},{5,13},{9,1},{13,5},{2,10},{6,14},... | collective-permute-start | bytes 316808 | tf_op jit(solution)/shard_map/ppermute | solution.py:122
  51.2 10.1 %collective-permute-start.17 = (bf16[32,1650]{1,0:T(8,128)(2,1)S(1)}, bf16[32,1650]{1,0:T(8,128)(2,1)S(1)}, u32[]{:S(2)}, u32[]{:S(2)}) collective-permute-start(bf16[32,1650]{1,0:T(8,128)(2,1)S(1)} %get-tuple-element.48), channel_id=1, source_target_pairs={{0,12},{4,8},{8,4},{12,0},{1,13},{5,9},{9,5},{13,1},{2,14},{6,10},... | collective-permute-start | bytes 316808 | tf_op jit(solution)/shard_map/ppermute | solution.py:122
  54.9 7.5 %collective-permute-start.21 = (bf16[32,1650]{1,0:T(8,128)(2,1)S(1)}, bf16[32,1650]{1,0:T(8,128)(2,1)S(1)}, u32[]{:S(2)}, u32[]{:S(2)}) collective-permute-start(bf16[32,1650]{1,0:T(8,128)(2,1)S(1)} %get-tuple-element.50), channel_id=1, source_target_pairs={{0,4},{4,0},{8,12},{12,8},{1,5},{5,1},{9,13},{13,9},{2,6},{6,2},{1... | collective-permute-start | bytes 316808 | tf_op jit(solution)/shard_map/ppermute | solution.py:122
  55.9 14.5 %collective-permute-start.22 = (bf16[32,1650]{1,0:T(8,128)(2,1)S(1)}, bf16[32,1650]{1,0:T(8,128)(2,1)S(1)}, u32[]{:S(2)}, u32[]{:S(2)}) collective-permute-start(bf16[32,1650]{1,0:T(8,128)(2,1)S(1)} %get-tuple-element.51), channel_id=1, source_target_pairs={{0,8},{4,12},{8,0},{12,4},{1,9},{5,13},{9,1},{13,5},{2,10},{6,14},... | collective-permute-start | bytes 316808 | tf_op jit(solution)/shard_map/ppermute | solution.py:122
  57.9 12.5 %collective-permute-start.23 = (bf16[32,1650]{1,0:T(8,128)(2,1)S(1)}, bf16[32,1650]{1,0:T(8,128)(2,1)S(1)}, u32[]{:S(2)}, u32[]{:S(2)}) collective-permute-start(bf16[32,1650]{1,0:T(8,128)(2,1)S(1)} %get-tuple-element.52), channel_id=1, source_target_pairs={{0,12},{4,8},{8,4},{12,0},{1,13},{5,9},{9,5},{13,1},{2,14},{6,10},... | collective-permute-start | bytes 316808 | tf_op jit(solution)/shard_map/ppermute | solution.py:122
  (3 other events, 45.5 us)

commit v4 on v3

--- a/solution.py
+++ b/solution.py
@@ -30,7 +30,8 @@
     turned = lax.dot_general(
         pick, layers_ref[...], (((1,), (1,)), ((), ())), preferred_element_type=F32
     ).astype(BF16)
-    for k, out in enumerate(outs):
+    for i, out in enumerate(outs):
+        k = (n_layer - i) % n_layer
         out[:, :rows_dev] = turned[k * each : (k + 1) * each]
     if half == 0:
         codes[...] = jnp.zeros_like(codes)
@@ -80,7 +81,8 @@
 
         lax.fori_loop(0, entries // unroll, step, 0)
     me = lax.axis_index("row")
-    for k, out in enumerate(outs):
+    for i, out in enumerate(outs):
+        k = (n_row - i) % n_row
         base = lax.bitwise_xor(me, k) * owned
         for s in range(owned):
             out[:, s * LANES : (s + 1) * LANES] = total[base + s].astype(BF16)
@@ -107,20 +109,22 @@
     )
     each = columns // n_row
     if aligned:
-        for k, out in enumerate(outs):
+        for i, out in enumerate(outs):
+            k = (n_row - i) % n_row
             out[...] = found[k * each : (k + 1) * each].astype(BF16)
     else:
         product[...] = found
-        for k, out in enumerate(outs):
+        for i, out in enumerate(outs):
+            k = (n_row - i) % n_row
             start = pl.multiple_of(lax.bitwise_xor(row, k) * each, each)
             out[...] = product[pl.ds(start, each), :].astype(BF16)
 
 
-def exchange(chunks, axis):
+def exchange(chunks, axis, sign=-1):
     n = len(chunks)
     return [
-        chunk if k == 0 else lax.ppermute(chunk, axis, [(i, i ^ k) for i in range(n)])
-        for k, chunk in enumerate(chunks)
+        lax.ppermute(chunk, axis, [(j, j ^ (sign * i % n)) for j in range(n)]) if i else chunk
+        for i, chunk in enumerate(chunks)
     ]
 
 
@@ -195,20 +199,18 @@
         )
         before = (shares[0],)
         received.append(exchange(shares, "row"))
-    pupils = []
-    for h in range(halves):
-        pupils += call(sum_kernel, [(each, points)], [], *received[h], after=before)
     results = []
     for h in range(halves):
-        pieces = exchange([pupils[h]] * n_layer, "layer")
+        (pupil,) = call(sum_kernel, [(each, points)], [], *received[h], after=before)
+        pieces = exchange([pupil] * n_layer, "layer", 1)
         partial = call(
             functools.partial(fit_kernel, n_layer, n_row),
             [(chunk // halves, actuators)] * n_row,
             [pltpu.VMEM((n_layer, each, points), BF16), pltpu.VMEM((per_half, actuators), F32)],
             fitting.T,
             *pieces,
-            after=pupils[h + 1 :],
         )
+        before = (partial[0],)
         results.append(exchange(partial, "row"))
     return jnp.concatenate([total_of(result) for result in results], 0)
 

time: 71.4 us -> 69.7 us (0.976)
  starting transfers between devices: 29.6 us -> 24.4 us
  waiting for transfers between devices: 26.6 us -> 30.2 us
    ppermute x24, starting transfers between devices: 29.6 us -> 24.4 us  [exchange(): lax.ppermute(chunk, axis, [(j, j ^ sign * i % n) for j in range(n)])]
    ppermute x24, waiting for transfers between devices: 26.6 us -> 30.2 us  [exchange(): lax.ppermute(chunk, axis, [(j, j ^ sign * i % n) for j in range(n)])]
  transfers between devices with their start and end apart: 24 -> 24, of which waited for: 7 -> 10; matrix products, arithmetic and copies ran while one was open for 0% -> 0% of each run, Pallas kernels for 15% -> 15%
where the time goes in v4:
time: 69.7 us; the launch traced here: 69.6 us
  waiting for transfers between devices  30.2 us (43%)
  starting transfers between devices  24.4 us (35%)
  Pallas kernels  10.9 us (16%)
  local copies, waits for them, and re-layouts  2.29 us (3%)
  other arithmetic  1.7 us (2%)
    ppermute x24, waiting for transfers between devices, exchange(): lax.ppermute(chunk, axis, [(j, j ^ sign * i % n) for j in range(n)])  30.2 us
    ppermute x24, starting transfers between devices, exchange(): lax.ppermute(chunk, axis, [(j, j ^ sign * i % n) for j in range(n)])  24.4 us
    pallas_call x9, Pallas kernels, call(): pl.pallas_call(body, out_shape=[jax.ShapeDtypeStruct(shape, BF16) for sha...  10.9 us
    unnamed x6, local copies, waits for them, and re-layouts  2.29 us
  transfers between devices with their start and end apart: 24, of which 10 were waited for; matrix products, arithmetic and copies ran while one was open for 0% of the time, Pallas kernels for 15%

profile of v4, /device:TPU:0, one launch (start us, length us, event | category | flops | bytes accessed | tf_op | source)
XLA Modules:
  0.0 69.6 jit_solution(2296577043005318475)
XLA Ops:
  0.9 1.3 %copy-done.1 = bf16[1,2048,256]{2,1,0:T(8,128)(2,1)S(1)} copy-done((bf16[1,2048,256]{2,1,0:T(8,128)(2,1)S(1)}, bf16[1,2048,256]{2,1,0:T(8,128)(2,1)}, u32[]{:S(2)}) %copy-start.1) | copy-done | bytes 1048600
  2.7 2.4 %collective-permute-start = (bf16[32,2176]{1,0:T(8,128)(2,1)S(1)}, bf16[32,2176]{1,0:T(8,128)(2,1)S(1)}, u32[]{:S(2)}, u32[]{:S(2)}) collective-permute-start(bf16[32,2176]{1,0:T(8,128)(2,1)S(1)} %get-tuple-element.31), channel_id=1, source_target_pairs={{0,3},{1,2},{2,1},{3,0},{4,7},{5,6},{6,5},{7,4},{8,11},{9,10},{10,... | collective-permute-start | bytes 417800 | tf_op jit(solution)/shard_map/ppermute | solution.py:126
  6.3 1.5 %collective-permute-start.6 = (bf16[32,2048]{1,0:T(8,128)(2,1)S(1)}, bf16[32,2048]{1,0:T(8,128)(2,1)S(1)}, u32[]{:S(2)}, u32[]{:S(2)}) collective-permute-start(bf16[32,2048]{1,0:T(8,128)(2,1)S(1)} %get-tuple-element.38), channel_id=1, source_target_pairs={{0,3},{1,2},{2,1},{3,0},{4,7},{5,6},{6,5},{7,4},{8,11},{9,10},{10,... | collective-permute-start | bytes 393224 | tf_op jit(solution)/shard_map/ppermute | solution.py:126
  8.5 0.9 %copy-done.2 = bf16[16,128,64]{1,2,0:T(8,128)(2,1)S(1)} copy-done((bf16[16,128,64]{1,2,0:T(8,128)(2,1)S(1)}, bf16[16,128,64]{1,2,0:T(8,128)(2,1)}, u32[]{:S(2)}) %copy-start.2) | copy-done | bytes 262168
  10.0 3.2 %collective-permute-done.1.refs_3_.refs_7_ = bf16[32,2176]{1,0:T(8,128)(2,1)S(1)} collective-permute-done((bf16[32,2176]{1,0:T(8,128)(2,1)S(1)}, bf16[32,2176]{1,0:T(8,128)(2,1)S(1)}, u32[]{:S(2)}, u32[]{:S(2)}) %collective-permute-start.1) | collective-permute-done | bytes 139296 | tf_op jit(solution)/shard_map/ppermute | solution.py:126
  13.2 2.6 %shard_map.76 = (bf16[32,2048]{1,0:T(8,128)(2,1)S(1)}, bf16[32,2048]{1,0:T(8,128)(2,1)S(1)}, bf16[32,2048]{1,0:T(8,128)(2,1)S(1)}, bf16[32,2048]{1,0:T(8,128)(2,1)S(1)}) custom-call(bf16[32,128,128]{2,1,0:T(8,128)(2,1)S(1)} %shard_map.75.refs_0_, bf16[32,2176]{1,0:T(8,128)(2,1)S(1)} %get-tuple-element.29.refs_2_.refs_1_.refs_5_, ...), custom_call_target="tpu_custom_call" | custom-call | tf_op jit(solution)/shard_map/pallas_call | solution.py:141
  15.8 3.7 %collective-permute-start.3 = (bf16[32,2048]{1,0:T(8,128)(2,1)S(1)}, bf16[32,2048]{1,0:T(8,128)(2,1)S(1)}, u32[]{:S(2)}, u32[]{:S(2)}) collective-permute-start(bf16[32,2048]{1,0:T(8,128)(2,1)S(1)} %get-tuple-element.35), channel_id=1, source_target_pairs={{0,12},{4,8},{8,4},{12,0},{1,13},{5,9},{9,5},{13,1},{2,14},{6,10},... | collective-permute-start | bytes 393224 | tf_op jit(solution)/shard_map/ppermute | solution.py:126
  20.2 2.5 %shard_map.77 = (bf16[32,2048]{1,0:T(8,128)(2,1)S(1)}, bf16[32,2048]{1,0:T(8,128)(2,1)S(1)}, bf16[32,2048]{1,0:T(8,128)(2,1)S(1)}, bf16[32,2048]{1,0:T(8,128)(2,1)S(1)}) custom-call(bf16[32,128,128]{2,1,0:T(8,128)(2,1)S(1)} %shard_map.75.refs_0_, bf16[32,2176]{1,0:T(8,128)(2,1)S(1)} %get-tuple-element.29.refs_2_.refs_1_.refs_5_, ...), custom_call_target="tpu_custom_call" | custom-call | tf_op jit(solution)/shard_map/pallas_call | solution.py:141
  22.8 1.3 %collective-permute-done.3.refs_1_ = bf16[32,2048]{1,0:T(8,128)(2,1)S(1)} collective-permute-done((bf16[32,2048]{1,0:T(8,128)(2,1)S(1)}, bf16[32,2048]{1,0:T(8,128)(2,1)S(1)}, u32[]{:S(2)}, u32[]{:S(2)}) %collective-permute-start.3) | collective-permute-done | bytes 131104 | tf_op jit(solution)/shard_map/ppermute | solution.py:126
  24.1 6.6 %collective-permute-done.4.refs_2_ = bf16[32,2048]{1,0:T(8,128)(2,1)S(1)} collective-permute-done((bf16[32,2048]{1,0:T(8,128)(2,1)S(1)}, bf16[32,2048]{1,0:T(8,128)(2,1)S(1)}, u32[]{:S(2)}, u32[]{:S(2)}) %collective-permute-start.4) | collective-permute-done | bytes 131104 | tf_op jit(solution)/shard_map/ppermute | solution.py:126
  31.3 1.2 %collective-permute-start.10 = (bf16[32,2048]{1,0:T(8,128)(2,1)S(1)}, bf16[32,2048]{1,0:T(8,128)(2,1)S(1)}, u32[]{:S(2)}, u32[]{:S(2)}) collective-permute-start(bf16[32,2048]{1,0:T(8,128)(2,1)S(1)} %shard_map.78.refs_1_), channel_id=1, source_target_pairs={{0,2},{1,3},{2,0},{3,1},{4,6},{5,7},{6,4},{7,5},{8,10},{9,11},{10,... | collective-permute-start | bytes 393224 | tf_op jit(solution)/shard_map/ppermute | solution.py:126
  32.7 2.5 %collective-permute-start.15 = (bf16[32,2048]{1,0:T(8,128)(2,1)S(1)}, bf16[32,2048]{1,0:T(8,128)(2,1)S(1)}, u32[]{:S(2)}, u32[]{:S(2)}) collective-permute-start(bf16[32,2048]{1,0:T(8,128)(2,1)S(1)} %get-tuple-element.46), channel_id=1, source_target_pairs={{0,12},{4,8},{8,4},{12,0},{1,13},{5,9},{9,5},{13,1},{2,14},{6,10},... | collective-permute-start | bytes 393224 | tf_op jit(solution)/shard_map/ppermute | solution.py:126
  35.2 1.3 %collective-permute-done.11.refs_4_ = bf16[32,2048]{1,0:T(8,128)(2,1)S(1)} collective-permute-done((bf16[32,2048]{1,0:T(8,128)(2,1)S(1)}, bf16[32,2048]{1,0:T(8,128)(2,1)S(1)}, u32[]{:S(2)}, u32[]{:S(2)}) %collective-permute-start.11) | collective-permute-done | bytes 131104 | tf_op jit(solution)/shard_map/ppermute | solution.py:126
  37.1 2.4 %collective-permute-done.10.refs_3_ = bf16[32,2048]{1,0:T(8,128)(2,1)S(1)} collective-permute-done((bf16[32,2048]{1,0:T(8,128)(2,1)S(1)}, bf16[32,2048]{1,0:T(8,128)(2,1)S(1)}, u32[]{:S(2)}, u32[]{:S(2)}) %collective-permute-start.10) | collective-permute-done | bytes 131104 | tf_op jit(solution)/shard_map/ppermute | solution.py:126
  39.5 2.3 %shard_map.79 = (bf16[32,1650]{1,0:T(8,128)(2,1)S(1)}, bf16[32,1650]{1,0:T(8,128)(2,1)S(1)}, bf16[32,1650]{1,0:T(8,128)(2,1)S(1)}, bf16[32,1650]{1,0:T(8,128)(2,1)S(1)}) custom-call(bf16[1650,2048]{1,0:T(8,128)(2,1)S(1)} %bitcast.4, bf16[32,2048]{1,0:T(8,128)(2,1)S(1)} %shard_map.78.refs_1_, bf16[32,2048]{1,0:T(8,128)(2,1)S(1)} %collective-permute-done.9.refs_2_, ...), custom_call_target="tpu_custom_call" | custom-call | tf_op jit(solution)/shard_map/pallas_call | solution.py:141
  41.7 4.3 %collective-permute-done.16.refs_2_ = bf16[32,2048]{1,0:T(8,128)(2,1)S(1)} collective-permute-done((bf16[32,2048]{1,0:T(8,128)(2,1)S(1)}, bf16[32,2048]{1,0:T(8,128)(2,1)S(1)}, u32[]{:S(2)}, u32[]{:S(2)}) %collective-permute-start.16) | collective-permute-done | bytes 131104 | tf_op jit(solution)/shard_map/ppermute | solution.py:126
  48.1 2.2 %collective-permute-start.12 = (bf16[32,1650]{1,0:T(8,128)(2,1)S(1)}, bf16[32,1650]{1,0:T(8,128)(2,1)S(1)}, u32[]{:S(2)}, u32[]{:S(2)}) collective-permute-start(bf16[32,1650]{1,0:T(8,128)(2,1)S(1)} %get-tuple-element.43), channel_id=1, source_target_pairs={{0,12},{4,8},{8,4},{12,0},{1,13},{5,9},{9,5},{13,1},{2,14},{6,10},... | collective-permute-start | bytes 316808 | tf_op jit(solution)/shard_map/ppermute | solution.py:126
  50.3 1.5 %collective-permute-done.20.refs_4_ = bf16[32,2048]{1,0:T(8,128)(2,1)S(1)} collective-permute-done((bf16[32,2048]{1,0:T(8,128)(2,1)S(1)}, bf16[32,2048]{1,0:T(8,128)(2,1)S(1)}, u32[]{:S(2)}, u32[]{:S(2)}) %collective-permute-start.20) | collective-permute-done | bytes 131104 | tf_op jit(solution)/shard_map/ppermute | solution.py:126
  52.5 2.4 %collective-permute-done.19.refs_3_ = bf16[32,2048]{1,0:T(8,128)(2,1)S(1)} collective-permute-done((bf16[32,2048]{1,0:T(8,128)(2,1)S(1)}, bf16[32,2048]{1,0:T(8,128)(2,1)S(1)}, u32[]{:S(2)}, u32[]{:S(2)}) %collective-permute-start.19) | collective-permute-done | bytes 131104 | tf_op jit(solution)/shard_map/ppermute | solution.py:126
  54.8 2.3 %shard_map.81 = (bf16[32,1650]{1,0:T(8,128)(2,1)S(1)}, bf16[32,1650]{1,0:T(8,128)(2,1)S(1)}, bf16[32,1650]{1,0:T(8,128)(2,1)S(1)}, bf16[32,1650]{1,0:T(8,128)(2,1)S(1)}) custom-call(bf16[1650,2048]{1,0:T(8,128)(2,1)S(1)} %bitcast.5, bf16[32,2048]{1,0:T(8,128)(2,1)S(1)} %shard_map.80.refs_1_, bf16[32,2048]{1,0:T(8,128)(2,1)S(1)} %collective-permute-done.18.refs_2_, ...), custom_call_target="tpu_custom_call" | custom-call | tf_op jit(solution)/shard_map/pallas_call | solution.py:141
  57.1 2.3 %collective-permute-start.21 = (bf16[32,1650]{1,0:T(8,128)(2,1)S(1)}, bf16[32,1650]{1,0:T(8,128)(2,1)S(1)}, u32[]{:S(2)}, u32[]{:S(2)}) collective-permute-start(bf16[32,1650]{1,0:T(8,128)(2,1)S(1)} %get-tuple-element.50), channel_id=1, source_target_pairs={{0,12},{4,8},{8,4},{12,0},{1,13},{5,9},{9,5},{13,1},{2,14},{6,10},... | collective-permute-start | bytes 316808 | tf_op jit(solution)/shard_map/ppermute | solution.py:126
  59.4 2.2 %collective-permute-start.23 = (bf16[32,1650]{1,0:T(8,128)(2,1)S(1)}, bf16[32,1650]{1,0:T(8,128)(2,1)S(1)}, u32[]{:S(2)}, u32[]{:S(2)}) collective-permute-start(bf16[32,1650]{1,0:T(8,128)(2,1)S(1)} %get-tuple-element.52), channel_id=1, source_target_pairs={{0,4},{4,0},{8,12},{12,8},{1,5},{5,1},{9,13},{13,9},{2,6},{6,2},{1... | collective-permute-start | bytes 316808 | tf_op jit(solution)/shard_map/ppermute | solution.py:126
  61.6 3.2 %collective-permute-done.21 = bf16[32,1650]{1,0:T(8,128)(2,1)S(1)} collective-permute-done((bf16[32,1650]{1,0:T(8,128)(2,1)S(1)}, bf16[32,1650]{1,0:T(8,128)(2,1)S(1)}, u32[]{:S(2)}, u32[]{:S(2)}) %collective-permute-start.21) | collective-permute-done | bytes 105632 | tf_op jit(solution)/shard_map/ppermute | solution.py:126
  64.9 3.9 %collective-permute-done.22 = bf16[32,1650]{1,0:T(8,128)(2,1)S(1)} collective-permute-done((bf16[32,1650]{1,0:T(8,128)(2,1)S(1)}, bf16[32,1650]{1,0:T(8,128)(2,1)S(1)}, u32[]{:S(2)}, u32[]{:S(2)}) %collective-permute-start.22) | collective-permute-done | bytes 105632 | tf_op jit(solution)/shard_map/ppermute | solution.py:126
  (43 shorter events, 9.4 us)
Async XLA Ops:
  2.7 6.9 %collective-permute-start = (bf16[32,2176]{1,0:T(8,128)(2,1)S(1)}, bf16[32,2176]{1,0:T(8,128)(2,1)S(1)}, u32[]{:S(2)}, u32[]{:S(2)}) collective-permute-start(bf16[32,2176]{1,0:T(8,128)(2,1)S(1)} %get-tuple-element.31), channel_id=1, source_target_pairs={{0,3},{1,2},{2,1},{3,0},{4,7},{5,6},{6,5},{7,4},{8,11},{9,10},{10,... | collective-permute-start | bytes 417800 | tf_op jit(solution)/shard_map/ppermute | solution.py:126
  5.1 8.1 %collective-permute-start.1 = (bf16[32,2176]{1,0:T(8,128)(2,1)S(1)}, bf16[32,2176]{1,0:T(8,128)(2,1)S(1)}, u32[]{:S(2)}, u32[]{:S(2)}) collective-permute-start(bf16[32,2176]{1,0:T(8,128)(2,1)S(1)} %get-tuple-element.32), channel_id=1, source_target_pairs={{0,2},{1,3},{2,0},{3,1},{4,6},{5,7},{6,4},{7,5},{8,10},{9,11},{10,... | collective-permute-start | bytes 417800 | tf_op jit(solution)/shard_map/ppermute | solution.py:126
  5.8 7.4 %collective-permute-start.2 = (bf16[32,2176]{1,0:T(8,128)(2,1)S(1)}, bf16[32,2176]{1,0:T(8,128)(2,1)S(1)}, u32[]{:S(2)}, u32[]{:S(2)}) collective-permute-start(bf16[32,2176]{1,0:T(8,128)(2,1)S(1)} %get-tuple-element.33), channel_id=1, source_target_pairs={{0,1},{1,0},{2,3},{3,2},{4,5},{5,4},{6,7},{7,6},{8,9},{9,8},{10,11... | collective-permute-start | bytes 417800 | tf_op jit(solution)/shard_map/ppermute | solution.py:126
  6.3 13.2 %collective-permute-start.6 = (bf16[32,2048]{1,0:T(8,128)(2,1)S(1)}, bf16[32,2048]{1,0:T(8,128)(2,1)S(1)}, u32[]{:S(2)}, u32[]{:S(2)}) collective-permute-start(bf16[32,2048]{1,0:T(8,128)(2,1)S(1)} %get-tuple-element.38), channel_id=1, source_target_pairs={{0,3},{1,2},{2,1},{3,0},{4,7},{5,6},{6,5},{7,4},{8,11},{9,10},{10,... | collective-permute-start | bytes 393224 | tf_op jit(solution)/shard_map/ppermute | solution.py:126
  7.8 12.4 %collective-permute-start.7 = (bf16[32,2048]{1,0:T(8,128)(2,1)S(1)}, bf16[32,2048]{1,0:T(8,128)(2,1)S(1)}, u32[]{:S(2)}, u32[]{:S(2)}) collective-permute-start(bf16[32,2048]{1,0:T(8,128)(2,1)S(1)} %get-tuple-element.39), channel_id=1, source_target_pairs={{0,2},{1,3},{2,0},{3,1},{4,6},{5,7},{6,4},{7,5},{8,10},{9,11},{10,... | collective-permute-start | bytes 393224 | tf_op jit(solution)/shard_map/ppermute | solution.py:126
  9.6 10.6 %collective-permute-start.8 = (bf16[32,2048]{1,0:T(8,128)(2,1)S(1)}, bf16[32,2048]{1,0:T(8,128)(2,1)S(1)}, u32[]{:S(2)}, u32[]{:S(2)}) collective-permute-start(bf16[32,2048]{1,0:T(8,128)(2,1)S(1)} %get-tuple-element.40), channel_id=1, source_target_pairs={{0,1},{1,0},{2,3},{3,2},{4,5},{5,4},{6,7},{7,6},{8,9},{9,8},{10,11... | collective-permute-start | bytes 393224 | tf_op jit(solution)/shard_map/ppermute | solution.py:126
  15.8 8.3 %collective-permute-start.3 = (bf16[32,2048]{1,0:T(8,128)(2,1)S(1)}, bf16[32,2048]{1,0:T(8,128)(2,1)S(1)}, u32[]{:S(2)}, u32[]{:S(2)}) collective-permute-start(bf16[32,2048]{1,0:T(8,128)(2,1)S(1)} %get-tuple-element.35), channel_id=1, source_target_pairs={{0,12},{4,8},{8,4},{12,0},{1,13},{5,9},{9,5},{13,1},{2,14},{6,10},... | collective-permute-start | bytes 393224 | tf_op jit(solution)/shard_map/ppermute | solution.py:126
  19.4 11.3 %collective-permute-start.4 = (bf16[32,2048]{1,0:T(8,128)(2,1)S(1)}, bf16[32,2048]{1,0:T(8,128)(2,1)S(1)}, u32[]{:S(2)}, u32[]{:S(2)}) collective-permute-start(bf16[32,2048]{1,0:T(8,128)(2,1)S(1)} %get-tuple-element.36), channel_id=1, source_target_pairs={{0,8},{4,12},{8,0},{12,4},{1,9},{5,13},{9,1},{13,5},{2,10},{6,14},... | collective-permute-start | bytes 393224 | tf_op jit(solution)/shard_map/ppermute | solution.py:126
  19.5 11.3 %collective-permute-start.5 = (bf16[32,2048]{1,0:T(8,128)(2,1)S(1)}, bf16[32,2048]{1,0:T(8,128)(2,1)S(1)}, u32[]{:S(2)}, u32[]{:S(2)}) collective-permute-start(bf16[32,2048]{1,0:T(8,128)(2,1)S(1)} %get-tuple-element.37), channel_id=1, source_target_pairs={{0,4},{4,0},{8,12},{12,8},{1,5},{5,1},{9,13},{13,9},{2,6},{6,2},{1... | collective-permute-start | bytes 393224 | tf_op jit(solution)/shard_map/ppermute | solution.py:126
  30.8 5.8 %collective-permute-start.11 = (bf16[32,2048]{1,0:T(8,128)(2,1)S(1)}, bf16[32,2048]{1,0:T(8,128)(2,1)S(1)}, u32[]{:S(2)}, u32[]{:S(2)}) collective-permute-start(bf16[32,2048]{1,0:T(8,128)(2,1)S(1)} %shard_map.78.refs_1_), channel_id=1, source_target_pairs={{0,3},{1,2},{2,1},{3,0},{4,7},{5,6},{6,5},{7,4},{8,11},{9,10},{10,... | collective-permute-start | bytes 393224 | tf_op jit(solution)/shard_map/ppermute | solution.py:126
  31.3 8.2 %collective-permute-start.10 = (bf16[32,2048]{1,0:T(8,128)(2,1)S(1)}, bf16[32,2048]{1,0:T(8,128)(2,1)S(1)}, u32[]{:S(2)}, u32[]{:S(2)}) collective-permute-start(bf16[32,2048]{1,0:T(8,128)(2,1)S(1)} %shard_map.78.refs_1_), channel_id=1, source_target_pairs={{0,2},{1,3},{2,0},{3,1},{4,6},{5,7},{6,4},{7,5},{8,10},{9,11},{10,... | collective-permute-start | bytes 393224 | tf_op jit(solution)/shard_map/ppermute | solution.py:126
  32.5 7.0 %collective-permute-start.9 = (bf16[32,2048]{1,0:T(8,128)(2,1)S(1)}, bf16[32,2048]{1,0:T(8,128)(2,1)S(1)}, u32[]{:S(2)}, u32[]{:S(2)}) collective-permute-start(bf16[32,2048]{1,0:T(8,128)(2,1)S(1)} %shard_map.78.refs_1_), channel_id=1, source_target_pairs={{0,1},{1,0},{2,3},{3,2},{4,5},{5,4},{6,7},{7,6},{8,9},{9,8},{10,11... | collective-permute-start | bytes 393224 | tf_op jit(solution)/shard_map/ppermute | solution.py:126
  32.7 9.0 %collective-permute-start.15 = (bf16[32,2048]{1,0:T(8,128)(2,1)S(1)}, bf16[32,2048]{1,0:T(8,128)(2,1)S(1)}, u32[]{:S(2)}, u32[]{:S(2)}) collective-permute-start(bf16[32,2048]{1,0:T(8,128)(2,1)S(1)} %get-tuple-element.46), channel_id=1, source_target_pairs={{0,12},{4,8},{8,4},{12,0},{1,13},{5,9},{9,5},{13,1},{2,14},{6,10},... | collective-permute-start | bytes 393224 | tf_op jit(solution)/shard_map/ppermute | solution.py:126
  35.2 10.9 %collective-permute-start.16 = (bf16[32,2048]{1,0:T(8,128)(2,1)S(1)}, bf16[32,2048]{1,0:T(8,128)(2,1)S(1)}, u32[]{:S(2)}, u32[]{:S(2)}) collective-permute-start(bf16[32,2048]{1,0:T(8,128)(2,1)S(1)} %get-tuple-element.47), channel_id=1, source_target_pairs={{0,8},{4,12},{8,0},{12,4},{1,9},{5,13},{9,1},{13,5},{2,10},{6,14},... | collective-permute-start | bytes 393224 | tf_op jit(solution)/shard_map/ppermute | solution.py:126
  36.5 9.5 %collective-permute-start.17 = (bf16[32,2048]{1,0:T(8,128)(2,1)S(1)}, bf16[32,2048]{1,0:T(8,128)(2,1)S(1)}, u32[]{:S(2)}, u32[]{:S(2)}) collective-permute-start(bf16[32,2048]{1,0:T(8,128)(2,1)S(1)} %get-tuple-element.48), channel_id=1, source_target_pairs={{0,4},{4,0},{8,12},{12,8},{1,5},{5,1},{9,13},{13,9},{2,6},{6,2},{1... | collective-permute-start | bytes 393224 | tf_op jit(solution)/shard_map/ppermute | solution.py:126
  46.1 5.7 %collective-permute-start.20 = (bf16[32,2048]{1,0:T(8,128)(2,1)S(1)}, bf16[32,2048]{1,0:T(8,128)(2,1)S(1)}, u32[]{:S(2)}, u32[]{:S(2)}) collective-permute-start(bf16[32,2048]{1,0:T(8,128)(2,1)S(1)} %shard_map.80.refs_1_), channel_id=1, source_target_pairs={{0,3},{1,2},{2,1},{3,0},{4,7},{5,6},{6,5},{7,4},{8,11},{9,10},{10,... | collective-permute-start | bytes 393224 | tf_op jit(solution)/shard_map/ppermute | solution.py:126
  47.1 7.7 %collective-permute-start.19 = (bf16[32,2048]{1,0:T(8,128)(2,1)S(1)}, bf16[32,2048]{1,0:T(8,128)(2,1)S(1)}, u32[]{:S(2)}, u32[]{:S(2)}) collective-permute-start(bf16[32,2048]{1,0:T(8,128)(2,1)S(1)} %shard_map.80.refs_1_), channel_id=1, source_target_pairs={{0,2},{1,3},{2,0},{3,1},{4,6},{5,7},{6,4},{7,5},{8,10},{9,11},{10,... | collective-permute-start | bytes 393224 | tf_op jit(solution)/shard_map/ppermute | solution.py:126
  47.8 7.0 %collective-permute-start.18 = (bf16[32,2048]{1,0:T(8,128)(2,1)S(1)}, bf16[32,2048]{1,0:T(8,128)(2,1)S(1)}, u32[]{:S(2)}, u32[]{:S(2)}) collective-permute-start(bf16[32,2048]{1,0:T(8,128)(2,1)S(1)} %shard_map.80.refs_1_), channel_id=1, source_target_pairs={{0,1},{1,0},{2,3},{3,2},{4,5},{5,4},{6,7},{7,6},{8,9},{9,8},{10,11... | collective-permute-start | bytes 393224 | tf_op jit(solution)/shard_map/ppermute | solution.py:126
  48.1 11.3 %collective-permute-start.12 = (bf16[32,1650]{1,0:T(8,128)(2,1)S(1)}, bf16[32,1650]{1,0:T(8,128)(2,1)S(1)}, u32[]{:S(2)}, u32[]{:S(2)}) collective-permute-start(bf16[32,1650]{1,0:T(8,128)(2,1)S(1)} %get-tuple-element.43), channel_id=1, source_target_pairs={{0,12},{4,8},{8,4},{12,0},{1,13},{5,9},{9,5},{13,1},{2,14},{6,10},... | collective-permute-start | bytes 316808 | tf_op jit(solution)/shard_map/ppermute | solution.py:126
  50.3 11.3 %collective-permute-start.13 = (bf16[32,1650]{1,0:T(8,128)(2,1)S(1)}, bf16[32,1650]{1,0:T(8,128)(2,1)S(1)}, u32[]{:S(2)}, u32[]{:S(2)}) collective-permute-start(bf16[32,1650]{1,0:T(8,128)(2,1)S(1)} %get-tuple-element.44), channel_id=1, source_target_pairs={{0,8},{4,12},{8,0},{12,4},{1,9},{5,13},{9,1},{13,5},{2,10},{6,14},... | collective-permute-start | bytes 316808 | tf_op jit(solution)/shard_map/ppermute | solution.py:126
  51.8 9.7 %collective-permute-start.14 = (bf16[32,1650]{1,0:T(8,128)(2,1)S(1)}, bf16[32,1650]{1,0:T(8,128)(2,1)S(1)}, u32[]{:S(2)}, u32[]{:S(2)}) collective-permute-start(bf16[32,1650]{1,0:T(8,128)(2,1)S(1)} %get-tuple-element.45), channel_id=1, source_target_pairs={{0,4},{4,0},{8,12},{12,8},{1,5},{5,1},{9,13},{13,9},{2,6},{6,2},{1... | collective-permute-start | bytes 316808 | tf_op jit(solution)/shard_map/ppermute | solution.py:126
  57.1 7.8 %collective-permute-start.21 = (bf16[32,1650]{1,0:T(8,128)(2,1)S(1)}, bf16[32,1650]{1,0:T(8,128)(2,1)S(1)}, u32[]{:S(2)}, u32[]{:S(2)}) collective-permute-start(bf16[32,1650]{1,0:T(8,128)(2,1)S(1)} %get-tuple-element.50), channel_id=1, source_target_pairs={{0,12},{4,8},{8,4},{12,0},{1,13},{5,9},{9,5},{13,1},{2,14},{6,10},... | collective-permute-start | bytes 316808 | tf_op jit(solution)/shard_map/ppermute | solution.py:126
  59.4 9.4 %collective-permute-start.22 = (bf16[32,1650]{1,0:T(8,128)(2,1)S(1)}, bf16[32,1650]{1,0:T(8,128)(2,1)S(1)}, u32[]{:S(2)}, u32[]{:S(2)}) collective-permute-start(bf16[32,1650]{1,0:T(8,128)(2,1)S(1)} %get-tuple-element.51), channel_id=1, source_target_pairs={{0,8},{4,12},{8,0},{12,4},{1,9},{5,13},{9,1},{13,5},{2,10},{6,14},... | collective-permute-start | bytes 316808 | tf_op jit(solution)/shard_map/ppermute | solution.py:126
  59.4 9.4 %collective-permute-start.23 = (bf16[32,1650]{1,0:T(8,128)(2,1)S(1)}, bf16[32,1650]{1,0:T(8,128)(2,1)S(1)}, u32[]{:S(2)}, u32[]{:S(2)}) collective-permute-start(bf16[32,1650]{1,0:T(8,128)(2,1)S(1)} %get-tuple-element.52), channel_id=1, source_target_pairs={{0,4},{4,0},{8,12},{12,8},{1,5},{5,1},{9,13},{13,9},{2,6},{6,2},{1... | collective-permute-start | bytes 316808 | tf_op jit(solution)/shard_map/ppermute | solution.py:126
  (3 other events, 41.7 us)

commit v5 on v4

--- a/solution.py
+++ b/solution.py
@@ -199,7 +199,7 @@
         )
         before = (shares[0],)
         received.append(exchange(shares, "row"))
-    results = []
+    results, ahead = [], tuple(received[-1][1:2])
     for h in range(halves):
         (pupil,) = call(sum_kernel, [(each, points)], [], *received[h], after=before)
         pieces = exchange([pupil] * n_layer, "layer", 1)
@@ -209,9 +209,11 @@
             [pltpu.VMEM((n_layer, each, points), BF16), pltpu.VMEM((per_half, actuators), F32)],
             fitting.T,
             *pieces,
+            after=ahead,
         )
         before = (partial[0],)
         results.append(exchange(partial, "row"))
+        ahead = tuple(results[-1][1:2])
     return jnp.concatenate([total_of(result) for result in results], 0)
 
 

time: 69.7 us -> 71.4 us (1.024)
  starting transfers between devices: 24.4 us -> 28.2 us
  waiting for transfers between devices: 30.2 us -> 28 us
    ppermute x24, starting transfers between devices: 24.4 us -> 28.2 us  [exchange(): lax.ppermute(chunk, axis, [(j, j ^ sign * i % n) for j in range(n)])]
    ppermute x24, waiting for transfers between devices: 30.2 us -> 28 us  [exchange(): lax.ppermute(chunk, axis, [(j, j ^ sign * i % n) for j in range(n)])]
where the time goes in v5:
time: 71.4 us; the launch traced here: 71.2 us
  starting transfers between devices  28.2 us (39%)
  waiting for transfers between devices  28 us (39%)
  Pallas kernels  10.9 us (15%)
  local copies, waits for them, and re-layouts  2.29 us (3%)
  other arithmetic  1.69 us (2%)
    ppermute x24, starting transfers between devices, exchange(): lax.ppermute(chunk, axis, [(j, j ^ sign * i % n) for j in range(n)])  28.2 us
    ppermute x24, waiting for transfers between devices, exchange(): lax.ppermute(chunk, axis, [(j, j ^ sign * i % n) for j in range(n)])  28 us
    pallas_call x9, Pallas kernels, call(): pl.pallas_call(body, out_shape=[jax.ShapeDtypeStruct(shape, BF16) for sha...  10.9 us
    unnamed x6, local copies, waits for them, and re-layouts  2.29 us
  transfers between devices with their start and end apart: 24, of which 10 were waited for; matrix products, arithmetic and copies ran while one was open for 0% of the time, Pallas kernels for 15%

profile of v5, /device:TPU:0, one launch (start us, length us, event | category | flops | bytes accessed | tf_op | source)
XLA Modules:
  0.0 71.2 jit_solution(32491907714992973)
XLA Ops:
  0.9 1.3 %copy-done.1 = bf16[1,2048,256]{2,1,0:T(8,128)(2,1)S(1)} copy-done((bf16[1,2048,256]{2,1,0:T(8,128)(2,1)S(1)}, bf16[1,2048,256]{2,1,0:T(8,128)(2,1)}, u32[]{:S(2)}) %copy-start.1) | copy-done | bytes 1048600
  2.7 2.4 %collective-permute-start = (bf16[32,2176]{1,0:T(8,128)(2,1)S(1)}, bf16[32,2176]{1,0:T(8,128)(2,1)S(1)}, u32[]{:S(2)}, u32[]{:S(2)}) collective-permute-start(bf16[32,2176]{1,0:T(8,128)(2,1)S(1)} %get-tuple-element.31), channel_id=1, source_target_pairs={{0,3},{1,2},{2,1},{3,0},{4,7},{5,6},{6,5},{7,4},{8,11},{9,10},{10,... | collective-permute-start | bytes 417800 | tf_op jit(solution)/shard_map/ppermute | solution.py:126
  6.3 1.5 %collective-permute-start.6 = (bf16[32,2048]{1,0:T(8,128)(2,1)S(1)}, bf16[32,2048]{1,0:T(8,128)(2,1)S(1)}, u32[]{:S(2)}, u32[]{:S(2)}) collective-permute-start(bf16[32,2048]{1,0:T(8,128)(2,1)S(1)} %get-tuple-element.38), channel_id=1, source_target_pairs={{0,3},{1,2},{2,1},{3,0},{4,7},{5,6},{6,5},{7,4},{8,11},{9,10},{10,... | collective-permute-start | bytes 393224 | tf_op jit(solution)/shard_map/ppermute | solution.py:126
  10.0 0.9 %copy-done.2 = bf16[16,128,64]{1,2,0:T(8,128)(2,1)S(1)} copy-done((bf16[16,128,64]{1,2,0:T(8,128)(2,1)S(1)}, bf16[16,128,64]{1,2,0:T(8,128)(2,1)}, u32[]{:S(2)}) %copy-start.2) | copy-done | bytes 262168
  11.2 2.0 %collective-permute-done.1.refs_3_.refs_7_ = bf16[32,2176]{1,0:T(8,128)(2,1)S(1)} collective-permute-done((bf16[32,2176]{1,0:T(8,128)(2,1)S(1)}, bf16[32,2176]{1,0:T(8,128)(2,1)S(1)}, u32[]{:S(2)}, u32[]{:S(2)}) %collective-permute-start.1) | collective-permute-done | bytes 139296 | tf_op jit(solution)/shard_map/ppermute | solution.py:126
  13.2 2.6 %shard_map.76 = (bf16[32,2048]{1,0:T(8,128)(2,1)S(1)}, bf16[32,2048]{1,0:T(8,128)(2,1)S(1)}, bf16[32,2048]{1,0:T(8,128)(2,1)S(1)}, bf16[32,2048]{1,0:T(8,128)(2,1)S(1)}) custom-call(bf16[32,128,128]{2,1,0:T(8,128)(2,1)S(1)} %shard_map.75.refs_0_, bf16[32,2176]{1,0:T(8,128)(2,1)S(1)} %get-tuple-element.29.refs_2_.refs_1_.refs_5_, ...), custom_call_target="tpu_custom_call" | custom-call | tf_op jit(solution)/shard_map/pallas_call | solution.py:141
  15.8 3.7 %collective-permute-start.3 = (bf16[32,2048]{1,0:T(8,128)(2,1)S(1)}, bf16[32,2048]{1,0:T(8,128)(2,1)S(1)}, u32[]{:S(2)}, u32[]{:S(2)}) collective-permute-start(bf16[32,2048]{1,0:T(8,128)(2,1)S(1)} %get-tuple-element.35), channel_id=1, source_target_pairs={{0,12},{4,8},{8,4},{12,0},{1,13},{5,9},{9,5},{13,1},{2,14},{6,10},... | collective-permute-start | bytes 393224 | tf_op jit(solution)/shard_map/ppermute | solution.py:126
  20.2 2.5 %shard_map.77 = (bf16[32,2048]{1,0:T(8,128)(2,1)S(1)}, bf16[32,2048]{1,0:T(8,128)(2,1)S(1)}, bf16[32,2048]{1,0:T(8,128)(2,1)S(1)}, bf16[32,2048]{1,0:T(8,128)(2,1)S(1)}) custom-call(bf16[32,128,128]{2,1,0:T(8,128)(2,1)S(1)} %shard_map.75.refs_0_, bf16[32,2176]{1,0:T(8,128)(2,1)S(1)} %get-tuple-element.29.refs_2_.refs_1_.refs_5_, ...), custom_call_target="tpu_custom_call" | custom-call | tf_op jit(solution)/shard_map/pallas_call | solution.py:141
  22.8 3.7 %collective-permute-start.12 = (bf16[32,2048]{1,0:T(8,128)(2,1)S(1)}, bf16[32,2048]{1,0:T(8,128)(2,1)S(1)}, u32[]{:S(2)}, u32[]{:S(2)}) collective-permute-start(bf16[32,2048]{1,0:T(8,128)(2,1)S(1)} %get-tuple-element.42), channel_id=1, source_target_pairs={{0,12},{4,8},{8,4},{12,0},{1,13},{5,9},{9,5},{13,1},{2,14},{6,10},... | collective-permute-start | bytes 393224 | tf_op jit(solution)/shard_map/ppermute | solution.py:126
  26.5 8.0 %collective-permute-done.4.refs_2_ = bf16[32,2048]{1,0:T(8,128)(2,1)S(1)} collective-permute-done((bf16[32,2048]{1,0:T(8,128)(2,1)S(1)}, bf16[32,2048]{1,0:T(8,128)(2,1)S(1)}, u32[]{:S(2)}, u32[]{:S(2)}) %collective-permute-start.4) | collective-permute-done | bytes 131104 | tf_op jit(solution)/shard_map/ppermute | solution.py:126
  34.6 1.5 %collective-permute-start.10 = (bf16[32,2048]{1,0:T(8,128)(2,1)S(1)}, bf16[32,2048]{1,0:T(8,128)(2,1)S(1)}, u32[]{:S(2)}, u32[]{:S(2)}) collective-permute-start(bf16[32,2048]{1,0:T(8,128)(2,1)S(1)} %shard_map.78.refs_1_), channel_id=1, source_target_pairs={{0,2},{1,3},{2,0},{3,1},{4,6},{5,7},{6,4},{7,5},{8,10},{9,11},{10,... | collective-permute-start | bytes 393224 | tf_op jit(solution)/shard_map/ppermute | solution.py:126
  36.5 3.0 %collective-permute-start.17 = (bf16[32,2048]{1,0:T(8,128)(2,1)S(1)}, bf16[32,2048]{1,0:T(8,128)(2,1)S(1)}, u32[]{:S(2)}, u32[]{:S(2)}) collective-permute-start(bf16[32,2048]{1,0:T(8,128)(2,1)S(1)} %get-tuple-element.48), channel_id=1, source_target_pairs={{0,4},{4,0},{8,12},{12,8},{1,5},{5,1},{9,13},{13,9},{2,6},{6,2},{1... | collective-permute-start | bytes 393224 | tf_op jit(solution)/shard_map/ppermute | solution.py:126
  40.4 2.8 %collective-permute-done.10.refs_3_ = bf16[32,2048]{1,0:T(8,128)(2,1)S(1)} collective-permute-done((bf16[32,2048]{1,0:T(8,128)(2,1)S(1)}, bf16[32,2048]{1,0:T(8,128)(2,1)S(1)}, u32[]{:S(2)}, u32[]{:S(2)}) %collective-permute-start.10) | collective-permute-done | bytes 131104 | tf_op jit(solution)/shard_map/ppermute | solution.py:126
  43.2 2.3 %shard_map.79 = (bf16[32,1650]{1,0:T(8,128)(2,1)S(1)}, bf16[32,1650]{1,0:T(8,128)(2,1)S(1)}, bf16[32,1650]{1,0:T(8,128)(2,1)S(1)}, bf16[32,1650]{1,0:T(8,128)(2,1)S(1)}) custom-call(bf16[1650,2048]{1,0:T(8,128)(2,1)S(1)} %bitcast.4, bf16[32,2048]{1,0:T(8,128)(2,1)S(1)} %shard_map.78.refs_1_, bf16[32,2048]{1,0:T(8,128)(2,1)S(1)} %collective-permute-done.9.refs_2_, ...), custom_call_target="tpu_custom_call" | custom-call | tf_op jit(solution)/shard_map/pallas_call | solution.py:141
  45.5 2.6 %collective-permute-start.13 = (bf16[32,1650]{1,0:T(8,128)(2,1)S(1)}, bf16[32,1650]{1,0:T(8,128)(2,1)S(1)}, u32[]{:S(2)}, u32[]{:S(2)}) collective-permute-start(bf16[32,1650]{1,0:T(8,128)(2,1)S(1)} %get-tuple-element.44), channel_id=1, source_target_pairs={{0,12},{4,8},{8,4},{12,0},{1,13},{5,9},{9,5},{13,1},{2,14},{6,10},... | collective-permute-start | bytes 316808 | tf_op jit(solution)/shard_map/ppermute | solution.py:126
  48.2 1.4 %collective-permute-start.19 = (bf16[32,2048]{1,0:T(8,128)(2,1)S(1)}, bf16[32,2048]{1,0:T(8,128)(2,1)S(1)}, u32[]{:S(2)}, u32[]{:S(2)}) collective-permute-start(bf16[32,2048]{1,0:T(8,128)(2,1)S(1)} %shard_map.80.refs_1_), channel_id=1, source_target_pairs={{0,2},{1,3},{2,0},{3,1},{4,6},{5,7},{6,4},{7,5},{8,10},{9,11},{10,... | collective-permute-start | bytes 393224 | tf_op jit(solution)/shard_map/ppermute | solution.py:126
  50.0 2.3 %collective-permute-done.13.refs_5_ = bf16[32,1650]{1,0:T(8,128)(2,1)S(1)} collective-permute-done((bf16[32,1650]{1,0:T(8,128)(2,1)S(1)}, bf16[32,1650]{1,0:T(8,128)(2,1)S(1)}, u32[]{:S(2)}, u32[]{:S(2)}) %collective-permute-start.13) | collective-permute-done | bytes 105632 | tf_op jit(solution)/shard_map/ppermute | solution.py:126
  52.3 1.6 %collective-permute-done.20.refs_4_ = bf16[32,2048]{1,0:T(8,128)(2,1)S(1)} collective-permute-done((bf16[32,2048]{1,0:T(8,128)(2,1)S(1)}, bf16[32,2048]{1,0:T(8,128)(2,1)S(1)}, u32[]{:S(2)}, u32[]{:S(2)}) %collective-permute-start.20) | collective-permute-done | bytes 131104 | tf_op jit(solution)/shard_map/ppermute | solution.py:126
  54.0 2.8 %collective-permute-done.19.refs_3_ = bf16[32,2048]{1,0:T(8,128)(2,1)S(1)} collective-permute-done((bf16[32,2048]{1,0:T(8,128)(2,1)S(1)}, bf16[32,2048]{1,0:T(8,128)(2,1)S(1)}, u32[]{:S(2)}, u32[]{:S(2)}) %collective-permute-start.19) | collective-permute-done | bytes 131104 | tf_op jit(solution)/shard_map/ppermute | solution.py:126
  56.8 2.3 %shard_map.81 = (bf16[32,1650]{1,0:T(8,128)(2,1)S(1)}, bf16[32,1650]{1,0:T(8,128)(2,1)S(1)}, bf16[32,1650]{1,0:T(8,128)(2,1)S(1)}, bf16[32,1650]{1,0:T(8,128)(2,1)S(1)}) custom-call(bf16[1650,2048]{1,0:T(8,128)(2,1)S(1)} %bitcast.5, bf16[32,2048]{1,0:T(8,128)(2,1)S(1)} %shard_map.80.refs_1_, bf16[32,2048]{1,0:T(8,128)(2,1)S(1)} %collective-permute-done.18.refs_2_, ...), custom_call_target="tpu_custom_call" | custom-call | tf_op jit(solution)/shard_map/pallas_call | solution.py:141
  59.1 1.4 %collective-permute-start.21 = (bf16[32,1650]{1,0:T(8,128)(2,1)S(1)}, bf16[32,1650]{1,0:T(8,128)(2,1)S(1)}, u32[]{:S(2)}, u32[]{:S(2)}) collective-permute-start(bf16[32,1650]{1,0:T(8,128)(2,1)S(1)} %get-tuple-element.50), channel_id=1, source_target_pairs={{0,12},{4,8},{8,4},{12,0},{1,13},{5,9},{9,5},{13,1},{2,14},{6,10},... | collective-permute-start | bytes 316808 | tf_op jit(solution)/shard_map/ppermute | solution.py:126
  60.4 3.1 %collective-permute-start.23 = (bf16[32,1650]{1,0:T(8,128)(2,1)S(1)}, bf16[32,1650]{1,0:T(8,128)(2,1)S(1)}, u32[]{:S(2)}, u32[]{:S(2)}) collective-permute-start(bf16[32,1650]{1,0:T(8,128)(2,1)S(1)} %get-tuple-element.52), channel_id=1, source_target_pairs={{0,4},{4,0},{8,12},{12,8},{1,5},{5,1},{9,13},{13,9},{2,6},{6,2},{1... | collective-permute-start | bytes 316808 | tf_op jit(solution)/shard_map/ppermute | solution.py:126
  63.6 3.3 %collective-permute-done.21 = bf16[32,1650]{1,0:T(8,128)(2,1)S(1)} collective-permute-done((bf16[32,1650]{1,0:T(8,128)(2,1)S(1)}, bf16[32,1650]{1,0:T(8,128)(2,1)S(1)}, u32[]{:S(2)}, u32[]{:S(2)}) %collective-permute-start.21) | collective-permute-done | bytes 105632 | tf_op jit(solution)/shard_map/ppermute | solution.py:126
  66.8 3.6 %collective-permute-done.22 = bf16[32,1650]{1,0:T(8,128)(2,1)S(1)} collective-permute-done((bf16[32,1650]{1,0:T(8,128)(2,1)S(1)}, bf16[32,1650]{1,0:T(8,128)(2,1)S(1)}, u32[]{:S(2)}, u32[]{:S(2)}) %collective-permute-start.22) | collective-permute-done | bytes 105632 | tf_op jit(solution)/shard_map/ppermute | solution.py:126
  (43 shorter events, 8.5 us)
Async XLA Ops:
  2.7 6.5 %collective-permute-start = (bf16[32,2176]{1,0:T(8,128)(2,1)S(1)}, bf16[32,2176]{1,0:T(8,128)(2,1)S(1)}, u32[]{:S(2)}, u32[]{:S(2)}) collective-permute-start(bf16[32,2176]{1,0:T(8,128)(2,1)S(1)} %get-tuple-element.31), channel_id=1, source_target_pairs={{0,3},{1,2},{2,1},{3,0},{4,7},{5,6},{6,5},{7,4},{8,11},{9,10},{10,... | collective-permute-start | bytes 417800 | tf_op jit(solution)/shard_map/ppermute | solution.py:126
  5.1 8.1 %collective-permute-start.1 = (bf16[32,2176]{1,0:T(8,128)(2,1)S(1)}, bf16[32,2176]{1,0:T(8,128)(2,1)S(1)}, u32[]{:S(2)}, u32[]{:S(2)}) collective-permute-start(bf16[32,2176]{1,0:T(8,128)(2,1)S(1)} %get-tuple-element.32), channel_id=1, source_target_pairs={{0,2},{1,3},{2,0},{3,1},{4,6},{5,7},{6,4},{7,5},{8,10},{9,11},{10,... | collective-permute-start | bytes 417800 | tf_op jit(solution)/shard_map/ppermute | solution.py:126
  5.8 7.4 %collective-permute-start.2 = (bf16[32,2176]{1,0:T(8,128)(2,1)S(1)}, bf16[32,2176]{1,0:T(8,128)(2,1)S(1)}, u32[]{:S(2)}, u32[]{:S(2)}) collective-permute-start(bf16[32,2176]{1,0:T(8,128)(2,1)S(1)} %get-tuple-element.33), channel_id=1, source_target_pairs={{0,1},{1,0},{2,3},{3,2},{4,5},{5,4},{6,7},{7,6},{8,9},{9,8},{10,11... | collective-permute-start | bytes 417800 | tf_op jit(solution)/shard_map/ppermute | solution.py:126
  6.3 13.2 %collective-permute-start.6 = (bf16[32,2048]{1,0:T(8,128)(2,1)S(1)}, bf16[32,2048]{1,0:T(8,128)(2,1)S(1)}, u32[]{:S(2)}, u32[]{:S(2)}) collective-permute-start(bf16[32,2048]{1,0:T(8,128)(2,1)S(1)} %get-tuple-element.38), channel_id=1, source_target_pairs={{0,3},{1,2},{2,1},{3,0},{4,7},{5,6},{6,5},{7,4},{8,11},{9,10},{10,... | collective-permute-start | bytes 393224 | tf_op jit(solution)/shard_map/ppermute | solution.py:126
  7.8 12.4 %collective-permute-start.7 = (bf16[32,2048]{1,0:T(8,128)(2,1)S(1)}, bf16[32,2048]{1,0:T(8,128)(2,1)S(1)}, u32[]{:S(2)}, u32[]{:S(2)}) collective-permute-start(bf16[32,2048]{1,0:T(8,128)(2,1)S(1)} %get-tuple-element.39), channel_id=1, source_target_pairs={{0,2},{1,3},{2,0},{3,1},{4,6},{5,7},{6,4},{7,5},{8,10},{9,11},{10,... | collective-permute-start | bytes 393224 | tf_op jit(solution)/shard_map/ppermute | solution.py:126
  9.2 11.0 %collective-permute-start.8 = (bf16[32,2048]{1,0:T(8,128)(2,1)S(1)}, bf16[32,2048]{1,0:T(8,128)(2,1)S(1)}, u32[]{:S(2)}, u32[]{:S(2)}) collective-permute-start(bf16[32,2048]{1,0:T(8,128)(2,1)S(1)} %get-tuple-element.40), channel_id=1, source_target_pairs={{0,1},{1,0},{2,3},{3,2},{4,5},{5,4},{6,7},{7,6},{8,9},{9,8},{10,11... | collective-permute-start | bytes 393224 | tf_op jit(solution)/shard_map/ppermute | solution.py:126
  15.8 10.7 %collective-permute-start.3 = (bf16[32,2048]{1,0:T(8,128)(2,1)S(1)}, bf16[32,2048]{1,0:T(8,128)(2,1)S(1)}, u32[]{:S(2)}, u32[]{:S(2)}) collective-permute-start(bf16[32,2048]{1,0:T(8,128)(2,1)S(1)} %get-tuple-element.35), channel_id=1, source_target_pairs={{0,12},{4,8},{8,4},{12,0},{1,13},{5,9},{9,5},{13,1},{2,14},{6,10},... | collective-permute-start | bytes 393224 | tf_op jit(solution)/shard_map/ppermute | solution.py:126
  19.4 15.0 %collective-permute-start.4 = (bf16[32,2048]{1,0:T(8,128)(2,1)S(1)}, bf16[32,2048]{1,0:T(8,128)(2,1)S(1)}, u32[]{:S(2)}, u32[]{:S(2)}) collective-permute-start(bf16[32,2048]{1,0:T(8,128)(2,1)S(1)} %get-tuple-element.36), channel_id=1, source_target_pairs={{0,8},{4,12},{8,0},{12,4},{1,9},{5,13},{9,1},{13,5},{2,10},{6,14},... | collective-permute-start | bytes 393224 | tf_op jit(solution)/shard_map/ppermute | solution.py:126
  19.5 15.0 %collective-permute-start.5 = (bf16[32,2048]{1,0:T(8,128)(2,1)S(1)}, bf16[32,2048]{1,0:T(8,128)(2,1)S(1)}, u32[]{:S(2)}, u32[]{:S(2)}) collective-permute-start(bf16[32,2048]{1,0:T(8,128)(2,1)S(1)} %get-tuple-element.37), channel_id=1, source_target_pairs={{0,4},{4,0},{8,12},{12,8},{1,5},{5,1},{9,13},{13,9},{2,6},{6,2},{1... | collective-permute-start | bytes 393224 | tf_op jit(solution)/shard_map/ppermute | solution.py:126
  22.8 13.7 %collective-permute-start.12 = (bf16[32,2048]{1,0:T(8,128)(2,1)S(1)}, bf16[32,2048]{1,0:T(8,128)(2,1)S(1)}, u32[]{:S(2)}, u32[]{:S(2)}) collective-permute-start(bf16[32,2048]{1,0:T(8,128)(2,1)S(1)} %get-tuple-element.42), channel_id=1, source_target_pairs={{0,12},{4,8},{8,4},{12,0},{1,13},{5,9},{9,5},{13,1},{2,14},{6,10},... | collective-permute-start | bytes 393224 | tf_op jit(solution)/shard_map/ppermute | solution.py:126
  34.5 5.9 %collective-permute-start.11 = (bf16[32,2048]{1,0:T(8,128)(2,1)S(1)}, bf16[32,2048]{1,0:T(8,128)(2,1)S(1)}, u32[]{:S(2)}, u32[]{:S(2)}) collective-permute-start(bf16[32,2048]{1,0:T(8,128)(2,1)S(1)} %shard_map.78.refs_1_), channel_id=1, source_target_pairs={{0,3},{1,2},{2,1},{3,0},{4,7},{5,6},{6,5},{7,4},{8,11},{9,10},{10,... | collective-permute-start | bytes 393224 | tf_op jit(solution)/shard_map/ppermute | solution.py:126
  34.6 8.6 %collective-permute-start.10 = (bf16[32,2048]{1,0:T(8,128)(2,1)S(1)}, bf16[32,2048]{1,0:T(8,128)(2,1)S(1)}, u32[]{:S(2)}, u32[]{:S(2)}) collective-permute-start(bf16[32,2048]{1,0:T(8,128)(2,1)S(1)} %shard_map.78.refs_1_), channel_id=1, source_target_pairs={{0,2},{1,3},{2,0},{3,1},{4,6},{5,7},{6,4},{7,5},{8,10},{9,11},{10,... | collective-permute-start | bytes 393224 | tf_op jit(solution)/shard_map/ppermute | solution.py:126
  36.1 7.1 %collective-permute-start.9 = (bf16[32,2048]{1,0:T(8,128)(2,1)S(1)}, bf16[32,2048]{1,0:T(8,128)(2,1)S(1)}, u32[]{:S(2)}, u32[]{:S(2)}) collective-permute-start(bf16[32,2048]{1,0:T(8,128)(2,1)S(1)} %shard_map.78.refs_1_), channel_id=1, source_target_pairs={{0,1},{1,0},{2,3},{3,2},{4,5},{5,4},{6,7},{7,6},{8,9},{9,8},{10,11... | collective-permute-start | bytes 393224 | tf_op jit(solution)/shard_map/ppermute | solution.py:126
  36.5 11.6 %collective-permute-start.16 = (bf16[32,2048]{1,0:T(8,128)(2,1)S(1)}, bf16[32,2048]{1,0:T(8,128)(2,1)S(1)}, u32[]{:S(2)}, u32[]{:S(2)}) collective-permute-start(bf16[32,2048]{1,0:T(8,128)(2,1)S(1)} %get-tuple-element.47), channel_id=1, source_target_pairs={{0,8},{4,12},{8,0},{12,4},{1,9},{5,13},{9,1},{13,5},{2,10},{6,14},... | collective-permute-start | bytes 393224 | tf_op jit(solution)/shard_map/ppermute | solution.py:126
  36.5 11.6 %collective-permute-start.17 = (bf16[32,2048]{1,0:T(8,128)(2,1)S(1)}, bf16[32,2048]{1,0:T(8,128)(2,1)S(1)}, u32[]{:S(2)}, u32[]{:S(2)}) collective-permute-start(bf16[32,2048]{1,0:T(8,128)(2,1)S(1)} %get-tuple-element.48), channel_id=1, source_target_pairs={{0,4},{4,0},{8,12},{12,8},{1,5},{5,1},{9,13},{13,9},{2,6},{6,2},{1... | collective-permute-start | bytes 393224 | tf_op jit(solution)/shard_map/ppermute | solution.py:126
  45.5 6.9 %collective-permute-start.13 = (bf16[32,1650]{1,0:T(8,128)(2,1)S(1)}, bf16[32,1650]{1,0:T(8,128)(2,1)S(1)}, u32[]{:S(2)}, u32[]{:S(2)}) collective-permute-start(bf16[32,1650]{1,0:T(8,128)(2,1)S(1)} %get-tuple-element.44), channel_id=1, source_target_pairs={{0,12},{4,8},{8,4},{12,0},{1,13},{5,9},{9,5},{13,1},{2,14},{6,10},... | collective-permute-start | bytes 316808 | tf_op jit(solution)/shard_map/ppermute | solution.py:126
  48.1 5.8 %collective-permute-start.20 = (bf16[32,2048]{1,0:T(8,128)(2,1)S(1)}, bf16[32,2048]{1,0:T(8,128)(2,1)S(1)}, u32[]{:S(2)}, u32[]{:S(2)}) collective-permute-start(bf16[32,2048]{1,0:T(8,128)(2,1)S(1)} %shard_map.80.refs_1_), channel_id=1, source_target_pairs={{0,3},{1,2},{2,1},{3,0},{4,7},{5,6},{6,5},{7,4},{8,11},{9,10},{10,... | collective-permute-start | bytes 393224 | tf_op jit(solution)/shard_map/ppermute | solution.py:126
  48.2 8.6 %collective-permute-start.19 = (bf16[32,2048]{1,0:T(8,128)(2,1)S(1)}, bf16[32,2048]{1,0:T(8,128)(2,1)S(1)}, u32[]{:S(2)}, u32[]{:S(2)}) collective-permute-start(bf16[32,2048]{1,0:T(8,128)(2,1)S(1)} %shard_map.80.refs_1_), channel_id=1, source_target_pairs={{0,2},{1,3},{2,0},{3,1},{4,6},{5,7},{6,4},{7,5},{8,10},{9,11},{10,... | collective-permute-start | bytes 393224 | tf_op jit(solution)/shard_map/ppermute | solution.py:126
  49.6 7.1 %collective-permute-start.18 = (bf16[32,2048]{1,0:T(8,128)(2,1)S(1)}, bf16[32,2048]{1,0:T(8,128)(2,1)S(1)}, u32[]{:S(2)}, u32[]{:S(2)}) collective-permute-start(bf16[32,2048]{1,0:T(8,128)(2,1)S(1)} %shard_map.80.refs_1_), channel_id=1, source_target_pairs={{0,1},{1,0},{2,3},{3,2},{4,5},{5,4},{6,7},{7,6},{8,9},{9,8},{10,11... | collective-permute-start | bytes 393224 | tf_op jit(solution)/shard_map/ppermute | solution.py:126
  50.0 13.5 %collective-permute-start.14 = (bf16[32,1650]{1,0:T(8,128)(2,1)S(1)}, bf16[32,1650]{1,0:T(8,128)(2,1)S(1)}, u32[]{:S(2)}, u32[]{:S(2)}) collective-permute-start(bf16[32,1650]{1,0:T(8,128)(2,1)S(1)} %get-tuple-element.45), channel_id=1, source_target_pairs={{0,8},{4,12},{8,0},{12,4},{1,9},{5,13},{9,1},{13,5},{2,10},{6,14},... | collective-permute-start | bytes 316808 | tf_op jit(solution)/shard_map/ppermute | solution.py:126
  52.3 11.2 %collective-permute-start.15 = (bf16[32,1650]{1,0:T(8,128)(2,1)S(1)}, bf16[32,1650]{1,0:T(8,128)(2,1)S(1)}, u32[]{:S(2)}, u32[]{:S(2)}) collective-permute-start(bf16[32,1650]{1,0:T(8,128)(2,1)S(1)} %get-tuple-element.46), channel_id=1, source_target_pairs={{0,4},{4,0},{8,12},{12,8},{1,5},{5,1},{9,13},{13,9},{2,6},{6,2},{1... | collective-permute-start | bytes 316808 | tf_op jit(solution)/shard_map/ppermute | solution.py:126
  59.1 7.8 %collective-permute-start.21 = (bf16[32,1650]{1,0:T(8,128)(2,1)S(1)}, bf16[32,1650]{1,0:T(8,128)(2,1)S(1)}, u32[]{:S(2)}, u32[]{:S(2)}) collective-permute-start(bf16[32,1650]{1,0:T(8,128)(2,1)S(1)} %get-tuple-element.50), channel_id=1, source_target_pairs={{0,12},{4,8},{8,4},{12,0},{1,13},{5,9},{9,5},{13,1},{2,14},{6,10},... | collective-permute-start | bytes 316808 | tf_op jit(solution)/shard_map/ppermute | solution.py:126
  60.4 10.0 %collective-permute-start.22 = (bf16[32,1650]{1,0:T(8,128)(2,1)S(1)}, bf16[32,1650]{1,0:T(8,128)(2,1)S(1)}, u32[]{:S(2)}, u32[]{:S(2)}) collective-permute-start(bf16[32,1650]{1,0:T(8,128)(2,1)S(1)} %get-tuple-element.51), channel_id=1, source_target_pairs={{0,8},{4,12},{8,0},{12,4},{1,9},{5,13},{9,1},{13,5},{2,10},{6,14},... | collective-permute-start | bytes 316808 | tf_op jit(solution)/shard_map/ppermute | solution.py:126
  60.4 10.0 %collective-permute-start.23 = (bf16[32,1650]{1,0:T(8,128)(2,1)S(1)}, bf16[32,1650]{1,0:T(8,128)(2,1)S(1)}, u32[]{:S(2)}, u32[]{:S(2)}) collective-permute-start(bf16[32,1650]{1,0:T(8,128)(2,1)S(1)} %get-tuple-element.52), channel_id=1, source_target_pairs={{0,4},{4,0},{8,12},{12,8},{1,5},{5,1},{9,13},{13,9},{2,6},{6,2},{1... | collective-permute-start | bytes 316808 | tf_op jit(solution)/shard_map/ppermute | solution.py:126
  (3 other events, 45.5 us)

commit v6 on v5

--- a/solution.py
+++ b/solution.py
@@ -120,12 +120,20 @@
             out[...] = product[pl.ds(start, each), :].astype(BF16)
 
 
-def exchange(chunks, axis, sign=-1):
+def trade(chunk, axis, k):
+    return lax.ppermute(chunk, axis, [(j, j ^ k) for j in range(lax.axis_size(axis))])
+
+
+def exchange(chunks, axis):
     n = len(chunks)
-    return [
-        lax.ppermute(chunk, axis, [(j, j ^ (sign * i % n)) for j in range(n)]) if i else chunk
-        for i, chunk in enumerate(chunks)
-    ]
+    return [trade(chunk, axis, n - i) if i else chunk for i, chunk in enumerate(chunks)]
+
+
+def gather(piece, axis, paired):
+    got = [piece]
+    for k in range(1, lax.axis_size(axis)):
+        got.append(trade(got[k - 1], axis, 1) if paired and k % 2 else trade(piece, axis, k))
+    return got
 
 
 def total_of(parts):
@@ -198,11 +206,13 @@
             after=before,
         )
         before = (shares[0],)
+        if h > 0:
+            shares, received[-1] = lax.optimization_barrier((shares, received[-1]))
         received.append(exchange(shares, "row"))
     results, ahead = [], tuple(received[-1][1:2])
     for h in range(halves):
         (pupil,) = call(sum_kernel, [(each, points)], [], *received[h], after=before)
-        pieces = exchange([pupil] * n_layer, "layer", 1)
+        pieces = gather(pupil, "layer", h == 0)
         partial = call(
             functools.partial(fit_kernel, n_layer, n_row),
             [(chunk // halves, actuators)] * n_row,

time: 71.4 us -> 69.6 us (0.975)
  waiting for transfers between devices: 28 us -> 25.2 us
  starting transfers between devices: 28.2 us -> 29.2 us
    ppermute x24, waiting for transfers between devices: 28 us -> 25.2 us  [trade(): lax.ppermute(chunk, axis, [(j, j ^ k) for j in range(lax.axis_size(axis))])]
    ppermute x24, starting transfers between devices: 28.2 us -> 29.2 us  [trade(): lax.ppermute(chunk, axis, [(j, j ^ k) for j in range(lax.axis_size(axis))])]
where the time goes in v6:
time: 69.6 us; the launch traced here: 69.4 us
  starting transfers between devices  29.2 us (42%)
  waiting for transfers between devices  25.2 us (36%)
  Pallas kernels  10.9 us (16%)
  local copies, waits for them, and re-layouts  2.29 us (3%)
  other arithmetic  1.7 us (2%)
    ppermute x24, starting transfers between devices, trade(): lax.ppermute(chunk, axis, [(j, j ^ k) for j in range(lax.axis_size(axis))])  29.2 us
    ppermute x24, waiting for transfers between devices, trade(): lax.ppermute(chunk, axis, [(j, j ^ k) for j in range(lax.axis_size(axis))])  25.2 us
    pallas_call x9, Pallas kernels, call(): pl.pallas_call(body, out_shape=[jax.ShapeDtypeStruct(shape, BF16) for sha...  10.9 us
    unnamed x6, local copies, waits for them, and re-layouts  2.29 us
  transfers between devices with their start and end apart: 24, of which 10 were waited for; matrix products, arithmetic and copies ran while one was open for 0% of the time, Pallas kernels for 15%

profile of v6, /device:TPU:0, one launch (start us, length us, event | category | flops | bytes accessed | tf_op | source)
XLA Modules:
  0.0 69.4 jit_solution(6959330416054801536)
XLA Ops:
  0.9 1.3 %copy-done.1 = bf16[1,2048,256]{2,1,0:T(8,128)(2,1)S(1)} copy-done((bf16[1,2048,256]{2,1,0:T(8,128)(2,1)S(1)}, bf16[1,2048,256]{2,1,0:T(8,128)(2,1)}, u32[]{:S(2)}) %copy-start.1) | copy-done | bytes 1048600
  2.7 2.4 %collective-permute-start = (bf16[32,2176]{1,0:T(8,128)(2,1)S(1)}, bf16[32,2176]{1,0:T(8,128)(2,1)S(1)}, u32[]{:S(2)}, u32[]{:S(2)}) collective-permute-start(bf16[32,2176]{1,0:T(8,128)(2,1)S(1)} %get-tuple-element.39), channel_id=1, source_target_pairs={{0,3},{1,2},{2,1},{3,0},{4,7},{5,6},{6,5},{7,4},{8,11},{9,10},{10,... | collective-permute-start | bytes 417800 | tf_op jit(solution)/shard_map/ppermute | solution.py:124
  6.3 1.5 %collective-permute-start.3 = (bf16[32,2048]{1,0:T(8,128)(2,1)S(1)}, bf16[32,2048]{1,0:T(8,128)(2,1)S(1)}, u32[]{:S(2)}, u32[]{:S(2)}) collective-permute-start(bf16[32,2048]{1,0:T(8,128)(2,1)S(1)} %get-tuple-element.42), channel_id=1, source_target_pairs={{0,3},{1,2},{2,1},{3,0},{4,7},{5,6},{6,5},{7,4},{8,11},{9,10},{10,... | collective-permute-start | bytes 393224 | tf_op jit(solution)/shard_map/ppermute | solution.py:124
  10.0 3.2 %collective-permute-done.1.refs_3_.refs_7_ = bf16[32,2176]{1,0:T(8,128)(2,1)S(1)} collective-permute-done((bf16[32,2176]{1,0:T(8,128)(2,1)S(1)}, bf16[32,2176]{1,0:T(8,128)(2,1)S(1)}, u32[]{:S(2)}, u32[]{:S(2)}) %collective-permute-start.1) | collective-permute-done | bytes 139296 | tf_op jit(solution)/shard_map/ppermute | solution.py:124
  13.2 2.6 %shard_map.76 = (bf16[32,2048]{1,0:T(8,128)(2,1)S(1)}, bf16[32,2048]{1,0:T(8,128)(2,1)S(1)}, bf16[32,2048]{1,0:T(8,128)(2,1)S(1)}, bf16[32,2048]{1,0:T(8,128)(2,1)S(1)}) custom-call(bf16[32,128,128]{2,1,0:T(8,128)(2,1)S(1)} %shard_map.75.refs_0_, bf16[32,2176]{1,0:T(8,128)(2,1)S(1)} %get-tuple-element.37.refs_2_.refs_1_.refs_5_, ...), custom_call_target="tpu_custom_call" | custom-call | tf_op jit(solution)/shard_map/pallas_call | solution.py:149
  15.8 3.7 %collective-permute-start.6 = (bf16[32,2048]{1,0:T(8,128)(2,1)S(1)}, bf16[32,2048]{1,0:T(8,128)(2,1)S(1)}, u32[]{:S(2)}, u32[]{:S(2)}) collective-permute-start(bf16[32,2048]{1,0:T(8,128)(2,1)S(1)} %get-tuple-element.50), channel_id=1, source_target_pairs={{0,12},{4,8},{8,4},{12,0},{1,13},{5,9},{9,5},{13,1},{2,14},{6,10},... | collective-permute-start | bytes 393224 | tf_op jit(solution)/shard_map/ppermute | solution.py:124
  20.2 2.5 %shard_map.77 = (bf16[32,2048]{1,0:T(8,128)(2,1)S(1)}, bf16[32,2048]{1,0:T(8,128)(2,1)S(1)}, bf16[32,2048]{1,0:T(8,128)(2,1)S(1)}, bf16[32,2048]{1,0:T(8,128)(2,1)S(1)}) custom-call(bf16[32,128,128]{2,1,0:T(8,128)(2,1)S(1)} %shard_map.75.refs_0_, bf16[32,2176]{1,0:T(8,128)(2,1)S(1)} %get-tuple-element.37.refs_2_.refs_1_.refs_5_, ...), custom_call_target="tpu_custom_call" | custom-call | tf_op jit(solution)/shard_map/pallas_call | solution.py:149
  22.8 1.3 %collective-permute-done.6.refs_1_ = bf16[32,2048]{1,0:T(8,128)(2,1)S(1)} collective-permute-done((bf16[32,2048]{1,0:T(8,128)(2,1)S(1)}, bf16[32,2048]{1,0:T(8,128)(2,1)S(1)}, u32[]{:S(2)}, u32[]{:S(2)}) %collective-permute-start.6) | collective-permute-done | bytes 131104 | tf_op jit(solution)/shard_map/ppermute | solution.py:124
  24.1 6.6 %collective-permute-done.7.refs_2_ = bf16[32,2048]{1,0:T(8,128)(2,1)S(1)} collective-permute-done((bf16[32,2048]{1,0:T(8,128)(2,1)S(1)}, bf16[32,2048]{1,0:T(8,128)(2,1)S(1)}, u32[]{:S(2)}, u32[]{:S(2)}) %collective-permute-start.7) | collective-permute-done | bytes 131104 | tf_op jit(solution)/shard_map/ppermute | solution.py:124
  30.8 1.6 %collective-permute-start.10 = (bf16[32,2048]{1,0:T(8,128)(2,1)S(1)}, bf16[32,2048]{1,0:T(8,128)(2,1)S(1)}, u32[]{:S(2)}, u32[]{:S(2)}) collective-permute-start(bf16[32,2048]{1,0:T(8,128)(2,1)S(1)} %shard_map.78.refs_1_), channel_id=1, source_target_pairs={{0,2},{1,3},{2,0},{3,1},{4,6},{5,7},{6,4},{7,5},{8,10},{9,11},{10,... | collective-permute-start | bytes 393224 | tf_op jit(solution)/shard_map/ppermute | solution.py:124
  32.4 2.5 %collective-permute-start.12 = (bf16[32,2048]{1,0:T(8,128)(2,1)S(1)}, bf16[32,2048]{1,0:T(8,128)(2,1)S(1)}, u32[]{:S(2)}, u32[]{:S(2)}) collective-permute-start(bf16[32,2048]{1,0:T(8,128)(2,1)S(1)} %get-tuple-element.57), channel_id=1, source_target_pairs={{0,12},{4,8},{8,4},{12,0},{1,13},{5,9},{9,5},{13,1},{2,14},{6,10},... | collective-permute-start | bytes 393224 | tf_op jit(solution)/shard_map/ppermute | solution.py:124
  35.8 3.1 %collective-permute-start.17 = (bf16[32,2048]{1,0:T(8,128)(2,1)S(1)}, bf16[32,2048]{1,0:T(8,128)(2,1)S(1)}, u32[]{:S(2)}, u32[]{:S(2)}) collective-permute-start(bf16[32,2048]{1,0:T(8,128)(2,1)S(1)} %get-tuple-element.64), channel_id=1, source_target_pairs={{0,4},{4,0},{8,12},{12,8},{1,5},{5,1},{9,13},{13,9},{2,6},{6,2},{1... | collective-permute-start | bytes 393224 | tf_op jit(solution)/shard_map/ppermute | solution.py:124
  38.9 1.7 %collective-permute-done.12.refs_5_.refs_1_ = bf16[32,2048]{1,0:T(8,128)(2,1)S(1)} collective-permute-done((bf16[32,2048]{1,0:T(8,128)(2,1)S(1)}, bf16[32,2048]{1,0:T(8,128)(2,1)S(1)}, u32[]{:S(2)}, u32[]{:S(2)}) %collective-permute-start.12) | collective-permute-done | bytes 131104 | tf_op jit(solution)/shard_map/ppermute | solution.py:124
  40.6 2.3 %shard_map.79 = (bf16[32,1650]{1,0:T(8,128)(2,1)S(1)}, bf16[32,1650]{1,0:T(8,128)(2,1)S(1)}, bf16[32,1650]{1,0:T(8,128)(2,1)S(1)}, bf16[32,1650]{1,0:T(8,128)(2,1)S(1)}) custom-call(bf16[1650,2048]{1,0:T(8,128)(2,1)S(1)} %bitcast.4, bf16[32,2048]{1,0:T(8,128)(2,1)S(1)} %shard_map.78.refs_1_, bf16[32,2048]{1,0:T(8,128)(2,1)S(1)} %collective-permute-done.9.refs_2_, ...), custom_call_target="tpu_custom_call" | custom-call | tf_op jit(solution)/shard_map/pallas_call | solution.py:149
  42.9 2.5 %collective-permute-start.13 = (bf16[32,1650]{1,0:T(8,128)(2,1)S(1)}, bf16[32,1650]{1,0:T(8,128)(2,1)S(1)}, u32[]{:S(2)}, u32[]{:S(2)}) collective-permute-start(bf16[32,1650]{1,0:T(8,128)(2,1)S(1)} %get-tuple-element.59), channel_id=1, source_target_pairs={{0,12},{4,8},{8,4},{12,0},{1,13},{5,9},{9,5},{13,1},{2,14},{6,10},... | collective-permute-start | bytes 316808 | tf_op jit(solution)/shard_map/ppermute | solution.py:124
  46.7 1.1 %collective-permute-start.19 = (bf16[32,2048]{1,0:T(8,128)(2,1)S(1)}, bf16[32,2048]{1,0:T(8,128)(2,1)S(1)}, u32[]{:S(2)}, u32[]{:S(2)}) collective-permute-start(bf16[32,2048]{1,0:T(8,128)(2,1)S(1)} %shard_map.80.refs_1_), channel_id=1, source_target_pairs={{0,2},{1,3},{2,0},{3,1},{4,6},{5,7},{6,4},{7,5},{8,10},{9,11},{10,... | collective-permute-start | bytes 393224 | tf_op jit(solution)/shard_map/ppermute | solution.py:124
  48.1 1.6 %collective-permute-start.14 = (bf16[32,1650]{1,0:T(8,128)(2,1)S(1)}, bf16[32,1650]{1,0:T(8,128)(2,1)S(1)}, u32[]{:S(2)}, u32[]{:S(2)}) collective-permute-start(bf16[32,1650]{1,0:T(8,128)(2,1)S(1)} %get-tuple-element.60), channel_id=1, source_target_pairs={{0,8},{4,12},{8,0},{12,4},{1,9},{5,13},{9,1},{13,5},{2,10},{6,14},... | collective-permute-start | bytes 316808 | tf_op jit(solution)/shard_map/ppermute | solution.py:124
  49.7 1.4 %collective-permute-start.15 = (bf16[32,1650]{1,0:T(8,128)(2,1)S(1)}, bf16[32,1650]{1,0:T(8,128)(2,1)S(1)}, u32[]{:S(2)}, u32[]{:S(2)}) collective-permute-start(bf16[32,1650]{1,0:T(8,128)(2,1)S(1)} %get-tuple-element.61), channel_id=1, source_target_pairs={{0,4},{4,0},{8,12},{12,8},{1,5},{5,1},{9,13},{13,9},{2,6},{6,2},{1... | collective-permute-start | bytes 316808 | tf_op jit(solution)/shard_map/ppermute | solution.py:124
  52.0 2.8 %collective-permute-done.19.refs_3_ = bf16[32,2048]{1,0:T(8,128)(2,1)S(1)} collective-permute-done((bf16[32,2048]{1,0:T(8,128)(2,1)S(1)}, bf16[32,2048]{1,0:T(8,128)(2,1)S(1)}, u32[]{:S(2)}, u32[]{:S(2)}) %collective-permute-start.19) | collective-permute-done | bytes 131104 | tf_op jit(solution)/shard_map/ppermute | solution.py:124
  54.9 2.3 %shard_map.81 = (bf16[32,1650]{1,0:T(8,128)(2,1)S(1)}, bf16[32,1650]{1,0:T(8,128)(2,1)S(1)}, bf16[32,1650]{1,0:T(8,128)(2,1)S(1)}, bf16[32,1650]{1,0:T(8,128)(2,1)S(1)}) custom-call(bf16[1650,2048]{1,0:T(8,128)(2,1)S(1)} %bitcast.5, bf16[32,2048]{1,0:T(8,128)(2,1)S(1)} %shard_map.80.refs_1_, bf16[32,2048]{1,0:T(8,128)(2,1)S(1)} %collective-permute-done.18.refs_2_, ...), custom_call_target="tpu_custom_call" | custom-call | tf_op jit(solution)/shard_map/pallas_call | solution.py:149
  57.2 2.2 %collective-permute-start.21 = (bf16[32,1650]{1,0:T(8,128)(2,1)S(1)}, bf16[32,1650]{1,0:T(8,128)(2,1)S(1)}, u32[]{:S(2)}, u32[]{:S(2)}) collective-permute-start(bf16[32,1650]{1,0:T(8,128)(2,1)S(1)} %get-tuple-element.66), channel_id=1, source_target_pairs={{0,12},{4,8},{8,4},{12,0},{1,13},{5,9},{9,5},{13,1},{2,14},{6,10},... | collective-permute-start | bytes 316808 | tf_op jit(solution)/shard_map/ppermute | solution.py:124
  59.3 2.3 %collective-permute-start.23 = (bf16[32,1650]{1,0:T(8,128)(2,1)S(1)}, bf16[32,1650]{1,0:T(8,128)(2,1)S(1)}, u32[]{:S(2)}, u32[]{:S(2)}) collective-permute-start(bf16[32,1650]{1,0:T(8,128)(2,1)S(1)} %get-tuple-element.68), channel_id=1, source_target_pairs={{0,4},{4,0},{8,12},{12,8},{1,5},{5,1},{9,13},{13,9},{2,6},{6,2},{1... | collective-permute-start | bytes 316808 | tf_op jit(solution)/shard_map/ppermute | solution.py:124
  61.7 3.3 %collective-permute-done.21 = bf16[32,1650]{1,0:T(8,128)(2,1)S(1)} collective-permute-done((bf16[32,1650]{1,0:T(8,128)(2,1)S(1)}, bf16[32,1650]{1,0:T(8,128)(2,1)S(1)}, u32[]{:S(2)}, u32[]{:S(2)}) %collective-permute-start.21) | collective-permute-done | bytes 105632 | tf_op jit(solution)/shard_map/ppermute | solution.py:124
  65.0 3.7 %collective-permute-done.22 = bf16[32,1650]{1,0:T(8,128)(2,1)S(1)} collective-permute-done((bf16[32,1650]{1,0:T(8,128)(2,1)S(1)}, bf16[32,1650]{1,0:T(8,128)(2,1)S(1)}, u32[]{:S(2)}, u32[]{:S(2)}) %collective-permute-start.22) | collective-permute-done | bytes 105632 | tf_op jit(solution)/shard_map/ppermute | solution.py:124
  (43 shorter events, 9.9 us)
Async XLA Ops:
  2.7 6.9 %collective-permute-start = (bf16[32,2176]{1,0:T(8,128)(2,1)S(1)}, bf16[32,2176]{1,0:T(8,128)(2,1)S(1)}, u32[]{:S(2)}, u32[]{:S(2)}) collective-permute-start(bf16[32,2176]{1,0:T(8,128)(2,1)S(1)} %get-tuple-element.39), channel_id=1, source_target_pairs={{0,3},{1,2},{2,1},{3,0},{4,7},{5,6},{6,5},{7,4},{8,11},{9,10},{10,... | collective-permute-start | bytes 417800 | tf_op jit(solution)/shard_map/ppermute | solution.py:124
  5.1 8.1 %collective-permute-start.1 = (bf16[32,2176]{1,0:T(8,128)(2,1)S(1)}, bf16[32,2176]{1,0:T(8,128)(2,1)S(1)}, u32[]{:S(2)}, u32[]{:S(2)}) collective-permute-start(bf16[32,2176]{1,0:T(8,128)(2,1)S(1)} %get-tuple-element.40), channel_id=1, source_target_pairs={{0,2},{1,3},{2,0},{3,1},{4,6},{5,7},{6,4},{7,5},{8,10},{9,11},{10,... | collective-permute-start | bytes 417800 | tf_op jit(solution)/shard_map/ppermute | solution.py:124
  5.8 7.4 %collective-permute-start.2 = (bf16[32,2176]{1,0:T(8,128)(2,1)S(1)}, bf16[32,2176]{1,0:T(8,128)(2,1)S(1)}, u32[]{:S(2)}, u32[]{:S(2)}) collective-permute-start(bf16[32,2176]{1,0:T(8,128)(2,1)S(1)} %get-tuple-element.41), channel_id=1, source_target_pairs={{0,1},{1,0},{2,3},{3,2},{4,5},{5,4},{6,7},{7,6},{8,9},{9,8},{10,11... | collective-permute-start | bytes 417800 | tf_op jit(solution)/shard_map/ppermute | solution.py:124
  6.3 13.2 %collective-permute-start.3 = (bf16[32,2048]{1,0:T(8,128)(2,1)S(1)}, bf16[32,2048]{1,0:T(8,128)(2,1)S(1)}, u32[]{:S(2)}, u32[]{:S(2)}) collective-permute-start(bf16[32,2048]{1,0:T(8,128)(2,1)S(1)} %get-tuple-element.42), channel_id=1, source_target_pairs={{0,3},{1,2},{2,1},{3,0},{4,7},{5,6},{6,5},{7,4},{8,11},{9,10},{10,... | collective-permute-start | bytes 393224 | tf_op jit(solution)/shard_map/ppermute | solution.py:124
  7.8 12.4 %collective-permute-start.4 = (bf16[32,2048]{1,0:T(8,128)(2,1)S(1)}, bf16[32,2048]{1,0:T(8,128)(2,1)S(1)}, u32[]{:S(2)}, u32[]{:S(2)}) collective-permute-start(bf16[32,2048]{1,0:T(8,128)(2,1)S(1)} %get-tuple-element.43), channel_id=1, source_target_pairs={{0,2},{1,3},{2,0},{3,1},{4,6},{5,7},{6,4},{7,5},{8,10},{9,11},{10,... | collective-permute-start | bytes 393224 | tf_op jit(solution)/shard_map/ppermute | solution.py:124
  9.6 10.6 %collective-permute-start.5 = (bf16[32,2048]{1,0:T(8,128)(2,1)S(1)}, bf16[32,2048]{1,0:T(8,128)(2,1)S(1)}, u32[]{:S(2)}, u32[]{:S(2)}) collective-permute-start(bf16[32,2048]{1,0:T(8,128)(2,1)S(1)} %get-tuple-element.44), channel_id=1, source_target_pairs={{0,1},{1,0},{2,3},{3,2},{4,5},{5,4},{6,7},{7,6},{8,9},{9,8},{10,11... | collective-permute-start | bytes 393224 | tf_op jit(solution)/shard_map/ppermute | solution.py:124
  15.8 8.3 %collective-permute-start.6 = (bf16[32,2048]{1,0:T(8,128)(2,1)S(1)}, bf16[32,2048]{1,0:T(8,128)(2,1)S(1)}, u32[]{:S(2)}, u32[]{:S(2)}) collective-permute-start(bf16[32,2048]{1,0:T(8,128)(2,1)S(1)} %get-tuple-element.50), channel_id=1, source_target_pairs={{0,12},{4,8},{8,4},{12,0},{1,13},{5,9},{9,5},{13,1},{2,14},{6,10},... | collective-permute-start | bytes 393224 | tf_op jit(solution)/shard_map/ppermute | solution.py:124
  19.4 11.2 %collective-permute-start.7 = (bf16[32,2048]{1,0:T(8,128)(2,1)S(1)}, bf16[32,2048]{1,0:T(8,128)(2,1)S(1)}, u32[]{:S(2)}, u32[]{:S(2)}) collective-permute-start(bf16[32,2048]{1,0:T(8,128)(2,1)S(1)} %get-tuple-element.51), channel_id=1, source_target_pairs={{0,8},{4,12},{8,0},{12,4},{1,9},{5,13},{9,1},{13,5},{2,10},{6,14},... | collective-permute-start | bytes 393224 | tf_op jit(solution)/shard_map/ppermute | solution.py:124
  19.5 11.2 %collective-permute-start.8 = (bf16[32,2048]{1,0:T(8,128)(2,1)S(1)}, bf16[32,2048]{1,0:T(8,128)(2,1)S(1)}, u32[]{:S(2)}, u32[]{:S(2)}) collective-permute-start(bf16[32,2048]{1,0:T(8,128)(2,1)S(1)} %get-tuple-element.52), channel_id=1, source_target_pairs={{0,4},{4,0},{8,12},{12,8},{1,5},{5,1},{9,13},{13,9},{2,6},{6,2},{1... | collective-permute-start | bytes 393224 | tf_op jit(solution)/shard_map/ppermute | solution.py:124
  30.8 5.0 %collective-permute-start.10 = (bf16[32,2048]{1,0:T(8,128)(2,1)S(1)}, bf16[32,2048]{1,0:T(8,128)(2,1)S(1)}, u32[]{:S(2)}, u32[]{:S(2)}) collective-permute-start(bf16[32,2048]{1,0:T(8,128)(2,1)S(1)} %shard_map.78.refs_1_), channel_id=1, source_target_pairs={{0,2},{1,3},{2,0},{3,1},{4,6},{5,7},{6,4},{7,5},{8,10},{9,11},{10,... | collective-permute-start | bytes 393224 | tf_op jit(solution)/shard_map/ppermute | solution.py:124
  32.4 6.5 %collective-permute-start.9 = (bf16[32,2048]{1,0:T(8,128)(2,1)S(1)}, bf16[32,2048]{1,0:T(8,128)(2,1)S(1)}, u32[]{:S(2)}, u32[]{:S(2)}) collective-permute-start(bf16[32,2048]{1,0:T(8,128)(2,1)S(1)} %shard_map.78.refs_1_), channel_id=1, source_target_pairs={{0,1},{1,0},{2,3},{3,2},{4,5},{5,4},{6,7},{7,6},{8,9},{9,8},{10,11... | collective-permute-start | bytes 393224 | tf_op jit(solution)/shard_map/ppermute | solution.py:124
  32.4 8.2 %collective-permute-start.12 = (bf16[32,2048]{1,0:T(8,128)(2,1)S(1)}, bf16[32,2048]{1,0:T(8,128)(2,1)S(1)}, u32[]{:S(2)}, u32[]{:S(2)}) collective-permute-start(bf16[32,2048]{1,0:T(8,128)(2,1)S(1)} %get-tuple-element.57), channel_id=1, source_target_pairs={{0,12},{4,8},{8,4},{12,0},{1,13},{5,9},{9,5},{13,1},{2,14},{6,10},... | collective-permute-start | bytes 393224 | tf_op jit(solution)/shard_map/ppermute | solution.py:124
  35.8 4.8 %collective-permute-start.11 = (bf16[32,2048]{1,0:T(8,128)(2,1)S(1)}, bf16[32,2048]{1,0:T(8,128)(2,1)S(1)}, u32[]{:S(2)}, u32[]{:S(2)}) collective-permute-start(bf16[32,2048]{1,0:T(8,128)(2,1)S(1)} %collective-permute-done.10.refs_3_), channel_id=1, source_target_pairs={{0,1},{1,0},{2,3},{3,2},{4,5},{5,4},{6,7},{7,6},{8,9},{9,8},{10,11... | collective-permute-start | bytes 393224 | tf_op jit(solution)/shard_map/ppermute | solution.py:124
  35.8 10.3 %collective-permute-start.16 = (bf16[32,2048]{1,0:T(8,128)(2,1)S(1)}, bf16[32,2048]{1,0:T(8,128)(2,1)S(1)}, u32[]{:S(2)}, u32[]{:S(2)}) collective-permute-start(bf16[32,2048]{1,0:T(8,128)(2,1)S(1)} %get-tuple-element.63), channel_id=1, source_target_pairs={{0,8},{4,12},{8,0},{12,4},{1,9},{5,13},{9,1},{13,5},{2,10},{6,14},... | collective-permute-start | bytes 393224 | tf_op jit(solution)/shard_map/ppermute | solution.py:124
  35.8 10.3 %collective-permute-start.17 = (bf16[32,2048]{1,0:T(8,128)(2,1)S(1)}, bf16[32,2048]{1,0:T(8,128)(2,1)S(1)}, u32[]{:S(2)}, u32[]{:S(2)}) collective-permute-start(bf16[32,2048]{1,0:T(8,128)(2,1)S(1)} %get-tuple-element.64), channel_id=1, source_target_pairs={{0,4},{4,0},{8,12},{12,8},{1,5},{5,1},{9,13},{13,9},{2,6},{6,2},{1... | collective-permute-start | bytes 393224 | tf_op jit(solution)/shard_map/ppermute | solution.py:124
  42.9 6.8 %collective-permute-start.13 = (bf16[32,1650]{1,0:T(8,128)(2,1)S(1)}, bf16[32,1650]{1,0:T(8,128)(2,1)S(1)}, u32[]{:S(2)}, u32[]{:S(2)}) collective-permute-start(bf16[32,1650]{1,0:T(8,128)(2,1)S(1)} %get-tuple-element.59), channel_id=1, source_target_pairs={{0,12},{4,8},{8,4},{12,0},{1,13},{5,9},{9,5},{13,1},{2,14},{6,10},... | collective-permute-start | bytes 316808 | tf_op jit(solution)/shard_map/ppermute | solution.py:124
  46.2 5.8 %collective-permute-start.20 = (bf16[32,2048]{1,0:T(8,128)(2,1)S(1)}, bf16[32,2048]{1,0:T(8,128)(2,1)S(1)}, u32[]{:S(2)}, u32[]{:S(2)}) collective-permute-start(bf16[32,2048]{1,0:T(8,128)(2,1)S(1)} %shard_map.80.refs_1_), channel_id=1, source_target_pairs={{0,3},{1,2},{2,1},{3,0},{4,7},{5,6},{6,5},{7,4},{8,11},{9,10},{10,... | collective-permute-start | bytes 393224 | tf_op jit(solution)/shard_map/ppermute | solution.py:124
  46.7 8.2 %collective-permute-start.19 = (bf16[32,2048]{1,0:T(8,128)(2,1)S(1)}, bf16[32,2048]{1,0:T(8,128)(2,1)S(1)}, u32[]{:S(2)}, u32[]{:S(2)}) collective-permute-start(bf16[32,2048]{1,0:T(8,128)(2,1)S(1)} %shard_map.80.refs_1_), channel_id=1, source_target_pairs={{0,2},{1,3},{2,0},{3,1},{4,6},{5,7},{6,4},{7,5},{8,10},{9,11},{10,... | collective-permute-start | bytes 393224 | tf_op jit(solution)/shard_map/ppermute | solution.py:124
  47.8 7.1 %collective-permute-start.18 = (bf16[32,2048]{1,0:T(8,128)(2,1)S(1)}, bf16[32,2048]{1,0:T(8,128)(2,1)S(1)}, u32[]{:S(2)}, u32[]{:S(2)}) collective-permute-start(bf16[32,2048]{1,0:T(8,128)(2,1)S(1)} %shard_map.80.refs_1_), channel_id=1, source_target_pairs={{0,1},{1,0},{2,3},{3,2},{4,5},{5,4},{6,7},{7,6},{8,9},{9,8},{10,11... | collective-permute-start | bytes 393224 | tf_op jit(solution)/shard_map/ppermute | solution.py:124
  48.1 13.5 %collective-permute-start.14 = (bf16[32,1650]{1,0:T(8,128)(2,1)S(1)}, bf16[32,1650]{1,0:T(8,128)(2,1)S(1)}, u32[]{:S(2)}, u32[]{:S(2)}) collective-permute-start(bf16[32,1650]{1,0:T(8,128)(2,1)S(1)} %get-tuple-element.60), channel_id=1, source_target_pairs={{0,8},{4,12},{8,0},{12,4},{1,9},{5,13},{9,1},{13,5},{2,10},{6,14},... | collective-permute-start | bytes 316808 | tf_op jit(solution)/shard_map/ppermute | solution.py:124
  49.7 11.9 %collective-permute-start.15 = (bf16[32,1650]{1,0:T(8,128)(2,1)S(1)}, bf16[32,1650]{1,0:T(8,128)(2,1)S(1)}, u32[]{:S(2)}, u32[]{:S(2)}) collective-permute-start(bf16[32,1650]{1,0:T(8,128)(2,1)S(1)} %get-tuple-element.61), channel_id=1, source_target_pairs={{0,4},{4,0},{8,12},{12,8},{1,5},{5,1},{9,13},{13,9},{2,6},{6,2},{1... | collective-permute-start | bytes 316808 | tf_op jit(solution)/shard_map/ppermute | solution.py:124
  57.2 7.8 %collective-permute-start.21 = (bf16[32,1650]{1,0:T(8,128)(2,1)S(1)}, bf16[32,1650]{1,0:T(8,128)(2,1)S(1)}, u32[]{:S(2)}, u32[]{:S(2)}) collective-permute-start(bf16[32,1650]{1,0:T(8,128)(2,1)S(1)} %get-tuple-element.66), channel_id=1, source_target_pairs={{0,12},{4,8},{8,4},{12,0},{1,13},{5,9},{9,5},{13,1},{2,14},{6,10},... | collective-permute-start | bytes 316808 | tf_op jit(solution)/shard_map/ppermute | solution.py:124
  59.3 9.3 %collective-permute-start.22 = (bf16[32,1650]{1,0:T(8,128)(2,1)S(1)}, bf16[32,1650]{1,0:T(8,128)(2,1)S(1)}, u32[]{:S(2)}, u32[]{:S(2)}) collective-permute-start(bf16[32,1650]{1,0:T(8,128)(2,1)S(1)} %get-tuple-element.67), channel_id=1, source_target_pairs={{0,8},{4,12},{8,0},{12,4},{1,9},{5,13},{9,1},{13,5},{2,10},{6,14},... | collective-permute-start | bytes 316808 | tf_op jit(solution)/shard_map/ppermute | solution.py:124
  59.3 9.3 %collective-permute-start.23 = (bf16[32,1650]{1,0:T(8,128)(2,1)S(1)}, bf16[32,1650]{1,0:T(8,128)(2,1)S(1)}, u32[]{:S(2)}, u32[]{:S(2)}) collective-permute-start(bf16[32,1650]{1,0:T(8,128)(2,1)S(1)} %get-tuple-element.68), channel_id=1, source_target_pairs={{0,4},{4,0},{8,12},{12,8},{1,5},{5,1},{9,13},{13,9},{2,6},{6,2},{1... | collective-permute-start | bytes 316808 | tf_op jit(solution)/shard_map/ppermute | solution.py:124
  (3 other events, 42.9 us)

commit v7 on v6

--- a/solution.py
+++ b/solution.py
@@ -180,6 +180,8 @@
             after=before,
         )
         before = (turned[0],)
+        if h > 0:
+            turned, parts[-1][1] = lax.optimization_barrier((turned, parts[-1][1]))
         parts.append(exchange(turned, "layer"))
     (padded,) = call(
         pad_kernel,

time: 69.6 us -> 69.9 us (level)
  no operation moved by 1% of the time
where the time goes in v7:
time: 69.9 us; the launch traced here: 69.8 us
  starting transfers between devices  29.3 us (42%)
  waiting for transfers between devices  25.4 us (36%)
  Pallas kernels  10.9 us (16%)
  local copies, waits for them, and re-layouts  2.29 us (3%)
  other arithmetic  1.7 us (2%)
    ppermute x24, starting transfers between devices, trade(): lax.ppermute(chunk, axis, [(j, j ^ k) for j in range(lax.axis_size(axis))])  29.3 us
    ppermute x24, waiting for transfers between devices, trade(): lax.ppermute(chunk, axis, [(j, j ^ k) for j in range(lax.axis_size(axis))])  25.4 us
    pallas_call x9, Pallas kernels, call(): pl.pallas_call(body, out_shape=[jax.ShapeDtypeStruct(shape, BF16) for sha...  10.9 us
    unnamed x6, local copies, waits for them, and re-layouts  2.29 us
  transfers between devices with their start and end apart: 24, of which 10 were waited for; matrix products, arithmetic and copies ran while one was open for 0% of the time, Pallas kernels for 15%

profile of v7, /device:TPU:0, one launch (start us, length us, event | category | flops | bytes accessed | tf_op | source)
XLA Modules:
  0.0 69.8 jit_solution(14215310546176485308)
XLA Ops:
  0.9 1.3 %copy-done.1 = bf16[1,2048,256]{2,1,0:T(8,128)(2,1)S(1)} copy-done((bf16[1,2048,256]{2,1,0:T(8,128)(2,1)S(1)}, bf16[1,2048,256]{2,1,0:T(8,128)(2,1)}, u32[]{:S(2)}) %copy-start.1) | copy-done | bytes 1048600
  2.7 2.4 %collective-permute-start = (bf16[32,2176]{1,0:T(8,128)(2,1)S(1)}, bf16[32,2176]{1,0:T(8,128)(2,1)S(1)}, u32[]{:S(2)}, u32[]{:S(2)}) collective-permute-start(bf16[32,2176]{1,0:T(8,128)(2,1)S(1)} %get-tuple-element.47), channel_id=1, source_target_pairs={{0,3},{1,2},{2,1},{3,0},{4,7},{5,6},{6,5},{7,4},{8,11},{9,10},{10,... | collective-permute-start | bytes 417800 | tf_op jit(solution)/shard_map/ppermute | solution.py:124
  6.3 2.9 %collective-permute-done.refs_2_.refs_6_ = bf16[32,2176]{1,0:T(8,128)(2,1)S(1)} collective-permute-done((bf16[32,2176]{1,0:T(8,128)(2,1)S(1)}, bf16[32,2176]{1,0:T(8,128)(2,1)S(1)}, u32[]{:S(2)}, u32[]{:S(2)}) %collective-permute-start) | collective-permute-done | bytes 139296 | tf_op jit(solution)/shard_map/ppermute | solution.py:124
  9.2 2.2 %collective-permute-start.3 = (bf16[32,2048]{1,0:T(8,128)(2,1)S(1)}, bf16[32,2048]{1,0:T(8,128)(2,1)S(1)}, u32[]{:S(2)}, u32[]{:S(2)}) collective-permute-start(bf16[32,2048]{1,0:T(8,128)(2,1)S(1)} %get-tuple-element.52), channel_id=1, source_target_pairs={{0,3},{1,2},{2,1},{3,0},{4,7},{5,6},{6,5},{7,4},{8,11},{9,10},{10,... | collective-permute-start | bytes 393224 | tf_op jit(solution)/shard_map/ppermute | solution.py:124
  13.1 2.6 %shard_map.76 = (bf16[32,2048]{1,0:T(8,128)(2,1)S(1)}, bf16[32,2048]{1,0:T(8,128)(2,1)S(1)}, bf16[32,2048]{1,0:T(8,128)(2,1)S(1)}, bf16[32,2048]{1,0:T(8,128)(2,1)S(1)}) custom-call(bf16[32,128,128]{2,1,0:T(8,128)(2,1)S(1)} %shard_map.75.refs_0_, bf16[32,2176]{1,0:T(8,128)(2,1)S(1)} %get-tuple-element.42.refs_2_.refs_1_.refs_5_, ...), custom_call_target="tpu_custom_call" | custom-call | tf_op jit(solution)/shard_map/pallas_call | solution.py:149
  15.7 3.9 %collective-permute-start.6 = (bf16[32,2048]{1,0:T(8,128)(2,1)S(1)}, bf16[32,2048]{1,0:T(8,128)(2,1)S(1)}, u32[]{:S(2)}, u32[]{:S(2)}) collective-permute-start(bf16[32,2048]{1,0:T(8,128)(2,1)S(1)} %get-tuple-element.60), channel_id=1, source_target_pairs={{0,12},{4,8},{8,4},{12,0},{1,13},{5,9},{9,5},{13,1},{2,14},{6,10},... | collective-permute-start | bytes 393224 | tf_op jit(solution)/shard_map/ppermute | solution.py:124
  20.2 2.5 %shard_map.77 = (bf16[32,2048]{1,0:T(8,128)(2,1)S(1)}, bf16[32,2048]{1,0:T(8,128)(2,1)S(1)}, bf16[32,2048]{1,0:T(8,128)(2,1)S(1)}, bf16[32,2048]{1,0:T(8,128)(2,1)S(1)}) custom-call(bf16[32,128,128]{2,1,0:T(8,128)(2,1)S(1)} %shard_map.75.refs_0_, bf16[32,2176]{1,0:T(8,128)(2,1)S(1)} %get-tuple-element.42.refs_2_.refs_1_.refs_5_, ...), custom_call_target="tpu_custom_call" | custom-call | tf_op jit(solution)/shard_map/pallas_call | solution.py:149
  22.7 1.2 %collective-permute-done.6.refs_1_ = bf16[32,2048]{1,0:T(8,128)(2,1)S(1)} collective-permute-done((bf16[32,2048]{1,0:T(8,128)(2,1)S(1)}, bf16[32,2048]{1,0:T(8,128)(2,1)S(1)}, u32[]{:S(2)}, u32[]{:S(2)}) %collective-permute-start.6) | collective-permute-done | bytes 131104 | tf_op jit(solution)/shard_map/ppermute | solution.py:124
  23.9 7.2 %collective-permute-done.7.refs_2_ = bf16[32,2048]{1,0:T(8,128)(2,1)S(1)} collective-permute-done((bf16[32,2048]{1,0:T(8,128)(2,1)S(1)}, bf16[32,2048]{1,0:T(8,128)(2,1)S(1)}, u32[]{:S(2)}, u32[]{:S(2)}) %collective-permute-start.7) | collective-permute-done | bytes 131104 | tf_op jit(solution)/shard_map/ppermute | solution.py:124
  31.2 1.6 %collective-permute-start.10 = (bf16[32,2048]{1,0:T(8,128)(2,1)S(1)}, bf16[32,2048]{1,0:T(8,128)(2,1)S(1)}, u32[]{:S(2)}, u32[]{:S(2)}) collective-permute-start(bf16[32,2048]{1,0:T(8,128)(2,1)S(1)} %shard_map.78.refs_1_), channel_id=1, source_target_pairs={{0,2},{1,3},{2,0},{3,1},{4,6},{5,7},{6,4},{7,5},{8,10},{9,11},{10,... | collective-permute-start | bytes 393224 | tf_op jit(solution)/shard_map/ppermute | solution.py:124
  32.8 2.5 %collective-permute-start.12 = (bf16[32,2048]{1,0:T(8,128)(2,1)S(1)}, bf16[32,2048]{1,0:T(8,128)(2,1)S(1)}, u32[]{:S(2)}, u32[]{:S(2)}) collective-permute-start(bf16[32,2048]{1,0:T(8,128)(2,1)S(1)} %get-tuple-element.67), channel_id=1, source_target_pairs={{0,12},{4,8},{8,4},{12,0},{1,13},{5,9},{9,5},{13,1},{2,14},{6,10},... | collective-permute-start | bytes 393224 | tf_op jit(solution)/shard_map/ppermute | solution.py:124
  36.2 3.0 %collective-permute-start.17 = (bf16[32,2048]{1,0:T(8,128)(2,1)S(1)}, bf16[32,2048]{1,0:T(8,128)(2,1)S(1)}, u32[]{:S(2)}, u32[]{:S(2)}) collective-permute-start(bf16[32,2048]{1,0:T(8,128)(2,1)S(1)} %get-tuple-element.74), channel_id=1, source_target_pairs={{0,4},{4,0},{8,12},{12,8},{1,5},{5,1},{9,13},{13,9},{2,6},{6,2},{1... | collective-permute-start | bytes 393224 | tf_op jit(solution)/shard_map/ppermute | solution.py:124
  39.2 1.7 %collective-permute-done.12.refs_5_.refs_1_ = bf16[32,2048]{1,0:T(8,128)(2,1)S(1)} collective-permute-done((bf16[32,2048]{1,0:T(8,128)(2,1)S(1)}, bf16[32,2048]{1,0:T(8,128)(2,1)S(1)}, u32[]{:S(2)}, u32[]{:S(2)}) %collective-permute-start.12) | collective-permute-done | bytes 131104 | tf_op jit(solution)/shard_map/ppermute | solution.py:124
  41.0 2.3 %shard_map.79 = (bf16[32,1650]{1,0:T(8,128)(2,1)S(1)}, bf16[32,1650]{1,0:T(8,128)(2,1)S(1)}, bf16[32,1650]{1,0:T(8,128)(2,1)S(1)}, bf16[32,1650]{1,0:T(8,128)(2,1)S(1)}) custom-call(bf16[1650,2048]{1,0:T(8,128)(2,1)S(1)} %bitcast.4, bf16[32,2048]{1,0:T(8,128)(2,1)S(1)} %shard_map.78.refs_1_, bf16[32,2048]{1,0:T(8,128)(2,1)S(1)} %collective-permute-done.9.refs_2_, ...), custom_call_target="tpu_custom_call" | custom-call | tf_op jit(solution)/shard_map/pallas_call | solution.py:149
  43.2 2.5 %collective-permute-start.13 = (bf16[32,1650]{1,0:T(8,128)(2,1)S(1)}, bf16[32,1650]{1,0:T(8,128)(2,1)S(1)}, u32[]{:S(2)}, u32[]{:S(2)}) collective-permute-start(bf16[32,1650]{1,0:T(8,128)(2,1)S(1)} %get-tuple-element.69), channel_id=1, source_target_pairs={{0,12},{4,8},{8,4},{12,0},{1,13},{5,9},{9,5},{13,1},{2,14},{6,10},... | collective-permute-start | bytes 316808 | tf_op jit(solution)/shard_map/ppermute | solution.py:124
  47.0 1.1 %collective-permute-start.19 = (bf16[32,2048]{1,0:T(8,128)(2,1)S(1)}, bf16[32,2048]{1,0:T(8,128)(2,1)S(1)}, u32[]{:S(2)}, u32[]{:S(2)}) collective-permute-start(bf16[32,2048]{1,0:T(8,128)(2,1)S(1)} %shard_map.80.refs_1_), channel_id=1, source_target_pairs={{0,2},{1,3},{2,0},{3,1},{4,6},{5,7},{6,4},{7,5},{8,10},{9,11},{10,... | collective-permute-start | bytes 393224 | tf_op jit(solution)/shard_map/ppermute | solution.py:124
  48.5 1.6 %collective-permute-start.14 = (bf16[32,1650]{1,0:T(8,128)(2,1)S(1)}, bf16[32,1650]{1,0:T(8,128)(2,1)S(1)}, u32[]{:S(2)}, u32[]{:S(2)}) collective-permute-start(bf16[32,1650]{1,0:T(8,128)(2,1)S(1)} %get-tuple-element.70), channel_id=1, source_target_pairs={{0,8},{4,12},{8,0},{12,4},{1,9},{5,13},{9,1},{13,5},{2,10},{6,14},... | collective-permute-start | bytes 316808 | tf_op jit(solution)/shard_map/ppermute | solution.py:124
  50.1 1.4 %collective-permute-start.15 = (bf16[32,1650]{1,0:T(8,128)(2,1)S(1)}, bf16[32,1650]{1,0:T(8,128)(2,1)S(1)}, u32[]{:S(2)}, u32[]{:S(2)}) collective-permute-start(bf16[32,1650]{1,0:T(8,128)(2,1)S(1)} %get-tuple-element.71), channel_id=1, source_target_pairs={{0,4},{4,0},{8,12},{12,8},{1,5},{5,1},{9,13},{13,9},{2,6},{6,2},{1... | collective-permute-start | bytes 316808 | tf_op jit(solution)/shard_map/ppermute | solution.py:124
  52.5 2.8 %collective-permute-done.19.refs_3_ = bf16[32,2048]{1,0:T(8,128)(2,1)S(1)} collective-permute-done((bf16[32,2048]{1,0:T(8,128)(2,1)S(1)}, bf16[32,2048]{1,0:T(8,128)(2,1)S(1)}, u32[]{:S(2)}, u32[]{:S(2)}) %collective-permute-start.19) | collective-permute-done | bytes 131104 | tf_op jit(solution)/shard_map/ppermute | solution.py:124
  55.3 2.3 %shard_map.81 = (bf16[32,1650]{1,0:T(8,128)(2,1)S(1)}, bf16[32,1650]{1,0:T(8,128)(2,1)S(1)}, bf16[32,1650]{1,0:T(8,128)(2,1)S(1)}, bf16[32,1650]{1,0:T(8,128)(2,1)S(1)}) custom-call(bf16[1650,2048]{1,0:T(8,128)(2,1)S(1)} %bitcast.5, bf16[32,2048]{1,0:T(8,128)(2,1)S(1)} %shard_map.80.refs_1_, bf16[32,2048]{1,0:T(8,128)(2,1)S(1)} %collective-permute-done.18.refs_2_, ...), custom_call_target="tpu_custom_call" | custom-call | tf_op jit(solution)/shard_map/pallas_call | solution.py:149
  57.6 2.1 %collective-permute-start.21 = (bf16[32,1650]{1,0:T(8,128)(2,1)S(1)}, bf16[32,1650]{1,0:T(8,128)(2,1)S(1)}, u32[]{:S(2)}, u32[]{:S(2)}) collective-permute-start(bf16[32,1650]{1,0:T(8,128)(2,1)S(1)} %get-tuple-element.76), channel_id=1, source_target_pairs={{0,12},{4,8},{8,4},{12,0},{1,13},{5,9},{9,5},{13,1},{2,14},{6,10},... | collective-permute-start | bytes 316808 | tf_op jit(solution)/shard_map/ppermute | solution.py:124
  59.7 2.3 %collective-permute-start.23 = (bf16[32,1650]{1,0:T(8,128)(2,1)S(1)}, bf16[32,1650]{1,0:T(8,128)(2,1)S(1)}, u32[]{:S(2)}, u32[]{:S(2)}) collective-permute-start(bf16[32,1650]{1,0:T(8,128)(2,1)S(1)} %get-tuple-element.78), channel_id=1, source_target_pairs={{0,4},{4,0},{8,12},{12,8},{1,5},{5,1},{9,13},{13,9},{2,6},{6,2},{1... | collective-permute-start | bytes 316808 | tf_op jit(solution)/shard_map/ppermute | solution.py:124
  62.1 3.3 %collective-permute-done.21 = bf16[32,1650]{1,0:T(8,128)(2,1)S(1)} collective-permute-done((bf16[32,1650]{1,0:T(8,128)(2,1)S(1)}, bf16[32,1650]{1,0:T(8,128)(2,1)S(1)}, u32[]{:S(2)}, u32[]{:S(2)}) %collective-permute-start.21) | collective-permute-done | bytes 105632 | tf_op jit(solution)/shard_map/ppermute | solution.py:124
  65.4 3.6 %collective-permute-done.22 = bf16[32,1650]{1,0:T(8,128)(2,1)S(1)} collective-permute-done((bf16[32,1650]{1,0:T(8,128)(2,1)S(1)}, bf16[32,1650]{1,0:T(8,128)(2,1)S(1)}, u32[]{:S(2)}, u32[]{:S(2)}) %collective-permute-start.22) | collective-permute-done | bytes 105632 | tf_op jit(solution)/shard_map/ppermute | solution.py:124
  (43 shorter events, 9.4 us)
Async XLA Ops:
  2.7 6.5 %collective-permute-start = (bf16[32,2176]{1,0:T(8,128)(2,1)S(1)}, bf16[32,2176]{1,0:T(8,128)(2,1)S(1)}, u32[]{:S(2)}, u32[]{:S(2)}) collective-permute-start(bf16[32,2176]{1,0:T(8,128)(2,1)S(1)} %get-tuple-element.47), channel_id=1, source_target_pairs={{0,3},{1,2},{2,1},{3,0},{4,7},{5,6},{6,5},{7,4},{8,11},{9,10},{10,... | collective-permute-start | bytes 417800 | tf_op jit(solution)/shard_map/ppermute | solution.py:124
  5.1 7.9 %collective-permute-start.1 = (bf16[32,2176]{1,0:T(8,128)(2,1)S(1)}, bf16[32,2176]{1,0:T(8,128)(2,1)S(1)}, u32[]{:S(2)}, u32[]{:S(2)}) collective-permute-start(bf16[32,2176]{1,0:T(8,128)(2,1)S(1)} %get-tuple-element.49), channel_id=1, source_target_pairs={{0,2},{1,3},{2,0},{3,1},{4,6},{5,7},{6,4},{7,5},{8,10},{9,11},{10,... | collective-permute-start | bytes 417800 | tf_op jit(solution)/shard_map/ppermute | solution.py:124
  5.8 7.3 %collective-permute-start.2 = (bf16[32,2176]{1,0:T(8,128)(2,1)S(1)}, bf16[32,2176]{1,0:T(8,128)(2,1)S(1)}, u32[]{:S(2)}, u32[]{:S(2)}) collective-permute-start(bf16[32,2176]{1,0:T(8,128)(2,1)S(1)} %get-tuple-element.50), channel_id=1, source_target_pairs={{0,1},{1,0},{2,3},{3,2},{4,5},{5,4},{6,7},{7,6},{8,9},{9,8},{10,11... | collective-permute-start | bytes 417800 | tf_op jit(solution)/shard_map/ppermute | solution.py:124
  9.2 10.3 %collective-permute-start.3 = (bf16[32,2048]{1,0:T(8,128)(2,1)S(1)}, bf16[32,2048]{1,0:T(8,128)(2,1)S(1)}, u32[]{:S(2)}, u32[]{:S(2)}) collective-permute-start(bf16[32,2048]{1,0:T(8,128)(2,1)S(1)} %get-tuple-element.52), channel_id=1, source_target_pairs={{0,3},{1,2},{2,1},{3,0},{4,7},{5,6},{6,5},{7,4},{8,11},{9,10},{10,... | collective-permute-start | bytes 393224 | tf_op jit(solution)/shard_map/ppermute | solution.py:124
  12.5 7.6 %collective-permute-start.4 = (bf16[32,2048]{1,0:T(8,128)(2,1)S(1)}, bf16[32,2048]{1,0:T(8,128)(2,1)S(1)}, u32[]{:S(2)}, u32[]{:S(2)}) collective-permute-start(bf16[32,2048]{1,0:T(8,128)(2,1)S(1)} %get-tuple-element.53), channel_id=1, source_target_pairs={{0,2},{1,3},{2,0},{3,1},{4,6},{5,7},{6,4},{7,5},{8,10},{9,11},{10,... | collective-permute-start | bytes 393224 | tf_op jit(solution)/shard_map/ppermute | solution.py:124
  12.9 7.3 %collective-permute-start.5 = (bf16[32,2048]{1,0:T(8,128)(2,1)S(1)}, bf16[32,2048]{1,0:T(8,128)(2,1)S(1)}, u32[]{:S(2)}, u32[]{:S(2)}) collective-permute-start(bf16[32,2048]{1,0:T(8,128)(2,1)S(1)} %get-tuple-element.54), channel_id=1, source_target_pairs={{0,1},{1,0},{2,3},{3,2},{4,5},{5,4},{6,7},{7,6},{8,9},{9,8},{10,11... | collective-permute-start | bytes 393224 | tf_op jit(solution)/shard_map/ppermute | solution.py:124
  15.7 8.2 %collective-permute-start.6 = (bf16[32,2048]{1,0:T(8,128)(2,1)S(1)}, bf16[32,2048]{1,0:T(8,128)(2,1)S(1)}, u32[]{:S(2)}, u32[]{:S(2)}) collective-permute-start(bf16[32,2048]{1,0:T(8,128)(2,1)S(1)} %get-tuple-element.60), channel_id=1, source_target_pairs={{0,12},{4,8},{8,4},{12,0},{1,13},{5,9},{9,5},{13,1},{2,14},{6,10},... | collective-permute-start | bytes 393224 | tf_op jit(solution)/shard_map/ppermute | solution.py:124
  19.5 11.6 %collective-permute-start.7 = (bf16[32,2048]{1,0:T(8,128)(2,1)S(1)}, bf16[32,2048]{1,0:T(8,128)(2,1)S(1)}, u32[]{:S(2)}, u32[]{:S(2)}) collective-permute-start(bf16[32,2048]{1,0:T(8,128)(2,1)S(1)} %get-tuple-element.61), channel_id=1, source_target_pairs={{0,8},{4,12},{8,0},{12,4},{1,9},{5,13},{9,1},{13,5},{2,10},{6,14},... | collective-permute-start | bytes 393224 | tf_op jit(solution)/shard_map/ppermute | solution.py:124
  19.5 11.6 %collective-permute-start.8 = (bf16[32,2048]{1,0:T(8,128)(2,1)S(1)}, bf16[32,2048]{1,0:T(8,128)(2,1)S(1)}, u32[]{:S(2)}, u32[]{:S(2)}) collective-permute-start(bf16[32,2048]{1,0:T(8,128)(2,1)S(1)} %get-tuple-element.62), channel_id=1, source_target_pairs={{0,4},{4,0},{8,12},{12,8},{1,5},{5,1},{9,13},{13,9},{2,6},{6,2},{1... | collective-permute-start | bytes 393224 | tf_op jit(solution)/shard_map/ppermute | solution.py:124
  31.2 5.0 %collective-permute-start.10 = (bf16[32,2048]{1,0:T(8,128)(2,1)S(1)}, bf16[32,2048]{1,0:T(8,128)(2,1)S(1)}, u32[]{:S(2)}, u32[]{:S(2)}) collective-permute-start(bf16[32,2048]{1,0:T(8,128)(2,1)S(1)} %shard_map.78.refs_1_), channel_id=1, source_target_pairs={{0,2},{1,3},{2,0},{3,1},{4,6},{5,7},{6,4},{7,5},{8,10},{9,11},{10,... | collective-permute-start | bytes 393224 | tf_op jit(solution)/shard_map/ppermute | solution.py:124
  32.8 6.5 %collective-permute-start.9 = (bf16[32,2048]{1,0:T(8,128)(2,1)S(1)}, bf16[32,2048]{1,0:T(8,128)(2,1)S(1)}, u32[]{:S(2)}, u32[]{:S(2)}) collective-permute-start(bf16[32,2048]{1,0:T(8,128)(2,1)S(1)} %shard_map.78.refs_1_), channel_id=1, source_target_pairs={{0,1},{1,0},{2,3},{3,2},{4,5},{5,4},{6,7},{7,6},{8,9},{9,8},{10,11... | collective-permute-start | bytes 393224 | tf_op jit(solution)/shard_map/ppermute | solution.py:124
  32.8 8.2 %collective-permute-start.12 = (bf16[32,2048]{1,0:T(8,128)(2,1)S(1)}, bf16[32,2048]{1,0:T(8,128)(2,1)S(1)}, u32[]{:S(2)}, u32[]{:S(2)}) collective-permute-start(bf16[32,2048]{1,0:T(8,128)(2,1)S(1)} %get-tuple-element.67), channel_id=1, source_target_pairs={{0,12},{4,8},{8,4},{12,0},{1,13},{5,9},{9,5},{13,1},{2,14},{6,10},... | collective-permute-start | bytes 393224 | tf_op jit(solution)/shard_map/ppermute | solution.py:124
  36.2 4.8 %collective-permute-start.11 = (bf16[32,2048]{1,0:T(8,128)(2,1)S(1)}, bf16[32,2048]{1,0:T(8,128)(2,1)S(1)}, u32[]{:S(2)}, u32[]{:S(2)}) collective-permute-start(bf16[32,2048]{1,0:T(8,128)(2,1)S(1)} %collective-permute-done.10.refs_3_), channel_id=1, source_target_pairs={{0,1},{1,0},{2,3},{3,2},{4,5},{5,4},{6,7},{7,6},{8,9},{9,8},{10,11... | collective-permute-start | bytes 393224 | tf_op jit(solution)/shard_map/ppermute | solution.py:124
  36.2 10.3 %collective-permute-start.16 = (bf16[32,2048]{1,0:T(8,128)(2,1)S(1)}, bf16[32,2048]{1,0:T(8,128)(2,1)S(1)}, u32[]{:S(2)}, u32[]{:S(2)}) collective-permute-start(bf16[32,2048]{1,0:T(8,128)(2,1)S(1)} %get-tuple-element.73), channel_id=1, source_target_pairs={{0,8},{4,12},{8,0},{12,4},{1,9},{5,13},{9,1},{13,5},{2,10},{6,14},... | collective-permute-start | bytes 393224 | tf_op jit(solution)/shard_map/ppermute | solution.py:124
  36.2 10.3 %collective-permute-start.17 = (bf16[32,2048]{1,0:T(8,128)(2,1)S(1)}, bf16[32,2048]{1,0:T(8,128)(2,1)S(1)}, u32[]{:S(2)}, u32[]{:S(2)}) collective-permute-start(bf16[32,2048]{1,0:T(8,128)(2,1)S(1)} %get-tuple-element.74), channel_id=1, source_target_pairs={{0,4},{4,0},{8,12},{12,8},{1,5},{5,1},{9,13},{13,9},{2,6},{6,2},{1... | collective-permute-start | bytes 393224 | tf_op jit(solution)/shard_map/ppermute | solution.py:124
  43.2 6.9 %collective-permute-start.13 = (bf16[32,1650]{1,0:T(8,128)(2,1)S(1)}, bf16[32,1650]{1,0:T(8,128)(2,1)S(1)}, u32[]{:S(2)}, u32[]{:S(2)}) collective-permute-start(bf16[32,1650]{1,0:T(8,128)(2,1)S(1)} %get-tuple-element.69), channel_id=1, source_target_pairs={{0,12},{4,8},{8,4},{12,0},{1,13},{5,9},{9,5},{13,1},{2,14},{6,10},... | collective-permute-start | bytes 316808 | tf_op jit(solution)/shard_map/ppermute | solution.py:124
  46.6 5.8 %collective-permute-start.20 = (bf16[32,2048]{1,0:T(8,128)(2,1)S(1)}, bf16[32,2048]{1,0:T(8,128)(2,1)S(1)}, u32[]{:S(2)}, u32[]{:S(2)}) collective-permute-start(bf16[32,2048]{1,0:T(8,128)(2,1)S(1)} %shard_map.80.refs_1_), channel_id=1, source_target_pairs={{0,3},{1,2},{2,1},{3,0},{4,7},{5,6},{6,5},{7,4},{8,11},{9,10},{10,... | collective-permute-start | bytes 393224 | tf_op jit(solution)/shard_map/ppermute | solution.py:124
  47.0 8.2 %collective-permute-start.19 = (bf16[32,2048]{1,0:T(8,128)(2,1)S(1)}, bf16[32,2048]{1,0:T(8,128)(2,1)S(1)}, u32[]{:S(2)}, u32[]{:S(2)}) collective-permute-start(bf16[32,2048]{1,0:T(8,128)(2,1)S(1)} %shard_map.80.refs_1_), channel_id=1, source_target_pairs={{0,2},{1,3},{2,0},{3,1},{4,6},{5,7},{6,4},{7,5},{8,10},{9,11},{10,... | collective-permute-start | bytes 393224 | tf_op jit(solution)/shard_map/ppermute | solution.py:124
  48.1 7.1 %collective-permute-start.18 = (bf16[32,2048]{1,0:T(8,128)(2,1)S(1)}, bf16[32,2048]{1,0:T(8,128)(2,1)S(1)}, u32[]{:S(2)}, u32[]{:S(2)}) collective-permute-start(bf16[32,2048]{1,0:T(8,128)(2,1)S(1)} %shard_map.80.refs_1_), channel_id=1, source_target_pairs={{0,1},{1,0},{2,3},{3,2},{4,5},{5,4},{6,7},{7,6},{8,9},{9,8},{10,11... | collective-permute-start | bytes 393224 | tf_op jit(solution)/shard_map/ppermute | solution.py:124
  48.5 13.5 %collective-permute-start.14 = (bf16[32,1650]{1,0:T(8,128)(2,1)S(1)}, bf16[32,1650]{1,0:T(8,128)(2,1)S(1)}, u32[]{:S(2)}, u32[]{:S(2)}) collective-permute-start(bf16[32,1650]{1,0:T(8,128)(2,1)S(1)} %get-tuple-element.70), channel_id=1, source_target_pairs={{0,8},{4,12},{8,0},{12,4},{1,9},{5,13},{9,1},{13,5},{2,10},{6,14},... | collective-permute-start | bytes 316808 | tf_op jit(solution)/shard_map/ppermute | solution.py:124
  50.1 11.9 %collective-permute-start.15 = (bf16[32,1650]{1,0:T(8,128)(2,1)S(1)}, bf16[32,1650]{1,0:T(8,128)(2,1)S(1)}, u32[]{:S(2)}, u32[]{:S(2)}) collective-permute-start(bf16[32,1650]{1,0:T(8,128)(2,1)S(1)} %get-tuple-element.71), channel_id=1, source_target_pairs={{0,4},{4,0},{8,12},{12,8},{1,5},{5,1},{9,13},{13,9},{2,6},{6,2},{1... | collective-permute-start | bytes 316808 | tf_op jit(solution)/shard_map/ppermute | solution.py:124
  57.6 7.8 %collective-permute-start.21 = (bf16[32,1650]{1,0:T(8,128)(2,1)S(1)}, bf16[32,1650]{1,0:T(8,128)(2,1)S(1)}, u32[]{:S(2)}, u32[]{:S(2)}) collective-permute-start(bf16[32,1650]{1,0:T(8,128)(2,1)S(1)} %get-tuple-element.76), channel_id=1, source_target_pairs={{0,12},{4,8},{8,4},{12,0},{1,13},{5,9},{9,5},{13,1},{2,14},{6,10},... | collective-permute-start | bytes 316808 | tf_op jit(solution)/shard_map/ppermute | solution.py:124
  59.7 9.3 %collective-permute-start.22 = (bf16[32,1650]{1,0:T(8,128)(2,1)S(1)}, bf16[32,1650]{1,0:T(8,128)(2,1)S(1)}, u32[]{:S(2)}, u32[]{:S(2)}) collective-permute-start(bf16[32,1650]{1,0:T(8,128)(2,1)S(1)} %get-tuple-element.77), channel_id=1, source_target_pairs={{0,8},{4,12},{8,0},{12,4},{1,9},{5,13},{9,1},{13,5},{2,10},{6,14},... | collective-permute-start | bytes 316808 | tf_op jit(solution)/shard_map/ppermute | solution.py:124
  59.7 9.3 %collective-permute-start.23 = (bf16[32,1650]{1,0:T(8,128)(2,1)S(1)}, bf16[32,1650]{1,0:T(8,128)(2,1)S(1)}, u32[]{:S(2)}, u32[]{:S(2)}) collective-permute-start(bf16[32,1650]{1,0:T(8,128)(2,1)S(1)} %get-tuple-element.78), channel_id=1, source_target_pairs={{0,4},{4,0},{8,12},{12,8},{1,5},{5,1},{9,13},{13,9},{2,6},{6,2},{1... | collective-permute-start | bytes 316808 | tf_op jit(solution)/shard_map/ppermute | solution.py:124
  (3 other events, 43.3 us)

commit v8 on v6

--- a/solution.py
+++ b/solution.py
@@ -88,18 +88,25 @@
             out[:, s * LANES : (s + 1) * LANES] = total[base + s].astype(BF16)
 
 
-def sum_kernel(*refs):
-    refs[-1][...] = sum(ref[...].astype(F32) for ref in refs[:-1]).astype(BF16)
-
-
-def fit_kernel(n_layer, n_row, fitting_ref, *refs):
-    pieces, outs = refs[:n_layer], refs[n_layer : n_layer + n_row]
+def sum_kernel(count, *refs):
+    found = sum(ref[...].astype(F32) for ref in refs[:count]).astype(BF16)
+    start = 0
+    for i, out in enumerate(refs[count:]):
+        rows = out.shape[0]
+        out[...] = found[start : start + rows]
+        start = 0 if i == 0 else start + rows
+
+
+def fit_kernel(places, n_row, fitting_ref, *refs):
+    pieces, outs = refs[: len(places)], refs[len(places) : len(places) + n_row]
     left, product = refs[-2], refs[-1]
-    aligned = n_layer == n_row
+    aligned = left.shape[0] == n_row
     me, row = lax.axis_index("layer"), lax.axis_index("row")
-    for j, piece in enumerate(pieces):
-        place = lax.bitwise_xor(me, j)
-        left[lax.bitwise_xor(place, row) if aligned else place] = piece[...]
+    for piece, spots in zip(pieces, places):
+        for k, of, to, count in spots:
+            place = lax.bitwise_xor(me, k)
+            place = lax.bitwise_xor(place, row) if aligned else place
+            left[place, to : to + count] = piece[of : of + count]
     columns = left.shape[0] * left.shape[1]
     found = lax.dot_general(
         left[...].reshape(columns, left.shape[2]),
@@ -130,10 +137,23 @@
 
 
 def gather(piece, axis, paired):
-    got = [piece]
-    for k in range(1, lax.axis_size(axis)):
+    got, n, rows = [piece], lax.axis_size(axis), piece.shape[0]
+    for k in range(1, n):
         got.append(trade(got[k - 1], axis, 1) if paired and k % 2 else trade(piece, axis, k))
-    return got
+    return got, [[(k, 0, 0, rows)] for k in range(n)]
+
+
+def gather_crossed(piece, first, second, axis, ahead):
+    rows, half = piece.shape[0], first.shape[0]
+    got = [piece, trade(piece, axis, 1)]
+    places = [[(0, 0, 0, rows)], [(1, 0, 0, rows)]]
+    for k in range(2, lax.axis_size(axis), 2):
+        upper, lower = trade(first, axis, k), trade(second, axis, k + 1)
+        upper, ahead = lax.optimization_barrier((upper, ahead))
+        got += [upper, lower, trade(jnp.concatenate([upper, lower], 0), axis, 1)]
+        places += [[(k, 0, 0, half)], [(k + 1, 0, half, half)]]
+        places.append([(k + 1, 0, 0, half), (k, half, half, half)])
+    return got, places
 
 
 def total_of(parts):
@@ -180,14 +200,17 @@
             after=before,
         )
         before = (turned[0],)
+        if h == 0:
+            (padded,) = call(
+                pad_kernel,
+                [(LANES // block_rows * weights, LANES, slice_rows)],
+                [],
+                jnp.swapaxes(table, 1, 2),
+                after=before,
+            )
+        else:
+            turned, parts[-1][1], padded = lax.optimization_barrier((turned, parts[-1][1], padded))
         parts.append(exchange(turned, "layer"))
-    (padded,) = call(
-        pad_kernel,
-        [(LANES // block_rows * weights, LANES, slice_rows)],
-        [],
-        jnp.swapaxes(table, 1, 2),
-        after=before,
-    )
 
     received, before = [], ()
     for h in range(halves):
@@ -211,19 +234,23 @@
         received.append(exchange(shares, "row"))
     results, ahead = [], tuple(received[-1][1:2])
     for h in range(halves):
-        (pupil,) = call(sum_kernel, [(each, points)], [], *received[h], after=before)
-        pieces = gather(pupil, "layer", h == 0)
+        shapes = [(each, points)] + [(each // 2, points)] * 2 * (h > 0)
+        pupil = call(functools.partial(sum_kernel, n_row), shapes, [], *received[h], after=before)
+        if h > 0:
+            pieces, places = gather_crossed(*pupil, "layer", ahead)
+        else:
+            pieces, places = gather(*pupil, "layer", True)
         partial = call(
-            functools.partial(fit_kernel, n_layer, n_row),
+            functools.partial(fit_kernel, places, n_row),
             [(chunk // halves, actuators)] * n_row,
             [pltpu.VMEM((n_layer, each, points), BF16), pltpu.VMEM((per_half, actuators), F32)],
             fitting.T,
             *pieces,
-            after=ahead,
+            after=ahead if h == 0 else (),
         )
         before = (partial[0],)
         results.append(exchange(partial, "row"))
-        ahead = tuple(results[-1][1:2])
+        ahead = results[-1][1]
     return jnp.concatenate([total_of(result) for result in results], 0)
 
 

time: 69.6 us -> 69.7 us (level)
  starting transfers between devices: 29.2 us -> 30.2 us
  waiting for transfers between devices: 25.2 us -> 24.4 us
    ppermute x24 -> x25, starting transfers between devices: 29.2 us -> 30.2 us  [trade(): lax.ppermute(chunk, axis, [(j, j ^ k) for j in range(lax.axis_size(axis))])]
    ppermute x24 -> x25, waiting for transfers between devices: 25.2 us -> 24.4 us  [trade(): lax.ppermute(chunk, axis, [(j, j ^ k) for j in range(lax.axis_size(axis))])]
  transfers between devices with their start and end apart: 24 -> 25, of which waited for: 10 -> 11; matrix products, arithmetic and copies ran while one was open for 0% -> 0% of each run, Pallas kernels for 15% -> 15%
where the time goes in v8:
time: 69.7 us; the launch traced here: 69.6 us
  starting transfers between devices  30.2 us (43%)
  waiting for transfers between devices  24.4 us (35%)
  Pallas kernels  10.9 us (16%)
  local copies, waits for them, and re-layouts  2.29 us (3%)
  other arithmetic  1.71 us (2%)
    ppermute x25, starting transfers between devices, trade(): lax.ppermute(chunk, axis, [(j, j ^ k) for j in range(lax.axis_size(axis))])  30.2 us
    ppermute x25, waiting for transfers between devices, trade(): lax.ppermute(chunk, axis, [(j, j ^ k) for j in range(lax.axis_size(axis))])  24.4 us
    pallas_call x9, Pallas kernels, call(): pl.pallas_call(body, out_shape=[jax.ShapeDtypeStruct(shape, BF16) for sha...  10.9 us
    unnamed x6, local copies, waits for them, and re-layouts  2.29 us
  transfers between devices with their start and end apart: 25, of which 11 were waited for; matrix products, arithmetic and copies ran while one was open for 0% of the time, Pallas kernels for 15%

profile of v8, /device:TPU:0, one launch (start us, length us, event | category | flops | bytes accessed | tf_op | source)
XLA Modules:
  0.0 69.6 jit_solution(7220217902661996389)
XLA Ops:
  0.9 1.3 %copy-done.1 = bf16[1,2048,256]{2,1,0:T(8,128)(2,1)S(1)} copy-done((bf16[1,2048,256]{2,1,0:T(8,128)(2,1)S(1)}, bf16[1,2048,256]{2,1,0:T(8,128)(2,1)}, u32[]{:S(2)}) %copy-start.1) | copy-done | bytes 1048600
  2.7 2.4 %collective-permute-start = (bf16[32,2176]{1,0:T(8,128)(2,1)S(1)}, bf16[32,2176]{1,0:T(8,128)(2,1)S(1)}, u32[]{:S(2)}, u32[]{:S(2)}) collective-permute-start(bf16[32,2176]{1,0:T(8,128)(2,1)S(1)} %get-tuple-element.52), channel_id=1, source_target_pairs={{0,3},{1,2},{2,1},{3,0},{4,7},{5,6},{6,5},{7,4},{8,11},{9,10},{10,... | collective-permute-start | bytes 417800 | tf_op jit(solution)/shard_map/ppermute | solution.py:131
  7.5 1.7 %collective-permute-done.refs_2_.refs_6_ = bf16[32,2176]{1,0:T(8,128)(2,1)S(1)} collective-permute-done((bf16[32,2176]{1,0:T(8,128)(2,1)S(1)}, bf16[32,2176]{1,0:T(8,128)(2,1)S(1)}, u32[]{:S(2)}, u32[]{:S(2)}) %collective-permute-start) | collective-permute-done | bytes 139296 | tf_op jit(solution)/shard_map/ppermute | solution.py:131
  9.2 2.2 %collective-permute-start.3 = (bf16[32,2048]{1,0:T(8,128)(2,1)S(1)}, bf16[32,2048]{1,0:T(8,128)(2,1)S(1)}, u32[]{:S(2)}, u32[]{:S(2)}) collective-permute-start(bf16[32,2048]{1,0:T(8,128)(2,1)S(1)} %get-tuple-element.58), channel_id=1, source_target_pairs={{0,3},{1,2},{2,1},{3,0},{4,7},{5,6},{6,5},{7,4},{8,11},{9,10},{10,... | collective-permute-start | bytes 393224 | tf_op jit(solution)/shard_map/ppermute | solution.py:131
  12.4 2.6 %shard_map.76 = (bf16[32,2048]{1,0:T(8,128)(2,1)S(1)}, bf16[32,2048]{1,0:T(8,128)(2,1)S(1)}, bf16[32,2048]{1,0:T(8,128)(2,1)S(1)}, bf16[32,2048]{1,0:T(8,128)(2,1)S(1)}) custom-call(bf16[32,128,128]{2,1,0:T(8,128)(2,1)S(1)} %shard_map.75.refs_0_, bf16[32,2176]{1,0:T(8,128)(2,1)S(1)} %get-tuple-element.47.refs_2_.refs_1_.refs_5_, ...), custom_call_target="tpu_custom_call" | custom-call | tf_op jit(solution)/shard_map/pallas_call | solution.py:169
  14.9 4.5 %collective-permute-start.6 = (bf16[32,2048]{1,0:T(8,128)(2,1)S(1)}, bf16[32,2048]{1,0:T(8,128)(2,1)S(1)}, u32[]{:S(2)}, u32[]{:S(2)}) collective-permute-start(bf16[32,2048]{1,0:T(8,128)(2,1)S(1)} %get-tuple-element.66), channel_id=1, source_target_pairs={{0,12},{4,8},{8,4},{12,0},{1,13},{5,9},{9,5},{13,1},{2,14},{6,10},... | collective-permute-start | bytes 393224 | tf_op jit(solution)/shard_map/ppermute | solution.py:131
  20.1 2.5 %shard_map.77 = (bf16[32,2048]{1,0:T(8,128)(2,1)S(1)}, bf16[32,2048]{1,0:T(8,128)(2,1)S(1)}, bf16[32,2048]{1,0:T(8,128)(2,1)S(1)}, bf16[32,2048]{1,0:T(8,128)(2,1)S(1)}) custom-call(bf16[32,128,128]{2,1,0:T(8,128)(2,1)S(1)} %shard_map.75.refs_0_, bf16[32,2176]{1,0:T(8,128)(2,1)S(1)} %get-tuple-element.47.refs_2_.refs_1_.refs_5_, ...), custom_call_target="tpu_custom_call" | custom-call | tf_op jit(solution)/shard_map/pallas_call | solution.py:169
  22.6 1.2 %collective-permute-done.6.refs_1_ = bf16[32,2048]{1,0:T(8,128)(2,1)S(1)} collective-permute-done((bf16[32,2048]{1,0:T(8,128)(2,1)S(1)}, bf16[32,2048]{1,0:T(8,128)(2,1)S(1)}, u32[]{:S(2)}, u32[]{:S(2)}) %collective-permute-start.6) | collective-permute-done | bytes 131104 | tf_op jit(solution)/shard_map/ppermute | solution.py:131
  23.8 6.9 %collective-permute-done.7.refs_2_ = bf16[32,2048]{1,0:T(8,128)(2,1)S(1)} collective-permute-done((bf16[32,2048]{1,0:T(8,128)(2,1)S(1)}, bf16[32,2048]{1,0:T(8,128)(2,1)S(1)}, u32[]{:S(2)}, u32[]{:S(2)}) %collective-permute-start.7) | collective-permute-done | bytes 131104 | tf_op jit(solution)/shard_map/ppermute | solution.py:131
  30.8 1.6 %collective-permute-start.10 = (bf16[32,2048]{1,0:T(8,128)(2,1)S(1)}, bf16[32,2048]{1,0:T(8,128)(2,1)S(1)}, u32[]{:S(2)}, u32[]{:S(2)}) collective-permute-start(bf16[32,2048]{1,0:T(8,128)(2,1)S(1)} %shard_map.78.refs_1_), channel_id=1, source_target_pairs={{0,2},{1,3},{2,0},{3,1},{4,6},{5,7},{6,4},{7,5},{8,10},{9,11},{10,... | collective-permute-start | bytes 393224 | tf_op jit(solution)/shard_map/ppermute | solution.py:131
  32.4 2.5 %collective-permute-start.12 = (bf16[32,2048]{1,0:T(8,128)(2,1)S(1)}, bf16[32,2048]{1,0:T(8,128)(2,1)S(1)}, u32[]{:S(2)}, u32[]{:S(2)}) collective-permute-start(bf16[32,2048]{1,0:T(8,128)(2,1)S(1)} %get-tuple-element.73), channel_id=1, source_target_pairs={{0,12},{4,8},{8,4},{12,0},{1,13},{5,9},{9,5},{13,1},{2,14},{6,10},... | collective-permute-start | bytes 393224 | tf_op jit(solution)/shard_map/ppermute | solution.py:131
  35.8 3.1 %collective-permute-start.17 = (bf16[32,2048]{1,0:T(8,128)(2,1)S(1)}, bf16[32,2048]{1,0:T(8,128)(2,1)S(1)}, u32[]{:S(2)}, u32[]{:S(2)}) collective-permute-start(bf16[32,2048]{1,0:T(8,128)(2,1)S(1)} %get-tuple-element.80), channel_id=1, source_target_pairs={{0,4},{4,0},{8,12},{12,8},{1,5},{5,1},{9,13},{13,9},{2,6},{6,2},{1... | collective-permute-start | bytes 393224 | tf_op jit(solution)/shard_map/ppermute | solution.py:131
  38.9 1.7 %collective-permute-done.12.refs_5_.refs_1_ = bf16[32,2048]{1,0:T(8,128)(2,1)S(1)} collective-permute-done((bf16[32,2048]{1,0:T(8,128)(2,1)S(1)}, bf16[32,2048]{1,0:T(8,128)(2,1)S(1)}, u32[]{:S(2)}, u32[]{:S(2)}) %collective-permute-start.12) | collective-permute-done | bytes 131104 | tf_op jit(solution)/shard_map/ppermute | solution.py:131
  40.6 2.3 %shard_map.79 = (bf16[32,1650]{1,0:T(8,128)(2,1)S(1)}, bf16[32,1650]{1,0:T(8,128)(2,1)S(1)}, bf16[32,1650]{1,0:T(8,128)(2,1)S(1)}, bf16[32,1650]{1,0:T(8,128)(2,1)S(1)}) custom-call(bf16[1650,2048]{1,0:T(8,128)(2,1)S(1)} %bitcast.4, bf16[32,2048]{1,0:T(8,128)(2,1)S(1)} %shard_map.78.refs_1_, bf16[32,2048]{1,0:T(8,128)(2,1)S(1)} %collective-permute-done.9.refs_2_, ...), custom_call_target="tpu_custom_call" | custom-call | tf_op jit(solution)/shard_map/pallas_call | solution.py:169
  42.9 2.5 %collective-permute-start.13 = (bf16[32,1650]{1,0:T(8,128)(2,1)S(1)}, bf16[32,1650]{1,0:T(8,128)(2,1)S(1)}, u32[]{:S(2)}, u32[]{:S(2)}) collective-permute-start(bf16[32,1650]{1,0:T(8,128)(2,1)S(1)} %get-tuple-element.75), channel_id=1, source_target_pairs={{0,12},{4,8},{8,4},{12,0},{1,13},{5,9},{9,5},{13,1},{2,14},{6,10},... | collective-permute-start | bytes 316808 | tf_op jit(solution)/shard_map/ppermute | solution.py:131
  46.2 1.0 %collective-permute-start.19 = (bf16[16,2048]{1,0:T(8,128)(2,1)S(1)}, bf16[16,2048]{1,0:T(8,128)(2,1)S(1)}, u32[]{:S(2)}, u32[]{:S(2)}) collective-permute-start(bf16[16,2048]{1,0:T(8,128)(2,1)S(1)} %get-tuple-element.82), channel_id=1, source_target_pairs={{0,2},{1,3},{2,0},{3,1},{4,6},{5,7},{6,4},{7,5},{8,10},{9,11},{10,... | collective-permute-start | bytes 196616 | tf_op jit(solution)/shard_map/ppermute | solution.py:131
  48.4 2.5 %collective-permute-done.19.refs_3_ = bf16[16,2048]{1,0:T(8,128)(2,1)S(1)} collective-permute-done((bf16[16,2048]{1,0:T(8,128)(2,1)S(1)}, bf16[16,2048]{1,0:T(8,128)(2,1)S(1)}, u32[]{:S(2)}, u32[]{:S(2)}) %collective-permute-start.19) | collective-permute-done | bytes 65568 | tf_op jit(solution)/shard_map/ppermute | solution.py:131
  51.8 1.1 %collective-permute-start.14 = (bf16[32,1650]{1,0:T(8,128)(2,1)S(1)}, bf16[32,1650]{1,0:T(8,128)(2,1)S(1)}, u32[]{:S(2)}, u32[]{:S(2)}) collective-permute-start(bf16[32,1650]{1,0:T(8,128)(2,1)S(1)} %get-tuple-element.76), channel_id=1, source_target_pairs={{0,8},{4,12},{8,0},{12,4},{1,9},{5,13},{9,1},{13,5},{2,10},{6,14},... | collective-permute-start | bytes 316808 | tf_op jit(solution)/shard_map/ppermute | solution.py:131
  52.9 1.6 %collective-permute-start.15 = (bf16[32,1650]{1,0:T(8,128)(2,1)S(1)}, bf16[32,1650]{1,0:T(8,128)(2,1)S(1)}, u32[]{:S(2)}, u32[]{:S(2)}) collective-permute-start(bf16[32,1650]{1,0:T(8,128)(2,1)S(1)} %get-tuple-element.77), channel_id=1, source_target_pairs={{0,4},{4,0},{8,12},{12,8},{1,5},{5,1},{9,13},{13,9},{2,6},{6,2},{1... | collective-permute-start | bytes 316808 | tf_op jit(solution)/shard_map/ppermute | solution.py:131
  54.5 2.3 %shard_map.81 = (bf16[32,1650]{1,0:T(8,128)(2,1)S(1)}, bf16[32,1650]{1,0:T(8,128)(2,1)S(1)}, bf16[32,1650]{1,0:T(8,128)(2,1)S(1)}, bf16[32,1650]{1,0:T(8,128)(2,1)S(1)}) custom-call(bf16[1650,2048]{1,0:T(8,128)(2,1)S(1)} %bitcast.5, bf16[32,2048]{1,0:T(8,128)(2,1)S(1)} %get-tuple-element.81.refs_1_, bf16[32,2048]{1,0:T(8,128)(2,1)S(1)} %collective-permute-done.18.refs_2_, ...), custom_call_target="tpu_custom_call" | custom-call | tf_op jit(solution)/shard_map/pallas_call | solution.py:169
  56.8 1.8 %collective-permute-start.22 = (bf16[32,1650]{1,0:T(8,128)(2,1)S(1)}, bf16[32,1650]{1,0:T(8,128)(2,1)S(1)}, u32[]{:S(2)}, u32[]{:S(2)}) collective-permute-start(bf16[32,1650]{1,0:T(8,128)(2,1)S(1)} %get-tuple-element.86), channel_id=1, source_target_pairs={{0,12},{4,8},{8,4},{12,0},{1,13},{5,9},{9,5},{13,1},{2,14},{6,10},... | collective-permute-start | bytes 316808 | tf_op jit(solution)/shard_map/ppermute | solution.py:131
  58.7 2.5 %collective-permute-start.24 = (bf16[32,1650]{1,0:T(8,128)(2,1)S(1)}, bf16[32,1650]{1,0:T(8,128)(2,1)S(1)}, u32[]{:S(2)}, u32[]{:S(2)}) collective-permute-start(bf16[32,1650]{1,0:T(8,128)(2,1)S(1)} %get-tuple-element.88), channel_id=1, source_target_pairs={{0,4},{4,0},{8,12},{12,8},{1,5},{5,1},{9,13},{13,9},{2,6},{6,2},{1... | collective-permute-start | bytes 316808 | tf_op jit(solution)/shard_map/ppermute | solution.py:131
  61.3 3.2 %collective-permute-done.22 = bf16[32,1650]{1,0:T(8,128)(2,1)S(1)} collective-permute-done((bf16[32,1650]{1,0:T(8,128)(2,1)S(1)}, bf16[32,1650]{1,0:T(8,128)(2,1)S(1)}, u32[]{:S(2)}, u32[]{:S(2)}) %collective-permute-start.22) | collective-permute-done | bytes 105632 | tf_op jit(solution)/shard_map/ppermute | solution.py:131
  64.6 4.2 %collective-permute-done.23 = bf16[32,1650]{1,0:T(8,128)(2,1)S(1)} collective-permute-done((bf16[32,1650]{1,0:T(8,128)(2,1)S(1)}, bf16[32,1650]{1,0:T(8,128)(2,1)S(1)}, u32[]{:S(2)}, u32[]{:S(2)}) %collective-permute-start.23) | collective-permute-done | bytes 105632 | tf_op jit(solution)/shard_map/ppermute | solution.py:131
  (46 shorter events, 10.2 us)
Async XLA Ops:
  2.7 6.5 %collective-permute-start = (bf16[32,2176]{1,0:T(8,128)(2,1)S(1)}, bf16[32,2176]{1,0:T(8,128)(2,1)S(1)}, u32[]{:S(2)}, u32[]{:S(2)}) collective-permute-start(bf16[32,2176]{1,0:T(8,128)(2,1)S(1)} %get-tuple-element.52), channel_id=1, source_target_pairs={{0,3},{1,2},{2,1},{3,0},{4,7},{5,6},{6,5},{7,4},{8,11},{9,10},{10,... | collective-permute-start | bytes 417800 | tf_op jit(solution)/shard_map/ppermute | solution.py:131
  5.1 7.2 %collective-permute-start.1 = (bf16[32,2176]{1,0:T(8,128)(2,1)S(1)}, bf16[32,2176]{1,0:T(8,128)(2,1)S(1)}, u32[]{:S(2)}, u32[]{:S(2)}) collective-permute-start(bf16[32,2176]{1,0:T(8,128)(2,1)S(1)} %get-tuple-element.55), channel_id=1, source_target_pairs={{0,2},{1,3},{2,0},{3,1},{4,6},{5,7},{6,4},{7,5},{8,10},{9,11},{10,... | collective-permute-start | bytes 417800 | tf_op jit(solution)/shard_map/ppermute | solution.py:131
  5.8 6.6 %collective-permute-start.2 = (bf16[32,2176]{1,0:T(8,128)(2,1)S(1)}, bf16[32,2176]{1,0:T(8,128)(2,1)S(1)}, u32[]{:S(2)}, u32[]{:S(2)}) collective-permute-start(bf16[32,2176]{1,0:T(8,128)(2,1)S(1)} %get-tuple-element.56), channel_id=1, source_target_pairs={{0,1},{1,0},{2,3},{3,2},{4,5},{5,4},{6,7},{7,6},{8,9},{9,8},{10,11... | collective-permute-start | bytes 417800 | tf_op jit(solution)/shard_map/ppermute | solution.py:131
  9.2 10.2 %collective-permute-start.3 = (bf16[32,2048]{1,0:T(8,128)(2,1)S(1)}, bf16[32,2048]{1,0:T(8,128)(2,1)S(1)}, u32[]{:S(2)}, u32[]{:S(2)}) collective-permute-start(bf16[32,2048]{1,0:T(8,128)(2,1)S(1)} %get-tuple-element.58), channel_id=1, source_target_pairs={{0,3},{1,2},{2,1},{3,0},{4,7},{5,6},{6,5},{7,4},{8,11},{9,10},{10,... | collective-permute-start | bytes 393224 | tf_op jit(solution)/shard_map/ppermute | solution.py:131
  11.4 8.7 %collective-permute-start.4 = (bf16[32,2048]{1,0:T(8,128)(2,1)S(1)}, bf16[32,2048]{1,0:T(8,128)(2,1)S(1)}, u32[]{:S(2)}, u32[]{:S(2)}) collective-permute-start(bf16[32,2048]{1,0:T(8,128)(2,1)S(1)} %get-tuple-element.59), channel_id=1, source_target_pairs={{0,2},{1,3},{2,0},{3,1},{4,6},{5,7},{6,4},{7,5},{8,10},{9,11},{10,... | collective-permute-start | bytes 393224 | tf_op jit(solution)/shard_map/ppermute | solution.py:131
  11.7 8.4 %collective-permute-start.5 = (bf16[32,2048]{1,0:T(8,128)(2,1)S(1)}, bf16[32,2048]{1,0:T(8,128)(2,1)S(1)}, u32[]{:S(2)}, u32[]{:S(2)}) collective-permute-start(bf16[32,2048]{1,0:T(8,128)(2,1)S(1)} %get-tuple-element.60), channel_id=1, source_target_pairs={{0,1},{1,0},{2,3},{3,2},{4,5},{5,4},{6,7},{7,6},{8,9},{9,8},{10,11... | collective-permute-start | bytes 393224 | tf_op jit(solution)/shard_map/ppermute | solution.py:131
  14.9 8.9 %collective-permute-start.6 = (bf16[32,2048]{1,0:T(8,128)(2,1)S(1)}, bf16[32,2048]{1,0:T(8,128)(2,1)S(1)}, u32[]{:S(2)}, u32[]{:S(2)}) collective-permute-start(bf16[32,2048]{1,0:T(8,128)(2,1)S(1)} %get-tuple-element.66), channel_id=1, source_target_pairs={{0,12},{4,8},{8,4},{12,0},{1,13},{5,9},{9,5},{13,1},{2,14},{6,10},... | collective-permute-start | bytes 393224 | tf_op jit(solution)/shard_map/ppermute | solution.py:131
  19.4 11.3 %collective-permute-start.7 = (bf16[32,2048]{1,0:T(8,128)(2,1)S(1)}, bf16[32,2048]{1,0:T(8,128)(2,1)S(1)}, u32[]{:S(2)}, u32[]{:S(2)}) collective-permute-start(bf16[32,2048]{1,0:T(8,128)(2,1)S(1)} %get-tuple-element.67), channel_id=1, source_target_pairs={{0,8},{4,12},{8,0},{12,4},{1,9},{5,13},{9,1},{13,5},{2,10},{6,14},... | collective-permute-start | bytes 393224 | tf_op jit(solution)/shard_map/ppermute | solution.py:131
  19.4 11.3 %collective-permute-start.8 = (bf16[32,2048]{1,0:T(8,128)(2,1)S(1)}, bf16[32,2048]{1,0:T(8,128)(2,1)S(1)}, u32[]{:S(2)}, u32[]{:S(2)}) collective-permute-start(bf16[32,2048]{1,0:T(8,128)(2,1)S(1)} %get-tuple-element.68), channel_id=1, source_target_pairs={{0,4},{4,0},{8,12},{12,8},{1,5},{5,1},{9,13},{13,9},{2,6},{6,2},{1... | collective-permute-start | bytes 393224 | tf_op jit(solution)/shard_map/ppermute | solution.py:131
  30.8 5.0 %collective-permute-start.10 = (bf16[32,2048]{1,0:T(8,128)(2,1)S(1)}, bf16[32,2048]{1,0:T(8,128)(2,1)S(1)}, u32[]{:S(2)}, u32[]{:S(2)}) collective-permute-start(bf16[32,2048]{1,0:T(8,128)(2,1)S(1)} %shard_map.78.refs_1_), channel_id=1, source_target_pairs={{0,2},{1,3},{2,0},{3,1},{4,6},{5,7},{6,4},{7,5},{8,10},{9,11},{10,... | collective-permute-start | bytes 393224 | tf_op jit(solution)/shard_map/ppermute | solution.py:131
  32.4 6.5 %collective-permute-start.9 = (bf16[32,2048]{1,0:T(8,128)(2,1)S(1)}, bf16[32,2048]{1,0:T(8,128)(2,1)S(1)}, u32[]{:S(2)}, u32[]{:S(2)}) collective-permute-start(bf16[32,2048]{1,0:T(8,128)(2,1)S(1)} %shard_map.78.refs_1_), channel_id=1, source_target_pairs={{0,1},{1,0},{2,3},{3,2},{4,5},{5,4},{6,7},{7,6},{8,9},{9,8},{10,11... | collective-permute-start | bytes 393224 | tf_op jit(solution)/shard_map/ppermute | solution.py:131
  32.4 8.2 %collective-permute-start.12 = (bf16[32,2048]{1,0:T(8,128)(2,1)S(1)}, bf16[32,2048]{1,0:T(8,128)(2,1)S(1)}, u32[]{:S(2)}, u32[]{:S(2)}) collective-permute-start(bf16[32,2048]{1,0:T(8,128)(2,1)S(1)} %get-tuple-element.73), channel_id=1, source_target_pairs={{0,12},{4,8},{8,4},{12,0},{1,13},{5,9},{9,5},{13,1},{2,14},{6,10},... | collective-permute-start | bytes 393224 | tf_op jit(solution)/shard_map/ppermute | solution.py:131
  35.8 4.8 %collective-permute-start.11 = (bf16[32,2048]{1,0:T(8,128)(2,1)S(1)}, bf16[32,2048]{1,0:T(8,128)(2,1)S(1)}, u32[]{:S(2)}, u32[]{:S(2)}) collective-permute-start(bf16[32,2048]{1,0:T(8,128)(2,1)S(1)} %collective-permute-done.10.refs_3_), channel_id=1, source_target_pairs={{0,1},{1,0},{2,3},{3,2},{4,5},{5,4},{6,7},{7,6},{8,9},{9,8},{10,11... | collective-permute-start | bytes 393224 | tf_op jit(solution)/shard_map/ppermute | solution.py:131
  35.8 10.3 %collective-permute-start.16 = (bf16[32,2048]{1,0:T(8,128)(2,1)S(1)}, bf16[32,2048]{1,0:T(8,128)(2,1)S(1)}, u32[]{:S(2)}, u32[]{:S(2)}) collective-permute-start(bf16[32,2048]{1,0:T(8,128)(2,1)S(1)} %get-tuple-element.79), channel_id=1, source_target_pairs={{0,8},{4,12},{8,0},{12,4},{1,9},{5,13},{9,1},{13,5},{2,10},{6,14},... | collective-permute-start | bytes 393224 | tf_op jit(solution)/shard_map/ppermute | solution.py:131
  35.8 10.3 %collective-permute-start.17 = (bf16[32,2048]{1,0:T(8,128)(2,1)S(1)}, bf16[32,2048]{1,0:T(8,128)(2,1)S(1)}, u32[]{:S(2)}, u32[]{:S(2)}) collective-permute-start(bf16[32,2048]{1,0:T(8,128)(2,1)S(1)} %get-tuple-element.80), channel_id=1, source_target_pairs={{0,4},{4,0},{8,12},{12,8},{1,5},{5,1},{9,13},{13,9},{2,6},{6,2},{1... | collective-permute-start | bytes 393224 | tf_op jit(solution)/shard_map/ppermute | solution.py:131
  42.9 8.1 %collective-permute-start.13 = (bf16[32,1650]{1,0:T(8,128)(2,1)S(1)}, bf16[32,1650]{1,0:T(8,128)(2,1)S(1)}, u32[]{:S(2)}, u32[]{:S(2)}) collective-permute-start(bf16[32,1650]{1,0:T(8,128)(2,1)S(1)} %get-tuple-element.75), channel_id=1, source_target_pairs={{0,12},{4,8},{8,4},{12,0},{1,13},{5,9},{9,5},{13,1},{2,14},{6,10},... | collective-permute-start | bytes 316808 | tf_op jit(solution)/shard_map/ppermute | solution.py:131
  46.2 4.7 %collective-permute-start.19 = (bf16[16,2048]{1,0:T(8,128)(2,1)S(1)}, bf16[16,2048]{1,0:T(8,128)(2,1)S(1)}, u32[]{:S(2)}, u32[]{:S(2)}) collective-permute-start(bf16[16,2048]{1,0:T(8,128)(2,1)S(1)} %get-tuple-element.82), channel_id=1, source_target_pairs={{0,2},{1,3},{2,0},{3,1},{4,6},{5,7},{6,4},{7,5},{8,10},{9,11},{10,... | collective-permute-start | bytes 196616 | tf_op jit(solution)/shard_map/ppermute | solution.py:131
  47.2 4.3 %collective-permute-start.20 = (bf16[16,2048]{1,0:T(8,128)(2,1)S(1)}, bf16[16,2048]{1,0:T(8,128)(2,1)S(1)}, u32[]{:S(2)}, u32[]{:S(2)}) collective-permute-start(bf16[16,2048]{1,0:T(8,128)(2,1)S(1)} %get-tuple-element.84), channel_id=1, source_target_pairs={{0,3},{1,2},{2,1},{3,0},{4,7},{5,6},{6,5},{7,4},{8,11},{9,10},{10,... | collective-permute-start | bytes 196616 | tf_op jit(solution)/shard_map/ppermute | solution.py:131
  47.5 7.0 %collective-permute-start.18 = (bf16[32,2048]{1,0:T(8,128)(2,1)S(1)}, bf16[32,2048]{1,0:T(8,128)(2,1)S(1)}, u32[]{:S(2)}, u32[]{:S(2)}) collective-permute-start(bf16[32,2048]{1,0:T(8,128)(2,1)S(1)} %get-tuple-element.81.refs_1_), channel_id=1, source_target_pairs={{0,1},{1,0},{2,3},{3,2},{4,5},{5,4},{6,7},{7,6},{8,9},{9,8},{10,11... | collective-permute-start | bytes 393224 | tf_op jit(solution)/shard_map/ppermute | solution.py:131
  51.8 9.4 %collective-permute-start.14 = (bf16[32,1650]{1,0:T(8,128)(2,1)S(1)}, bf16[32,1650]{1,0:T(8,128)(2,1)S(1)}, u32[]{:S(2)}, u32[]{:S(2)}) collective-permute-start(bf16[32,1650]{1,0:T(8,128)(2,1)S(1)} %get-tuple-element.76), channel_id=1, source_target_pairs={{0,8},{4,12},{8,0},{12,4},{1,9},{5,13},{9,1},{13,5},{2,10},{6,14},... | collective-permute-start | bytes 316808 | tf_op jit(solution)/shard_map/ppermute | solution.py:131
  52.9 8.4 %collective-permute-start.15 = (bf16[32,1650]{1,0:T(8,128)(2,1)S(1)}, bf16[32,1650]{1,0:T(8,128)(2,1)S(1)}, u32[]{:S(2)}, u32[]{:S(2)}) collective-permute-start(bf16[32,1650]{1,0:T(8,128)(2,1)S(1)} %get-tuple-element.77), channel_id=1, source_target_pairs={{0,4},{4,0},{8,12},{12,8},{1,5},{5,1},{9,13},{13,9},{2,6},{6,2},{1... | collective-permute-start | bytes 316808 | tf_op jit(solution)/shard_map/ppermute | solution.py:131
  56.8 7.8 %collective-permute-start.22 = (bf16[32,1650]{1,0:T(8,128)(2,1)S(1)}, bf16[32,1650]{1,0:T(8,128)(2,1)S(1)}, u32[]{:S(2)}, u32[]{:S(2)}) collective-permute-start(bf16[32,1650]{1,0:T(8,128)(2,1)S(1)} %get-tuple-element.86), channel_id=1, source_target_pairs={{0,12},{4,8},{8,4},{12,0},{1,13},{5,9},{9,5},{13,1},{2,14},{6,10},... | collective-permute-start | bytes 316808 | tf_op jit(solution)/shard_map/ppermute | solution.py:131
  58.6 10.2 %collective-permute-start.23 = (bf16[32,1650]{1,0:T(8,128)(2,1)S(1)}, bf16[32,1650]{1,0:T(8,128)(2,1)S(1)}, u32[]{:S(2)}, u32[]{:S(2)}) collective-permute-start(bf16[32,1650]{1,0:T(8,128)(2,1)S(1)} %get-tuple-element.87), channel_id=1, source_target_pairs={{0,8},{4,12},{8,0},{12,4},{1,9},{5,13},{9,1},{13,5},{2,10},{6,14},... | collective-permute-start | bytes 316808 | tf_op jit(solution)/shard_map/ppermute | solution.py:131
  58.7 10.1 %collective-permute-start.24 = (bf16[32,1650]{1,0:T(8,128)(2,1)S(1)}, bf16[32,1650]{1,0:T(8,128)(2,1)S(1)}, u32[]{:S(2)}, u32[]{:S(2)}) collective-permute-start(bf16[32,1650]{1,0:T(8,128)(2,1)S(1)} %get-tuple-element.88), channel_id=1, source_target_pairs={{0,4},{4,0},{8,12},{12,8},{1,5},{5,1},{9,13},{13,9},{2,6},{6,2},{1... | collective-permute-start | bytes 316808 | tf_op jit(solution)/shard_map/ppermute | solution.py:131
  (4 other events, 45.9 us)

commit v9 on v6

--- a/solution.py
+++ b/solution.py
@@ -98,7 +98,7 @@
     aligned = n_layer == n_row
     me, row = lax.axis_index("layer"), lax.axis_index("row")
     for j, piece in enumerate(pieces):
-        place = lax.bitwise_xor(me, j)
+        place = lax.bitwise_xor(me, (j + 1) % n_layer)
         left[lax.bitwise_xor(place, row) if aligned else place] = piece[...]
     columns = left.shape[0] * left.shape[1]
     found = lax.dot_general(
@@ -129,13 +129,6 @@
     return [trade(chunk, axis, n - i) if i else chunk for i, chunk in enumerate(chunks)]
 
 
-def gather(piece, axis, paired):
-    got = [piece]
-    for k in range(1, lax.axis_size(axis)):
-        got.append(trade(got[k - 1], axis, 1) if paired and k % 2 else trade(piece, axis, k))
-    return got
-
-
 def total_of(parts):
     return sum(part.astype(F32) for part in parts).astype(BF16)
 
@@ -180,14 +173,17 @@
             after=before,
         )
         before = (turned[0],)
+        if h == 0:
+            (padded,) = call(
+                pad_kernel,
+                [(LANES // block_rows * weights, LANES, slice_rows)],
+                [],
+                jnp.swapaxes(table, 1, 2),
+                after=before,
+            )
+        else:
+            turned, parts[-1][1], padded = lax.optimization_barrier((turned, parts[-1][1], padded))
         parts.append(exchange(turned, "layer"))
-    (padded,) = call(
-        pad_kernel,
-        [(LANES // block_rows * weights, LANES, slice_rows)],
-        [],
-        jnp.swapaxes(table, 1, 2),
-        after=before,
-    )
 
     received, before = [], ()
     for h in range(halves):
@@ -209,21 +205,21 @@
         if h > 0:
             shares, received[-1] = lax.optimization_barrier((shares, received[-1]))
         received.append(exchange(shares, "row"))
-    results, ahead = [], tuple(received[-1][1:2])
-    for h in range(halves):
-        (pupil,) = call(sum_kernel, [(each, points)], [], *received[h], after=before)
-        pieces = gather(pupil, "layer", h == 0)
+    pupils = []
+    for h in range(halves):
+        pupils += call(sum_kernel, [(each, points)], [], *received[h], after=before)
+    results = []
+    for h in range(halves):
+        pieces = exchange([pupils[h]] * n_layer, "layer")[::-1]
         partial = call(
             functools.partial(fit_kernel, n_layer, n_row),
             [(chunk // halves, actuators)] * n_row,
             [pltpu.VMEM((n_layer, each, points), BF16), pltpu.VMEM((per_half, actuators), F32)],
             fitting.T,
             *pieces,
-            after=ahead,
+            after=pupils[h + 1 :],
         )
-        before = (partial[0],)
         results.append(exchange(partial, "row"))
-        ahead = tuple(results[-1][1:2])
     return jnp.concatenate([total_of(result) for result in results], 0)
 
 

time: 69.6 us -> 69.4 us (level)
  starting transfers between devices: 29.2 us -> 27.7 us
  waiting for transfers between devices: 25.2 us -> 26.5 us
    ppermute x24, starting transfers between devices: 29.2 us -> 27.7 us  [trade(): lax.ppermute(chunk, axis, [(j, j ^ k) for j in range(lax.axis_size(axis))])]
    ppermute x24, waiting for transfers between devices: 25.2 us -> 26.5 us  [trade(): lax.ppermute(chunk, axis, [(j, j ^ k) for j in range(lax.axis_size(axis))])]
  transfers between devices with their start and end apart: 24 -> 24, of which waited for: 10 -> 9; matrix products, arithmetic and copies ran while one was open for 0% -> 0% of each run, Pallas kernels for 15% -> 15%
where the time goes in v9:
time: 69.4 us; the launch traced here: 69.2 us
  starting transfers between devices  27.7 us (40%)
  waiting for transfers between devices  26.5 us (38%)
  Pallas kernels  10.9 us (16%)
  local copies, waits for them, and re-layouts  2.29 us (3%)
  other arithmetic  1.7 us (2%)
    ppermute x24, starting transfers between devices, trade(): lax.ppermute(chunk, axis, [(j, j ^ k) for j in range(lax.axis_size(axis))])  27.7 us
    ppermute x24, waiting for transfers between devices, trade(): lax.ppermute(chunk, axis, [(j, j ^ k) for j in range(lax.axis_size(axis))])  26.5 us
    pallas_call x9, Pallas kernels, call(): pl.pallas_call(body, out_shape=[jax.ShapeDtypeStruct(shape, BF16) for sha...  10.9 us
    unnamed x6, local copies, waits for them, and re-layouts  2.29 us
  transfers between devices with their start and end apart: 24, of which 9 were waited for; matrix products, arithmetic and copies ran while one was open for 0% of the time, Pallas kernels for 15%

profile of v9, /device:TPU:0, one launch (start us, length us, event | category | flops | bytes accessed | tf_op | source)
XLA Modules:
  0.0 69.2 jit_solution(2753502508312319583)
XLA Ops:
  0.9 1.3 %copy-done.1 = bf16[1,2048,256]{2,1,0:T(8,128)(2,1)S(1)} copy-done((bf16[1,2048,256]{2,1,0:T(8,128)(2,1)S(1)}, bf16[1,2048,256]{2,1,0:T(8,128)(2,1)}, u32[]{:S(2)}) %copy-start.1) | copy-done | bytes 1048600
  2.7 2.4 %collective-permute-start = (bf16[32,2176]{1,0:T(8,128)(2,1)S(1)}, bf16[32,2176]{1,0:T(8,128)(2,1)S(1)}, u32[]{:S(2)}, u32[]{:S(2)}) collective-permute-start(bf16[32,2176]{1,0:T(8,128)(2,1)S(1)} %get-tuple-element.48), channel_id=1, source_target_pairs={{0,3},{1,2},{2,1},{3,0},{4,7},{5,6},{6,5},{7,4},{8,11},{9,10},{10,... | collective-permute-start | bytes 417800 | tf_op jit(solution)/shard_map/ppermute | solution.py:124
  6.3 0.9 %copy-done.2 = bf16[16,128,64]{1,2,0:T(8,128)(2,1)S(1)} copy-done((bf16[16,128,64]{1,2,0:T(8,128)(2,1)S(1)}, bf16[16,128,64]{1,2,0:T(8,128)(2,1)}, u32[]{:S(2)}) %copy-start.2) | copy-done | bytes 262168
  7.5 1.7 %collective-permute-done.refs_2_.refs_6_ = bf16[32,2176]{1,0:T(8,128)(2,1)S(1)} collective-permute-done((bf16[32,2176]{1,0:T(8,128)(2,1)S(1)}, bf16[32,2176]{1,0:T(8,128)(2,1)S(1)}, u32[]{:S(2)}, u32[]{:S(2)}) %collective-permute-start) | collective-permute-done | bytes 139296 | tf_op jit(solution)/shard_map/ppermute | solution.py:124
  9.2 2.2 %collective-permute-start.3 = (bf16[32,2048]{1,0:T(8,128)(2,1)S(1)}, bf16[32,2048]{1,0:T(8,128)(2,1)S(1)}, u32[]{:S(2)}, u32[]{:S(2)}) collective-permute-start(bf16[32,2048]{1,0:T(8,128)(2,1)S(1)} %get-tuple-element.54), channel_id=1, source_target_pairs={{0,3},{1,2},{2,1},{3,0},{4,7},{5,6},{6,5},{7,4},{8,11},{9,10},{10,... | collective-permute-start | bytes 393224 | tf_op jit(solution)/shard_map/ppermute | solution.py:124
  12.4 2.6 %shard_map.76 = (bf16[32,2048]{1,0:T(8,128)(2,1)S(1)}, bf16[32,2048]{1,0:T(8,128)(2,1)S(1)}, bf16[32,2048]{1,0:T(8,128)(2,1)S(1)}, bf16[32,2048]{1,0:T(8,128)(2,1)S(1)}) custom-call(bf16[32,128,128]{2,1,0:T(8,128)(2,1)S(1)} %shard_map.75.refs_0_, bf16[32,2176]{1,0:T(8,128)(2,1)S(1)} %get-tuple-element.43.refs_2_.refs_1_.refs_5_, ...), custom_call_target="tpu_custom_call" | custom-call | tf_op jit(solution)/shard_map/pallas_call | solution.py:142
  14.9 4.5 %collective-permute-start.6 = (bf16[32,2048]{1,0:T(8,128)(2,1)S(1)}, bf16[32,2048]{1,0:T(8,128)(2,1)S(1)}, u32[]{:S(2)}, u32[]{:S(2)}) collective-permute-start(bf16[32,2048]{1,0:T(8,128)(2,1)S(1)} %get-tuple-element.62), channel_id=1, source_target_pairs={{0,12},{4,8},{8,4},{12,0},{1,13},{5,9},{9,5},{13,1},{2,14},{6,10},... | collective-permute-start | bytes 393224 | tf_op jit(solution)/shard_map/ppermute | solution.py:124
  20.1 2.6 %shard_map.77 = (bf16[32,2048]{1,0:T(8,128)(2,1)S(1)}, bf16[32,2048]{1,0:T(8,128)(2,1)S(1)}, bf16[32,2048]{1,0:T(8,128)(2,1)S(1)}, bf16[32,2048]{1,0:T(8,128)(2,1)S(1)}) custom-call(bf16[32,128,128]{2,1,0:T(8,128)(2,1)S(1)} %shard_map.75.refs_0_, bf16[32,2176]{1,0:T(8,128)(2,1)S(1)} %get-tuple-element.43.refs_2_.refs_1_.refs_5_, ...), custom_call_target="tpu_custom_call" | custom-call | tf_op jit(solution)/shard_map/pallas_call | solution.py:142
  22.6 1.2 %collective-permute-done.6.refs_1_ = bf16[32,2048]{1,0:T(8,128)(2,1)S(1)} collective-permute-done((bf16[32,2048]{1,0:T(8,128)(2,1)S(1)}, bf16[32,2048]{1,0:T(8,128)(2,1)S(1)}, u32[]{:S(2)}, u32[]{:S(2)}) %collective-permute-start.6) | collective-permute-done | bytes 131104 | tf_op jit(solution)/shard_map/ppermute | solution.py:124
  23.8 6.9 %collective-permute-done.7.refs_2_ = bf16[32,2048]{1,0:T(8,128)(2,1)S(1)} collective-permute-done((bf16[32,2048]{1,0:T(8,128)(2,1)S(1)}, bf16[32,2048]{1,0:T(8,128)(2,1)S(1)}, u32[]{:S(2)}, u32[]{:S(2)}) %collective-permute-start.7) | collective-permute-done | bytes 131104 | tf_op jit(solution)/shard_map/ppermute | solution.py:124
  30.7 2.6 %collective-permute-start.12 = (bf16[32,2048]{1,0:T(8,128)(2,1)S(1)}, bf16[32,2048]{1,0:T(8,128)(2,1)S(1)}, u32[]{:S(2)}, u32[]{:S(2)}) collective-permute-start(bf16[32,2048]{1,0:T(8,128)(2,1)S(1)} %get-tuple-element.70), channel_id=1, source_target_pairs={{0,12},{4,8},{8,4},{12,0},{1,13},{5,9},{9,5},{13,1},{2,14},{6,10},... | collective-permute-start | bytes 393224 | tf_op jit(solution)/shard_map/ppermute | solution.py:124
  33.4 1.7 %collective-permute-start.14 = (bf16[32,2048]{1,0:T(8,128)(2,1)S(1)}, bf16[32,2048]{1,0:T(8,128)(2,1)S(1)}, u32[]{:S(2)}, u32[]{:S(2)}) collective-permute-start(bf16[32,2048]{1,0:T(8,128)(2,1)S(1)} %get-tuple-element.72), channel_id=1, source_target_pairs={{0,4},{4,0},{8,12},{12,8},{1,5},{5,1},{9,13},{13,9},{2,6},{6,2},{1... | collective-permute-start | bytes 393224 | tf_op jit(solution)/shard_map/ppermute | solution.py:124
  35.2 1.6 %collective-permute-start.10 = (bf16[32,2048]{1,0:T(8,128)(2,1)S(1)}, bf16[32,2048]{1,0:T(8,128)(2,1)S(1)}, u32[]{:S(2)}, u32[]{:S(2)}) collective-permute-start(bf16[32,2048]{1,0:T(8,128)(2,1)S(1)} %shard_map.78.refs_4_), channel_id=1, source_target_pairs={{0,2},{1,3},{2,0},{3,1},{4,6},{5,7},{6,4},{7,5},{8,10},{9,11},{10,... | collective-permute-start | bytes 393224 | tf_op jit(solution)/shard_map/ppermute | solution.py:124
  36.8 2.1 %collective-permute-done.12.refs_1_ = bf16[32,2048]{1,0:T(8,128)(2,1)S(1)} collective-permute-done((bf16[32,2048]{1,0:T(8,128)(2,1)S(1)}, bf16[32,2048]{1,0:T(8,128)(2,1)S(1)}, u32[]{:S(2)}, u32[]{:S(2)}) %collective-permute-start.12) | collective-permute-done | bytes 131104 | tf_op jit(solution)/shard_map/ppermute | solution.py:124
  38.9 4.4 %collective-permute-done.13.refs_2_ = bf16[32,2048]{1,0:T(8,128)(2,1)S(1)} collective-permute-done((bf16[32,2048]{1,0:T(8,128)(2,1)S(1)}, bf16[32,2048]{1,0:T(8,128)(2,1)S(1)}, u32[]{:S(2)}, u32[]{:S(2)}) %collective-permute-start.13) | collective-permute-done | bytes 131104 | tf_op jit(solution)/shard_map/ppermute | solution.py:124
  43.5 0.9 %collective-permute-start.20 = (bf16[32,2048]{1,0:T(8,128)(2,1)S(1)}, bf16[32,2048]{1,0:T(8,128)(2,1)S(1)}, u32[]{:S(2)}, u32[]{:S(2)}) collective-permute-start(bf16[32,2048]{1,0:T(8,128)(2,1)S(1)} %shard_map.79.refs_5_.refs_4_), channel_id=1, source_target_pairs={{0,3},{1,2},{2,1},{3,0},{4,7},{5,6},{6,5},{7,4},{8,11},{9,10},{10,... | collective-permute-start | bytes 393224 | tf_op jit(solution)/shard_map/ppermute | solution.py:124
  45.4 2.3 %shard_map.80 = (bf16[32,1650]{1,0:T(8,128)(2,1)S(1)}, bf16[32,1650]{1,0:T(8,128)(2,1)S(1)}, bf16[32,1650]{1,0:T(8,128)(2,1)S(1)}, bf16[32,1650]{1,0:T(8,128)(2,1)S(1)}) custom-call(bf16[1650,2048]{1,0:T(8,128)(2,1)S(1)} %bitcast.4, bf16[32,2048]{1,0:T(8,128)(2,1)S(1)} %collective-permute-done.9.refs_1_, ...), custom_call_target="tpu_custom_call" | custom-call | tf_op jit(solution)/shard_map/pallas_call | solution.py:142
  47.7 1.9 %collective-permute-start.15 = (bf16[32,1650]{1,0:T(8,128)(2,1)S(1)}, bf16[32,1650]{1,0:T(8,128)(2,1)S(1)}, u32[]{:S(2)}, u32[]{:S(2)}) collective-permute-start(bf16[32,1650]{1,0:T(8,128)(2,1)S(1)} %get-tuple-element.74), channel_id=1, source_target_pairs={{0,12},{4,8},{8,4},{12,0},{1,13},{5,9},{9,5},{13,1},{2,14},{6,10},... | collective-permute-start | bytes 316808 | tf_op jit(solution)/shard_map/ppermute | solution.py:124
  49.6 2.5 %collective-permute-start.17 = (bf16[32,1650]{1,0:T(8,128)(2,1)S(1)}, bf16[32,1650]{1,0:T(8,128)(2,1)S(1)}, u32[]{:S(2)}, u32[]{:S(2)}) collective-permute-start(bf16[32,1650]{1,0:T(8,128)(2,1)S(1)} %get-tuple-element.76), channel_id=1, source_target_pairs={{0,4},{4,0},{8,12},{12,8},{1,5},{5,1},{9,13},{13,9},{2,6},{6,2},{1... | collective-permute-start | bytes 316808 | tf_op jit(solution)/shard_map/ppermute | solution.py:124
  52.1 2.3 %shard_map.81 = (bf16[32,1650]{1,0:T(8,128)(2,1)S(1)}, bf16[32,1650]{1,0:T(8,128)(2,1)S(1)}, bf16[32,1650]{1,0:T(8,128)(2,1)S(1)}, bf16[32,1650]{1,0:T(8,128)(2,1)S(1)}) custom-call(bf16[1650,2048]{1,0:T(8,128)(2,1)S(1)} %bitcast.5, bf16[32,2048]{1,0:T(8,128)(2,1)S(1)} %collective-permute-done.18.refs_1_, ...), custom_call_target="tpu_custom_call" | custom-call | tf_op jit(solution)/shard_map/pallas_call | solution.py:142
  54.4 1.9 %collective-permute-start.21 = (bf16[32,1650]{1,0:T(8,128)(2,1)S(1)}, bf16[32,1650]{1,0:T(8,128)(2,1)S(1)}, u32[]{:S(2)}, u32[]{:S(2)}) collective-permute-start(bf16[32,1650]{1,0:T(8,128)(2,1)S(1)} %get-tuple-element.78), channel_id=1, source_target_pairs={{0,12},{4,8},{8,4},{12,0},{1,13},{5,9},{9,5},{13,1},{2,14},{6,10},... | collective-permute-start | bytes 316808 | tf_op jit(solution)/shard_map/ppermute | solution.py:124
  56.4 2.5 %collective-permute-start.23 = (bf16[32,1650]{1,0:T(8,128)(2,1)S(1)}, bf16[32,1650]{1,0:T(8,128)(2,1)S(1)}, u32[]{:S(2)}, u32[]{:S(2)}) collective-permute-start(bf16[32,1650]{1,0:T(8,128)(2,1)S(1)} %get-tuple-element.80), channel_id=1, source_target_pairs={{0,4},{4,0},{8,12},{12,8},{1,5},{5,1},{9,13},{13,9},{2,6},{6,2},{1... | collective-permute-start | bytes 316808 | tf_op jit(solution)/shard_map/ppermute | solution.py:124
  59.8 2.5 %collective-permute-done.21 = bf16[32,1650]{1,0:T(8,128)(2,1)S(1)} collective-permute-done((bf16[32,1650]{1,0:T(8,128)(2,1)S(1)}, bf16[32,1650]{1,0:T(8,128)(2,1)S(1)}, u32[]{:S(2)}, u32[]{:S(2)}) %collective-permute-start.21) | collective-permute-done | bytes 105632 | tf_op jit(solution)/shard_map/ppermute | solution.py:124
  62.2 6.2 %collective-permute-done.22 = bf16[32,1650]{1,0:T(8,128)(2,1)S(1)} collective-permute-done((bf16[32,1650]{1,0:T(8,128)(2,1)S(1)}, bf16[32,1650]{1,0:T(8,128)(2,1)S(1)}, u32[]{:S(2)}, u32[]{:S(2)}) %collective-permute-start.22) | collective-permute-done | bytes 105632 | tf_op jit(solution)/shard_map/ppermute | solution.py:124
  (43 shorter events, 7.2 us)
Async XLA Ops:
  2.7 6.5 %collective-permute-start = (bf16[32,2176]{1,0:T(8,128)(2,1)S(1)}, bf16[32,2176]{1,0:T(8,128)(2,1)S(1)}, u32[]{:S(2)}, u32[]{:S(2)}) collective-permute-start(bf16[32,2176]{1,0:T(8,128)(2,1)S(1)} %get-tuple-element.48), channel_id=1, source_target_pairs={{0,3},{1,2},{2,1},{3,0},{4,7},{5,6},{6,5},{7,4},{8,11},{9,10},{10,... | collective-permute-start | bytes 417800 | tf_op jit(solution)/shard_map/ppermute | solution.py:124
  5.1 7.2 %collective-permute-start.1 = (bf16[32,2176]{1,0:T(8,128)(2,1)S(1)}, bf16[32,2176]{1,0:T(8,128)(2,1)S(1)}, u32[]{:S(2)}, u32[]{:S(2)}) collective-permute-start(bf16[32,2176]{1,0:T(8,128)(2,1)S(1)} %get-tuple-element.51), channel_id=1, source_target_pairs={{0,2},{1,3},{2,0},{3,1},{4,6},{5,7},{6,4},{7,5},{8,10},{9,11},{10,... | collective-permute-start | bytes 417800 | tf_op jit(solution)/shard_map/ppermute | solution.py:124
  5.8 6.6 %collective-permute-start.2 = (bf16[32,2176]{1,0:T(8,128)(2,1)S(1)}, bf16[32,2176]{1,0:T(8,128)(2,1)S(1)}, u32[]{:S(2)}, u32[]{:S(2)}) collective-permute-start(bf16[32,2176]{1,0:T(8,128)(2,1)S(1)} %get-tuple-element.52), channel_id=1, source_target_pairs={{0,1},{1,0},{2,3},{3,2},{4,5},{5,4},{6,7},{7,6},{8,9},{9,8},{10,11... | collective-permute-start | bytes 417800 | tf_op jit(solution)/shard_map/ppermute | solution.py:124
  9.2 10.2 %collective-permute-start.3 = (bf16[32,2048]{1,0:T(8,128)(2,1)S(1)}, bf16[32,2048]{1,0:T(8,128)(2,1)S(1)}, u32[]{:S(2)}, u32[]{:S(2)}) collective-permute-start(bf16[32,2048]{1,0:T(8,128)(2,1)S(1)} %get-tuple-element.54), channel_id=1, source_target_pairs={{0,3},{1,2},{2,1},{3,0},{4,7},{5,6},{6,5},{7,4},{8,11},{9,10},{10,... | collective-permute-start | bytes 393224 | tf_op jit(solution)/shard_map/ppermute | solution.py:124
  11.4 8.7 %collective-permute-start.4 = (bf16[32,2048]{1,0:T(8,128)(2,1)S(1)}, bf16[32,2048]{1,0:T(8,128)(2,1)S(1)}, u32[]{:S(2)}, u32[]{:S(2)}) collective-permute-start(bf16[32,2048]{1,0:T(8,128)(2,1)S(1)} %get-tuple-element.55), channel_id=1, source_target_pairs={{0,2},{1,3},{2,0},{3,1},{4,6},{5,7},{6,4},{7,5},{8,10},{9,11},{10,... | collective-permute-start | bytes 393224 | tf_op jit(solution)/shard_map/ppermute | solution.py:124
  11.7 8.4 %collective-permute-start.5 = (bf16[32,2048]{1,0:T(8,128)(2,1)S(1)}, bf16[32,2048]{1,0:T(8,128)(2,1)S(1)}, u32[]{:S(2)}, u32[]{:S(2)}) collective-permute-start(bf16[32,2048]{1,0:T(8,128)(2,1)S(1)} %get-tuple-element.56), channel_id=1, source_target_pairs={{0,1},{1,0},{2,3},{3,2},{4,5},{5,4},{6,7},{7,6},{8,9},{9,8},{10,11... | collective-permute-start | bytes 393224 | tf_op jit(solution)/shard_map/ppermute | solution.py:124
  14.9 8.9 %collective-permute-start.6 = (bf16[32,2048]{1,0:T(8,128)(2,1)S(1)}, bf16[32,2048]{1,0:T(8,128)(2,1)S(1)}, u32[]{:S(2)}, u32[]{:S(2)}) collective-permute-start(bf16[32,2048]{1,0:T(8,128)(2,1)S(1)} %get-tuple-element.62), channel_id=1, source_target_pairs={{0,12},{4,8},{8,4},{12,0},{1,13},{5,9},{9,5},{13,1},{2,14},{6,10},... | collective-permute-start | bytes 393224 | tf_op jit(solution)/shard_map/ppermute | solution.py:124
  19.4 11.3 %collective-permute-start.7 = (bf16[32,2048]{1,0:T(8,128)(2,1)S(1)}, bf16[32,2048]{1,0:T(8,128)(2,1)S(1)}, u32[]{:S(2)}, u32[]{:S(2)}) collective-permute-start(bf16[32,2048]{1,0:T(8,128)(2,1)S(1)} %get-tuple-element.63), channel_id=1, source_target_pairs={{0,8},{4,12},{8,0},{12,4},{1,9},{5,13},{9,1},{13,5},{2,10},{6,14},... | collective-permute-start | bytes 393224 | tf_op jit(solution)/shard_map/ppermute | solution.py:124
  19.4 11.3 %collective-permute-start.8 = (bf16[32,2048]{1,0:T(8,128)(2,1)S(1)}, bf16[32,2048]{1,0:T(8,128)(2,1)S(1)}, u32[]{:S(2)}, u32[]{:S(2)}) collective-permute-start(bf16[32,2048]{1,0:T(8,128)(2,1)S(1)} %get-tuple-element.64), channel_id=1, source_target_pairs={{0,4},{4,0},{8,12},{12,8},{1,5},{5,1},{9,13},{13,9},{2,6},{6,2},{1... | collective-permute-start | bytes 393224 | tf_op jit(solution)/shard_map/ppermute | solution.py:124
  30.7 8.2 %collective-permute-start.12 = (bf16[32,2048]{1,0:T(8,128)(2,1)S(1)}, bf16[32,2048]{1,0:T(8,128)(2,1)S(1)}, u32[]{:S(2)}, u32[]{:S(2)}) collective-permute-start(bf16[32,2048]{1,0:T(8,128)(2,1)S(1)} %get-tuple-element.70), channel_id=1, source_target_pairs={{0,12},{4,8},{8,4},{12,0},{1,13},{5,9},{9,5},{13,1},{2,14},{6,10},... | collective-permute-start | bytes 393224 | tf_op jit(solution)/shard_map/ppermute | solution.py:124
  33.4 10.0 %collective-permute-start.13 = (bf16[32,2048]{1,0:T(8,128)(2,1)S(1)}, bf16[32,2048]{1,0:T(8,128)(2,1)S(1)}, u32[]{:S(2)}, u32[]{:S(2)}) collective-permute-start(bf16[32,2048]{1,0:T(8,128)(2,1)S(1)} %get-tuple-element.71), channel_id=1, source_target_pairs={{0,8},{4,12},{8,0},{12,4},{1,9},{5,13},{9,1},{13,5},{2,10},{6,14},... | collective-permute-start | bytes 393224 | tf_op jit(solution)/shard_map/ppermute | solution.py:124
  33.4 10.0 %collective-permute-start.14 = (bf16[32,2048]{1,0:T(8,128)(2,1)S(1)}, bf16[32,2048]{1,0:T(8,128)(2,1)S(1)}, u32[]{:S(2)}, u32[]{:S(2)}) collective-permute-start(bf16[32,2048]{1,0:T(8,128)(2,1)S(1)} %get-tuple-element.72), channel_id=1, source_target_pairs={{0,4},{4,0},{8,12},{12,8},{1,5},{5,1},{9,13},{13,9},{2,6},{6,2},{1... | collective-permute-start | bytes 393224 | tf_op jit(solution)/shard_map/ppermute | solution.py:124
  35.2 10.0 %collective-permute-start.11 = (bf16[32,2048]{1,0:T(8,128)(2,1)S(1)}, bf16[32,2048]{1,0:T(8,128)(2,1)S(1)}, u32[]{:S(2)}, u32[]{:S(2)}) collective-permute-start(bf16[32,2048]{1,0:T(8,128)(2,1)S(1)} %shard_map.78.refs_4_), channel_id=1, source_target_pairs={{0,3},{1,2},{2,1},{3,0},{4,7},{5,6},{6,5},{7,4},{8,11},{9,10},{10,... | collective-permute-start | bytes 393224 | tf_op jit(solution)/shard_map/ppermute | solution.py:124
  35.2 10.2 %collective-permute-start.10 = (bf16[32,2048]{1,0:T(8,128)(2,1)S(1)}, bf16[32,2048]{1,0:T(8,128)(2,1)S(1)}, u32[]{:S(2)}, u32[]{:S(2)}) collective-permute-start(bf16[32,2048]{1,0:T(8,128)(2,1)S(1)} %shard_map.78.refs_4_), channel_id=1, source_target_pairs={{0,2},{1,3},{2,0},{3,1},{4,6},{5,7},{6,4},{7,5},{8,10},{9,11},{10,... | collective-permute-start | bytes 393224 | tf_op jit(solution)/shard_map/ppermute | solution.py:124
  38.9 6.5 %collective-permute-start.9 = (bf16[32,2048]{1,0:T(8,128)(2,1)S(1)}, bf16[32,2048]{1,0:T(8,128)(2,1)S(1)}, u32[]{:S(2)}, u32[]{:S(2)}) collective-permute-start(bf16[32,2048]{1,0:T(8,128)(2,1)S(1)} %shard_map.78.refs_4_), channel_id=1, source_target_pairs={{0,1},{1,0},{2,3},{3,2},{4,5},{5,4},{6,7},{7,6},{8,9},{9,8},{10,11... | collective-permute-start | bytes 393224 | tf_op jit(solution)/shard_map/ppermute | solution.py:124
  43.5 6.2 %collective-permute-start.20 = (bf16[32,2048]{1,0:T(8,128)(2,1)S(1)}, bf16[32,2048]{1,0:T(8,128)(2,1)S(1)}, u32[]{:S(2)}, u32[]{:S(2)}) collective-permute-start(bf16[32,2048]{1,0:T(8,128)(2,1)S(1)} %shard_map.79.refs_5_.refs_4_), channel_id=1, source_target_pairs={{0,3},{1,2},{2,1},{3,0},{4,7},{5,6},{6,5},{7,4},{8,11},{9,10},{10,... | collective-permute-start | bytes 393224 | tf_op jit(solution)/shard_map/ppermute | solution.py:124
  44.4 7.8 %collective-permute-start.19 = (bf16[32,2048]{1,0:T(8,128)(2,1)S(1)}, bf16[32,2048]{1,0:T(8,128)(2,1)S(1)}, u32[]{:S(2)}, u32[]{:S(2)}) collective-permute-start(bf16[32,2048]{1,0:T(8,128)(2,1)S(1)} %shard_map.79.refs_5_.refs_4_), channel_id=1, source_target_pairs={{0,2},{1,3},{2,0},{3,1},{4,6},{5,7},{6,4},{7,5},{8,10},{9,11},{10,... | collective-permute-start | bytes 393224 | tf_op jit(solution)/shard_map/ppermute | solution.py:124
  45.1 7.0 %collective-permute-start.18 = (bf16[32,2048]{1,0:T(8,128)(2,1)S(1)}, bf16[32,2048]{1,0:T(8,128)(2,1)S(1)}, u32[]{:S(2)}, u32[]{:S(2)}) collective-permute-start(bf16[32,2048]{1,0:T(8,128)(2,1)S(1)} %shard_map.79.refs_5_.refs_4_), channel_id=1, source_target_pairs={{0,1},{1,0},{2,3},{3,2},{4,5},{5,4},{6,7},{7,6},{8,9},{9,8},{10,11... | collective-permute-start | bytes 393224 | tf_op jit(solution)/shard_map/ppermute | solution.py:124
  47.7 8.7 %collective-permute-start.15 = (bf16[32,1650]{1,0:T(8,128)(2,1)S(1)}, bf16[32,1650]{1,0:T(8,128)(2,1)S(1)}, u32[]{:S(2)}, u32[]{:S(2)}) collective-permute-start(bf16[32,1650]{1,0:T(8,128)(2,1)S(1)} %get-tuple-element.74), channel_id=1, source_target_pairs={{0,12},{4,8},{8,4},{12,0},{1,13},{5,9},{9,5},{13,1},{2,14},{6,10},... | collective-permute-start | bytes 316808 | tf_op jit(solution)/shard_map/ppermute | solution.py:124
  49.6 10.1 %collective-permute-start.16 = (bf16[32,1650]{1,0:T(8,128)(2,1)S(1)}, bf16[32,1650]{1,0:T(8,128)(2,1)S(1)}, u32[]{:S(2)}, u32[]{:S(2)}) collective-permute-start(bf16[32,1650]{1,0:T(8,128)(2,1)S(1)} %get-tuple-element.75), channel_id=1, source_target_pairs={{0,8},{4,12},{8,0},{12,4},{1,9},{5,13},{9,1},{13,5},{2,10},{6,14},... | collective-permute-start | bytes 316808 | tf_op jit(solution)/shard_map/ppermute | solution.py:124
  49.6 10.1 %collective-permute-start.17 = (bf16[32,1650]{1,0:T(8,128)(2,1)S(1)}, bf16[32,1650]{1,0:T(8,128)(2,1)S(1)}, u32[]{:S(2)}, u32[]{:S(2)}) collective-permute-start(bf16[32,1650]{1,0:T(8,128)(2,1)S(1)} %get-tuple-element.76), channel_id=1, source_target_pairs={{0,4},{4,0},{8,12},{12,8},{1,5},{5,1},{9,13},{13,9},{2,6},{6,2},{1... | collective-permute-start | bytes 316808 | tf_op jit(solution)/shard_map/ppermute | solution.py:124
  54.4 7.8 %collective-permute-start.21 = (bf16[32,1650]{1,0:T(8,128)(2,1)S(1)}, bf16[32,1650]{1,0:T(8,128)(2,1)S(1)}, u32[]{:S(2)}, u32[]{:S(2)}) collective-permute-start(bf16[32,1650]{1,0:T(8,128)(2,1)S(1)} %get-tuple-element.78), channel_id=1, source_target_pairs={{0,12},{4,8},{8,4},{12,0},{1,13},{5,9},{9,5},{13,1},{2,14},{6,10},... | collective-permute-start | bytes 316808 | tf_op jit(solution)/shard_map/ppermute | solution.py:124
  56.4 12.1 %collective-permute-start.22 = (bf16[32,1650]{1,0:T(8,128)(2,1)S(1)}, bf16[32,1650]{1,0:T(8,128)(2,1)S(1)}, u32[]{:S(2)}, u32[]{:S(2)}) collective-permute-start(bf16[32,1650]{1,0:T(8,128)(2,1)S(1)} %get-tuple-element.79), channel_id=1, source_target_pairs={{0,8},{4,12},{8,0},{12,4},{1,9},{5,13},{9,1},{13,5},{2,10},{6,14},... | collective-permute-start | bytes 316808 | tf_op jit(solution)/shard_map/ppermute | solution.py:124
  56.4 12.1 %collective-permute-start.23 = (bf16[32,1650]{1,0:T(8,128)(2,1)S(1)}, bf16[32,1650]{1,0:T(8,128)(2,1)S(1)}, u32[]{:S(2)}, u32[]{:S(2)}) collective-permute-start(bf16[32,1650]{1,0:T(8,128)(2,1)S(1)} %get-tuple-element.80), channel_id=1, source_target_pairs={{0,4},{4,0},{8,12},{12,8},{1,5},{5,1},{9,13},{13,9},{2,6},{6,2},{1... | collective-permute-start | bytes 316808 | tf_op jit(solution)/shard_map/ppermute | solution.py:124
  (3 other events, 47.7 us)

commit v10 on v9

--- a/solution.py
+++ b/solution.py
@@ -133,7 +133,7 @@
     return sum(part.astype(F32) for part in parts).astype(BF16)
 
 
-def call(kernel, shapes, scratch, *args, after=()):
+def call(kernel, shapes, scratch, *args, after=(), fused=None):
     given = len(args)
 
     def body(*refs):
@@ -145,7 +145,7 @@
         in_specs=[VMEM] * len(args) + [ANY] * len(after),
         out_specs=[VMEM] * len(shapes),
         scratch_shapes=scratch,
-        compiler_params=pltpu.CompilerParams(**PARAMS),
+        compiler_params=pltpu.CompilerParams(allow_input_fusion=fused, **PARAMS),
     )(*args, *after)
 
 
@@ -169,8 +169,9 @@
             [(each, rows_dev + (LANES if h == 0 else 0))] * n_layer,
             [pltpu.VMEM((CODE_ROWS, LANES), jnp.int32)],
             layers[0],
-            indices,
+            indices if h == 0 else before[0],
             after=before,
+            fused=None if h else [False, True],
         )
         before = (turned[0],)
         if h == 0:

time: 69.4 us -> 69.4 us (level)
  no operation moved by 1% of the time
where the time goes in v10:
time: 69.4 us; the launch traced here: 69.2 us
  starting transfers between devices  27.7 us (40%)
  waiting for transfers between devices  26.5 us (38%)
  Pallas kernels  10.9 us (16%)
  local copies, waits for them, and re-layouts  2.29 us (3%)
  other arithmetic  1.7 us (2%)
    ppermute x24, starting transfers between devices, trade(): lax.ppermute(chunk, axis, [(j, j ^ k) for j in range(lax.axis_size(axis))])  27.7 us
    ppermute x24, waiting for transfers between devices, trade(): lax.ppermute(chunk, axis, [(j, j ^ k) for j in range(lax.axis_size(axis))])  26.5 us
    pallas_call x9, Pallas kernels, call(): pl.pallas_call(body, out_shape=[jax.ShapeDtypeStruct(shape, BF16) for sha...  10.9 us
    unnamed x6, local copies, waits for them, and re-layouts  2.29 us
  transfers between devices with their start and end apart: 24, of which 9 were waited for; matrix products, arithmetic and copies ran while one was open for 0% of the time, Pallas kernels for 15%

profile of v10, /device:TPU:0, one launch (start us, length us, event | category | flops | bytes accessed | tf_op | source)
XLA Modules:
  0.0 69.2 jit_solution(5213516742251534025)
XLA Ops:
  0.9 1.3 %copy-done.1 = bf16[1,2048,256]{2,1,0:T(8,128)(2,1)S(1)} copy-done((bf16[1,2048,256]{2,1,0:T(8,128)(2,1)S(1)}, bf16[1,2048,256]{2,1,0:T(8,128)(2,1)}, u32[]{:S(2)}) %copy-start.1) | copy-done | bytes 1048600
  2.7 2.4 %collective-permute-start = (bf16[32,2176]{1,0:T(8,128)(2,1)S(1)}, bf16[32,2176]{1,0:T(8,128)(2,1)S(1)}, u32[]{:S(2)}, u32[]{:S(2)}) collective-permute-start(bf16[32,2176]{1,0:T(8,128)(2,1)S(1)} %get-tuple-element.48), channel_id=1, source_target_pairs={{0,3},{1,2},{2,1},{3,0},{4,7},{5,6},{6,5},{7,4},{8,11},{9,10},{10,... | collective-permute-start | bytes 417800 | tf_op jit(solution)/shard_map/ppermute | solution.py:124
  6.3 0.9 %copy-done.2 = bf16[16,128,64]{1,2,0:T(8,128)(2,1)S(1)} copy-done((bf16[16,128,64]{1,2,0:T(8,128)(2,1)S(1)}, bf16[16,128,64]{1,2,0:T(8,128)(2,1)}, u32[]{:S(2)}) %copy-start.2) | copy-done | bytes 262168
  7.5 1.7 %collective-permute-done.refs_2_.refs_6_ = bf16[32,2176]{1,0:T(8,128)(2,1)S(1)} collective-permute-done((bf16[32,2176]{1,0:T(8,128)(2,1)S(1)}, bf16[32,2176]{1,0:T(8,128)(2,1)S(1)}, u32[]{:S(2)}, u32[]{:S(2)}) %collective-permute-start) | collective-permute-done | bytes 139296 | tf_op jit(solution)/shard_map/ppermute | solution.py:124
  9.2 2.2 %collective-permute-start.3 = (bf16[32,2048]{1,0:T(8,128)(2,1)S(1)}, bf16[32,2048]{1,0:T(8,128)(2,1)S(1)}, u32[]{:S(2)}, u32[]{:S(2)}) collective-permute-start(bf16[32,2048]{1,0:T(8,128)(2,1)S(1)} %get-tuple-element.54), channel_id=1, source_target_pairs={{0,3},{1,2},{2,1},{3,0},{4,7},{5,6},{6,5},{7,4},{8,11},{9,10},{10,... | collective-permute-start | bytes 393224 | tf_op jit(solution)/shard_map/ppermute | solution.py:124
  12.4 2.6 %shard_map.76 = (bf16[32,2048]{1,0:T(8,128)(2,1)S(1)}, bf16[32,2048]{1,0:T(8,128)(2,1)S(1)}, bf16[32,2048]{1,0:T(8,128)(2,1)S(1)}, bf16[32,2048]{1,0:T(8,128)(2,1)S(1)}) custom-call(bf16[32,128,128]{2,1,0:T(8,128)(2,1)S(1)} %shard_map.75.refs_0_, bf16[32,2176]{1,0:T(8,128)(2,1)S(1)} %get-tuple-element.43.refs_1_.refs_2_.refs_5_, ...), custom_call_target="tpu_custom_call" | custom-call | tf_op jit(solution)/shard_map/pallas_call | solution.py:142
  14.9 4.5 %collective-permute-start.6 = (bf16[32,2048]{1,0:T(8,128)(2,1)S(1)}, bf16[32,2048]{1,0:T(8,128)(2,1)S(1)}, u32[]{:S(2)}, u32[]{:S(2)}) collective-permute-start(bf16[32,2048]{1,0:T(8,128)(2,1)S(1)} %get-tuple-element.62), channel_id=1, source_target_pairs={{0,12},{4,8},{8,4},{12,0},{1,13},{5,9},{9,5},{13,1},{2,14},{6,10},... | collective-permute-start | bytes 393224 | tf_op jit(solution)/shard_map/ppermute | solution.py:124
  20.1 2.5 %shard_map.77 = (bf16[32,2048]{1,0:T(8,128)(2,1)S(1)}, bf16[32,2048]{1,0:T(8,128)(2,1)S(1)}, bf16[32,2048]{1,0:T(8,128)(2,1)S(1)}, bf16[32,2048]{1,0:T(8,128)(2,1)S(1)}) custom-call(bf16[32,128,128]{2,1,0:T(8,128)(2,1)S(1)} %shard_map.75.refs_0_, bf16[32,2176]{1,0:T(8,128)(2,1)S(1)} %get-tuple-element.43.refs_1_.refs_2_.refs_5_, ...), custom_call_target="tpu_custom_call" | custom-call | tf_op jit(solution)/shard_map/pallas_call | solution.py:142
  22.6 1.2 %collective-permute-done.6.refs_1_ = bf16[32,2048]{1,0:T(8,128)(2,1)S(1)} collective-permute-done((bf16[32,2048]{1,0:T(8,128)(2,1)S(1)}, bf16[32,2048]{1,0:T(8,128)(2,1)S(1)}, u32[]{:S(2)}, u32[]{:S(2)}) %collective-permute-start.6) | collective-permute-done | bytes 131104 | tf_op jit(solution)/shard_map/ppermute | solution.py:124
  23.8 6.9 %collective-permute-done.7.refs_2_ = bf16[32,2048]{1,0:T(8,128)(2,1)S(1)} collective-permute-done((bf16[32,2048]{1,0:T(8,128)(2,1)S(1)}, bf16[32,2048]{1,0:T(8,128)(2,1)S(1)}, u32[]{:S(2)}, u32[]{:S(2)}) %collective-permute-start.7) | collective-permute-done | bytes 131104 | tf_op jit(solution)/shard_map/ppermute | solution.py:124
  30.7 2.7 %collective-permute-start.12 = (bf16[32,2048]{1,0:T(8,128)(2,1)S(1)}, bf16[32,2048]{1,0:T(8,128)(2,1)S(1)}, u32[]{:S(2)}, u32[]{:S(2)}) collective-permute-start(bf16[32,2048]{1,0:T(8,128)(2,1)S(1)} %get-tuple-element.70), channel_id=1, source_target_pairs={{0,12},{4,8},{8,4},{12,0},{1,13},{5,9},{9,5},{13,1},{2,14},{6,10},... | collective-permute-start | bytes 393224 | tf_op jit(solution)/shard_map/ppermute | solution.py:124
  33.4 1.7 %collective-permute-start.14 = (bf16[32,2048]{1,0:T(8,128)(2,1)S(1)}, bf16[32,2048]{1,0:T(8,128)(2,1)S(1)}, u32[]{:S(2)}, u32[]{:S(2)}) collective-permute-start(bf16[32,2048]{1,0:T(8,128)(2,1)S(1)} %get-tuple-element.72), channel_id=1, source_target_pairs={{0,4},{4,0},{8,12},{12,8},{1,5},{5,1},{9,13},{13,9},{2,6},{6,2},{1... | collective-permute-start | bytes 393224 | tf_op jit(solution)/shard_map/ppermute | solution.py:124
  35.2 1.6 %collective-permute-start.10 = (bf16[32,2048]{1,0:T(8,128)(2,1)S(1)}, bf16[32,2048]{1,0:T(8,128)(2,1)S(1)}, u32[]{:S(2)}, u32[]{:S(2)}) collective-permute-start(bf16[32,2048]{1,0:T(8,128)(2,1)S(1)} %shard_map.78.refs_4_), channel_id=1, source_target_pairs={{0,2},{1,3},{2,0},{3,1},{4,6},{5,7},{6,4},{7,5},{8,10},{9,11},{10,... | collective-permute-start | bytes 393224 | tf_op jit(solution)/shard_map/ppermute | solution.py:124
  36.8 2.1 %collective-permute-done.12.refs_1_ = bf16[32,2048]{1,0:T(8,128)(2,1)S(1)} collective-permute-done((bf16[32,2048]{1,0:T(8,128)(2,1)S(1)}, bf16[32,2048]{1,0:T(8,128)(2,1)S(1)}, u32[]{:S(2)}, u32[]{:S(2)}) %collective-permute-start.12) | collective-permute-done | bytes 131104 | tf_op jit(solution)/shard_map/ppermute | solution.py:124
  38.9 4.5 %collective-permute-done.13.refs_2_ = bf16[32,2048]{1,0:T(8,128)(2,1)S(1)} collective-permute-done((bf16[32,2048]{1,0:T(8,128)(2,1)S(1)}, bf16[32,2048]{1,0:T(8,128)(2,1)S(1)}, u32[]{:S(2)}, u32[]{:S(2)}) %collective-permute-start.13) | collective-permute-done | bytes 131104 | tf_op jit(solution)/shard_map/ppermute | solution.py:124
  43.5 0.9 %collective-permute-start.20 = (bf16[32,2048]{1,0:T(8,128)(2,1)S(1)}, bf16[32,2048]{1,0:T(8,128)(2,1)S(1)}, u32[]{:S(2)}, u32[]{:S(2)}) collective-permute-start(bf16[32,2048]{1,0:T(8,128)(2,1)S(1)} %shard_map.79.refs_5_.refs_4_), channel_id=1, source_target_pairs={{0,3},{1,2},{2,1},{3,0},{4,7},{5,6},{6,5},{7,4},{8,11},{9,10},{10,... | collective-permute-start | bytes 393224 | tf_op jit(solution)/shard_map/ppermute | solution.py:124
  45.4 2.3 %shard_map.80 = (bf16[32,1650]{1,0:T(8,128)(2,1)S(1)}, bf16[32,1650]{1,0:T(8,128)(2,1)S(1)}, bf16[32,1650]{1,0:T(8,128)(2,1)S(1)}, bf16[32,1650]{1,0:T(8,128)(2,1)S(1)}) custom-call(bf16[1650,2048]{1,0:T(8,128)(2,1)S(1)} %bitcast.4, bf16[32,2048]{1,0:T(8,128)(2,1)S(1)} %collective-permute-done.9.refs_1_, ...), custom_call_target="tpu_custom_call" | custom-call | tf_op jit(solution)/shard_map/pallas_call | solution.py:142
  47.7 2.0 %collective-permute-start.15 = (bf16[32,1650]{1,0:T(8,128)(2,1)S(1)}, bf16[32,1650]{1,0:T(8,128)(2,1)S(1)}, u32[]{:S(2)}, u32[]{:S(2)}) collective-permute-start(bf16[32,1650]{1,0:T(8,128)(2,1)S(1)} %get-tuple-element.74), channel_id=1, source_target_pairs={{0,12},{4,8},{8,4},{12,0},{1,13},{5,9},{9,5},{13,1},{2,14},{6,10},... | collective-permute-start | bytes 316808 | tf_op jit(solution)/shard_map/ppermute | solution.py:124
  49.6 2.5 %collective-permute-start.17 = (bf16[32,1650]{1,0:T(8,128)(2,1)S(1)}, bf16[32,1650]{1,0:T(8,128)(2,1)S(1)}, u32[]{:S(2)}, u32[]{:S(2)}) collective-permute-start(bf16[32,1650]{1,0:T(8,128)(2,1)S(1)} %get-tuple-element.76), channel_id=1, source_target_pairs={{0,4},{4,0},{8,12},{12,8},{1,5},{5,1},{9,13},{13,9},{2,6},{6,2},{1... | collective-permute-start | bytes 316808 | tf_op jit(solution)/shard_map/ppermute | solution.py:124
  52.1 2.3 %shard_map.81 = (bf16[32,1650]{1,0:T(8,128)(2,1)S(1)}, bf16[32,1650]{1,0:T(8,128)(2,1)S(1)}, bf16[32,1650]{1,0:T(8,128)(2,1)S(1)}, bf16[32,1650]{1,0:T(8,128)(2,1)S(1)}) custom-call(bf16[1650,2048]{1,0:T(8,128)(2,1)S(1)} %bitcast.5, bf16[32,2048]{1,0:T(8,128)(2,1)S(1)} %collective-permute-done.18.refs_1_, ...), custom_call_target="tpu_custom_call" | custom-call | tf_op jit(solution)/shard_map/pallas_call | solution.py:142
  54.4 2.0 %collective-permute-start.21 = (bf16[32,1650]{1,0:T(8,128)(2,1)S(1)}, bf16[32,1650]{1,0:T(8,128)(2,1)S(1)}, u32[]{:S(2)}, u32[]{:S(2)}) collective-permute-start(bf16[32,1650]{1,0:T(8,128)(2,1)S(1)} %get-tuple-element.78), channel_id=1, source_target_pairs={{0,12},{4,8},{8,4},{12,0},{1,13},{5,9},{9,5},{13,1},{2,14},{6,10},... | collective-permute-start | bytes 316808 | tf_op jit(solution)/shard_map/ppermute | solution.py:124
  56.4 2.5 %collective-permute-start.23 = (bf16[32,1650]{1,0:T(8,128)(2,1)S(1)}, bf16[32,1650]{1,0:T(8,128)(2,1)S(1)}, u32[]{:S(2)}, u32[]{:S(2)}) collective-permute-start(bf16[32,1650]{1,0:T(8,128)(2,1)S(1)} %get-tuple-element.80), channel_id=1, source_target_pairs={{0,4},{4,0},{8,12},{12,8},{1,5},{5,1},{9,13},{13,9},{2,6},{6,2},{1... | collective-permute-start | bytes 316808 | tf_op jit(solution)/shard_map/ppermute | solution.py:124
  59.7 2.5 %collective-permute-done.21 = bf16[32,1650]{1,0:T(8,128)(2,1)S(1)} collective-permute-done((bf16[32,1650]{1,0:T(8,128)(2,1)S(1)}, bf16[32,1650]{1,0:T(8,128)(2,1)S(1)}, u32[]{:S(2)}, u32[]{:S(2)}) %collective-permute-start.21) | collective-permute-done | bytes 105632 | tf_op jit(solution)/shard_map/ppermute | solution.py:124
  62.2 6.2 %collective-permute-done.22 = bf16[32,1650]{1,0:T(8,128)(2,1)S(1)} collective-permute-done((bf16[32,1650]{1,0:T(8,128)(2,1)S(1)}, bf16[32,1650]{1,0:T(8,128)(2,1)S(1)}, u32[]{:S(2)}, u32[]{:S(2)}) %collective-permute-start.22) | collective-permute-done | bytes 105632 | tf_op jit(solution)/shard_map/ppermute | solution.py:124
  (43 shorter events, 7.2 us)
Async XLA Ops:
  2.7 6.5 %collective-permute-start = (bf16[32,2176]{1,0:T(8,128)(2,1)S(1)}, bf16[32,2176]{1,0:T(8,128)(2,1)S(1)}, u32[]{:S(2)}, u32[]{:S(2)}) collective-permute-start(bf16[32,2176]{1,0:T(8,128)(2,1)S(1)} %get-tuple-element.48), channel_id=1, source_target_pairs={{0,3},{1,2},{2,1},{3,0},{4,7},{5,6},{6,5},{7,4},{8,11},{9,10},{10,... | collective-permute-start | bytes 417800 | tf_op jit(solution)/shard_map/ppermute | solution.py:124
  5.1 7.2 %collective-permute-start.1 = (bf16[32,2176]{1,0:T(8,128)(2,1)S(1)}, bf16[32,2176]{1,0:T(8,128)(2,1)S(1)}, u32[]{:S(2)}, u32[]{:S(2)}) collective-permute-start(bf16[32,2176]{1,0:T(8,128)(2,1)S(1)} %get-tuple-element.51), channel_id=1, source_target_pairs={{0,2},{1,3},{2,0},{3,1},{4,6},{5,7},{6,4},{7,5},{8,10},{9,11},{10,... | collective-permute-start | bytes 417800 | tf_op jit(solution)/shard_map/ppermute | solution.py:124
  5.8 6.6 %collective-permute-start.2 = (bf16[32,2176]{1,0:T(8,128)(2,1)S(1)}, bf16[32,2176]{1,0:T(8,128)(2,1)S(1)}, u32[]{:S(2)}, u32[]{:S(2)}) collective-permute-start(bf16[32,2176]{1,0:T(8,128)(2,1)S(1)} %get-tuple-element.52), channel_id=1, source_target_pairs={{0,1},{1,0},{2,3},{3,2},{4,5},{5,4},{6,7},{7,6},{8,9},{9,8},{10,11... | collective-permute-start | bytes 417800 | tf_op jit(solution)/shard_map/ppermute | solution.py:124
  9.2 10.2 %collective-permute-start.3 = (bf16[32,2048]{1,0:T(8,128)(2,1)S(1)}, bf16[32,2048]{1,0:T(8,128)(2,1)S(1)}, u32[]{:S(2)}, u32[]{:S(2)}) collective-permute-start(bf16[32,2048]{1,0:T(8,128)(2,1)S(1)} %get-tuple-element.54), channel_id=1, source_target_pairs={{0,3},{1,2},{2,1},{3,0},{4,7},{5,6},{6,5},{7,4},{8,11},{9,10},{10,... | collective-permute-start | bytes 393224 | tf_op jit(solution)/shard_map/ppermute | solution.py:124
  11.4 8.7 %collective-permute-start.4 = (bf16[32,2048]{1,0:T(8,128)(2,1)S(1)}, bf16[32,2048]{1,0:T(8,128)(2,1)S(1)}, u32[]{:S(2)}, u32[]{:S(2)}) collective-permute-start(bf16[32,2048]{1,0:T(8,128)(2,1)S(1)} %get-tuple-element.55), channel_id=1, source_target_pairs={{0,2},{1,3},{2,0},{3,1},{4,6},{5,7},{6,4},{7,5},{8,10},{9,11},{10,... | collective-permute-start | bytes 393224 | tf_op jit(solution)/shard_map/ppermute | solution.py:124
  11.7 8.4 %collective-permute-start.5 = (bf16[32,2048]{1,0:T(8,128)(2,1)S(1)}, bf16[32,2048]{1,0:T(8,128)(2,1)S(1)}, u32[]{:S(2)}, u32[]{:S(2)}) collective-permute-start(bf16[32,2048]{1,0:T(8,128)(2,1)S(1)} %get-tuple-element.56), channel_id=1, source_target_pairs={{0,1},{1,0},{2,3},{3,2},{4,5},{5,4},{6,7},{7,6},{8,9},{9,8},{10,11... | collective-permute-start | bytes 393224 | tf_op jit(solution)/shard_map/ppermute | solution.py:124
  14.9 8.9 %collective-permute-start.6 = (bf16[32,2048]{1,0:T(8,128)(2,1)S(1)}, bf16[32,2048]{1,0:T(8,128)(2,1)S(1)}, u32[]{:S(2)}, u32[]{:S(2)}) collective-permute-start(bf16[32,2048]{1,0:T(8,128)(2,1)S(1)} %get-tuple-element.62), channel_id=1, source_target_pairs={{0,12},{4,8},{8,4},{12,0},{1,13},{5,9},{9,5},{13,1},{2,14},{6,10},... | collective-permute-start | bytes 393224 | tf_op jit(solution)/shard_map/ppermute | solution.py:124
  19.4 11.3 %collective-permute-start.7 = (bf16[32,2048]{1,0:T(8,128)(2,1)S(1)}, bf16[32,2048]{1,0:T(8,128)(2,1)S(1)}, u32[]{:S(2)}, u32[]{:S(2)}) collective-permute-start(bf16[32,2048]{1,0:T(8,128)(2,1)S(1)} %get-tuple-element.63), channel_id=1, source_target_pairs={{0,8},{4,12},{8,0},{12,4},{1,9},{5,13},{9,1},{13,5},{2,10},{6,14},... | collective-permute-start | bytes 393224 | tf_op jit(solution)/shard_map/ppermute | solution.py:124
  19.4 11.3 %collective-permute-start.8 = (bf16[32,2048]{1,0:T(8,128)(2,1)S(1)}, bf16[32,2048]{1,0:T(8,128)(2,1)S(1)}, u32[]{:S(2)}, u32[]{:S(2)}) collective-permute-start(bf16[32,2048]{1,0:T(8,128)(2,1)S(1)} %get-tuple-element.64), channel_id=1, source_target_pairs={{0,4},{4,0},{8,12},{12,8},{1,5},{5,1},{9,13},{13,9},{2,6},{6,2},{1... | collective-permute-start | bytes 393224 | tf_op jit(solution)/shard_map/ppermute | solution.py:124
  30.7 8.2 %collective-permute-start.12 = (bf16[32,2048]{1,0:T(8,128)(2,1)S(1)}, bf16[32,2048]{1,0:T(8,128)(2,1)S(1)}, u32[]{:S(2)}, u32[]{:S(2)}) collective-permute-start(bf16[32,2048]{1,0:T(8,128)(2,1)S(1)} %get-tuple-element.70), channel_id=1, source_target_pairs={{0,12},{4,8},{8,4},{12,0},{1,13},{5,9},{9,5},{13,1},{2,14},{6,10},... | collective-permute-start | bytes 393224 | tf_op jit(solution)/shard_map/ppermute | solution.py:124
  33.4 10.0 %collective-permute-start.13 = (bf16[32,2048]{1,0:T(8,128)(2,1)S(1)}, bf16[32,2048]{1,0:T(8,128)(2,1)S(1)}, u32[]{:S(2)}, u32[]{:S(2)}) collective-permute-start(bf16[32,2048]{1,0:T(8,128)(2,1)S(1)} %get-tuple-element.71), channel_id=1, source_target_pairs={{0,8},{4,12},{8,0},{12,4},{1,9},{5,13},{9,1},{13,5},{2,10},{6,14},... | collective-permute-start | bytes 393224 | tf_op jit(solution)/shard_map/ppermute | solution.py:124
  33.4 10.0 %collective-permute-start.14 = (bf16[32,2048]{1,0:T(8,128)(2,1)S(1)}, bf16[32,2048]{1,0:T(8,128)(2,1)S(1)}, u32[]{:S(2)}, u32[]{:S(2)}) collective-permute-start(bf16[32,2048]{1,0:T(8,128)(2,1)S(1)} %get-tuple-element.72), channel_id=1, source_target_pairs={{0,4},{4,0},{8,12},{12,8},{1,5},{5,1},{9,13},{13,9},{2,6},{6,2},{1... | collective-permute-start | bytes 393224 | tf_op jit(solution)/shard_map/ppermute | solution.py:124
  35.2 10.0 %collective-permute-start.11 = (bf16[32,2048]{1,0:T(8,128)(2,1)S(1)}, bf16[32,2048]{1,0:T(8,128)(2,1)S(1)}, u32[]{:S(2)}, u32[]{:S(2)}) collective-permute-start(bf16[32,2048]{1,0:T(8,128)(2,1)S(1)} %shard_map.78.refs_4_), channel_id=1, source_target_pairs={{0,3},{1,2},{2,1},{3,0},{4,7},{5,6},{6,5},{7,4},{8,11},{9,10},{10,... | collective-permute-start | bytes 393224 | tf_op jit(solution)/shard_map/ppermute | solution.py:124
  35.2 10.2 %collective-permute-start.10 = (bf16[32,2048]{1,0:T(8,128)(2,1)S(1)}, bf16[32,2048]{1,0:T(8,128)(2,1)S(1)}, u32[]{:S(2)}, u32[]{:S(2)}) collective-permute-start(bf16[32,2048]{1,0:T(8,128)(2,1)S(1)} %shard_map.78.refs_4_), channel_id=1, source_target_pairs={{0,2},{1,3},{2,0},{3,1},{4,6},{5,7},{6,4},{7,5},{8,10},{9,11},{10,... | collective-permute-start | bytes 393224 | tf_op jit(solution)/shard_map/ppermute | solution.py:124
  38.9 6.5 %collective-permute-start.9 = (bf16[32,2048]{1,0:T(8,128)(2,1)S(1)}, bf16[32,2048]{1,0:T(8,128)(2,1)S(1)}, u32[]{:S(2)}, u32[]{:S(2)}) collective-permute-start(bf16[32,2048]{1,0:T(8,128)(2,1)S(1)} %shard_map.78.refs_4_), channel_id=1, source_target_pairs={{0,1},{1,0},{2,3},{3,2},{4,5},{5,4},{6,7},{7,6},{8,9},{9,8},{10,11... | collective-permute-start | bytes 393224 | tf_op jit(solution)/shard_map/ppermute | solution.py:124
  43.5 6.2 %collective-permute-start.20 = (bf16[32,2048]{1,0:T(8,128)(2,1)S(1)}, bf16[32,2048]{1,0:T(8,128)(2,1)S(1)}, u32[]{:S(2)}, u32[]{:S(2)}) collective-permute-start(bf16[32,2048]{1,0:T(8,128)(2,1)S(1)} %shard_map.79.refs_5_.refs_4_), channel_id=1, source_target_pairs={{0,3},{1,2},{2,1},{3,0},{4,7},{5,6},{6,5},{7,4},{8,11},{9,10},{10,... | collective-permute-start | bytes 393224 | tf_op jit(solution)/shard_map/ppermute | solution.py:124
  44.4 7.8 %collective-permute-start.19 = (bf16[32,2048]{1,0:T(8,128)(2,1)S(1)}, bf16[32,2048]{1,0:T(8,128)(2,1)S(1)}, u32[]{:S(2)}, u32[]{:S(2)}) collective-permute-start(bf16[32,2048]{1,0:T(8,128)(2,1)S(1)} %shard_map.79.refs_5_.refs_4_), channel_id=1, source_target_pairs={{0,2},{1,3},{2,0},{3,1},{4,6},{5,7},{6,4},{7,5},{8,10},{9,11},{10,... | collective-permute-start | bytes 393224 | tf_op jit(solution)/shard_map/ppermute | solution.py:124
  45.1 7.0 %collective-permute-start.18 = (bf16[32,2048]{1,0:T(8,128)(2,1)S(1)}, bf16[32,2048]{1,0:T(8,128)(2,1)S(1)}, u32[]{:S(2)}, u32[]{:S(2)}) collective-permute-start(bf16[32,2048]{1,0:T(8,128)(2,1)S(1)} %shard_map.79.refs_5_.refs_4_), channel_id=1, source_target_pairs={{0,1},{1,0},{2,3},{3,2},{4,5},{5,4},{6,7},{7,6},{8,9},{9,8},{10,11... | collective-permute-start | bytes 393224 | tf_op jit(solution)/shard_map/ppermute | solution.py:124
  47.7 8.7 %collective-permute-start.15 = (bf16[32,1650]{1,0:T(8,128)(2,1)S(1)}, bf16[32,1650]{1,0:T(8,128)(2,1)S(1)}, u32[]{:S(2)}, u32[]{:S(2)}) collective-permute-start(bf16[32,1650]{1,0:T(8,128)(2,1)S(1)} %get-tuple-element.74), channel_id=1, source_target_pairs={{0,12},{4,8},{8,4},{12,0},{1,13},{5,9},{9,5},{13,1},{2,14},{6,10},... | collective-permute-start | bytes 316808 | tf_op jit(solution)/shard_map/ppermute | solution.py:124
  49.6 10.0 %collective-permute-start.16 = (bf16[32,1650]{1,0:T(8,128)(2,1)S(1)}, bf16[32,1650]{1,0:T(8,128)(2,1)S(1)}, u32[]{:S(2)}, u32[]{:S(2)}) collective-permute-start(bf16[32,1650]{1,0:T(8,128)(2,1)S(1)} %get-tuple-element.75), channel_id=1, source_target_pairs={{0,8},{4,12},{8,0},{12,4},{1,9},{5,13},{9,1},{13,5},{2,10},{6,14},... | collective-permute-start | bytes 316808 | tf_op jit(solution)/shard_map/ppermute | solution.py:124
  49.6 10.0 %collective-permute-start.17 = (bf16[32,1650]{1,0:T(8,128)(2,1)S(1)}, bf16[32,1650]{1,0:T(8,128)(2,1)S(1)}, u32[]{:S(2)}, u32[]{:S(2)}) collective-permute-start(bf16[32,1650]{1,0:T(8,128)(2,1)S(1)} %get-tuple-element.76), channel_id=1, source_target_pairs={{0,4},{4,0},{8,12},{12,8},{1,5},{5,1},{9,13},{13,9},{2,6},{6,2},{1... | collective-permute-start | bytes 316808 | tf_op jit(solution)/shard_map/ppermute | solution.py:124
  54.4 7.8 %collective-permute-start.21 = (bf16[32,1650]{1,0:T(8,128)(2,1)S(1)}, bf16[32,1650]{1,0:T(8,128)(2,1)S(1)}, u32[]{:S(2)}, u32[]{:S(2)}) collective-permute-start(bf16[32,1650]{1,0:T(8,128)(2,1)S(1)} %get-tuple-element.78), channel_id=1, source_target_pairs={{0,12},{4,8},{8,4},{12,0},{1,13},{5,9},{9,5},{13,1},{2,14},{6,10},... | collective-permute-start | bytes 316808 | tf_op jit(solution)/shard_map/ppermute | solution.py:124
  56.4 12.0 %collective-permute-start.22 = (bf16[32,1650]{1,0:T(8,128)(2,1)S(1)}, bf16[32,1650]{1,0:T(8,128)(2,1)S(1)}, u32[]{:S(2)}, u32[]{:S(2)}) collective-permute-start(bf16[32,1650]{1,0:T(8,128)(2,1)S(1)} %get-tuple-element.79), channel_id=1, source_target_pairs={{0,8},{4,12},{8,0},{12,4},{1,9},{5,13},{9,1},{13,5},{2,10},{6,14},... | collective-permute-start | bytes 316808 | tf_op jit(solution)/shard_map/ppermute | solution.py:124
  56.4 12.0 %collective-permute-start.23 = (bf16[32,1650]{1,0:T(8,128)(2,1)S(1)}, bf16[32,1650]{1,0:T(8,128)(2,1)S(1)}, u32[]{:S(2)}, u32[]{:S(2)}) collective-permute-start(bf16[32,1650]{1,0:T(8,128)(2,1)S(1)} %get-tuple-element.80), channel_id=1, source_target_pairs={{0,4},{4,0},{8,12},{12,8},{1,5},{5,1},{9,13},{13,9},{2,6},{6,2},{1... | collective-permute-start | bytes 316808 | tf_op jit(solution)/shard_map/ppermute | solution.py:124
  (3 other events, 47.7 us)

commit v11 on v9

--- a/solution.py
+++ b/solution.py
@@ -42,19 +42,15 @@
             out[:CODE_ROWS, rows_dev:] = tail
 
 
-def pad_kernel(table_ref, padded):
-    weights, block_rows = table_ref.shape[:2]
-    padded[...] = jnp.zeros_like(padded)
-    for half in range(LANES // block_rows):
-        start = half * block_rows
-        padded[half * weights : (half + 1) * weights, start : start + block_rows] = table_ref[...]
-
-
-def pupil_kernel(n_layer, n_row, entries, unroll, padded, *refs):
+def near_kernel(table_ref, near):
+    near[...] = table_ref[...]
+
+
+def pupil_kernel(n_layer, n_row, entries, block_rows, near, *refs):
     coded, parts = refs[:n_layer], refs[n_layer : 2 * n_layer]
     outs = refs[2 * n_layer : 2 * n_layer + n_row]
-    total, codes, code, sem = refs[-4:]
-    weights = padded.shape[0] // 2
+    total, codes, code, shifted, sem = refs[-5:]
+    packed = LANES // block_rows
     owned = outs[0].shape[1] // LANES
     for j, ref in enumerate(coded):
         tail = ref[:CODE_ROWS, ref.shape[1] - LANES :]
@@ -62,24 +58,24 @@
     copy = pltpu.make_async_copy(codes, code, sem)
     copy.start()
     total[...] = jnp.zeros_like(total)
+    for j, part in enumerate(parts):
+        rows = shifted.shape[3]
+        found = part[:, :rows].astype(F32)
+        for p in range(packed):
+            moved = pltpu.roll(found, rows - p * block_rows, 1) if p else found
+            shifted[j, p] = moved.astype(BF16)
     copy.wait()
-    for j, part in enumerate(parts):
-        base = j * CODE_ROWS
-
-        def step(group, carry):
-            terms = []
-            for u in range(unroll):
-                e = group * unroll + u
-                block = code[base + 2, e]
-                source = part[:, pl.ds(pl.multiple_of((block // 2) * LANES, LANES), LANES)]
-                weight = padded[lax.rem(block, 2) * weights + code[base + 3, e]]
-                dest = code[base, e] * owned + code[base + 1, e]
-                terms.append((dest, jnp.dot(source, weight, preferred_element_type=F32)))
-            for dest, term in terms:
-                total[dest] += term
-            return carry
-
-        lax.fori_loop(0, entries // unroll, step, 0)
+    for j in range(n_layer):
+        base, terms = j * CODE_ROWS, []
+        for e in range(entries):
+            block = code[base + 2, e]
+            lanes = pl.ds(pl.multiple_of((block // packed) * LANES, LANES), LANES)
+            source = shifted[j, lax.rem(block, packed), :, lanes][:, :block_rows]
+            weight = near[code[base + 3, e]]
+            dest = code[base, e] * owned + code[base + 1, e]
+            terms.append((dest, jnp.dot(source, weight, preferred_element_type=F32)))
+        for dest, term in terms:
+            total[dest] += term
     me = lax.axis_index("row")
     for i, out in enumerate(outs):
         k = (n_row - i) % n_row
@@ -90,6 +86,16 @@
 
 def sum_kernel(*refs):
     refs[-1][...] = sum(ref[...].astype(F32) for ref in refs[:-1]).astype(BF16)
+
+
+def finish_kernel(*refs):
+    parts, out = refs[:-1], refs[-1]
+    rows = parts[0].shape[0]
+    halves = out.shape[0] // rows
+    each = len(parts) // halves
+    for h in range(halves):
+        found = sum(part[...].astype(F32) for part in parts[h * each : (h + 1) * each])
+        out[h * rows : (h + 1) * rows] = found.astype(BF16)
 
 
 def fit_kernel(n_layer, n_row, fitting_ref, *refs):
@@ -129,10 +135,6 @@
     return [trade(chunk, axis, n - i) if i else chunk for i, chunk in enumerate(chunks)]
 
 
-def total_of(parts):
-    return sum(part.astype(F32) for part in parts).astype(BF16)
-
-
 def call(kernel, shapes, scratch, *args, after=()):
     given = len(args)
 
@@ -174,29 +176,30 @@
         )
         before = (turned[0],)
         if h == 0:
-            (padded,) = call(
-                pad_kernel,
-                [(LANES // block_rows * weights, LANES, slice_rows)],
+            (near,) = call(
+                near_kernel,
+                [(weights, block_rows, slice_rows)],
                 [],
                 jnp.swapaxes(table, 1, 2),
                 after=before,
             )
         else:
-            turned, parts[-1][1], padded = lax.optimization_barrier((turned, parts[-1][1], padded))
+            turned, parts[-1][1], near = lax.optimization_barrier((turned, parts[-1][1], near))
         parts.append(exchange(turned, "layer"))
 
     received, before = [], ()
     for h in range(halves):
         shares = call(
-            functools.partial(pupil_kernel, n_layer, n_row, entries, entries),
+            functools.partial(pupil_kernel, n_layer, n_row, entries, block_rows),
             [(each, points)] * n_row,
             [
                 pltpu.VMEM((n_row * owned, each, slice_rows), F32),
                 pltpu.VMEM((n_layer * CODE_ROWS, LANES), jnp.int32),
                 pltpu.SMEM((n_layer * CODE_ROWS, LANES), jnp.int32),
+                pltpu.VMEM((n_layer, LANES // block_rows, each, rows_dev), BF16),
                 pltpu.SemaphoreType.DMA,
             ],
-            padded,
+            near,
             *parts[0],
             *parts[h],
             after=before,
@@ -220,7 +223,8 @@
             after=pupils[h + 1 :],
         )
         results.append(exchange(partial, "row"))
-    return jnp.concatenate([total_of(result) for result in results], 0)
+    (out,) = call(finish_kernel, [(chunk, actuators)], [], *(part for got in results for part in got))
+    return out
 
 
 def solution(mesh):

time: 69.4 us -> 69.3 us (level)
  other arithmetic: 1.7 us -> 0.86 us
    concatenate x1 -> x0, other arithmetic: 0.7 us -> none  [local(): return jnp.concatenate([total_of(result) for result in results], 0)]
    pallas_call x9 -> x10, Pallas kernels: 10.9 us -> 11.4 us  [call(): pl.pallas_call(body, out_shape=[jax.ShapeDtypeStruct(shape, BF16) for sha...]
where the time goes in v11:
time: 69.3 us; the launch traced here: 69.2 us
  starting transfers between devices  27.7 us (40%)
  waiting for transfers between devices  26.7 us (39%)
  Pallas kernels  11.4 us (16%)
  local copies, waits for them, and re-layouts  2.29 us (3%)
  other arithmetic  0.86 us (1%)
    ppermute x24, starting transfers between devices, trade(): lax.ppermute(chunk, axis, [(j, j ^ k) for j in range(lax.axis_size(axis))])  27.7 us
    ppermute x24, waiting for transfers between devices, trade(): lax.ppermute(chunk, axis, [(j, j ^ k) for j in range(lax.axis_size(axis))])  26.7 us
    pallas_call x10, Pallas kernels, call(): pl.pallas_call(body, out_shape=[jax.ShapeDtypeStruct(shape, BF16) for sha...  11.4 us
    unnamed x6, local copies, waits for them, and re-layouts  2.29 us
  transfers between devices with their start and end apart: 24, of which 9 were waited for; matrix products, arithmetic and copies ran while one was open for 0% of the time, Pallas kernels for 15%

profile of v11, /device:TPU:0, one launch (start us, length us, event | category | flops | bytes accessed | tf_op | source)
XLA Modules:
  0.0 69.2 jit_solution(12127843236646798060)
XLA Ops:
  0.9 1.3 %copy-done.1 = bf16[1,2048,256]{2,1,0:T(8,128)(2,1)S(1)} copy-done((bf16[1,2048,256]{2,1,0:T(8,128)(2,1)S(1)}, bf16[1,2048,256]{2,1,0:T(8,128)(2,1)}, u32[]{:S(2)}) %copy-start.1) | copy-done | bytes 1048600
  2.7 2.4 %collective-permute-start = (bf16[32,2176]{1,0:T(8,128)(2,1)S(1)}, bf16[32,2176]{1,0:T(8,128)(2,1)S(1)}, u32[]{:S(2)}, u32[]{:S(2)}) collective-permute-start(bf16[32,2176]{1,0:T(8,128)(2,1)S(1)} %get-tuple-element.48), channel_id=1, source_target_pairs={{0,3},{1,2},{2,1},{3,0},{4,7},{5,6},{6,5},{7,4},{8,11},{9,10},{10,... | collective-permute-start | bytes 417800 | tf_op jit(solution)/shard_map/ppermute | solution.py:130
  6.3 0.9 %copy-done.2 = bf16[16,128,64]{1,2,0:T(8,128)(2,1)S(1)} copy-done((bf16[16,128,64]{1,2,0:T(8,128)(2,1)S(1)}, bf16[16,128,64]{1,2,0:T(8,128)(2,1)}, u32[]{:S(2)}) %copy-start.2) | copy-done | bytes 262168
  7.3 1.9 %collective-permute-done.refs_2_.refs_6_ = bf16[32,2176]{1,0:T(8,128)(2,1)S(1)} collective-permute-done((bf16[32,2176]{1,0:T(8,128)(2,1)S(1)}, bf16[32,2176]{1,0:T(8,128)(2,1)S(1)}, u32[]{:S(2)}, u32[]{:S(2)}) %collective-permute-start) | collective-permute-done | bytes 139296 | tf_op jit(solution)/shard_map/ppermute | solution.py:130
  9.2 2.2 %collective-permute-start.3 = (bf16[32,2048]{1,0:T(8,128)(2,1)S(1)}, bf16[32,2048]{1,0:T(8,128)(2,1)S(1)}, u32[]{:S(2)}, u32[]{:S(2)}) collective-permute-start(bf16[32,2048]{1,0:T(8,128)(2,1)S(1)} %get-tuple-element.54), channel_id=1, source_target_pairs={{0,3},{1,2},{2,1},{3,0},{4,7},{5,6},{6,5},{7,4},{8,11},{9,10},{10,... | collective-permute-start | bytes 393224 | tf_op jit(solution)/shard_map/ppermute | solution.py:130
  12.4 2.5 %shard_map.76 = (bf16[32,2048]{1,0:T(8,128)(2,1)S(1)}, bf16[32,2048]{1,0:T(8,128)(2,1)S(1)}, bf16[32,2048]{1,0:T(8,128)(2,1)S(1)}, bf16[32,2048]{1,0:T(8,128)(2,1)S(1)}) custom-call(bf16[16,64,128]{2,1,0:T(8,128)(2,1)S(1)} %shard_map.75.refs_0_, bf16[32,2176]{1,0:T(8,128)(2,1)S(1)} %get-tuple-element.43.refs_2_.refs_1_.refs_5_, ...), custom_call_target="tpu_custom_call" | custom-call | tf_op jit(solution)/shard_map/pallas_call | solution.py:144
  14.9 4.5 %collective-permute-start.6 = (bf16[32,2048]{1,0:T(8,128)(2,1)S(1)}, bf16[32,2048]{1,0:T(8,128)(2,1)S(1)}, u32[]{:S(2)}, u32[]{:S(2)}) collective-permute-start(bf16[32,2048]{1,0:T(8,128)(2,1)S(1)} %get-tuple-element.62), channel_id=1, source_target_pairs={{0,12},{4,8},{8,4},{12,0},{1,13},{5,9},{9,5},{13,1},{2,14},{6,10},... | collective-permute-start | bytes 393224 | tf_op jit(solution)/shard_map/ppermute | solution.py:130
  20.0 2.5 %shard_map.77 = (bf16[32,2048]{1,0:T(8,128)(2,1)S(1)}, bf16[32,2048]{1,0:T(8,128)(2,1)S(1)}, bf16[32,2048]{1,0:T(8,128)(2,1)S(1)}, bf16[32,2048]{1,0:T(8,128)(2,1)S(1)}) custom-call(bf16[16,64,128]{2,1,0:T(8,128)(2,1)S(1)} %shard_map.75.refs_0_, bf16[32,2176]{1,0:T(8,128)(2,1)S(1)} %get-tuple-element.43.refs_2_.refs_1_.refs_5_, ...), custom_call_target="tpu_custom_call" | custom-call | tf_op jit(solution)/shard_map/pallas_call | solution.py:144
  22.5 1.2 %collective-permute-done.6.refs_1_ = bf16[32,2048]{1,0:T(8,128)(2,1)S(1)} collective-permute-done((bf16[32,2048]{1,0:T(8,128)(2,1)S(1)}, bf16[32,2048]{1,0:T(8,128)(2,1)S(1)}, u32[]{:S(2)}, u32[]{:S(2)}) %collective-permute-start.6) | collective-permute-done | bytes 131104 | tf_op jit(solution)/shard_map/ppermute | solution.py:130
  23.7 6.9 %collective-permute-done.7.refs_2_ = bf16[32,2048]{1,0:T(8,128)(2,1)S(1)} collective-permute-done((bf16[32,2048]{1,0:T(8,128)(2,1)S(1)}, bf16[32,2048]{1,0:T(8,128)(2,1)S(1)}, u32[]{:S(2)}, u32[]{:S(2)}) %collective-permute-start.7) | collective-permute-done | bytes 131104 | tf_op jit(solution)/shard_map/ppermute | solution.py:130
  30.6 2.7 %collective-permute-start.12 = (bf16[32,2048]{1,0:T(8,128)(2,1)S(1)}, bf16[32,2048]{1,0:T(8,128)(2,1)S(1)}, u32[]{:S(2)}, u32[]{:S(2)}) collective-permute-start(bf16[32,2048]{1,0:T(8,128)(2,1)S(1)} %get-tuple-element.70), channel_id=1, source_target_pairs={{0,12},{4,8},{8,4},{12,0},{1,13},{5,9},{9,5},{13,1},{2,14},{6,10},... | collective-permute-start | bytes 393224 | tf_op jit(solution)/shard_map/ppermute | solution.py:130
  33.3 1.7 %collective-permute-start.14 = (bf16[32,2048]{1,0:T(8,128)(2,1)S(1)}, bf16[32,2048]{1,0:T(8,128)(2,1)S(1)}, u32[]{:S(2)}, u32[]{:S(2)}) collective-permute-start(bf16[32,2048]{1,0:T(8,128)(2,1)S(1)} %get-tuple-element.72), channel_id=1, source_target_pairs={{0,4},{4,0},{8,12},{12,8},{1,5},{5,1},{9,13},{13,9},{2,6},{6,2},{1... | collective-permute-start | bytes 393224 | tf_op jit(solution)/shard_map/ppermute | solution.py:130
  35.2 1.6 %collective-permute-start.10 = (bf16[32,2048]{1,0:T(8,128)(2,1)S(1)}, bf16[32,2048]{1,0:T(8,128)(2,1)S(1)}, u32[]{:S(2)}, u32[]{:S(2)}) collective-permute-start(bf16[32,2048]{1,0:T(8,128)(2,1)S(1)} %shard_map.78.refs_4_), channel_id=1, source_target_pairs={{0,2},{1,3},{2,0},{3,1},{4,6},{5,7},{6,4},{7,5},{8,10},{9,11},{10,... | collective-permute-start | bytes 393224 | tf_op jit(solution)/shard_map/ppermute | solution.py:130
  36.8 2.1 %collective-permute-done.12.refs_1_ = bf16[32,2048]{1,0:T(8,128)(2,1)S(1)} collective-permute-done((bf16[32,2048]{1,0:T(8,128)(2,1)S(1)}, bf16[32,2048]{1,0:T(8,128)(2,1)S(1)}, u32[]{:S(2)}, u32[]{:S(2)}) %collective-permute-start.12) | collective-permute-done | bytes 131104 | tf_op jit(solution)/shard_map/ppermute | solution.py:130
  38.9 4.4 %collective-permute-done.13.refs_2_ = bf16[32,2048]{1,0:T(8,128)(2,1)S(1)} collective-permute-done((bf16[32,2048]{1,0:T(8,128)(2,1)S(1)}, bf16[32,2048]{1,0:T(8,128)(2,1)S(1)}, u32[]{:S(2)}, u32[]{:S(2)}) %collective-permute-start.13) | collective-permute-done | bytes 131104 | tf_op jit(solution)/shard_map/ppermute | solution.py:130
  43.4 0.9 %collective-permute-start.20 = (bf16[32,2048]{1,0:T(8,128)(2,1)S(1)}, bf16[32,2048]{1,0:T(8,128)(2,1)S(1)}, u32[]{:S(2)}, u32[]{:S(2)}) collective-permute-start(bf16[32,2048]{1,0:T(8,128)(2,1)S(1)} %shard_map.79.refs_5_.refs_4_), channel_id=1, source_target_pairs={{0,3},{1,2},{2,1},{3,0},{4,7},{5,6},{6,5},{7,4},{8,11},{9,10},{10,... | collective-permute-start | bytes 393224 | tf_op jit(solution)/shard_map/ppermute | solution.py:130
  45.3 2.3 %shard_map.80 = (bf16[32,1650]{1,0:T(8,128)(2,1)S(1)}, bf16[32,1650]{1,0:T(8,128)(2,1)S(1)}, bf16[32,1650]{1,0:T(8,128)(2,1)S(1)}, bf16[32,1650]{1,0:T(8,128)(2,1)S(1)}) custom-call(bf16[1650,2048]{1,0:T(8,128)(2,1)S(1)} %bitcast.4, bf16[32,2048]{1,0:T(8,128)(2,1)S(1)} %collective-permute-done.9.refs_1_, ...), custom_call_target="tpu_custom_call" | custom-call | tf_op jit(solution)/shard_map/pallas_call | solution.py:144
  47.6 1.9 %collective-permute-start.15 = (bf16[32,1650]{1,0:T(8,128)(2,1)S(1)}, bf16[32,1650]{1,0:T(8,128)(2,1)S(1)}, u32[]{:S(2)}, u32[]{:S(2)}) collective-permute-start(bf16[32,1650]{1,0:T(8,128)(2,1)S(1)} %get-tuple-element.74), channel_id=1, source_target_pairs={{0,12},{4,8},{8,4},{12,0},{1,13},{5,9},{9,5},{13,1},{2,14},{6,10},... | collective-permute-start | bytes 316808 | tf_op jit(solution)/shard_map/ppermute | solution.py:130
  49.6 2.5 %collective-permute-start.17 = (bf16[32,1650]{1,0:T(8,128)(2,1)S(1)}, bf16[32,1650]{1,0:T(8,128)(2,1)S(1)}, u32[]{:S(2)}, u32[]{:S(2)}) collective-permute-start(bf16[32,1650]{1,0:T(8,128)(2,1)S(1)} %get-tuple-element.76), channel_id=1, source_target_pairs={{0,4},{4,0},{8,12},{12,8},{1,5},{5,1},{9,13},{13,9},{2,6},{6,2},{1... | collective-permute-start | bytes 316808 | tf_op jit(solution)/shard_map/ppermute | solution.py:130
  52.1 2.3 %shard_map.81 = (bf16[32,1650]{1,0:T(8,128)(2,1)S(1)}, bf16[32,1650]{1,0:T(8,128)(2,1)S(1)}, bf16[32,1650]{1,0:T(8,128)(2,1)S(1)}, bf16[32,1650]{1,0:T(8,128)(2,1)S(1)}) custom-call(bf16[1650,2048]{1,0:T(8,128)(2,1)S(1)} %bitcast.5, bf16[32,2048]{1,0:T(8,128)(2,1)S(1)} %collective-permute-done.18.refs_1_, ...), custom_call_target="tpu_custom_call" | custom-call | tf_op jit(solution)/shard_map/pallas_call | solution.py:144
  54.4 1.9 %collective-permute-start.21 = (bf16[32,1650]{1,0:T(8,128)(2,1)S(1)}, bf16[32,1650]{1,0:T(8,128)(2,1)S(1)}, u32[]{:S(2)}, u32[]{:S(2)}) collective-permute-start(bf16[32,1650]{1,0:T(8,128)(2,1)S(1)} %get-tuple-element.78), channel_id=1, source_target_pairs={{0,12},{4,8},{8,4},{12,0},{1,13},{5,9},{9,5},{13,1},{2,14},{6,10},... | collective-permute-start | bytes 316808 | tf_op jit(solution)/shard_map/ppermute | solution.py:130
  56.3 2.5 %collective-permute-start.23 = (bf16[32,1650]{1,0:T(8,128)(2,1)S(1)}, bf16[32,1650]{1,0:T(8,128)(2,1)S(1)}, u32[]{:S(2)}, u32[]{:S(2)}) collective-permute-start(bf16[32,1650]{1,0:T(8,128)(2,1)S(1)} %get-tuple-element.80), channel_id=1, source_target_pairs={{0,4},{4,0},{8,12},{12,8},{1,5},{5,1},{9,13},{13,9},{2,6},{6,2},{1... | collective-permute-start | bytes 316808 | tf_op jit(solution)/shard_map/ppermute | solution.py:130
  59.6 2.6 %collective-permute-done.21.refs_5_ = bf16[32,1650]{1,0:T(8,128)(2,1)S(1)} collective-permute-done((bf16[32,1650]{1,0:T(8,128)(2,1)S(1)}, bf16[32,1650]{1,0:T(8,128)(2,1)S(1)}, u32[]{:S(2)}, u32[]{:S(2)}) %collective-permute-start.21) | collective-permute-done | bytes 105632 | tf_op jit(solution)/shard_map/ppermute | solution.py:130
  62.2 6.2 %collective-permute-done.22.refs_6_ = bf16[32,1650]{1,0:T(8,128)(2,1)S(1)} collective-permute-done((bf16[32,1650]{1,0:T(8,128)(2,1)S(1)}, bf16[32,1650]{1,0:T(8,128)(2,1)S(1)}, u32[]{:S(2)}, u32[]{:S(2)}) %collective-permute-start.22) | collective-permute-done | bytes 105632 | tf_op jit(solution)/shard_map/ppermute | solution.py:130
  (41 shorter events, 7.0 us)
Async XLA Ops:
  2.7 6.5 %collective-permute-start = (bf16[32,2176]{1,0:T(8,128)(2,1)S(1)}, bf16[32,2176]{1,0:T(8,128)(2,1)S(1)}, u32[]{:S(2)}, u32[]{:S(2)}) collective-permute-start(bf16[32,2176]{1,0:T(8,128)(2,1)S(1)} %get-tuple-element.48), channel_id=1, source_target_pairs={{0,3},{1,2},{2,1},{3,0},{4,7},{5,6},{6,5},{7,4},{8,11},{9,10},{10,... | collective-permute-start | bytes 417800 | tf_op jit(solution)/shard_map/ppermute | solution.py:130
  5.1 7.2 %collective-permute-start.1 = (bf16[32,2176]{1,0:T(8,128)(2,1)S(1)}, bf16[32,2176]{1,0:T(8,128)(2,1)S(1)}, u32[]{:S(2)}, u32[]{:S(2)}) collective-permute-start(bf16[32,2176]{1,0:T(8,128)(2,1)S(1)} %get-tuple-element.51), channel_id=1, source_target_pairs={{0,2},{1,3},{2,0},{3,1},{4,6},{5,7},{6,4},{7,5},{8,10},{9,11},{10,... | collective-permute-start | bytes 417800 | tf_op jit(solution)/shard_map/ppermute | solution.py:130
  5.8 6.6 %collective-permute-start.2 = (bf16[32,2176]{1,0:T(8,128)(2,1)S(1)}, bf16[32,2176]{1,0:T(8,128)(2,1)S(1)}, u32[]{:S(2)}, u32[]{:S(2)}) collective-permute-start(bf16[32,2176]{1,0:T(8,128)(2,1)S(1)} %get-tuple-element.52), channel_id=1, source_target_pairs={{0,1},{1,0},{2,3},{3,2},{4,5},{5,4},{6,7},{7,6},{8,9},{9,8},{10,11... | collective-permute-start | bytes 417800 | tf_op jit(solution)/shard_map/ppermute | solution.py:130
  9.2 10.1 %collective-permute-start.3 = (bf16[32,2048]{1,0:T(8,128)(2,1)S(1)}, bf16[32,2048]{1,0:T(8,128)(2,1)S(1)}, u32[]{:S(2)}, u32[]{:S(2)}) collective-permute-start(bf16[32,2048]{1,0:T(8,128)(2,1)S(1)} %get-tuple-element.54), channel_id=1, source_target_pairs={{0,3},{1,2},{2,1},{3,0},{4,7},{5,6},{6,5},{7,4},{8,11},{9,10},{10,... | collective-permute-start | bytes 393224 | tf_op jit(solution)/shard_map/ppermute | solution.py:130
  11.4 8.6 %collective-permute-start.4 = (bf16[32,2048]{1,0:T(8,128)(2,1)S(1)}, bf16[32,2048]{1,0:T(8,128)(2,1)S(1)}, u32[]{:S(2)}, u32[]{:S(2)}) collective-permute-start(bf16[32,2048]{1,0:T(8,128)(2,1)S(1)} %get-tuple-element.55), channel_id=1, source_target_pairs={{0,2},{1,3},{2,0},{3,1},{4,6},{5,7},{6,4},{7,5},{8,10},{9,11},{10,... | collective-permute-start | bytes 393224 | tf_op jit(solution)/shard_map/ppermute | solution.py:130
  11.7 8.3 %collective-permute-start.5 = (bf16[32,2048]{1,0:T(8,128)(2,1)S(1)}, bf16[32,2048]{1,0:T(8,128)(2,1)S(1)}, u32[]{:S(2)}, u32[]{:S(2)}) collective-permute-start(bf16[32,2048]{1,0:T(8,128)(2,1)S(1)} %get-tuple-element.56), channel_id=1, source_target_pairs={{0,1},{1,0},{2,3},{3,2},{4,5},{5,4},{6,7},{7,6},{8,9},{9,8},{10,11... | collective-permute-start | bytes 393224 | tf_op jit(solution)/shard_map/ppermute | solution.py:130
  14.9 8.9 %collective-permute-start.6 = (bf16[32,2048]{1,0:T(8,128)(2,1)S(1)}, bf16[32,2048]{1,0:T(8,128)(2,1)S(1)}, u32[]{:S(2)}, u32[]{:S(2)}) collective-permute-start(bf16[32,2048]{1,0:T(8,128)(2,1)S(1)} %get-tuple-element.62), channel_id=1, source_target_pairs={{0,12},{4,8},{8,4},{12,0},{1,13},{5,9},{9,5},{13,1},{2,14},{6,10},... | collective-permute-start | bytes 393224 | tf_op jit(solution)/shard_map/ppermute | solution.py:130
  19.3 11.3 %collective-permute-start.7 = (bf16[32,2048]{1,0:T(8,128)(2,1)S(1)}, bf16[32,2048]{1,0:T(8,128)(2,1)S(1)}, u32[]{:S(2)}, u32[]{:S(2)}) collective-permute-start(bf16[32,2048]{1,0:T(8,128)(2,1)S(1)} %get-tuple-element.63), channel_id=1, source_target_pairs={{0,8},{4,12},{8,0},{12,4},{1,9},{5,13},{9,1},{13,5},{2,10},{6,14},... | collective-permute-start | bytes 393224 | tf_op jit(solution)/shard_map/ppermute | solution.py:130
  19.3 11.3 %collective-permute-start.8 = (bf16[32,2048]{1,0:T(8,128)(2,1)S(1)}, bf16[32,2048]{1,0:T(8,128)(2,1)S(1)}, u32[]{:S(2)}, u32[]{:S(2)}) collective-permute-start(bf16[32,2048]{1,0:T(8,128)(2,1)S(1)} %get-tuple-element.64), channel_id=1, source_target_pairs={{0,4},{4,0},{8,12},{12,8},{1,5},{5,1},{9,13},{13,9},{2,6},{6,2},{1... | collective-permute-start | bytes 393224 | tf_op jit(solution)/shard_map/ppermute | solution.py:130
  30.6 8.2 %collective-permute-start.12 = (bf16[32,2048]{1,0:T(8,128)(2,1)S(1)}, bf16[32,2048]{1,0:T(8,128)(2,1)S(1)}, u32[]{:S(2)}, u32[]{:S(2)}) collective-permute-start(bf16[32,2048]{1,0:T(8,128)(2,1)S(1)} %get-tuple-element.70), channel_id=1, source_target_pairs={{0,12},{4,8},{8,4},{12,0},{1,13},{5,9},{9,5},{13,1},{2,14},{6,10},... | collective-permute-start | bytes 393224 | tf_op jit(solution)/shard_map/ppermute | solution.py:130
  33.3 10.0 %collective-permute-start.13 = (bf16[32,2048]{1,0:T(8,128)(2,1)S(1)}, bf16[32,2048]{1,0:T(8,128)(2,1)S(1)}, u32[]{:S(2)}, u32[]{:S(2)}) collective-permute-start(bf16[32,2048]{1,0:T(8,128)(2,1)S(1)} %get-tuple-element.71), channel_id=1, source_target_pairs={{0,8},{4,12},{8,0},{12,4},{1,9},{5,13},{9,1},{13,5},{2,10},{6,14},... | collective-permute-start | bytes 393224 | tf_op jit(solution)/shard_map/ppermute | solution.py:130
  33.3 10.0 %collective-permute-start.14 = (bf16[32,2048]{1,0:T(8,128)(2,1)S(1)}, bf16[32,2048]{1,0:T(8,128)(2,1)S(1)}, u32[]{:S(2)}, u32[]{:S(2)}) collective-permute-start(bf16[32,2048]{1,0:T(8,128)(2,1)S(1)} %get-tuple-element.72), channel_id=1, source_target_pairs={{0,4},{4,0},{8,12},{12,8},{1,5},{5,1},{9,13},{13,9},{2,6},{6,2},{1... | collective-permute-start | bytes 393224 | tf_op jit(solution)/shard_map/ppermute | solution.py:130
  35.1 10.0 %collective-permute-start.11 = (bf16[32,2048]{1,0:T(8,128)(2,1)S(1)}, bf16[32,2048]{1,0:T(8,128)(2,1)S(1)}, u32[]{:S(2)}, u32[]{:S(2)}) collective-permute-start(bf16[32,2048]{1,0:T(8,128)(2,1)S(1)} %shard_map.78.refs_4_), channel_id=1, source_target_pairs={{0,3},{1,2},{2,1},{3,0},{4,7},{5,6},{6,5},{7,4},{8,11},{9,10},{10,... | collective-permute-start | bytes 393224 | tf_op jit(solution)/shard_map/ppermute | solution.py:130
  35.2 10.2 %collective-permute-start.10 = (bf16[32,2048]{1,0:T(8,128)(2,1)S(1)}, bf16[32,2048]{1,0:T(8,128)(2,1)S(1)}, u32[]{:S(2)}, u32[]{:S(2)}) collective-permute-start(bf16[32,2048]{1,0:T(8,128)(2,1)S(1)} %shard_map.78.refs_4_), channel_id=1, source_target_pairs={{0,2},{1,3},{2,0},{3,1},{4,6},{5,7},{6,4},{7,5},{8,10},{9,11},{10,... | collective-permute-start | bytes 393224 | tf_op jit(solution)/shard_map/ppermute | solution.py:130
  38.9 6.5 %collective-permute-start.9 = (bf16[32,2048]{1,0:T(8,128)(2,1)S(1)}, bf16[32,2048]{1,0:T(8,128)(2,1)S(1)}, u32[]{:S(2)}, u32[]{:S(2)}) collective-permute-start(bf16[32,2048]{1,0:T(8,128)(2,1)S(1)} %shard_map.78.refs_4_), channel_id=1, source_target_pairs={{0,1},{1,0},{2,3},{3,2},{4,5},{5,4},{6,7},{7,6},{8,9},{9,8},{10,11... | collective-permute-start | bytes 393224 | tf_op jit(solution)/shard_map/ppermute | solution.py:130
  43.4 6.2 %collective-permute-start.20 = (bf16[32,2048]{1,0:T(8,128)(2,1)S(1)}, bf16[32,2048]{1,0:T(8,128)(2,1)S(1)}, u32[]{:S(2)}, u32[]{:S(2)}) collective-permute-start(bf16[32,2048]{1,0:T(8,128)(2,1)S(1)} %shard_map.79.refs_5_.refs_4_), channel_id=1, source_target_pairs={{0,3},{1,2},{2,1},{3,0},{4,7},{5,6},{6,5},{7,4},{8,11},{9,10},{10,... | collective-permute-start | bytes 393224 | tf_op jit(solution)/shard_map/ppermute | solution.py:130
  44.3 7.8 %collective-permute-start.19 = (bf16[32,2048]{1,0:T(8,128)(2,1)S(1)}, bf16[32,2048]{1,0:T(8,128)(2,1)S(1)}, u32[]{:S(2)}, u32[]{:S(2)}) collective-permute-start(bf16[32,2048]{1,0:T(8,128)(2,1)S(1)} %shard_map.79.refs_5_.refs_4_), channel_id=1, source_target_pairs={{0,2},{1,3},{2,0},{3,1},{4,6},{5,7},{6,4},{7,5},{8,10},{9,11},{10,... | collective-permute-start | bytes 393224 | tf_op jit(solution)/shard_map/ppermute | solution.py:130
  45.1 7.0 %collective-permute-start.18 = (bf16[32,2048]{1,0:T(8,128)(2,1)S(1)}, bf16[32,2048]{1,0:T(8,128)(2,1)S(1)}, u32[]{:S(2)}, u32[]{:S(2)}) collective-permute-start(bf16[32,2048]{1,0:T(8,128)(2,1)S(1)} %shard_map.79.refs_5_.refs_4_), channel_id=1, source_target_pairs={{0,1},{1,0},{2,3},{3,2},{4,5},{5,4},{6,7},{7,6},{8,9},{9,8},{10,11... | collective-permute-start | bytes 393224 | tf_op jit(solution)/shard_map/ppermute | solution.py:130
  47.6 8.7 %collective-permute-start.15 = (bf16[32,1650]{1,0:T(8,128)(2,1)S(1)}, bf16[32,1650]{1,0:T(8,128)(2,1)S(1)}, u32[]{:S(2)}, u32[]{:S(2)}) collective-permute-start(bf16[32,1650]{1,0:T(8,128)(2,1)S(1)} %get-tuple-element.74), channel_id=1, source_target_pairs={{0,12},{4,8},{8,4},{12,0},{1,13},{5,9},{9,5},{13,1},{2,14},{6,10},... | collective-permute-start | bytes 316808 | tf_op jit(solution)/shard_map/ppermute | solution.py:130
  49.6 10.1 %collective-permute-start.16 = (bf16[32,1650]{1,0:T(8,128)(2,1)S(1)}, bf16[32,1650]{1,0:T(8,128)(2,1)S(1)}, u32[]{:S(2)}, u32[]{:S(2)}) collective-permute-start(bf16[32,1650]{1,0:T(8,128)(2,1)S(1)} %get-tuple-element.75), channel_id=1, source_target_pairs={{0,8},{4,12},{8,0},{12,4},{1,9},{5,13},{9,1},{13,5},{2,10},{6,14},... | collective-permute-start | bytes 316808 | tf_op jit(solution)/shard_map/ppermute | solution.py:130
  49.6 10.0 %collective-permute-start.17 = (bf16[32,1650]{1,0:T(8,128)(2,1)S(1)}, bf16[32,1650]{1,0:T(8,128)(2,1)S(1)}, u32[]{:S(2)}, u32[]{:S(2)}) collective-permute-start(bf16[32,1650]{1,0:T(8,128)(2,1)S(1)} %get-tuple-element.76), channel_id=1, source_target_pairs={{0,4},{4,0},{8,12},{12,8},{1,5},{5,1},{9,13},{13,9},{2,6},{6,2},{1... | collective-permute-start | bytes 316808 | tf_op jit(solution)/shard_map/ppermute | solution.py:130
  54.4 7.8 %collective-permute-start.21 = (bf16[32,1650]{1,0:T(8,128)(2,1)S(1)}, bf16[32,1650]{1,0:T(8,128)(2,1)S(1)}, u32[]{:S(2)}, u32[]{:S(2)}) collective-permute-start(bf16[32,1650]{1,0:T(8,128)(2,1)S(1)} %get-tuple-element.78), channel_id=1, source_target_pairs={{0,12},{4,8},{8,4},{12,0},{1,13},{5,9},{9,5},{13,1},{2,14},{6,10},... | collective-permute-start | bytes 316808 | tf_op jit(solution)/shard_map/ppermute | solution.py:130
  56.3 12.1 %collective-permute-start.22 = (bf16[32,1650]{1,0:T(8,128)(2,1)S(1)}, bf16[32,1650]{1,0:T(8,128)(2,1)S(1)}, u32[]{:S(2)}, u32[]{:S(2)}) collective-permute-start(bf16[32,1650]{1,0:T(8,128)(2,1)S(1)} %get-tuple-element.79), channel_id=1, source_target_pairs={{0,8},{4,12},{8,0},{12,4},{1,9},{5,13},{9,1},{13,5},{2,10},{6,14},... | collective-permute-start | bytes 316808 | tf_op jit(solution)/shard_map/ppermute | solution.py:130
  56.3 12.1 %collective-permute-start.23 = (bf16[32,1650]{1,0:T(8,128)(2,1)S(1)}, bf16[32,1650]{1,0:T(8,128)(2,1)S(1)}, u32[]{:S(2)}, u32[]{:S(2)}) collective-permute-start(bf16[32,1650]{1,0:T(8,128)(2,1)S(1)} %get-tuple-element.80), channel_id=1, source_target_pairs={{0,4},{4,0},{8,12},{12,8},{1,5},{5,1},{9,13},{13,9},{2,6},{6,2},{1... | collective-permute-start | bytes 316808 | tf_op jit(solution)/shard_map/ppermute | solution.py:130
  (3 other events, 47.6 us)

commit v12 on v9

--- a/solution.py
+++ b/solution.py
@@ -13,6 +13,10 @@
 VMEM = pl.BlockSpec(memory_space=pltpu.VMEM)
 ANY = pl.BlockSpec(memory_space=pl.ANY)
 PARAMS = dict(vmem_limit_bytes=16 * 1024 * 1024)
+
+
+def partners(n):
+    return [0, n // 2] + [k for k in range(n - 1, 0, -1) if k != n // 2]
 
 
 def turn_kernel(n_layer, n_row, halves, half, layers_ref, extra_ref, *refs):
@@ -31,7 +35,7 @@
         pick, layers_ref[...], (((1,), (1,)), ((), ())), preferred_element_type=F32
     ).astype(BF16)
     for i, out in enumerate(outs):
-        k = (n_layer - i) % n_layer
+        k = partners(n_layer)[i]
         out[:, :rows_dev] = turned[k * each : (k + 1) * each]
     if half == 0:
         codes[...] = jnp.zeros_like(codes)
@@ -82,7 +86,7 @@
         lax.fori_loop(0, entries // unroll, step, 0)
     me = lax.axis_index("row")
     for i, out in enumerate(outs):
-        k = (n_row - i) % n_row
+        k = partners(n_row)[i]
         base = lax.bitwise_xor(me, k) * owned
         for s in range(owned):
             out[:, s * LANES : (s + 1) * LANES] = total[base + s].astype(BF16)
@@ -98,7 +102,7 @@
     aligned = n_layer == n_row
     me, row = lax.axis_index("layer"), lax.axis_index("row")
     for j, piece in enumerate(pieces):
-        place = lax.bitwise_xor(me, (j + 1) % n_layer)
+        place = lax.bitwise_xor(me, partners(n_layer)[n_layer - 1 - j])
         left[lax.bitwise_xor(place, row) if aligned else place] = piece[...]
     columns = left.shape[0] * left.shape[1]
     found = lax.dot_general(
@@ -110,12 +114,12 @@
     each = columns // n_row
     if aligned:
         for i, out in enumerate(outs):
-            k = (n_row - i) % n_row
+            k = partners(n_row)[i]
             out[...] = found[k * each : (k + 1) * each].astype(BF16)
     else:
         product[...] = found
         for i, out in enumerate(outs):
-            k = (n_row - i) % n_row
+            k = partners(n_row)[i]
             start = pl.multiple_of(lax.bitwise_xor(row, k) * each, each)
             out[...] = product[pl.ds(start, each), :].astype(BF16)
 
@@ -126,7 +130,7 @@
 
 def exchange(chunks, axis):
     n = len(chunks)
-    return [trade(chunk, axis, n - i) if i else chunk for i, chunk in enumerate(chunks)]
+    return [trade(chunk, axis, partners(n)[i]) if i else chunk for i, chunk in enumerate(chunks)]
 
 
 def total_of(parts):

time: 69.4 us -> 70.1 us (1.010)
  waiting for transfers between devices: 26.5 us -> 27.6 us
    ppermute x24, waiting for transfers between devices: 26.5 us -> 27.6 us  [trade(): lax.ppermute(chunk, axis, [(j, j ^ k) for j in range(lax.axis_size(axis))])]
where the time goes in v12:
time: 70.1 us; the launch traced here: 70 us
  waiting for transfers between devices  27.6 us (39%)
  starting transfers between devices  27.4 us (39%)
  Pallas kernels  10.9 us (16%)
  local copies, waits for them, and re-layouts  2.29 us (3%)
  other arithmetic  1.7 us (2%)
    ppermute x24, waiting for transfers between devices, trade(): lax.ppermute(chunk, axis, [(j, j ^ k) for j in range(lax.axis_size(axis))])  27.6 us
    ppermute x24, starting transfers between devices, trade(): lax.ppermute(chunk, axis, [(j, j ^ k) for j in range(lax.axis_size(axis))])  27.4 us
    pallas_call x9, Pallas kernels, call(): pl.pallas_call(body, out_shape=[jax.ShapeDtypeStruct(shape, BF16) for sha...  10.9 us
    unnamed x6, local copies, waits for them, and re-layouts  2.29 us
  transfers between devices with their start and end apart: 24, of which 9 were waited for; matrix products, arithmetic and copies ran while one was open for 0% of the time, Pallas kernels for 15%

profile of v12, /device:TPU:0, one launch (start us, length us, event | category | flops | bytes accessed | tf_op | source)
XLA Modules:
  0.0 70.0 jit_solution(16774994128366886732)
XLA Ops:
  0.0 0.9 %pad_add_fusion.refs_1_ = s32[4,32]{1,0:T(4,128)S(1)} fusion(s32[1,32]{1,0:T(1,128)} %param.13, s32[1,32]{1,0:T(1,128)} %param.12, s32[1,32]{1,0:T(1,128)} %param.11, s32[1,32]{1,0:T(1,128)} %bitcast.9), kind=kLoop, calls=%fused_computation.3 | loop fusion | flops 384 | bytes 1024 | tf_op jit(solution)/shard_map/concatenate | solution.py:168
  0.9 1.3 %copy-done.1 = bf16[1,2048,256]{2,1,0:T(8,128)(2,1)S(1)} copy-done((bf16[1,2048,256]{2,1,0:T(8,128)(2,1)S(1)}, bf16[1,2048,256]{2,1,0:T(8,128)(2,1)}, u32[]{:S(2)}) %copy-start.1) | copy-done | bytes 1048600
  2.7 3.0 %collective-permute-start = (bf16[32,2176]{1,0:T(8,128)(2,1)S(1)}, bf16[32,2176]{1,0:T(8,128)(2,1)S(1)}, u32[]{:S(2)}, u32[]{:S(2)}) collective-permute-start(bf16[32,2176]{1,0:T(8,128)(2,1)S(1)} %get-tuple-element.48), channel_id=1, source_target_pairs={{0,2},{1,3},{2,0},{3,1},{4,6},{5,7},{6,4},{7,5},{8,10},{9,11},{10,... | collective-permute-start | bytes 417800 | tf_op jit(solution)/shard_map/ppermute | solution.py:128
  6.4 0.9 %copy-done.2 = bf16[16,128,64]{1,2,0:T(8,128)(2,1)S(1)} copy-done((bf16[16,128,64]{1,2,0:T(8,128)(2,1)S(1)}, bf16[16,128,64]{1,2,0:T(8,128)(2,1)}, u32[]{:S(2)}) %copy-start.2) | copy-done | bytes 262168
  7.5 2.4 %collective-permute-done.refs_2_.refs_6_ = bf16[32,2176]{1,0:T(8,128)(2,1)S(1)} collective-permute-done((bf16[32,2176]{1,0:T(8,128)(2,1)S(1)}, bf16[32,2176]{1,0:T(8,128)(2,1)S(1)}, u32[]{:S(2)}, u32[]{:S(2)}) %collective-permute-start) | collective-permute-done | bytes 139296 | tf_op jit(solution)/shard_map/ppermute | solution.py:128
  10.0 2.3 %collective-permute-start.3 = (bf16[32,2048]{1,0:T(8,128)(2,1)S(1)}, bf16[32,2048]{1,0:T(8,128)(2,1)S(1)}, u32[]{:S(2)}, u32[]{:S(2)}) collective-permute-start(bf16[32,2048]{1,0:T(8,128)(2,1)S(1)} %get-tuple-element.54), channel_id=1, source_target_pairs={{0,2},{1,3},{2,0},{3,1},{4,6},{5,7},{6,4},{7,5},{8,10},{9,11},{10,... | collective-permute-start | bytes 393224 | tf_op jit(solution)/shard_map/ppermute | solution.py:128
  12.8 2.6 %shard_map.76 = (bf16[32,2048]{1,0:T(8,128)(2,1)S(1)}, bf16[32,2048]{1,0:T(8,128)(2,1)S(1)}, bf16[32,2048]{1,0:T(8,128)(2,1)S(1)}, bf16[32,2048]{1,0:T(8,128)(2,1)S(1)}) custom-call(bf16[32,128,128]{2,1,0:T(8,128)(2,1)S(1)} %shard_map.75.refs_0_, bf16[32,2176]{1,0:T(8,128)(2,1)S(1)} %get-tuple-element.43.refs_2_.refs_1_.refs_5_, ...), custom_call_target="tpu_custom_call" | custom-call | tf_op jit(solution)/shard_map/pallas_call | solution.py:146
  15.3 2.6 %collective-permute-start.6 = (bf16[32,2048]{1,0:T(8,128)(2,1)S(1)}, bf16[32,2048]{1,0:T(8,128)(2,1)S(1)}, u32[]{:S(2)}, u32[]{:S(2)}) collective-permute-start(bf16[32,2048]{1,0:T(8,128)(2,1)S(1)} %get-tuple-element.62), channel_id=1, source_target_pairs={{0,8},{4,12},{8,0},{12,4},{1,9},{5,13},{9,1},{13,5},{2,10},{6,14},... | collective-permute-start | bytes 393224 | tf_op jit(solution)/shard_map/ppermute | solution.py:128
  18.0 1.4 %collective-permute-start.7 = (bf16[32,2048]{1,0:T(8,128)(2,1)S(1)}, bf16[32,2048]{1,0:T(8,128)(2,1)S(1)}, u32[]{:S(2)}, u32[]{:S(2)}) collective-permute-start(bf16[32,2048]{1,0:T(8,128)(2,1)S(1)} %get-tuple-element.63), channel_id=1, source_target_pairs={{0,12},{4,8},{8,4},{12,0},{1,13},{5,9},{9,5},{13,1},{2,14},{6,10},... | collective-permute-start | bytes 393224 | tf_op jit(solution)/shard_map/ppermute | solution.py:128
  19.6 2.5 %shard_map.77 = (bf16[32,2048]{1,0:T(8,128)(2,1)S(1)}, bf16[32,2048]{1,0:T(8,128)(2,1)S(1)}, bf16[32,2048]{1,0:T(8,128)(2,1)S(1)}, bf16[32,2048]{1,0:T(8,128)(2,1)S(1)}) custom-call(bf16[32,128,128]{2,1,0:T(8,128)(2,1)S(1)} %shard_map.75.refs_0_, bf16[32,2176]{1,0:T(8,128)(2,1)S(1)} %get-tuple-element.43.refs_2_.refs_1_.refs_5_, ...), custom_call_target="tpu_custom_call" | custom-call | tf_op jit(solution)/shard_map/pallas_call | solution.py:146
  22.1 6.1 %collective-permute-done.6.refs_1_ = bf16[32,2048]{1,0:T(8,128)(2,1)S(1)} collective-permute-done((bf16[32,2048]{1,0:T(8,128)(2,1)S(1)}, bf16[32,2048]{1,0:T(8,128)(2,1)S(1)}, u32[]{:S(2)}, u32[]{:S(2)}) %collective-permute-start.6) | collective-permute-done | bytes 131104 | tf_op jit(solution)/shard_map/ppermute | solution.py:128
  28.3 1.0 %collective-permute-done.8.refs_3_ = bf16[32,2048]{1,0:T(8,128)(2,1)S(1)} collective-permute-done((bf16[32,2048]{1,0:T(8,128)(2,1)S(1)}, bf16[32,2048]{1,0:T(8,128)(2,1)S(1)}, u32[]{:S(2)}, u32[]{:S(2)}) %collective-permute-start.8) | collective-permute-done | bytes 131104 | tf_op jit(solution)/shard_map/ppermute | solution.py:128
  29.3 4.1 %collective-permute-start.12 = (bf16[32,2048]{1,0:T(8,128)(2,1)S(1)}, bf16[32,2048]{1,0:T(8,128)(2,1)S(1)}, u32[]{:S(2)}, u32[]{:S(2)}) collective-permute-start(bf16[32,2048]{1,0:T(8,128)(2,1)S(1)} %get-tuple-element.70), channel_id=1, source_target_pairs={{0,8},{4,12},{8,0},{12,4},{1,9},{5,13},{9,1},{13,5},{2,10},{6,14},... | collective-permute-start | bytes 393224 | tf_op jit(solution)/shard_map/ppermute | solution.py:128
  34.0 1.7 %collective-permute-start.11 = (bf16[32,2048]{1,0:T(8,128)(2,1)S(1)}, bf16[32,2048]{1,0:T(8,128)(2,1)S(1)}, u32[]{:S(2)}, u32[]{:S(2)}) collective-permute-start(bf16[32,2048]{1,0:T(8,128)(2,1)S(1)} %shard_map.78.refs_4_), channel_id=1, source_target_pairs={{0,2},{1,3},{2,0},{3,1},{4,6},{5,7},{6,4},{7,5},{8,10},{9,11},{10,... | collective-permute-start | bytes 393224 | tf_op jit(solution)/shard_map/ppermute | solution.py:128
  35.8 7.3 %collective-permute-done.12.refs_1_ = bf16[32,2048]{1,0:T(8,128)(2,1)S(1)} collective-permute-done((bf16[32,2048]{1,0:T(8,128)(2,1)S(1)}, bf16[32,2048]{1,0:T(8,128)(2,1)S(1)}, u32[]{:S(2)}, u32[]{:S(2)}) %collective-permute-start.12) | collective-permute-done | bytes 131104 | tf_op jit(solution)/shard_map/ppermute | solution.py:128
  43.0 1.1 %collective-permute-done.14.refs_3_ = bf16[32,2048]{1,0:T(8,128)(2,1)S(1)} collective-permute-done((bf16[32,2048]{1,0:T(8,128)(2,1)S(1)}, bf16[32,2048]{1,0:T(8,128)(2,1)S(1)}, u32[]{:S(2)}, u32[]{:S(2)}) %collective-permute-start.14) | collective-permute-done | bytes 131104 | tf_op jit(solution)/shard_map/ppermute | solution.py:128
  44.2 1.8 %collective-permute-start.20 = (bf16[32,2048]{1,0:T(8,128)(2,1)S(1)}, bf16[32,2048]{1,0:T(8,128)(2,1)S(1)}, u32[]{:S(2)}, u32[]{:S(2)}) collective-permute-start(bf16[32,2048]{1,0:T(8,128)(2,1)S(1)} %shard_map.79.refs_5_.refs_4_), channel_id=1, source_target_pairs={{0,2},{1,3},{2,0},{3,1},{4,6},{5,7},{6,4},{7,5},{8,10},{9,11},{10,... | collective-permute-start | bytes 393224 | tf_op jit(solution)/shard_map/ppermute | solution.py:128
  46.4 2.3 %shard_map.80 = (bf16[32,1650]{1,0:T(8,128)(2,1)S(1)}, bf16[32,1650]{1,0:T(8,128)(2,1)S(1)}, bf16[32,1650]{1,0:T(8,128)(2,1)S(1)}, bf16[32,1650]{1,0:T(8,128)(2,1)S(1)}) custom-call(bf16[1650,2048]{1,0:T(8,128)(2,1)S(1)} %bitcast.4, bf16[32,2048]{1,0:T(8,128)(2,1)S(1)} %collective-permute-done.9.refs_1_, ...), custom_call_target="tpu_custom_call" | custom-call | tf_op jit(solution)/shard_map/pallas_call | solution.py:146
  48.7 1.8 %collective-permute-start.15 = (bf16[32,1650]{1,0:T(8,128)(2,1)S(1)}, bf16[32,1650]{1,0:T(8,128)(2,1)S(1)}, u32[]{:S(2)}, u32[]{:S(2)}) collective-permute-start(bf16[32,1650]{1,0:T(8,128)(2,1)S(1)} %get-tuple-element.74), channel_id=1, source_target_pairs={{0,8},{4,12},{8,0},{12,4},{1,9},{5,13},{9,1},{13,5},{2,10},{6,14},... | collective-permute-start | bytes 316808 | tf_op jit(solution)/shard_map/ppermute | solution.py:128
  50.6 2.6 %collective-permute-start.16 = (bf16[32,1650]{1,0:T(8,128)(2,1)S(1)}, bf16[32,1650]{1,0:T(8,128)(2,1)S(1)}, u32[]{:S(2)}, u32[]{:S(2)}) collective-permute-start(bf16[32,1650]{1,0:T(8,128)(2,1)S(1)} %get-tuple-element.75), channel_id=1, source_target_pairs={{0,12},{4,8},{8,4},{12,0},{1,13},{5,9},{9,5},{13,1},{2,14},{6,10},... | collective-permute-start | bytes 316808 | tf_op jit(solution)/shard_map/ppermute | solution.py:128
  53.2 2.3 %shard_map.81 = (bf16[32,1650]{1,0:T(8,128)(2,1)S(1)}, bf16[32,1650]{1,0:T(8,128)(2,1)S(1)}, bf16[32,1650]{1,0:T(8,128)(2,1)S(1)}, bf16[32,1650]{1,0:T(8,128)(2,1)S(1)}) custom-call(bf16[1650,2048]{1,0:T(8,128)(2,1)S(1)} %bitcast.5, bf16[32,2048]{1,0:T(8,128)(2,1)S(1)} %collective-permute-done.18.refs_1_, ...), custom_call_target="tpu_custom_call" | custom-call | tf_op jit(solution)/shard_map/pallas_call | solution.py:146
  55.5 1.9 %collective-permute-start.21 = (bf16[32,1650]{1,0:T(8,128)(2,1)S(1)}, bf16[32,1650]{1,0:T(8,128)(2,1)S(1)}, u32[]{:S(2)}, u32[]{:S(2)}) collective-permute-start(bf16[32,1650]{1,0:T(8,128)(2,1)S(1)} %get-tuple-element.78), channel_id=1, source_target_pairs={{0,8},{4,12},{8,0},{12,4},{1,9},{5,13},{9,1},{13,5},{2,10},{6,14},... | collective-permute-start | bytes 316808 | tf_op jit(solution)/shard_map/ppermute | solution.py:128
  57.3 2.6 %collective-permute-start.22 = (bf16[32,1650]{1,0:T(8,128)(2,1)S(1)}, bf16[32,1650]{1,0:T(8,128)(2,1)S(1)}, u32[]{:S(2)}, u32[]{:S(2)}) collective-permute-start(bf16[32,1650]{1,0:T(8,128)(2,1)S(1)} %get-tuple-element.79), channel_id=1, source_target_pairs={{0,12},{4,8},{8,4},{12,0},{1,13},{5,9},{9,5},{13,1},{2,14},{6,10},... | collective-permute-start | bytes 316808 | tf_op jit(solution)/shard_map/ppermute | solution.py:128
  60.7 8.5 %collective-permute-done.21 = bf16[32,1650]{1,0:T(8,128)(2,1)S(1)} collective-permute-done((bf16[32,1650]{1,0:T(8,128)(2,1)S(1)}, bf16[32,1650]{1,0:T(8,128)(2,1)S(1)}, u32[]{:S(2)}, u32[]{:S(2)}) %collective-permute-start.21) | collective-permute-done | bytes 105632 | tf_op jit(solution)/shard_map/ppermute | solution.py:128
  (43 shorter events, 4.8 us)
Async XLA Ops:
  2.7 7.3 %collective-permute-start = (bf16[32,2176]{1,0:T(8,128)(2,1)S(1)}, bf16[32,2176]{1,0:T(8,128)(2,1)S(1)}, u32[]{:S(2)}, u32[]{:S(2)}) collective-permute-start(bf16[32,2176]{1,0:T(8,128)(2,1)S(1)} %get-tuple-element.48), channel_id=1, source_target_pairs={{0,2},{1,3},{2,0},{3,1},{4,6},{5,7},{6,4},{7,5},{8,10},{9,11},{10,... | collective-permute-start | bytes 417800 | tf_op jit(solution)/shard_map/ppermute | solution.py:128
  5.7 7.1 %collective-permute-start.1 = (bf16[32,2176]{1,0:T(8,128)(2,1)S(1)}, bf16[32,2176]{1,0:T(8,128)(2,1)S(1)}, u32[]{:S(2)}, u32[]{:S(2)}) collective-permute-start(bf16[32,2176]{1,0:T(8,128)(2,1)S(1)} %get-tuple-element.51), channel_id=1, source_target_pairs={{0,3},{1,2},{2,1},{3,0},{4,7},{5,6},{6,5},{7,4},{8,11},{9,10},{10,... | collective-permute-start | bytes 417800 | tf_op jit(solution)/shard_map/ppermute | solution.py:128
  5.7 7.1 %collective-permute-start.2 = (bf16[32,2176]{1,0:T(8,128)(2,1)S(1)}, bf16[32,2176]{1,0:T(8,128)(2,1)S(1)}, u32[]{:S(2)}, u32[]{:S(2)}) collective-permute-start(bf16[32,2176]{1,0:T(8,128)(2,1)S(1)} %get-tuple-element.52), channel_id=1, source_target_pairs={{0,1},{1,0},{2,3},{3,2},{4,5},{5,4},{6,7},{7,6},{8,9},{9,8},{10,11... | collective-permute-start | bytes 417800 | tf_op jit(solution)/shard_map/ppermute | solution.py:128
  10.0 9.4 %collective-permute-start.3 = (bf16[32,2048]{1,0:T(8,128)(2,1)S(1)}, bf16[32,2048]{1,0:T(8,128)(2,1)S(1)}, u32[]{:S(2)}, u32[]{:S(2)}) collective-permute-start(bf16[32,2048]{1,0:T(8,128)(2,1)S(1)} %get-tuple-element.54), channel_id=1, source_target_pairs={{0,2},{1,3},{2,0},{3,1},{4,6},{5,7},{6,4},{7,5},{8,10},{9,11},{10,... | collective-permute-start | bytes 393224 | tf_op jit(solution)/shard_map/ppermute | solution.py:128
  12.3 7.3 %collective-permute-start.4 = (bf16[32,2048]{1,0:T(8,128)(2,1)S(1)}, bf16[32,2048]{1,0:T(8,128)(2,1)S(1)}, u32[]{:S(2)}, u32[]{:S(2)}) collective-permute-start(bf16[32,2048]{1,0:T(8,128)(2,1)S(1)} %get-tuple-element.55), channel_id=1, source_target_pairs={{0,3},{1,2},{2,1},{3,0},{4,7},{5,6},{6,5},{7,4},{8,11},{9,10},{10,... | collective-permute-start | bytes 393224 | tf_op jit(solution)/shard_map/ppermute | solution.py:128
  12.3 7.3 %collective-permute-start.5 = (bf16[32,2048]{1,0:T(8,128)(2,1)S(1)}, bf16[32,2048]{1,0:T(8,128)(2,1)S(1)}, u32[]{:S(2)}, u32[]{:S(2)}) collective-permute-start(bf16[32,2048]{1,0:T(8,128)(2,1)S(1)} %get-tuple-element.56), channel_id=1, source_target_pairs={{0,1},{1,0},{2,3},{3,2},{4,5},{5,4},{6,7},{7,6},{8,9},{9,8},{10,11... | collective-permute-start | bytes 393224 | tf_op jit(solution)/shard_map/ppermute | solution.py:128
  15.3 12.9 %collective-permute-start.6 = (bf16[32,2048]{1,0:T(8,128)(2,1)S(1)}, bf16[32,2048]{1,0:T(8,128)(2,1)S(1)}, u32[]{:S(2)}, u32[]{:S(2)}) collective-permute-start(bf16[32,2048]{1,0:T(8,128)(2,1)S(1)} %get-tuple-element.62), channel_id=1, source_target_pairs={{0,8},{4,12},{8,0},{12,4},{1,9},{5,13},{9,1},{13,5},{2,10},{6,14},... | collective-permute-start | bytes 393224 | tf_op jit(solution)/shard_map/ppermute | solution.py:128
  18.0 10.3 %collective-permute-start.7 = (bf16[32,2048]{1,0:T(8,128)(2,1)S(1)}, bf16[32,2048]{1,0:T(8,128)(2,1)S(1)}, u32[]{:S(2)}, u32[]{:S(2)}) collective-permute-start(bf16[32,2048]{1,0:T(8,128)(2,1)S(1)} %get-tuple-element.63), channel_id=1, source_target_pairs={{0,12},{4,8},{8,4},{12,0},{1,13},{5,9},{9,5},{13,1},{2,14},{6,10},... | collective-permute-start | bytes 393224 | tf_op jit(solution)/shard_map/ppermute | solution.py:128
  19.3 9.9 %collective-permute-start.8 = (bf16[32,2048]{1,0:T(8,128)(2,1)S(1)}, bf16[32,2048]{1,0:T(8,128)(2,1)S(1)}, u32[]{:S(2)}, u32[]{:S(2)}) collective-permute-start(bf16[32,2048]{1,0:T(8,128)(2,1)S(1)} %get-tuple-element.64), channel_id=1, source_target_pairs={{0,4},{4,0},{8,12},{12,8},{1,5},{5,1},{9,13},{13,9},{2,6},{6,2},{1... | collective-permute-start | bytes 393224 | tf_op jit(solution)/shard_map/ppermute | solution.py:128
  29.3 13.8 %collective-permute-start.12 = (bf16[32,2048]{1,0:T(8,128)(2,1)S(1)}, bf16[32,2048]{1,0:T(8,128)(2,1)S(1)}, u32[]{:S(2)}, u32[]{:S(2)}) collective-permute-start(bf16[32,2048]{1,0:T(8,128)(2,1)S(1)} %get-tuple-element.70), channel_id=1, source_target_pairs={{0,8},{4,12},{8,0},{12,4},{1,9},{5,13},{9,1},{13,5},{2,10},{6,14},... | collective-permute-start | bytes 393224 | tf_op jit(solution)/shard_map/ppermute | solution.py:128
  33.4 9.7 %collective-permute-start.13 = (bf16[32,2048]{1,0:T(8,128)(2,1)S(1)}, bf16[32,2048]{1,0:T(8,128)(2,1)S(1)}, u32[]{:S(2)}, u32[]{:S(2)}) collective-permute-start(bf16[32,2048]{1,0:T(8,128)(2,1)S(1)} %get-tuple-element.71), channel_id=1, source_target_pairs={{0,12},{4,8},{8,4},{12,0},{1,13},{5,9},{9,5},{13,1},{2,14},{6,10},... | collective-permute-start | bytes 393224 | tf_op jit(solution)/shard_map/ppermute | solution.py:128
  33.8 10.3 %collective-permute-start.14 = (bf16[32,2048]{1,0:T(8,128)(2,1)S(1)}, bf16[32,2048]{1,0:T(8,128)(2,1)S(1)}, u32[]{:S(2)}, u32[]{:S(2)}) collective-permute-start(bf16[32,2048]{1,0:T(8,128)(2,1)S(1)} %get-tuple-element.72), channel_id=1, source_target_pairs={{0,4},{4,0},{8,12},{12,8},{1,5},{5,1},{9,13},{13,9},{2,6},{6,2},{1... | collective-permute-start | bytes 393224 | tf_op jit(solution)/shard_map/ppermute | solution.py:128
  34.0 12.0 %collective-permute-start.11 = (bf16[32,2048]{1,0:T(8,128)(2,1)S(1)}, bf16[32,2048]{1,0:T(8,128)(2,1)S(1)}, u32[]{:S(2)}, u32[]{:S(2)}) collective-permute-start(bf16[32,2048]{1,0:T(8,128)(2,1)S(1)} %shard_map.78.refs_4_), channel_id=1, source_target_pairs={{0,2},{1,3},{2,0},{3,1},{4,6},{5,7},{6,4},{7,5},{8,10},{9,11},{10,... | collective-permute-start | bytes 393224 | tf_op jit(solution)/shard_map/ppermute | solution.py:128
  35.8 10.7 %collective-permute-start.10 = (bf16[32,2048]{1,0:T(8,128)(2,1)S(1)}, bf16[32,2048]{1,0:T(8,128)(2,1)S(1)}, u32[]{:S(2)}, u32[]{:S(2)}) collective-permute-start(bf16[32,2048]{1,0:T(8,128)(2,1)S(1)} %shard_map.78.refs_4_), channel_id=1, source_target_pairs={{0,3},{1,2},{2,1},{3,0},{4,7},{5,6},{6,5},{7,4},{8,11},{9,10},{10,... | collective-permute-start | bytes 393224 | tf_op jit(solution)/shard_map/ppermute | solution.py:128
  43.0 3.4 %collective-permute-start.9 = (bf16[32,2048]{1,0:T(8,128)(2,1)S(1)}, bf16[32,2048]{1,0:T(8,128)(2,1)S(1)}, u32[]{:S(2)}, u32[]{:S(2)}) collective-permute-start(bf16[32,2048]{1,0:T(8,128)(2,1)S(1)} %shard_map.78.refs_4_), channel_id=1, source_target_pairs={{0,1},{1,0},{2,3},{3,2},{4,5},{5,4},{6,7},{7,6},{8,9},{9,8},{10,11... | collective-permute-start | bytes 393224 | tf_op jit(solution)/shard_map/ppermute | solution.py:128
  44.2 9.0 %collective-permute-start.20 = (bf16[32,2048]{1,0:T(8,128)(2,1)S(1)}, bf16[32,2048]{1,0:T(8,128)(2,1)S(1)}, u32[]{:S(2)}, u32[]{:S(2)}) collective-permute-start(bf16[32,2048]{1,0:T(8,128)(2,1)S(1)} %shard_map.79.refs_5_.refs_4_), channel_id=1, source_target_pairs={{0,2},{1,3},{2,0},{3,1},{4,6},{5,7},{6,4},{7,5},{8,10},{9,11},{10,... | collective-permute-start | bytes 393224 | tf_op jit(solution)/shard_map/ppermute | solution.py:128
  46.0 7.2 %collective-permute-start.19 = (bf16[32,2048]{1,0:T(8,128)(2,1)S(1)}, bf16[32,2048]{1,0:T(8,128)(2,1)S(1)}, u32[]{:S(2)}, u32[]{:S(2)}) collective-permute-start(bf16[32,2048]{1,0:T(8,128)(2,1)S(1)} %shard_map.79.refs_5_.refs_4_), channel_id=1, source_target_pairs={{0,3},{1,2},{2,1},{3,0},{4,7},{5,6},{6,5},{7,4},{8,11},{9,10},{10,... | collective-permute-start | bytes 393224 | tf_op jit(solution)/shard_map/ppermute | solution.py:128
  46.0 7.2 %collective-permute-start.18 = (bf16[32,2048]{1,0:T(8,128)(2,1)S(1)}, bf16[32,2048]{1,0:T(8,128)(2,1)S(1)}, u32[]{:S(2)}, u32[]{:S(2)}) collective-permute-start(bf16[32,2048]{1,0:T(8,128)(2,1)S(1)} %shard_map.79.refs_5_.refs_4_), channel_id=1, source_target_pairs={{0,1},{1,0},{2,3},{3,2},{4,5},{5,4},{6,7},{7,6},{8,9},{9,8},{10,11... | collective-permute-start | bytes 393224 | tf_op jit(solution)/shard_map/ppermute | solution.py:128
  48.7 11.6 %collective-permute-start.15 = (bf16[32,1650]{1,0:T(8,128)(2,1)S(1)}, bf16[32,1650]{1,0:T(8,128)(2,1)S(1)}, u32[]{:S(2)}, u32[]{:S(2)}) collective-permute-start(bf16[32,1650]{1,0:T(8,128)(2,1)S(1)} %get-tuple-element.74), channel_id=1, source_target_pairs={{0,8},{4,12},{8,0},{12,4},{1,9},{5,13},{9,1},{13,5},{2,10},{6,14},... | collective-permute-start | bytes 316808 | tf_op jit(solution)/shard_map/ppermute | solution.py:128
  50.6 9.8 %collective-permute-start.16 = (bf16[32,1650]{1,0:T(8,128)(2,1)S(1)}, bf16[32,1650]{1,0:T(8,128)(2,1)S(1)}, u32[]{:S(2)}, u32[]{:S(2)}) collective-permute-start(bf16[32,1650]{1,0:T(8,128)(2,1)S(1)} %get-tuple-element.75), channel_id=1, source_target_pairs={{0,12},{4,8},{8,4},{12,0},{1,13},{5,9},{9,5},{13,1},{2,14},{6,10},... | collective-permute-start | bytes 316808 | tf_op jit(solution)/shard_map/ppermute | solution.py:128
  53.2 7.5 %collective-permute-start.17 = (bf16[32,1650]{1,0:T(8,128)(2,1)S(1)}, bf16[32,1650]{1,0:T(8,128)(2,1)S(1)}, u32[]{:S(2)}, u32[]{:S(2)}) collective-permute-start(bf16[32,1650]{1,0:T(8,128)(2,1)S(1)} %get-tuple-element.76), channel_id=1, source_target_pairs={{0,4},{4,0},{8,12},{12,8},{1,5},{5,1},{9,13},{13,9},{2,6},{6,2},{1... | collective-permute-start | bytes 316808 | tf_op jit(solution)/shard_map/ppermute | solution.py:128
  55.5 13.7 %collective-permute-start.21 = (bf16[32,1650]{1,0:T(8,128)(2,1)S(1)}, bf16[32,1650]{1,0:T(8,128)(2,1)S(1)}, u32[]{:S(2)}, u32[]{:S(2)}) collective-permute-start(bf16[32,1650]{1,0:T(8,128)(2,1)S(1)} %get-tuple-element.78), channel_id=1, source_target_pairs={{0,8},{4,12},{8,0},{12,4},{1,9},{5,13},{9,1},{13,5},{2,10},{6,14},... | collective-permute-start | bytes 316808 | tf_op jit(solution)/shard_map/ppermute | solution.py:128
  57.3 11.9 %collective-permute-start.22 = (bf16[32,1650]{1,0:T(8,128)(2,1)S(1)}, bf16[32,1650]{1,0:T(8,128)(2,1)S(1)}, u32[]{:S(2)}, u32[]{:S(2)}) collective-permute-start(bf16[32,1650]{1,0:T(8,128)(2,1)S(1)} %get-tuple-element.79), channel_id=1, source_target_pairs={{0,12},{4,8},{8,4},{12,0},{1,13},{5,9},{9,5},{13,1},{2,14},{6,10},... | collective-permute-start | bytes 316808 | tf_op jit(solution)/shard_map/ppermute | solution.py:128
  60.4 8.8 %collective-permute-start.23 = (bf16[32,1650]{1,0:T(8,128)(2,1)S(1)}, bf16[32,1650]{1,0:T(8,128)(2,1)S(1)}, u32[]{:S(2)}, u32[]{:S(2)}) collective-permute-start(bf16[32,1650]{1,0:T(8,128)(2,1)S(1)} %get-tuple-element.80), channel_id=1, source_target_pairs={{0,4},{4,0},{8,12},{12,8},{1,5},{5,1},{9,13},{13,9},{2,6},{6,2},{1... | collective-permute-start | bytes 316808 | tf_op jit(solution)/shard_map/ppermute | solution.py:128
  (3 other events, 48.7 us)

commit v13 on v9

--- a/solution.py
+++ b/solution.py
@@ -12,7 +12,7 @@
 F32, BF16 = jnp.float32, jnp.bfloat16
 VMEM = pl.BlockSpec(memory_space=pltpu.VMEM)
 ANY = pl.BlockSpec(memory_space=pl.ANY)
-PARAMS = dict(vmem_limit_bytes=16 * 1024 * 1024)
+PARAMS = dict(vmem_limit_bytes=24 * 1024 * 1024)
 
 
 def turn_kernel(n_layer, n_row, halves, half, layers_ref, extra_ref, *refs):
@@ -53,7 +53,7 @@
 def pupil_kernel(n_layer, n_row, entries, unroll, padded, *refs):
     coded, parts = refs[:n_layer], refs[n_layer : 2 * n_layer]
     outs = refs[2 * n_layer : 2 * n_layer + n_row]
-    total, codes, code, sem = refs[-4:]
+    totals, (codes, code, sem) = refs[-5:-3], refs[-3:]
     weights = padded.shape[0] // 2
     owned = outs[0].shape[1] // LANES
     for j, ref in enumerate(coded):
@@ -61,7 +61,8 @@
         codes[j * CODE_ROWS : (j + 1) * CODE_ROWS] = tail.astype(F32).astype(jnp.int32)
     copy = pltpu.make_async_copy(codes, code, sem)
     copy.start()
-    total[...] = jnp.zeros_like(total)
+    for total in totals:
+        total[...] = jnp.zeros_like(total)
     copy.wait()
     for j, part in enumerate(parts):
         base = j * CODE_ROWS
@@ -75,8 +76,8 @@
                 weight = padded[lax.rem(block, 2) * weights + code[base + 3, e]]
                 dest = code[base, e] * owned + code[base + 1, e]
                 terms.append((dest, jnp.dot(source, weight, preferred_element_type=F32)))
-            for dest, term in terms:
-                total[dest] += term
+            for i, (dest, term) in enumerate(terms):
+                totals[i % 2][dest] += term
             return carry
 
         lax.fori_loop(0, entries // unroll, step, 0)
@@ -85,7 +86,7 @@
         k = (n_row - i) % n_row
         base = lax.bitwise_xor(me, k) * owned
         for s in range(owned):
-            out[:, s * LANES : (s + 1) * LANES] = total[base + s].astype(BF16)
+            out[:, s * LANES : (s + 1) * LANES] = (totals[0][base + s] + totals[1][base + s]).astype(BF16)
 
 
 def sum_kernel(*refs):
@@ -192,6 +193,7 @@
             [(each, points)] * n_row,
             [
                 pltpu.VMEM((n_row * owned, each, slice_rows), F32),
+                pltpu.VMEM((n_row * owned, each, slice_rows), F32),
                 pltpu.VMEM((n_layer * CODE_ROWS, LANES), jnp.int32),
                 pltpu.SMEM((n_layer * CODE_ROWS, LANES), jnp.int32),
                 pltpu.SemaphoreType.DMA,

time: 69.4 us -> 69.5 us (level)
  no operation moved by 1% of the time
where the time goes in v13:
time: 69.5 us; the launch traced here: 69.3 us
  starting transfers between devices  27.7 us (40%)
  waiting for transfers between devices  26.3 us (38%)
  Pallas kernels  11.2 us (16%)
  local copies, waits for them, and re-layouts  2.29 us (3%)
  other arithmetic  1.7 us (2%)
    ppermute x24, starting transfers between devices, trade(): lax.ppermute(chunk, axis, [(j, j ^ k) for j in range(lax.axis_size(axis))])  27.7 us
    ppermute x24, waiting for transfers between devices, trade(): lax.ppermute(chunk, axis, [(j, j ^ k) for j in range(lax.axis_size(axis))])  26.3 us
    pallas_call x9, Pallas kernels, call(): pl.pallas_call(body, out_shape=[jax.ShapeDtypeStruct(shape, BF16) for sha...  11.2 us
    unnamed x6, local copies, waits for them, and re-layouts  2.29 us
  transfers between devices with their start and end apart: 24, of which 9 were waited for; matrix products, arithmetic and copies ran while one was open for 0% of the time, Pallas kernels for 15%

profile of v13, /device:TPU:0, one launch (start us, length us, event | category | flops | bytes accessed | tf_op | source)
XLA Modules:
  0.0 69.3 jit_solution(17482941529584526351)
XLA Ops:
  0.9 1.3 %copy-done.1 = bf16[1,2048,256]{2,1,0:T(8,128)(2,1)S(1)} copy-done((bf16[1,2048,256]{2,1,0:T(8,128)(2,1)S(1)}, bf16[1,2048,256]{2,1,0:T(8,128)(2,1)}, u32[]{:S(2)}) %copy-start.1) | copy-done | bytes 1048600
  2.7 2.4 %collective-permute-start = (bf16[32,2176]{1,0:T(8,128)(2,1)S(1)}, bf16[32,2176]{1,0:T(8,128)(2,1)S(1)}, u32[]{:S(2)}, u32[]{:S(2)}) collective-permute-start(bf16[32,2176]{1,0:T(8,128)(2,1)S(1)} %get-tuple-element.48), channel_id=1, source_target_pairs={{0,3},{1,2},{2,1},{3,0},{4,7},{5,6},{6,5},{7,4},{8,11},{9,10},{10,... | collective-permute-start | bytes 417800 | tf_op jit(solution)/shard_map/ppermute | solution.py:125
  6.3 0.9 %copy-done.2 = bf16[16,128,64]{1,2,0:T(8,128)(2,1)S(1)} copy-done((bf16[16,128,64]{1,2,0:T(8,128)(2,1)S(1)}, bf16[16,128,64]{1,2,0:T(8,128)(2,1)}, u32[]{:S(2)}) %copy-start.2) | copy-done | bytes 262168
  7.5 1.7 %collective-permute-done.refs_2_.refs_6_ = bf16[32,2176]{1,0:T(8,128)(2,1)S(1)} collective-permute-done((bf16[32,2176]{1,0:T(8,128)(2,1)S(1)}, bf16[32,2176]{1,0:T(8,128)(2,1)S(1)}, u32[]{:S(2)}, u32[]{:S(2)}) %collective-permute-start) | collective-permute-done | bytes 139296 | tf_op jit(solution)/shard_map/ppermute | solution.py:125
  9.2 2.2 %collective-permute-start.3 = (bf16[32,2048]{1,0:T(8,128)(2,1)S(1)}, bf16[32,2048]{1,0:T(8,128)(2,1)S(1)}, u32[]{:S(2)}, u32[]{:S(2)}) collective-permute-start(bf16[32,2048]{1,0:T(8,128)(2,1)S(1)} %get-tuple-element.54), channel_id=1, source_target_pairs={{0,3},{1,2},{2,1},{3,0},{4,7},{5,6},{6,5},{7,4},{8,11},{9,10},{10,... | collective-permute-start | bytes 393224 | tf_op jit(solution)/shard_map/ppermute | solution.py:125
  12.4 2.7 %shard_map.76 = (bf16[32,2048]{1,0:T(8,128)(2,1)S(1)}, bf16[32,2048]{1,0:T(8,128)(2,1)S(1)}, bf16[32,2048]{1,0:T(8,128)(2,1)S(1)}, bf16[32,2048]{1,0:T(8,128)(2,1)S(1)}) custom-call(bf16[32,128,128]{2,1,0:T(8,128)(2,1)S(1)} %shard_map.75.refs_0_, bf16[32,2176]{1,0:T(8,128)(2,1)S(1)} %get-tuple-element.43.refs_2_.refs_1_.refs_5_, ...), custom_call_target="tpu_custom_call" | custom-call | tf_op jit(solution)/shard_map/pallas_call | solution.py:143
  15.0 4.5 %collective-permute-start.6 = (bf16[32,2048]{1,0:T(8,128)(2,1)S(1)}, bf16[32,2048]{1,0:T(8,128)(2,1)S(1)}, u32[]{:S(2)}, u32[]{:S(2)}) collective-permute-start(bf16[32,2048]{1,0:T(8,128)(2,1)S(1)} %get-tuple-element.62), channel_id=1, source_target_pairs={{0,12},{4,8},{8,4},{12,0},{1,13},{5,9},{9,5},{13,1},{2,14},{6,10},... | collective-permute-start | bytes 393224 | tf_op jit(solution)/shard_map/ppermute | solution.py:125
  20.2 2.7 %shard_map.77 = (bf16[32,2048]{1,0:T(8,128)(2,1)S(1)}, bf16[32,2048]{1,0:T(8,128)(2,1)S(1)}, bf16[32,2048]{1,0:T(8,128)(2,1)S(1)}, bf16[32,2048]{1,0:T(8,128)(2,1)S(1)}) custom-call(bf16[32,128,128]{2,1,0:T(8,128)(2,1)S(1)} %shard_map.75.refs_0_, bf16[32,2176]{1,0:T(8,128)(2,1)S(1)} %get-tuple-element.43.refs_2_.refs_1_.refs_5_, ...), custom_call_target="tpu_custom_call" | custom-call | tf_op jit(solution)/shard_map/pallas_call | solution.py:143
  22.8 1.1 %collective-permute-done.6.refs_1_ = bf16[32,2048]{1,0:T(8,128)(2,1)S(1)} collective-permute-done((bf16[32,2048]{1,0:T(8,128)(2,1)S(1)}, bf16[32,2048]{1,0:T(8,128)(2,1)S(1)}, u32[]{:S(2)}, u32[]{:S(2)}) %collective-permute-start.6) | collective-permute-done | bytes 131104 | tf_op jit(solution)/shard_map/ppermute | solution.py:125
  23.9 6.9 %collective-permute-done.7.refs_2_ = bf16[32,2048]{1,0:T(8,128)(2,1)S(1)} collective-permute-done((bf16[32,2048]{1,0:T(8,128)(2,1)S(1)}, bf16[32,2048]{1,0:T(8,128)(2,1)S(1)}, u32[]{:S(2)}, u32[]{:S(2)}) %collective-permute-start.7) | collective-permute-done | bytes 131104 | tf_op jit(solution)/shard_map/ppermute | solution.py:125
  30.8 2.6 %collective-permute-start.12 = (bf16[32,2048]{1,0:T(8,128)(2,1)S(1)}, bf16[32,2048]{1,0:T(8,128)(2,1)S(1)}, u32[]{:S(2)}, u32[]{:S(2)}) collective-permute-start(bf16[32,2048]{1,0:T(8,128)(2,1)S(1)} %get-tuple-element.70), channel_id=1, source_target_pairs={{0,12},{4,8},{8,4},{12,0},{1,13},{5,9},{9,5},{13,1},{2,14},{6,10},... | collective-permute-start | bytes 393224 | tf_op jit(solution)/shard_map/ppermute | solution.py:125
  33.5 1.7 %collective-permute-start.14 = (bf16[32,2048]{1,0:T(8,128)(2,1)S(1)}, bf16[32,2048]{1,0:T(8,128)(2,1)S(1)}, u32[]{:S(2)}, u32[]{:S(2)}) collective-permute-start(bf16[32,2048]{1,0:T(8,128)(2,1)S(1)} %get-tuple-element.72), channel_id=1, source_target_pairs={{0,4},{4,0},{8,12},{12,8},{1,5},{5,1},{9,13},{13,9},{2,6},{6,2},{1... | collective-permute-start | bytes 393224 | tf_op jit(solution)/shard_map/ppermute | solution.py:125
  35.4 1.6 %collective-permute-start.10 = (bf16[32,2048]{1,0:T(8,128)(2,1)S(1)}, bf16[32,2048]{1,0:T(8,128)(2,1)S(1)}, u32[]{:S(2)}, u32[]{:S(2)}) collective-permute-start(bf16[32,2048]{1,0:T(8,128)(2,1)S(1)} %shard_map.78.refs_4_), channel_id=1, source_target_pairs={{0,2},{1,3},{2,0},{3,1},{4,6},{5,7},{6,4},{7,5},{8,10},{9,11},{10,... | collective-permute-start | bytes 393224 | tf_op jit(solution)/shard_map/ppermute | solution.py:125
  37.0 2.1 %collective-permute-done.12.refs_1_ = bf16[32,2048]{1,0:T(8,128)(2,1)S(1)} collective-permute-done((bf16[32,2048]{1,0:T(8,128)(2,1)S(1)}, bf16[32,2048]{1,0:T(8,128)(2,1)S(1)}, u32[]{:S(2)}, u32[]{:S(2)}) %collective-permute-start.12) | collective-permute-done | bytes 131104 | tf_op jit(solution)/shard_map/ppermute | solution.py:125
  39.1 4.5 %collective-permute-done.13.refs_2_ = bf16[32,2048]{1,0:T(8,128)(2,1)S(1)} collective-permute-done((bf16[32,2048]{1,0:T(8,128)(2,1)S(1)}, bf16[32,2048]{1,0:T(8,128)(2,1)S(1)}, u32[]{:S(2)}, u32[]{:S(2)}) %collective-permute-start.13) | collective-permute-done | bytes 131104 | tf_op jit(solution)/shard_map/ppermute | solution.py:125
  43.6 0.9 %collective-permute-start.20 = (bf16[32,2048]{1,0:T(8,128)(2,1)S(1)}, bf16[32,2048]{1,0:T(8,128)(2,1)S(1)}, u32[]{:S(2)}, u32[]{:S(2)}) collective-permute-start(bf16[32,2048]{1,0:T(8,128)(2,1)S(1)} %shard_map.79.refs_5_.refs_4_), channel_id=1, source_target_pairs={{0,3},{1,2},{2,1},{3,0},{4,7},{5,6},{6,5},{7,4},{8,11},{9,10},{10,... | collective-permute-start | bytes 393224 | tf_op jit(solution)/shard_map/ppermute | solution.py:125
  45.5 2.3 %shard_map.80 = (bf16[32,1650]{1,0:T(8,128)(2,1)S(1)}, bf16[32,1650]{1,0:T(8,128)(2,1)S(1)}, bf16[32,1650]{1,0:T(8,128)(2,1)S(1)}, bf16[32,1650]{1,0:T(8,128)(2,1)S(1)}) custom-call(bf16[1650,2048]{1,0:T(8,128)(2,1)S(1)} %bitcast.4, bf16[32,2048]{1,0:T(8,128)(2,1)S(1)} %collective-permute-done.9.refs_1_, ...), custom_call_target="tpu_custom_call" | custom-call | tf_op jit(solution)/shard_map/pallas_call | solution.py:143
  47.8 1.9 %collective-permute-start.15 = (bf16[32,1650]{1,0:T(8,128)(2,1)S(1)}, bf16[32,1650]{1,0:T(8,128)(2,1)S(1)}, u32[]{:S(2)}, u32[]{:S(2)}) collective-permute-start(bf16[32,1650]{1,0:T(8,128)(2,1)S(1)} %get-tuple-element.74), channel_id=1, source_target_pairs={{0,12},{4,8},{8,4},{12,0},{1,13},{5,9},{9,5},{13,1},{2,14},{6,10},... | collective-permute-start | bytes 316808 | tf_op jit(solution)/shard_map/ppermute | solution.py:125
  49.7 2.5 %collective-permute-start.17 = (bf16[32,1650]{1,0:T(8,128)(2,1)S(1)}, bf16[32,1650]{1,0:T(8,128)(2,1)S(1)}, u32[]{:S(2)}, u32[]{:S(2)}) collective-permute-start(bf16[32,1650]{1,0:T(8,128)(2,1)S(1)} %get-tuple-element.76), channel_id=1, source_target_pairs={{0,4},{4,0},{8,12},{12,8},{1,5},{5,1},{9,13},{13,9},{2,6},{6,2},{1... | collective-permute-start | bytes 316808 | tf_op jit(solution)/shard_map/ppermute | solution.py:125
  52.3 2.3 %shard_map.81 = (bf16[32,1650]{1,0:T(8,128)(2,1)S(1)}, bf16[32,1650]{1,0:T(8,128)(2,1)S(1)}, bf16[32,1650]{1,0:T(8,128)(2,1)S(1)}, bf16[32,1650]{1,0:T(8,128)(2,1)S(1)}) custom-call(bf16[1650,2048]{1,0:T(8,128)(2,1)S(1)} %bitcast.5, bf16[32,2048]{1,0:T(8,128)(2,1)S(1)} %collective-permute-done.18.refs_1_, ...), custom_call_target="tpu_custom_call" | custom-call | tf_op jit(solution)/shard_map/pallas_call | solution.py:143
  54.5 1.9 %collective-permute-start.21 = (bf16[32,1650]{1,0:T(8,128)(2,1)S(1)}, bf16[32,1650]{1,0:T(8,128)(2,1)S(1)}, u32[]{:S(2)}, u32[]{:S(2)}) collective-permute-start(bf16[32,1650]{1,0:T(8,128)(2,1)S(1)} %get-tuple-element.78), channel_id=1, source_target_pairs={{0,12},{4,8},{8,4},{12,0},{1,13},{5,9},{9,5},{13,1},{2,14},{6,10},... | collective-permute-start | bytes 316808 | tf_op jit(solution)/shard_map/ppermute | solution.py:125
  56.5 2.5 %collective-permute-start.23 = (bf16[32,1650]{1,0:T(8,128)(2,1)S(1)}, bf16[32,1650]{1,0:T(8,128)(2,1)S(1)}, u32[]{:S(2)}, u32[]{:S(2)}) collective-permute-start(bf16[32,1650]{1,0:T(8,128)(2,1)S(1)} %get-tuple-element.80), channel_id=1, source_target_pairs={{0,4},{4,0},{8,12},{12,8},{1,5},{5,1},{9,13},{13,9},{2,6},{6,2},{1... | collective-permute-start | bytes 316808 | tf_op jit(solution)/shard_map/ppermute | solution.py:125
  59.8 2.5 %collective-permute-done.21 = bf16[32,1650]{1,0:T(8,128)(2,1)S(1)} collective-permute-done((bf16[32,1650]{1,0:T(8,128)(2,1)S(1)}, bf16[32,1650]{1,0:T(8,128)(2,1)S(1)}, u32[]{:S(2)}, u32[]{:S(2)}) %collective-permute-start.21) | collective-permute-done | bytes 105632 | tf_op jit(solution)/shard_map/ppermute | solution.py:125
  62.3 6.2 %collective-permute-done.22 = bf16[32,1650]{1,0:T(8,128)(2,1)S(1)} collective-permute-done((bf16[32,1650]{1,0:T(8,128)(2,1)S(1)}, bf16[32,1650]{1,0:T(8,128)(2,1)S(1)}, u32[]{:S(2)}, u32[]{:S(2)}) %collective-permute-start.22) | collective-permute-done | bytes 105632 | tf_op jit(solution)/shard_map/ppermute | solution.py:125
  (43 shorter events, 7.2 us)
Async XLA Ops:
  2.7 6.5 %collective-permute-start = (bf16[32,2176]{1,0:T(8,128)(2,1)S(1)}, bf16[32,2176]{1,0:T(8,128)(2,1)S(1)}, u32[]{:S(2)}, u32[]{:S(2)}) collective-permute-start(bf16[32,2176]{1,0:T(8,128)(2,1)S(1)} %get-tuple-element.48), channel_id=1, source_target_pairs={{0,3},{1,2},{2,1},{3,0},{4,7},{5,6},{6,5},{7,4},{8,11},{9,10},{10,... | collective-permute-start | bytes 417800 | tf_op jit(solution)/shard_map/ppermute | solution.py:125
  5.1 7.2 %collective-permute-start.1 = (bf16[32,2176]{1,0:T(8,128)(2,1)S(1)}, bf16[32,2176]{1,0:T(8,128)(2,1)S(1)}, u32[]{:S(2)}, u32[]{:S(2)}) collective-permute-start(bf16[32,2176]{1,0:T(8,128)(2,1)S(1)} %get-tuple-element.51), channel_id=1, source_target_pairs={{0,2},{1,3},{2,0},{3,1},{4,6},{5,7},{6,4},{7,5},{8,10},{9,11},{10,... | collective-permute-start | bytes 417800 | tf_op jit(solution)/shard_map/ppermute | solution.py:125
  5.8 6.6 %collective-permute-start.2 = (bf16[32,2176]{1,0:T(8,128)(2,1)S(1)}, bf16[32,2176]{1,0:T(8,128)(2,1)S(1)}, u32[]{:S(2)}, u32[]{:S(2)}) collective-permute-start(bf16[32,2176]{1,0:T(8,128)(2,1)S(1)} %get-tuple-element.52), channel_id=1, source_target_pairs={{0,1},{1,0},{2,3},{3,2},{4,5},{5,4},{6,7},{7,6},{8,9},{9,8},{10,11... | collective-permute-start | bytes 417800 | tf_op jit(solution)/shard_map/ppermute | solution.py:125
  9.2 10.3 %collective-permute-start.3 = (bf16[32,2048]{1,0:T(8,128)(2,1)S(1)}, bf16[32,2048]{1,0:T(8,128)(2,1)S(1)}, u32[]{:S(2)}, u32[]{:S(2)}) collective-permute-start(bf16[32,2048]{1,0:T(8,128)(2,1)S(1)} %get-tuple-element.54), channel_id=1, source_target_pairs={{0,3},{1,2},{2,1},{3,0},{4,7},{5,6},{6,5},{7,4},{8,11},{9,10},{10,... | collective-permute-start | bytes 393224 | tf_op jit(solution)/shard_map/ppermute | solution.py:125
  11.4 8.8 %collective-permute-start.4 = (bf16[32,2048]{1,0:T(8,128)(2,1)S(1)}, bf16[32,2048]{1,0:T(8,128)(2,1)S(1)}, u32[]{:S(2)}, u32[]{:S(2)}) collective-permute-start(bf16[32,2048]{1,0:T(8,128)(2,1)S(1)} %get-tuple-element.55), channel_id=1, source_target_pairs={{0,2},{1,3},{2,0},{3,1},{4,6},{5,7},{6,4},{7,5},{8,10},{9,11},{10,... | collective-permute-start | bytes 393224 | tf_op jit(solution)/shard_map/ppermute | solution.py:125
  11.7 8.5 %collective-permute-start.5 = (bf16[32,2048]{1,0:T(8,128)(2,1)S(1)}, bf16[32,2048]{1,0:T(8,128)(2,1)S(1)}, u32[]{:S(2)}, u32[]{:S(2)}) collective-permute-start(bf16[32,2048]{1,0:T(8,128)(2,1)S(1)} %get-tuple-element.56), channel_id=1, source_target_pairs={{0,1},{1,0},{2,3},{3,2},{4,5},{5,4},{6,7},{7,6},{8,9},{9,8},{10,11... | collective-permute-start | bytes 393224 | tf_op jit(solution)/shard_map/ppermute | solution.py:125
  15.0 8.9 %collective-permute-start.6 = (bf16[32,2048]{1,0:T(8,128)(2,1)S(1)}, bf16[32,2048]{1,0:T(8,128)(2,1)S(1)}, u32[]{:S(2)}, u32[]{:S(2)}) collective-permute-start(bf16[32,2048]{1,0:T(8,128)(2,1)S(1)} %get-tuple-element.62), channel_id=1, source_target_pairs={{0,12},{4,8},{8,4},{12,0},{1,13},{5,9},{9,5},{13,1},{2,14},{6,10},... | collective-permute-start | bytes 393224 | tf_op jit(solution)/shard_map/ppermute | solution.py:125
  19.5 11.3 %collective-permute-start.7 = (bf16[32,2048]{1,0:T(8,128)(2,1)S(1)}, bf16[32,2048]{1,0:T(8,128)(2,1)S(1)}, u32[]{:S(2)}, u32[]{:S(2)}) collective-permute-start(bf16[32,2048]{1,0:T(8,128)(2,1)S(1)} %get-tuple-element.63), channel_id=1, source_target_pairs={{0,8},{4,12},{8,0},{12,4},{1,9},{5,13},{9,1},{13,5},{2,10},{6,14},... | collective-permute-start | bytes 393224 | tf_op jit(solution)/shard_map/ppermute | solution.py:125
  19.5 11.3 %collective-permute-start.8 = (bf16[32,2048]{1,0:T(8,128)(2,1)S(1)}, bf16[32,2048]{1,0:T(8,128)(2,1)S(1)}, u32[]{:S(2)}, u32[]{:S(2)}) collective-permute-start(bf16[32,2048]{1,0:T(8,128)(2,1)S(1)} %get-tuple-element.64), channel_id=1, source_target_pairs={{0,4},{4,0},{8,12},{12,8},{1,5},{5,1},{9,13},{13,9},{2,6},{6,2},{1... | collective-permute-start | bytes 393224 | tf_op jit(solution)/shard_map/ppermute | solution.py:125
  30.8 8.2 %collective-permute-start.12 = (bf16[32,2048]{1,0:T(8,128)(2,1)S(1)}, bf16[32,2048]{1,0:T(8,128)(2,1)S(1)}, u32[]{:S(2)}, u32[]{:S(2)}) collective-permute-start(bf16[32,2048]{1,0:T(8,128)(2,1)S(1)} %get-tuple-element.70), channel_id=1, source_target_pairs={{0,12},{4,8},{8,4},{12,0},{1,13},{5,9},{9,5},{13,1},{2,14},{6,10},... | collective-permute-start | bytes 393224 | tf_op jit(solution)/shard_map/ppermute | solution.py:125
  33.5 10.0 %collective-permute-start.13 = (bf16[32,2048]{1,0:T(8,128)(2,1)S(1)}, bf16[32,2048]{1,0:T(8,128)(2,1)S(1)}, u32[]{:S(2)}, u32[]{:S(2)}) collective-permute-start(bf16[32,2048]{1,0:T(8,128)(2,1)S(1)} %get-tuple-element.71), channel_id=1, source_target_pairs={{0,8},{4,12},{8,0},{12,4},{1,9},{5,13},{9,1},{13,5},{2,10},{6,14},... | collective-permute-start | bytes 393224 | tf_op jit(solution)/shard_map/ppermute | solution.py:125
  33.5 10.0 %collective-permute-start.14 = (bf16[32,2048]{1,0:T(8,128)(2,1)S(1)}, bf16[32,2048]{1,0:T(8,128)(2,1)S(1)}, u32[]{:S(2)}, u32[]{:S(2)}) collective-permute-start(bf16[32,2048]{1,0:T(8,128)(2,1)S(1)} %get-tuple-element.72), channel_id=1, source_target_pairs={{0,4},{4,0},{8,12},{12,8},{1,5},{5,1},{9,13},{13,9},{2,6},{6,2},{1... | collective-permute-start | bytes 393224 | tf_op jit(solution)/shard_map/ppermute | solution.py:125
  35.3 10.0 %collective-permute-start.11 = (bf16[32,2048]{1,0:T(8,128)(2,1)S(1)}, bf16[32,2048]{1,0:T(8,128)(2,1)S(1)}, u32[]{:S(2)}, u32[]{:S(2)}) collective-permute-start(bf16[32,2048]{1,0:T(8,128)(2,1)S(1)} %shard_map.78.refs_4_), channel_id=1, source_target_pairs={{0,3},{1,2},{2,1},{3,0},{4,7},{5,6},{6,5},{7,4},{8,11},{9,10},{10,... | collective-permute-start | bytes 393224 | tf_op jit(solution)/shard_map/ppermute | solution.py:125
  35.4 10.2 %collective-permute-start.10 = (bf16[32,2048]{1,0:T(8,128)(2,1)S(1)}, bf16[32,2048]{1,0:T(8,128)(2,1)S(1)}, u32[]{:S(2)}, u32[]{:S(2)}) collective-permute-start(bf16[32,2048]{1,0:T(8,128)(2,1)S(1)} %shard_map.78.refs_4_), channel_id=1, source_target_pairs={{0,2},{1,3},{2,0},{3,1},{4,6},{5,7},{6,4},{7,5},{8,10},{9,11},{10,... | collective-permute-start | bytes 393224 | tf_op jit(solution)/shard_map/ppermute | solution.py:125
  39.0 6.5 %collective-permute-start.9 = (bf16[32,2048]{1,0:T(8,128)(2,1)S(1)}, bf16[32,2048]{1,0:T(8,128)(2,1)S(1)}, u32[]{:S(2)}, u32[]{:S(2)}) collective-permute-start(bf16[32,2048]{1,0:T(8,128)(2,1)S(1)} %shard_map.78.refs_4_), channel_id=1, source_target_pairs={{0,1},{1,0},{2,3},{3,2},{4,5},{5,4},{6,7},{7,6},{8,9},{9,8},{10,11... | collective-permute-start | bytes 393224 | tf_op jit(solution)/shard_map/ppermute | solution.py:125
  43.6 6.2 %collective-permute-start.20 = (bf16[32,2048]{1,0:T(8,128)(2,1)S(1)}, bf16[32,2048]{1,0:T(8,128)(2,1)S(1)}, u32[]{:S(2)}, u32[]{:S(2)}) collective-permute-start(bf16[32,2048]{1,0:T(8,128)(2,1)S(1)} %shard_map.79.refs_5_.refs_4_), channel_id=1, source_target_pairs={{0,3},{1,2},{2,1},{3,0},{4,7},{5,6},{6,5},{7,4},{8,11},{9,10},{10,... | collective-permute-start | bytes 393224 | tf_op jit(solution)/shard_map/ppermute | solution.py:125
  44.5 7.8 %collective-permute-start.19 = (bf16[32,2048]{1,0:T(8,128)(2,1)S(1)}, bf16[32,2048]{1,0:T(8,128)(2,1)S(1)}, u32[]{:S(2)}, u32[]{:S(2)}) collective-permute-start(bf16[32,2048]{1,0:T(8,128)(2,1)S(1)} %shard_map.79.refs_5_.refs_4_), channel_id=1, source_target_pairs={{0,2},{1,3},{2,0},{3,1},{4,6},{5,7},{6,4},{7,5},{8,10},{9,11},{10,... | collective-permute-start | bytes 393224 | tf_op jit(solution)/shard_map/ppermute | solution.py:125
  45.2 7.0 %collective-permute-start.18 = (bf16[32,2048]{1,0:T(8,128)(2,1)S(1)}, bf16[32,2048]{1,0:T(8,128)(2,1)S(1)}, u32[]{:S(2)}, u32[]{:S(2)}) collective-permute-start(bf16[32,2048]{1,0:T(8,128)(2,1)S(1)} %shard_map.79.refs_5_.refs_4_), channel_id=1, source_target_pairs={{0,1},{1,0},{2,3},{3,2},{4,5},{5,4},{6,7},{7,6},{8,9},{9,8},{10,11... | collective-permute-start | bytes 393224 | tf_op jit(solution)/shard_map/ppermute | solution.py:125
  47.8 8.7 %collective-permute-start.15 = (bf16[32,1650]{1,0:T(8,128)(2,1)S(1)}, bf16[32,1650]{1,0:T(8,128)(2,1)S(1)}, u32[]{:S(2)}, u32[]{:S(2)}) collective-permute-start(bf16[32,1650]{1,0:T(8,128)(2,1)S(1)} %get-tuple-element.74), channel_id=1, source_target_pairs={{0,12},{4,8},{8,4},{12,0},{1,13},{5,9},{9,5},{13,1},{2,14},{6,10},... | collective-permute-start | bytes 316808 | tf_op jit(solution)/shard_map/ppermute | solution.py:125
  49.7 10.0 %collective-permute-start.16 = (bf16[32,1650]{1,0:T(8,128)(2,1)S(1)}, bf16[32,1650]{1,0:T(8,128)(2,1)S(1)}, u32[]{:S(2)}, u32[]{:S(2)}) collective-permute-start(bf16[32,1650]{1,0:T(8,128)(2,1)S(1)} %get-tuple-element.75), channel_id=1, source_target_pairs={{0,8},{4,12},{8,0},{12,4},{1,9},{5,13},{9,1},{13,5},{2,10},{6,14},... | collective-permute-start | bytes 316808 | tf_op jit(solution)/shard_map/ppermute | solution.py:125
  49.7 10.0 %collective-permute-start.17 = (bf16[32,1650]{1,0:T(8,128)(2,1)S(1)}, bf16[32,1650]{1,0:T(8,128)(2,1)S(1)}, u32[]{:S(2)}, u32[]{:S(2)}) collective-permute-start(bf16[32,1650]{1,0:T(8,128)(2,1)S(1)} %get-tuple-element.76), channel_id=1, source_target_pairs={{0,4},{4,0},{8,12},{12,8},{1,5},{5,1},{9,13},{13,9},{2,6},{6,2},{1... | collective-permute-start | bytes 316808 | tf_op jit(solution)/shard_map/ppermute | solution.py:125
  54.5 7.8 %collective-permute-start.21 = (bf16[32,1650]{1,0:T(8,128)(2,1)S(1)}, bf16[32,1650]{1,0:T(8,128)(2,1)S(1)}, u32[]{:S(2)}, u32[]{:S(2)}) collective-permute-start(bf16[32,1650]{1,0:T(8,128)(2,1)S(1)} %get-tuple-element.78), channel_id=1, source_target_pairs={{0,12},{4,8},{8,4},{12,0},{1,13},{5,9},{9,5},{13,1},{2,14},{6,10},... | collective-permute-start | bytes 316808 | tf_op jit(solution)/shard_map/ppermute | solution.py:125
  56.5 12.1 %collective-permute-start.22 = (bf16[32,1650]{1,0:T(8,128)(2,1)S(1)}, bf16[32,1650]{1,0:T(8,128)(2,1)S(1)}, u32[]{:S(2)}, u32[]{:S(2)}) collective-permute-start(bf16[32,1650]{1,0:T(8,128)(2,1)S(1)} %get-tuple-element.79), channel_id=1, source_target_pairs={{0,8},{4,12},{8,0},{12,4},{1,9},{5,13},{9,1},{13,5},{2,10},{6,14},... | collective-permute-start | bytes 316808 | tf_op jit(solution)/shard_map/ppermute | solution.py:125
  56.5 12.1 %collective-permute-start.23 = (bf16[32,1650]{1,0:T(8,128)(2,1)S(1)}, bf16[32,1650]{1,0:T(8,128)(2,1)S(1)}, u32[]{:S(2)}, u32[]{:S(2)}) collective-permute-start(bf16[32,1650]{1,0:T(8,128)(2,1)S(1)} %get-tuple-element.80), channel_id=1, source_target_pairs={{0,4},{4,0},{8,12},{12,8},{1,5},{5,1},{9,13},{13,9},{2,6},{6,2},{1... | collective-permute-start | bytes 316808 | tf_op jit(solution)/shard_map/ppermute | solution.py:125
  (3 other events, 47.8 us)
